TPU v7x, 128 devices: a whole 4x4x4 slice. The times are simulated.
128 devices in a mesh: grp: 2 (over core), vocab: 32 (over x, y_hi, z), tok: 2 (over y_lo).
Axes of the slice: x: 4, y: 4 (y_hi: 2, y_lo: 2; y = y_hi * 2 + y_lo), z: 4, core: 2. Of those that a mesh axis runs over, the one named last changes fastest.
Arguments:
- teacher_states: bfloat16 [256, 16384], P(('grp', 'vocab', 'tok')), may hold values from -80 to 80
- teacher_gain: bfloat16 [16384], replicated, may hold values from 0.5 to 1.5
- teacher_head: bfloat16 [16384, 64128], P(None, ('grp', 'vocab', 'tok')), may hold values from -30 to 30
- student_states: bfloat16 [256, 4096], P(('grp', 'vocab', 'tok')), may hold values from -80 to 80
- student_gain: bfloat16 [4096], replicated, may hold values from 0.5 to 1.5
- student_head: bfloat16 [4096, 64128], P(None, ('grp', 'vocab', 'tok')), may hold values from -30 to 30
- token_ids: int32 [256], replicated, may hold values from 0 to 64127
- ffn_gain: bfloat16 [4096], replicated, may hold values from 0.5 to 1.5
- gate_weight: bfloat16 [4096, 14336], P(None, ('grp', 'vocab', 'tok')), may hold values from -0.09375 to 0.09375
- up_weight: bfloat16 [4096, 14336], P(None, ('grp', 'vocab', 'tok')), may hold values from -0.09375 to 0.09375
- down_weight: bfloat16 [14336, 4096], P(('grp', 'vocab', 'tok')), may hold values from -0.046875 to 0.046875
- token_weight: float32 [256], replicated, may hold values from 300 to 3000
Outputs:
- divergence: float32 [256], replicated
- state_grad: float32 [256, 4096], P(('grp', 'vocab', 'tok'))
All inputs are finite; a program needn't handle non-finite values.
Results may differ from a plain program's by a relative error of at most 0.008.
Values may be sent and summed in bfloat16 or wider, within the bound.
No kernel may reach another device: no remote copies, remote signals or barrier semaphores. Data moves between devices by JAX's collectives and lax.ppermute only.
A program may use at most 128 MiB of HBM per device.

v0:
```python
import jax
import jax.numpy as jnp
from jax import lax
from jax.sharding import PartitionSpec as P

eps = 1e-05


def scaled_rows(values, gain):
    inverse = lax.rsqrt(jnp.mean(values * values, axis=-1, keepdims=True) + eps)
    return values * inverse * gain.astype(jnp.float32)


def norm_back(upstream, values, gain):
    inverse = lax.rsqrt(jnp.mean(values * values, axis=-1, keepdims=True) + eps)
    gained = upstream * gain.astype(jnp.float32)
    return inverse * gained - values * inverse**3 * jnp.mean(
        gained * values, axis=-1, keepdims=True
    )


def row_product(left, right):
    return lax.dot_general(
        left, right, (((1,), (1,)), ((), ())), preferred_element_type=jnp.float32
    )


def shards(
    teacher_states,
    teacher_gain,
    teacher_head,
    student_states,
    student_gain,
    student_head,
    token_ids,
    ffn_gain,
    gate_weight,
    up_weight,
    down_weight,
    token_weight,
):
    teacher_all, student_all = (
        lax.all_gather(teacher_states, ("grp", "vocab", "tok"), axis=0, tiled=True),
        lax.all_gather(student_states, ("grp", "vocab", "tok"), axis=0, tiled=True),
    )
    teacher_rows = scaled_rows(teacher_all.astype(jnp.float32), teacher_gain).astype(jnp.bfloat16)
    student_rows = scaled_rows(student_all.astype(jnp.float32), student_gain).astype(jnp.bfloat16)
    teacher_logits = jnp.dot(teacher_rows, teacher_head, preferred_element_type=jnp.float32)
    student_logits = jnp.dot(student_rows, student_head, preferred_element_type=jnp.float32)
    teacher_peak, student_peak = lax.pmax(
        (jnp.max(teacher_logits, axis=1), jnp.max(student_logits, axis=1)), ("grp", "vocab", "tok")
    )
    teacher_exp = jnp.exp(teacher_logits - teacher_peak[:, None])
    student_exp = jnp.exp(student_logits - student_peak[:, None])
    teacher_total, student_total, cross = lax.psum(
        (
            jnp.sum(teacher_exp, axis=1),
            jnp.sum(student_exp, axis=1),
            jnp.sum(teacher_exp * (teacher_logits - student_logits), axis=1),
        ),
        ("grp", "vocab", "tok"),
    )
    divergence = (
        cross / teacher_total
        - teacher_peak
        - jnp.log(teacher_total)
        + student_peak
        + jnp.log(student_total)
    )
    teacher_prob = teacher_exp / teacher_total[:, None]
    student_prob = student_exp / student_total[:, None]
    logit_grad = (token_weight[:, None] * (student_prob - teacher_prob)).astype(jnp.bfloat16)
    row_term = row_product(logit_grad, student_head)
    share = student_states.shape[0]
    device = lax.axis_index(("grp", "vocab", "tok"))
    first_row = device * share
    vocab_local = student_head.shape[1]
    local_ids = token_ids - device * vocab_local
    inside = (local_ids >= 0) & (local_ids < vocab_local)
    clipped = jnp.clip(local_ids, 0, vocab_local - 1)
    picked = jnp.take(student_head, clipped, axis=1).T.astype(jnp.float32)
    embed_term = jnp.where(inside[:, None], picked, 0.0)
    embedded, row_grad = lax.psum((embed_term, row_term), ("grp", "vocab", "tok"))
    final_grad = norm_back(row_grad, student_all.astype(jnp.float32), student_gain)
    ffn_rows = scaled_rows(embedded, ffn_gain).astype(jnp.bfloat16)
    final_half = final_grad.astype(jnp.bfloat16)
    final_own = lax.dynamic_slice_in_dim(final_grad, first_row, share, 0)
    embed_own = lax.dynamic_slice_in_dim(embedded, first_row, share, 0)
    gate = jnp.dot(ffn_rows, gate_weight, preferred_element_type=jnp.float32)
    upper = jnp.dot(ffn_rows, up_weight, preferred_element_type=jnp.float32)
    act_grad = row_product(final_half, down_weight)
    sigmoid_gate = jax.nn.sigmoid(gate)
    gate_grad = (act_grad * upper * sigmoid_gate * (1.0 + gate * (1.0 - sigmoid_gate))).astype(
        jnp.bfloat16
    )
    upper_grad = (act_grad * gate * sigmoid_gate).astype(jnp.bfloat16)
    ffn_own_grad = lax.psum_scatter(
        row_product(gate_grad, gate_weight) + row_product(upper_grad, up_weight),
        ("grp", "vocab", "tok"),
        scatter_dimension=0,
        tiled=True,
    )
    state_grad = final_own + norm_back(ffn_own_grad, embed_own, ffn_gain)
    return (divergence, state_grad)


def solution(mesh):
    in_specs = (
        P(("grp", "vocab", "tok"), None),
        P(),
        P(None, ("grp", "vocab", "tok")),
        P(("grp", "vocab", "tok"), None),
        P(),
        P(None, ("grp", "vocab", "tok")),
        P(),
        P(),
        P(None, ("grp", "vocab", "tok")),
        P(None, ("grp", "vocab", "tok")),
        P(("grp", "vocab", "tok"), None),
        P(),
    )
    out_specs = (P(), P(("grp", "vocab", "tok"), None))
    return jax.shard_map(shards, mesh=mesh, in_specs=in_specs, out_specs=out_specs, check_vma=False)
```

profile of v0, /device:TPU:0, one launch (start us, length us, event | category | flops | bytes accessed | tf_op | source)
XLA Modules:
  0.0 924.1 jit_solution(6477723950919831315)
XLA Ops:
  7.2 0.7 all-gather.7.cloned.1.call-update
  8.0 0.7 all-gather.5.cloned.1.call-update
  8.7 0.8 convert_element_type.44
  9.5 0.7 convert_element_type.47
  10.2 0.7 compare_and_fusion
  10.9 6.6 gather_fusion
  17.5 2.9 convert_select_fusion
  20.4 186.7 %all-gather.7.cloned.1.call-done = bf16[128,2,4096]{2,1,0:T(2,128)(2,1)} async-done(((bf16[1,2,4096]{2,1,0:T(2,128)(2,1)}), bf16[128,2,4096]{2,1,0:T(2,128)(2,1)}) %all-gather.7.cloned.1.call-update) | async-done | bytes 2097168 | tf_op jit(solution)/shard_map/all_gather | solution.py:44
  207.0 4.4 reshape.84
  211.5 2.7 multiply_reduce_fusion.3
  214.2 0.7 copy-done.1
  214.9 3.8 fusion.28
  218.7 191.9 %all-gather.5.cloned.1.call-done = bf16[128,2,16384]{2,1,0:T(2,128)(2,1)} async-done(((bf16[1,2,16384]{2,1,0:T(2,128)(2,1)}), bf16[128,2,16384]{2,1,0:T(2,128)(2,1)}) %all-gather.5.cloned.1.call-update) | async-done | bytes 8388624 | tf_op jit(solution)/shard_map/all_gather | solution.py:43
  410.6 14.0 %reshape.83 = f32[256,16384]{1,0:T(8,128)} reshape(bf16[128,2,16384]{2,1,0:T(2,128)(2,1)} %all-gather.5.cloned.1.call-done) | data formatting | bytes 25165824 | tf_op jit(solution)/shard_map/convert_element_type | solution.py:46
  424.6 7.0 multiply_reduce_fusion
  431.6 13.6 %fusion.27 = (f32[256]{0:T(256)S(1)}, f32[256,501]{0,1:T(8,128)S(1)}) fusion(bf16[16384,501]{0,1:T(8,128)(2,1)} %param.14, f32[256,16384]{1,0:T(8,128)} %reshape.83, f32[16384]{0:T(1024)S(1)} %convert_element_type.44, f32[256]{0:T(256)S(1)} %add_rsqrt_fusion.2), kind=kOutput, calls=%fused_computation.62 | convolution fusion | flops 4215403520 | bytes 33774592 | tf_op jit(solution)/shard_map/dot_general | solution.py:48
  445.2 63.0 %all-reduce.3 = (f32[256]{0:T(256)S(1)}, f32[256]{0:T(256)S(1)}) all-reduce(f32[256]{0:T(256)S(1)} %get-tuple-element.21, f32[256]{0:T(256)S(1)} %get-tuple-element.23), channel_id=1, replica_groups=mesh['grp'=2,'vocab'=32,'tok'=2] {'grp','vocab','tok'}, use_global_device_ids=true, to_apply=%region_2.0 | all-reduce | flops 512 | bytes 4096 | tf_op jit(solution)/shard_map/pmax | solution.py:50
  508.4 63.4 %all-reduce.1 = (f32[256]{0:T(256)S(1)}, f32[256]{0:T(256)S(1)}, f32[256]{0:T(256)S(1)}) all-reduce(f32[256]{0:T(256)S(1)} %get-tuple-element.6, f32[256]{0:T(256)S(1)} %get-tuple-element.5, f32[256]{0:T(256)S(1)} %get-tuple-element.4), channel_id=1, replica_groups=mesh['grp'=2,'vocab'=32,'tok'=2] {'grp','vocab','tok'}, use_global_device_ids=true, to_apply=%region_11.0 | all-reduce | flops 768 | bytes 6144 | tf_op jit(solution)/shard_map/psum | solution.py:55
  571.9 5.6 fusion.14
  578.1 157.4 %all-reduce.9.cloned.1.call-done = (f32[256,4096]{1,0:T(8,128)}, f32[256,4096]{1,0:T(8,128)}) async-done(((f32[256,4096]{1,0:T(8,128)}, f32[256,4096]{1,0:T(8,128)}), (f32[256,4096]{1,0:T(8,128)}, f32[256,4096]{1,0:T(8,128)})) %all-reduce.9.cloned.1.call-update) | async-done | bytes 8388624 | tf_op jit(solution)/shard_map/psum | solution.py:83
  735.6 2.7 multiply_reduce_fusion.1
  738.3 0.7 copy-done.2
  739.0 3.0 multiply_reduce_fusion.2
  742.5 4.4 multiply_convert_fusion.2
  746.9 1.9 copy-done.4
  748.8 2.0 fusion.4
  750.8 0.8 fusion.29
  751.7 5.7 fusion.11
  757.3 4.9 convolution_add_fusion
  762.8 151.8 %all-reduce.7.cloned.1.call-done = f32[256,4096]{1,0:T(8,128)} async-done(((f32[256,4096]{1,0:T(8,128)}), f32[256,4096]{1,0:T(8,128)}) %all-reduce.7.cloned.1.call-update) | async-done | bytes 4194320
  914.7 1.2 multiply_reduce_fusion.6
  915.9 1.7 subtract_add_fusion
  (29 shorter events, 2.1 us)
Async XLA Ops:
  7.2 744.5 %copy-start = (bf16[4096,112]{0,1:T(8,128)(2,1)S(1)}, bf16[4096,112]{0,1:T(8,128)(2,1)}, u32[]{:S(2)}) copy-start(bf16[4096,112]{0,1:T(8,128)(2,1)} %param.21) | copy-start | bytes 2752516
  7.2 199.8 %all-gather.7.cloned.1.call-start = ((), (), s32[]{:S(2)}) async-start(), calls=%async_computation.1 | async-start | bytes 2113536 | tf_op jit(solution)/shard_map/all_gather | solution.py:44
  7.9 402.7 %all-gather.5.cloned.1.call-start = ((), (), s32[]{:S(2)}) async-start(), calls=%async_computation | async-start | bytes 8454144 | tf_op jit(solution)/shard_map/all_gather | solution.py:43
  8.7 726.9 %all-reduce.9.cloned.1.call-start = ((), (), s32[]{:S(2)}) async-start(), calls=%async_computation.3 | async-start | bytes 16777216 | tf_op jit(solution)/shard_map/psum | solution.py:83
  211.5 3.4 copy-start.1
  431.6 140.3 %copy-start.7 = (f32[256]{0:T(256)S(1)}, f32[256]{0:T(256)}, u32[]{:S(2)}) copy-start(f32[256]{0:T(256)} %param.23) | copy-start | bytes 3076
  577.4 0.7 copy-start.6
  577.4 337.2 %all-reduce.7.cloned.1.call-start = ((), (), s32[]{:S(2)}) async-start(), calls=%async_computation.2 | async-start | bytes 8388608
  735.6 3.4 copy-start.2
  739.0 3.4 copy-start.3
  746.8 2.0 copy-start.4
  746.8 4.0 copy-start.5
Sparse Core Ops, SparseCore 0:
  9.7 197.2 all-gather.6
  208.7 201.8 all-gather.4
  577.6 157.9 all-reduce.8
  762.4 152.2 all-reduce.6
where the time goes:
time: 926 us; the launch traced here: 924 us
  waiting for transfers between devices  689 us (74%)
  blocking collectives  126 us (14%)
  matrix products  36.4 us (4%)
  local copies, waits for them, and re-layouts  29.5 us (3%)
  other arithmetic  28.6 us (3%)
  between operations  13.9 us (2%)
    all_gather x1, waiting for transfers between devices, shards(): lax.all_gather(teacher_states, ('grp', 'vocab', 'tok'), axis=0, tiled=True)  192 us
    all_gather x1, waiting for transfers between devices, shards(): lax.all_gather(student_states, ('grp', 'vocab', 'tok'), axis=0, tiled=True)  187 us
    psum x1, waiting for transfers between devices, shards(): lax.psum((embed_term, row_term), ('grp', 'vocab', 'tok'))  157 us
    unnamed x5, waiting for transfers between devices  153 us
    psum x1, blocking collectives, shards(): lax.psum((jnp.sum(teacher_exp, axis=1), jnp.sum(student_exp, axis=1), jnp...  63.4 us
    pmax x1, blocking collectives, shards(): lax.pmax((jnp.max(teacher_logits, axis=1), jnp.max(student_logits, axis=1...  63 us
  transfers between devices with their start and end apart: 4, of which 4 were waited for; matrix products, arithmetic and copies ran while one was open for 3% of the time, Pallas kernels for 0%

commit v1 on v0

v1 whole, which is shorter than its diff:
```python
import functools

import jax
import jax.numpy as jnp
from jax import lax
from jax.experimental import pallas as pl
from jax.experimental.pallas import tpu as pltpu
from jax.sharding import Mesh
from jax.sharding import PartitionSpec as P

eps = 1e-05
SHAPE = (2, 4, 2, 4, 2)
AXES = ("core", "x", "yh", "z", "yl")
CHIPS = AXES[1:]
CORES = 2
LIMIT = 40 * 1024 * 1024


def scaled_rows(values, gain):
    inverse = lax.rsqrt(jnp.mean(values * values, axis=-1, keepdims=True) + eps)
    return values * inverse * gain.astype(jnp.float32)


def norm_back(upstream, values, gain):
    inverse = lax.rsqrt(jnp.mean(values * values, axis=-1, keepdims=True) + eps)
    gained = upstream * gain.astype(jnp.float32)
    return inverse * gained - values * inverse**3 * jnp.mean(
        gained * values, axis=-1, keepdims=True
    )


def row_product(left, right):
    return lax.dot_general(
        left, right, (((1,), (1,)), ((), ())), preferred_element_type=jnp.float32
    )


def swap_cores(values):
    return lax.ppermute(values, "core", [(0, 1), (1, 0)])


def exchange(blocks, axes):
    return lax.all_to_all(blocks, axes, split_axis=0, concat_axis=0, tiled=True)


def rows_kernel(
    core_ref, teacher_ref, teacher_gain, student_ref, student_gain, keep_ref, send_ref
):
    column = 0
    for values, gain in ((student_ref, student_gain), (teacher_ref, teacher_gain)):
        half = values.shape[1] // 2
        every = values[...].astype(jnp.float32)
        inverse = lax.rsqrt(jnp.mean(every * every, axis=-1, keepdims=True) + eps)
        for part, out in ((core_ref[0], keep_ref), (1 - core_ref[0], send_ref)):
            place = pl.ds(pl.multiple_of(part * half, half), half)
            rows = values[:, place].astype(jnp.float32) * inverse
            rows = rows * gain[:, place].astype(jnp.float32)
            out[:, column : column + half] = rows.astype(jnp.bfloat16)
        column = column + half


def spread_kernel(core_ref, keep_ref, came_ref, *out_refs):
    keep, came = keep_ref[...].astype(jnp.float32), came_ref[...].astype(jnp.float32)
    first = core_ref[0] == 0
    rows = jnp.concatenate([jnp.where(first, keep, came), jnp.where(first, came, keep)], axis=0)
    rows = rows.astype(jnp.bfloat16)
    column = 0
    for out in out_refs:
        width = out.shape[2]
        out[...] = jnp.broadcast_to(rows[None, :, column : column + width], out.shape)
        column = column + width


GROUPS = (
    ((0, 0, 2048), (1, 0, 1408)),
    ((1, 1408, 1152), (1, 2560, 1152), (1, 3712, 1152)),
    ((1, 4864, 1664), (1, 6528, 1664)),
)
WIDTHS = tuple(sum(p[2] for p in group) for group in GROUPS)


def group_order(group):
    place = lax.broadcasted_iota(jnp.int32, (256, 256), 1)
    source = lax.broadcasted_iota(jnp.int32, (256, 256), 0)
    x, yh, z, yl = (place >> 6) & 3, (place >> 5) & 1, (place >> 3) & 3, (place >> 2) & 1
    if group == 1:
        wanted = (z << 6) | (x << 4) | (yh << 3) | (yl << 2) | (place & 3)
    else:
        wanted = (yh << 7) | (yl << 6) | (x << 4) | (z << 2) | (place & 3)
    return (source == wanted).astype(jnp.bfloat16)


def reordered(values, group):
    moves = group_order(group)
    high = values.astype(jnp.bfloat16)
    rest = values - high.astype(jnp.float32)
    middle = rest.astype(jnp.bfloat16)
    low = (rest - middle.astype(jnp.float32)).astype(jnp.bfloat16)
    high, middle, low = (
        jnp.dot(part, moves, preferred_element_type=jnp.float32) for part in (high, middle, low)
    )
    return (high + middle) + low


def softmax_stats(teacher, student, stats_out):
    teacher_peak = jnp.max(teacher, axis=0, keepdims=True)
    student_peak = jnp.max(student, axis=0, keepdims=True)
    teacher_exp = jnp.exp(teacher - teacher_peak)
    teacher_total = jnp.sum(teacher_exp, axis=0, keepdims=True)
    student_total = jnp.sum(jnp.exp(student - student_peak), axis=0, keepdims=True)
    cross = jnp.sum(teacher_exp * (teacher - student), axis=0, keepdims=True)
    stats = (
        teacher_peak + jnp.log(teacher_total),
        student_peak + jnp.log(student_total),
        cross / teacher_total,
    )
    stats_out[...] = jnp.zeros_like(stats_out)
    for i, row in enumerate(stats):
        stats_out[i : i + 1, :] = row[:, :128]
        stats_out[i + 3 : i + 4, :] = row[:, 128:]


def logits_kernel(group, pieces, sums, stats, place_ref, *refs):
    piece_refs, refs = refs[:pieces], refs[pieces:]
    heads, refs = refs[:2], refs[2:]
    sum_refs, refs = refs[:sums], refs[sums:]
    student_out = None
    if group == 0:
        student_out, refs = refs[0], refs[1:]
    teacher_out, refs = refs[0], refs[1:]
    if stats:
        stats_out, refs = refs[0], refs[1:]
    rows, head, row_sems, head_sems = refs
    copies = []
    column = 0
    for i, (kind, start, width) in enumerate(GROUPS[group]):
        columns = slice(column, column + width)
        size = heads[kind].shape[1] // 2
        start = pl.multiple_of(place_ref[0] * size + start, 128)
        copy = pltpu.make_async_copy(
            heads[kind].at[:, pl.ds(start, width)], head.at[:, columns], head_sems.at[i]
        )
        copy.start()
        needed = [copy]
        for m, piece in enumerate(piece_refs):
            tokens = piece.shape[0]
            at = pl.multiple_of((place_ref[1] ^ m) * tokens, tokens)
            copy = pltpu.make_async_copy(
                piece.at[:, columns], rows.at[pl.ds(at, tokens), columns], row_sems.at[i, m]
            )
            copy.start()
            needed.append(copy)
        copies.append((kind, columns, needed))
        column = column + width
    teacher = None
    for kind, columns, needed in copies:
        for copy in needed:
            copy.wait()
        term = row_product(head[:, columns], rows[:, columns])
        if kind == 0:
            student_out[...] = sum_refs[1][...] + term if sums else term
        else:
            teacher = term if teacher is None else teacher + term
    if group > 0:
        teacher = reordered(teacher, group)
    if sums:
        teacher = sum_refs[0][...] + teacher
    teacher_out[...] = teacher
    if stats:
        softmax_stats(teacher, sum_refs[1][...], stats_out)


def logits_part(group, place, pieces, student_head_t, teacher_head_t, sums=(), stats=False):
    vocab, tokens, width = teacher_head_t.shape[0], 256, WIDTHS[group]
    shape = jax.ShapeDtypeStruct((vocab, tokens), jnp.float32)
    count = 2 if group == 0 else 1
    out_shape = [shape] * count
    if stats:
        out_shape = out_shape + [jax.ShapeDtypeStruct((8, 128), jnp.float32)]
    vmem, anywhere = pl.BlockSpec(memory_space=pltpu.VMEM), pl.BlockSpec(memory_space=pl.ANY)
    rows_shape = (tokens, width)
    scratch = [
        pltpu.VMEM((vocab, width), jnp.bfloat16),
        pltpu.SemaphoreType.DMA((len(GROUPS[group]), 4)),
        pltpu.SemaphoreType.DMA((len(GROUPS[group]),)),
    ]
    if len(pieces) > 1:
        out_shape = out_shape + [jax.ShapeDtypeStruct(rows_shape, jnp.bfloat16)]
    else:
        scratch = [pltpu.VMEM(rows_shape, jnp.bfloat16)] + scratch
    return pl.pallas_call(
        functools.partial(logits_kernel, group, len(pieces), len(sums), stats),
        in_specs=[pl.BlockSpec(memory_space=pltpu.SMEM)]
        + [anywhere] * (len(pieces) + 2)
        + [vmem] * len(sums),
        out_specs=[vmem] * len(out_shape),
        out_shape=out_shape,
        scratch_shapes=scratch,
        compiler_params=pltpu.CompilerParams(vmem_limit_bytes=LIMIT),
        cost_estimate=pl.CostEstimate(
            flops=2 * vocab * tokens * width,
            bytes_accessed=(vocab + tokens) * width * 2,
            transcendentals=0,
        ),
        name="logits",
    )(place, *pieces, student_head_t, teacher_head_t, *sums)


def one_hot_rows(core):
    place = lax.broadcasted_iota(jnp.int32, (256, 256), 0)
    column = lax.broadcasted_iota(jnp.int32, (256, 256), 1)
    source = (((place >> 1) & 63) << 2) | (((place >> 7) ^ core) << 1) | (place & 1)
    return (column == source).astype(jnp.bfloat16)


def row_grad_kernel(
    core_ref, every_ref, weight_ref, teacher_ref, student_ref, head_ref,
    own_ref, send_ref, divergence_ref, grad,
):
    @pl.when(pl.program_id(0) == 0)
    def _():
        every = every_ref[...]
        peak = jnp.max(every, axis=0)
        scaled = jnp.exp(every - peak[None])
        total = jnp.sum(scaled, axis=0)
        lse = peak + jnp.log(total)
        cross = jnp.sum(scaled * pltpu.roll(every, 6, 1), axis=0) / total
        teacher_lse = jnp.concatenate([lse[0:1], lse[3:4]], axis=1)
        student_lse = jnp.concatenate([lse[1:2], lse[4:5]], axis=1)
        divergence_ref[...] = (
            jnp.concatenate([cross[0:1], cross[3:4]], axis=1) - teacher_lse + student_lse
        )
        logit_grad = weight_ref[...] * (
            jnp.exp(student_ref[...] - student_lse) - jnp.exp(teacher_ref[...] - teacher_lse)
        )
        grad[...] = row_product(
            one_hot_rows(core_ref[0]), logit_grad.astype(jnp.bfloat16)
        ).astype(jnp.bfloat16)

    out = jnp.dot(grad[...], head_ref[...], preferred_element_type=jnp.float32)
    own_ref[...] = out[:128]
    send_ref[...] = out[128:].astype(jnp.bfloat16)


def row_grad_part(core, every, weight, teacher, student, student_head_t):
    vocab, width = student_head_t.shape
    tokens = weight.shape[1]
    columns = 1024
    return pl.pallas_call(
        row_grad_kernel,
        grid_spec=pltpu.PrefetchScalarGridSpec(
            num_scalar_prefetch=1,
            grid=(width // columns,),
            in_specs=[
                pl.BlockSpec(every.shape, lambda i, c: (0, 0, 0)),
                pl.BlockSpec(weight.shape, lambda i, c: (0, 0)),
                pl.BlockSpec(teacher.shape, lambda i, c: (0, 0)),
                pl.BlockSpec(student.shape, lambda i, c: (0, 0)),
                pl.BlockSpec((vocab, columns), lambda i, c: (0, i)),
            ],
            out_specs=[
                pl.BlockSpec((tokens // 2, columns), lambda i, c: (0, i)),
                pl.BlockSpec((tokens // 2, columns), lambda i, c: (0, i)),
                pl.BlockSpec((1, tokens), lambda i, c: (0, 0)),
            ],
            scratch_shapes=[pltpu.VMEM((tokens, vocab), jnp.bfloat16)],
        ),
        out_shape=[
            jax.ShapeDtypeStruct((tokens // 2, width), jnp.float32),
            jax.ShapeDtypeStruct((tokens // 2, width), jnp.bfloat16),
            jax.ShapeDtypeStruct((1, tokens), jnp.float32),
        ],
        compiler_params=pltpu.CompilerParams(vmem_limit_bytes=LIMIT),
        cost_estimate=pl.CostEstimate(
            flops=2 * vocab * tokens * width,
            bytes_accessed=vocab * width * 2 + tokens * width * 3,
            transcendentals=2 * vocab * tokens,
        ),
        name="row_grad",
    )(core, every, weight, teacher, student, student_head_t)


def gate_kernel(own_ref, other_ref, weight_ref, out_ref):
    out_ref[:, :128] = row_product(weight_ref[...], own_ref[...])
    out_ref[:, 128:] = row_product(weight_ref[...], other_ref[...])


def gate_part(own, other, weights_t):
    hidden, tokens = weights_t.shape[0], 2 * own.shape[0]
    return pl.pallas_call(
        gate_kernel,
        out_shape=jax.ShapeDtypeStruct((hidden, tokens), jnp.float32),
        compiler_params=pltpu.CompilerParams(vmem_limit_bytes=LIMIT),
        cost_estimate=pl.CostEstimate(
            flops=2 * hidden * tokens * own.shape[1],
            bytes_accessed=(hidden + tokens) * own.shape[1] * 2,
            transcendentals=0,
        ),
        name="gate_upper",
    )(own, other, weights_t)


def ffn_grad_kernel(own_ref, other_ref, down_ref, hidden_ref, weight_ref, own_out, send_out):
    units = down_ref.shape[0]
    act_grad = jnp.concatenate(
        [row_product(down_ref[...], own_ref[...]), row_product(down_ref[...], other_ref[...])],
        axis=1,
    )
    gate, upper = hidden_ref[:units, :], hidden_ref[units:, :]
    sigmoid_gate = jax.nn.sigmoid(gate)
    gate_grad = act_grad * upper * sigmoid_gate * (1.0 + gate * (1.0 - sigmoid_gate))
    upper_grad = act_grad * gate * sigmoid_gate
    grads = jnp.concatenate([gate_grad, upper_grad], axis=0).astype(jnp.bfloat16)
    tokens = grads.shape[1]
    same = lax.broadcasted_iota(jnp.int32, (tokens, tokens), 0) == lax.broadcasted_iota(
        jnp.int32, (tokens, tokens), 1
    )
    grads = row_product(same.astype(jnp.bfloat16), grads).astype(jnp.bfloat16)
    out = jnp.dot(grads, weight_ref[...], preferred_element_type=jnp.float32)
    own_out[...] = out[: tokens // 2]
    send_out[...] = out[tokens // 2 :].astype(jnp.bfloat16)


def ffn_grad_part(own, other, down, hidden, weights_t):
    rows, width = own.shape
    return pl.pallas_call(
        ffn_grad_kernel,
        out_shape=[
            jax.ShapeDtypeStruct((rows, width), jnp.float32),
            jax.ShapeDtypeStruct((rows, width), jnp.bfloat16),
        ],
        compiler_params=pltpu.CompilerParams(vmem_limit_bytes=LIMIT),
        cost_estimate=pl.CostEstimate(
            flops=12 * down.shape[0] * rows * width,
            bytes_accessed=(3 * down.shape[0] + 5 * rows) * width * 2,
            transcendentals=0,
        ),
        name="ffn_grad",
    )(own, other, down, hidden, weights_t)


def owned_sum(own, send):
    half = (own.astype(jnp.float32) + swap_cores(send).astype(jnp.float32)).astype(jnp.bfloat16)
    blocks = half.reshape(half.shape[0] // 2, 2, half.shape[1])
    return jnp.sum(exchange(blocks, CHIPS).astype(jnp.float32), axis=0)


def every_row(rows):
    chips = 64
    own = exchange(jnp.broadcast_to(rows[None], (chips,) + rows.shape), CHIPS)
    own = own.reshape(chips * rows.shape[0], rows.shape[1])
    return own, swap_cores(own)


def shards(
    teacher_states,
    teacher_gain,
    teacher_head,
    student_states,
    student_gain,
    student_head,
    token_ids,
    ffn_gain,
    gate_weight,
    up_weight,
    down_weight,
    token_weight,
):
    core = lax.axis_index("core")
    device = lax.axis_index(AXES)
    own_half = jnp.full((1,), core, jnp.int32)

    student_own = student_states.astype(jnp.float32)
    smem = pl.BlockSpec(memory_space=pltpu.SMEM)
    vmem = pl.BlockSpec(memory_space=pltpu.VMEM)
    width = sum(WIDTHS)
    half_shape = jax.ShapeDtypeStruct((2, width), jnp.bfloat16)
    keep, send = pl.pallas_call(
        rows_kernel,
        in_specs=[smem] + [vmem] * 4,
        out_shape=[half_shape, half_shape],
        name="rows",
    )(
        own_half,
        teacher_states,
        teacher_gain.reshape(1, -1),
        student_states,
        student_gain.reshape(1, -1),
    )
    came = swap_cores(send)
    spread = pl.pallas_call(
        spread_kernel,
        in_specs=[smem] + [vmem] * 2,
        out_shape=[jax.ShapeDtypeStruct((16, 4, w), jnp.bfloat16) for w in WIDTHS],
        name="spread",
    )(own_half, keep, came)
    planes = (("yh", "z", "yl"), ("x", "yh", "yl"), ("x", "z"))
    lines = ("x", "z", ("yh", "yl"))
    places = [lax.axis_index(line) for line in lines]
    pieces = []
    for blocks, plane, line in zip(spread, planes, lines):
        block = exchange(blocks, plane)
        block = block.reshape(block.shape[0] * block.shape[1], block.shape[2])
        pieces.append(
            [block]
            + [lax.ppermute(block, line, [(i, i ^ m) for i in range(4)]) for m in (1, 2, 3)]
        )

    vocab_local = student_head.shape[1]
    ids = token_ids.reshape(2, 128)
    ids = jnp.where(core == 0, ids, ids[::-1]).reshape(256) - device * vocab_local
    chosen = (ids[:, None] == jnp.arange(vocab_local)[None, :]).astype(jnp.bfloat16)
    picked = row_product(chosen, student_head).astype(jnp.bfloat16)
    embedded = owned_sum(picked[:128], picked[128:])
    ffn_rows = every_row(scaled_rows(embedded, ffn_gain).astype(jnp.bfloat16))
    weights_t = jnp.concatenate([gate_weight.T, up_weight.T], axis=0)
    hidden = gate_part(*ffn_rows, weights_t)

    heads = (student_head.T, teacher_head.T)
    place = [jnp.stack([core, p]).astype(jnp.int32) for p in places]
    student, teacher, assembled = logits_part(0, place[0], pieces[0], *heads)
    others = [swap_cores(assembled)]
    for g in (1, 2):
        teacher, assembled = logits_part(g, place[g], pieces[g], *heads, (teacher,))
        others.append(swap_cores(assembled))
    place = jnp.stack([1 - core, 0 * core]).astype(jnp.int32)
    student, teacher = logits_part(0, place, others[:1], *heads, (teacher, student))
    (teacher,) = logits_part(1, place, others[1:2], *heads, (teacher,))
    teacher, stats = logits_part(2, place, others[2:], *heads, (teacher, student), True)
    every = exchange(jnp.broadcast_to(stats[None], (128,) + stats.shape), AXES)
    weight = token_weight.reshape(2, 64, 2).transpose(1, 0, 2).reshape(1, 256)
    own, send, divergence = row_grad_part(
        own_half, every, weight, teacher, student, heads[0]
    )
    divergence = divergence.reshape(64, 2, 2).transpose(1, 0, 2).reshape(256)

    row_grad = owned_sum(own, send)
    final_grad = norm_back(row_grad, student_own, student_gain)
    final_half = every_row(final_grad.astype(jnp.bfloat16))
    ffn_grad = owned_sum(*ffn_grad_part(*final_half, down_weight, hidden, weights_t))
    state_grad = final_grad + norm_back(ffn_grad, embedded, ffn_gain)
    return (divergence, state_grad)


def solution(mesh):
    fine = Mesh(mesh.devices.reshape(SHAPE), AXES)
    in_specs = (
        P(AXES, None),
        P(),
        P(None, AXES),
        P(AXES, None),
        P(),
        P(None, AXES),
        P(),
        P(),
        P(None, AXES),
        P(None, AXES),
        P(AXES, None),
        P(),
    )
    out_specs = (P(), P(AXES, None))
    return jax.shard_map(shards, mesh=fine, in_specs=in_specs, out_specs=out_specs, check_vma=False)
```

time: 926 us -> 284 us (0.31)
  waiting for transfers between devices: 689 us -> 116 us
  blocking collectives: 126 us -> 17.8 us
  starting transfers between devices: 0.16 us -> 62.5 us
  Pallas kernels: 0 us -> 35.9 us
  matrix products: 36.4 us -> 4.88 us
  other arithmetic: 28.6 us -> 12.2 us
  between operations: 13.9 us -> 1.08 us
    all_gather x2 -> x0, waiting for transfers between devices: 379 us -> none  [the longest x1 192 us: shards(): lax.all_gather(teacher_states, ('grp', 'vocab', 'tok'), axis=0, tiled=True)]
    psum x1 -> x0, waiting for transfers between devices: 157 us -> none  [shards(): lax.psum((embed_term, row_term), ('grp', 'vocab', 'tok'))]
    unnamed x5 -> x0, waiting for transfers between devices: 153 us -> none
    all_to_all x0 -> x8, waiting for transfers between devices: none -> 110 us  [exchange(): return lax.all_to_all(blocks, axes, split_axis=0, concat_axis=0, tiled=True)]
    psum x1 -> x0, blocking collectives: 63.4 us -> none  [shards(): lax.psum((jnp.sum(teacher_exp, axis=1), jnp.sum(student_exp, axis=1), jnp...]
    pmax x1 -> x0, blocking collectives: 63 us -> none  [shards(): lax.pmax((jnp.max(teacher_logits, axis=1), jnp.max(student_logits, axis=1...]
    all_to_all x0 -> x8, starting transfers between devices: none -> 44.7 us  [exchange(): return lax.all_to_all(blocks, axes, split_axis=0, concat_axis=0, tiled=True)]
    pallas_call x0 -> x11, Pallas kernels: none -> 35.9 us  [the longest x6 25.7 us: logits_part(): pl.pallas_call(functools.partial(logits_kernel, group, len(pieces), len(s...]
  transfers between devices with their start and end apart: 4 -> 26, of which waited for: 4 -> 11; matrix products, arithmetic and copies ran while one was open for 3% -> 8% of each run, Pallas kernels for 0% -> 11%
where the time goes in v1:
time: 284 us; the launch traced here: 282 us
  waiting for transfers between devices  116 us (41%)
  starting transfers between devices  62.5 us (22%)
  Pallas kernels  35.9 us (13%)
  local copies, waits for them, and re-layouts  32.1 us (11%)
  blocking collectives  17.8 us (6%)
  other arithmetic  12.2 us (4%)
  matrix products  4.88 us (2%)
    all_to_all x8, waiting for transfers between devices, exchange(): return lax.all_to_all(blocks, axes, split_axis=0, concat_axis=0, tiled=True)  110 us
    all_to_all x8, starting transfers between devices, exchange(): return lax.all_to_all(blocks, axes, split_axis=0, concat_axis=0, tiled=True)  44.7 us
    pallas_call x6, Pallas kernels, logits_part(): pl.pallas_call(functools.partial(logits_kernel, group, len(pieces), len(s...  25.7 us
    all_to_all x1, blocking collectives, exchange(): return lax.all_to_all(blocks, axes, split_axis=0, concat_axis=0, tiled=True)  17.8 us
    ppermute x9, starting transfers between devices, shards(): lax.ppermute(block, line, [(i, i ^ m) for i in range(4)])  16 us
    unnamed x32, local copies, waits for them, and re-layouts  11.6 us
  transfers between devices with their start and end apart: 26, of which 11 were waited for; matrix products, arithmetic and copies ran while one was open for 8% of the time, Pallas kernels for 11%

profile of v1, /device:TPU:0, one launch (start us, length us, event | category | flops | bytes accessed | tf_op | source)
XLA Modules:
  0.0 282.3 jit_solution(5340519798649667044)
XLA Ops:
  9.1 17.8 %all_to_all.45 = bf16[16,4,3456]{2,1,0:T(4,128)(2,1)S(1)} all-to-all(bf16[16,4,3456]{2,1,0:T(4,128)(2,1)} %get-tuple-element.26), channel_id=1, replica_groups=mesh['core'=2,'x'=4,'yh'=2,'z'=4,'yl'=2] {'x','yh','yl'}, dimensions={0} | all-to-all | bytes 884736 | tf_op jit(solution)/shard_map/all_to_all | solution.py:43
  26.9 6.3 %all-to-all-start.2 = ((bf16[16,4,3456]{2,1,0:T(4,128)(2,1)}), bf16[16,4,3456]{2,1,0:T(4,128)(2,1)S(1)}, u32[]{:S(2)}, u32[]{:S(2)}) async-start(bf16[16,4,3456]{2,1,0:T(4,128)(2,1)} %get-tuple-element.27), calls=%async_computation.2 | async-start | bytes 884736 | tf_op jit(solution)/shard_map/all_to_all | solution.py:43
  35.3 7.5 %all-to-all-done.2 = bf16[16,4,3456]{2,1,0:T(4,128)(2,1)S(1)} async-done(((bf16[16,4,3456]{2,1,0:T(4,128)(2,1)}), bf16[16,4,3456]{2,1,0:T(4,128)(2,1)S(1)}, u32[]{:S(2)}, u32[]{:S(2)}) %all-to-all-start.2) | async-done | bytes 442400 | tf_op jit(solution)/shard_map/all_to_all | solution.py:43
  43.3 2.3 collective-permute-start.8
  47.8 4.2 %all-to-all-start = ((bf16[16,4,3328]{2,1,0:T(4,128)(2,1)}), bf16[16,4,3328]{2,1,0:T(4,128)(2,1)}, u32[]{:S(2)}, u32[]{:S(2)}) async-start(bf16[16,4,3328]{2,1,0:T(4,128)(2,1)} %get-tuple-element.25), calls=%async_computation | async-start | bytes 851968 | tf_op jit(solution)/shard_map/all_to_all | solution.py:43
  52.0 3.3 %collective-permute-start.5 = (bf16[64,3456]{1,0:T(8,128)(2,1)S(1)}, bf16[64,3456]{1,0:T(8,128)(2,1)S(1)}, u32[]{:S(2)}, u32[]{:S(2)}) collective-permute-start(bf16[64,3456]{1,0:T(8,128)(2,1)S(1)} %reshape.131.refs_0_), channel_id=1, source_target_pairs={{0,4},{2,6},{4,0},{6,2},{1,5},{3,7},{5,1},{7,3},{8,12},{10,14},{12... | collective-permute-start | bytes 1327112 | tf_op jit(solution)/shard_map/ppermute | solution.py:406
  56.4 13.6 %all-to-all-done = bf16[16,4,3328]{2,1,0:T(4,128)(2,1)} async-done(((bf16[16,4,3328]{2,1,0:T(4,128)(2,1)}), bf16[16,4,3328]{2,1,0:T(4,128)(2,1)}, u32[]{:S(2)}, u32[]{:S(2)}) %all-to-all-start) | async-done | bytes 426016 | tf_op jit(solution)/shard_map/all_to_all | solution.py:43
  71.5 2.5 collective-permute-start.2
  78.3 3.5 %logits.6 = (f32[501,256]{1,0:T(8,128)S(1)}, f32[501,256]{1,0:T(8,128)S(1)}, bf16[256,3456]{1,0:T(8,128)(2,1)}) custom-call(s32[2]{0:T(128)S(1)} %pad_add_fusion.3.place_ref, bf16[64,3456]{1,0:T(8,128)(2,1)S(1)} %reshape.132.refs_0_, bf16[64,3456]{1,0:T(8,128)(2,1)S(1)} %collective-permute-done.7.refs_1_, ...), custom_call_target="tpu_custom_call" | custom-call | flops 886505472 | bytes 5232384 | tf_op jit(solution)/shard_map/logits/pallas_call | solution.py:191
  82.6 4.5 %logits.7 = (f32[501,256]{1,0:T(8,128)S(1)}, bf16[256,3456]{1,0:T(8,128)(2,1)}) custom-call(s32[2]{0:T(128)S(1)} %pad_add_fusion.2.place_ref, bf16[64,3456]{1,0:T(8,128)(2,1)S(1)} %reshape.131.refs_0_, bf16[64,3456]{1,0:T(8,128)(2,1)S(1)} %collective-permute-done.4.refs_1_, bf16[64,3456]{1,0:T(8,128)(2,1)S(1)} %collective-permute-done.5.refs_2_, ...), custom_call_target="tpu_custom_call" | custom-call | flops 886505472 | bytes 5232384 | tf_op jit(solution)/shard_map/logits/pallas_call | solution.py:191
  87.8 2.5 collective-permute-done.3.refs_3_
  90.3 4.7 %logits.8 = (f32[501,256]{1,0:T(8,128)S(1)}, bf16[256,3328]{1,0:T(8,128)(2,1)}) custom-call(s32[2]{0:T(128)S(1)} %pad_add_fusion.1.place_ref, bf16[64,3328]{1,0:T(8,128)(2,1)S(1)} %reshape.130.refs_0_, bf16[64,3328]{1,0:T(8,128)(2,1)} %collective-permute-done.1.refs_1_, bf16[64,3328]{1,0:T(8,128)(2,1)} %collective-permute-done.2.refs_2_, ...), custom_call_target="tpu_custom_call" | custom-call | flops 853671936 | bytes 5038592 | tf_op jit(solution)/shard_map/logits/pallas_call | solution.py:191
  95.8 4.9 %convolution_convert_fusion = bf16[256,4096]{1,0:T(8,128)(2,1)} fusion(bf16[4096,501]{0,1:T(8,128)(2,1)} %param.17, s32[256]{0:T(256)S(1)} %subtract_bitcast_fusion), kind=kOutput, calls=%fused_computation | convolution fusion | flops 1051849984 | bytes 6202368 | tf_op jit(solution)/shard_map/dot_general | solution.py:33
  100.7 2.4 slice.9
  106.9 3.2 %logits.9 = (f32[501,256]{1,0:T(8,128)S(1)}, f32[501,256]{1,0:T(8,128)S(1)}) custom-call(s32[2]{0:T(128)S(1)} %pad_add_fusion.place_ref, bf16[256,3456]{1,0:T(8,128)(2,1)S(1)} %collective-permute-done.12.refs_0_, bf16[501,4096]{1,0:T(8,128)(2,1)S(1)} %bitcast.19, bf16[501,16384]{1,0:T(8,128)(2,1)} %bitcast.26, f32[501,256]{1,0:T(8,128)S(1)} %copy-done.7, ...), custom_call_target="tpu_custom_call" | custom-call | flops 886505472 | bytes 5232384 | tf_op jit(solution)/shard_map/logits/pallas_call | solution.py:191
  110.2 4.8 %logits.10.refs_3_ = f32[501,256]{1,0:T(8,128)S(1)} custom-call(s32[2]{0:T(128)S(1)} %pad_add_fusion.place_ref, bf16[256,3456]{1,0:T(8,128)(2,1)} %collective-permute-done.11.refs_0_, bf16[501,4096]{1,0:T(8,128)(2,1)S(1)} %bitcast.20, bf16[501,16384]{1,0:T(8,128)(2,1)} %bitcast.27, f32[501,256]{1,0:T(8,128)S(1)} %get-tuple-element.35.refs_3_), custom_call_target="tpu_custom_call" | custom-call | flops 886505472 | bytes 5232384 | tf_op jit(solution)/shard_map/logits/pallas_call | solution.py:191
  114.9 5.0 %logits.11 = (f32[501,256]{1,0:T(8,128)S(1)}, f32[8,128]{1,0:T(8,128)S(1)}) custom-call(s32[2]{0:T(128)S(1)} %pad_add_fusion.place_ref, bf16[256,3328]{1,0:T(8,128)(2,1)} %collective-permute-done.10.refs_0_, bf16[501,4096]{1,0:T(8,128)(2,1)S(1)} %bitcast.21, bf16[501,16384]{1,0:T(8,128)(2,1)} %bitcast.28, f32[501,256]{1,0:T(8,128)S(1)} %logits.10.refs_3_, ...), custom_call_target="tpu_custom_call" | custom-call | flops 853671936 | bytes 5038592 | tf_op jit(solution)/shard_map/logits/pallas_call | solution.py:191
  121.6 8.5 %all-to-all-start.3 = ((f32[128,8,128]{2,1,0:T(8,128)}), f32[128,8,128]{2,1,0:T(8,128)S(1)}, u32[]{:S(2)}, u32[]{:S(2)}) async-start(f32[128,8,128]{2,1,0:T(8,128)} %broadcast_in_dim.9), calls=%async_computation.3 | async-start | bytes 1048576 | tf_op jit(solution)/shard_map/all_to_all | solution.py:43
  133.4 9.7 %all-to-all-done.3.every_ref = f32[128,8,128]{2,1,0:T(8,128)S(1)} async-done(((f32[128,8,128]{2,1,0:T(8,128)}), f32[128,8,128]{2,1,0:T(8,128)S(1)}, u32[]{:S(2)}, u32[]{:S(2)}) %all-to-all-start.3) | async-done | bytes 524320 | tf_op jit(solution)/shard_map/all_to_all | solution.py:43
  143.1 5.9 %all-to-all-start.5 = ((bf16[64,2,4096]{2,1,0:T(2,128)(2,1)}), bf16[64,2,4096]{2,1,0:T(2,128)(2,1)}, u32[]{:S(2)}, u32[]{:S(2)}) async-start(bf16[64,2,4096]{2,1,0:T(2,128)(2,1)} %reshape.139), calls=%async_computation.5 | async-start | bytes 2097152 | tf_op jit(solution)/shard_map/all_to_all | solution.py:43
  152.6 3.8 %row_grad.1 = (f32[128,4096]{1,0:T(8,128)S(1)}, bf16[128,4096]{1,0:T(8,128)(2,1)}, f32[1,256]{1,0:T(1,128)S(1)}) custom-call(s32[1]{0:T(128)} %bitcast.core_ref, f32[128,8,128]{2,1,0:T(8,128)S(1)} %all-to-all-done.3.every_ref, f32[1,256]{1,0:T(1,128)S(1)} %reshape.134.weight_ref, f32[501,256]{1,0:T(8,128)S(1)} %copy-done.9, ...), custom_call_target="tpu_custom_call" | custom-call | flops 1050673152 | bytes 7249920 | tf_op jit(solution)/shard_map/row_grad/pallas_call | solution.py:249
  156.4 11.4 %all-to-all-done.5 = bf16[64,2,4096]{2,1,0:T(2,128)(2,1)} async-done(((bf16[64,2,4096]{2,1,0:T(2,128)(2,1)}), bf16[64,2,4096]{2,1,0:T(2,128)(2,1)}, u32[]{:S(2)}, u32[]{:S(2)}) %all-to-all-start.5) | async-done | bytes 1048608 | tf_op jit(solution)/shard_map/all_to_all | solution.py:43
  170.0 2.4 add_convert_fusion.2
  172.4 2.5 reshape.137
  175.0 4.7 %all-to-all-start.4 = ((bf16[64,2,4096]{2,1,0:T(2,128)(2,1)}), bf16[64,2,4096]{2,1,0:T(2,128)(2,1)S(1)}, u32[]{:S(2)}, u32[]{:S(2)}) async-start(bf16[64,2,4096]{2,1,0:T(2,128)(2,1)} %reshape.137), calls=%async_computation.4 | async-start | bytes 2097152 | tf_op jit(solution)/shard_map/all_to_all | solution.py:43
  179.8 17.7 %all-to-all-done.4 = bf16[64,2,4096]{2,1,0:T(2,128)(2,1)S(1)} async-done(((bf16[64,2,4096]{2,1,0:T(2,128)(2,1)}), bf16[64,2,4096]{2,1,0:T(2,128)(2,1)S(1)}, u32[]{:S(2)}, u32[]{:S(2)}) %all-to-all-start.4) | async-done | bytes 1048608 | tf_op jit(solution)/shard_map/all_to_all | solution.py:43
  199.5 4.9 %all-to-all-start.7 = ((bf16[64,2,4096]{2,1,0:T(2,128)(2,1)}), bf16[64,2,4096]{2,1,0:T(2,128)(2,1)S(1)}, u32[]{:S(2)}, u32[]{:S(2)}) async-start(bf16[64,2,4096]{2,1,0:T(2,128)(2,1)} %broadcast_in_dim.11), calls=%async_computation.7 | async-start | bytes 2097152 | tf_op jit(solution)/shard_map/all_to_all | solution.py:43
  205.5 16.1 %all-to-all-done.7 = bf16[64,2,4096]{2,1,0:T(2,128)(2,1)S(1)} async-done(((bf16[64,2,4096]{2,1,0:T(2,128)(2,1)}), bf16[64,2,4096]{2,1,0:T(2,128)(2,1)S(1)}, u32[]{:S(2)}, u32[]{:S(2)}) %all-to-all-start.7) | async-done | bytes 1048608 | tf_op jit(solution)/shard_map/all_to_all | solution.py:43
  223.6 5.5 %all-to-all-start.6 = ((bf16[64,2,4096]{2,1,0:T(2,128)(2,1)}), bf16[64,2,4096]{2,1,0:T(2,128)(2,1)}, u32[]{:S(2)}, u32[]{:S(2)}) async-start(bf16[64,2,4096]{2,1,0:T(2,128)(2,1)} %broadcast_in_dim.10), calls=%async_computation.6 | async-start | bytes 2097152 | tf_op jit(solution)/shard_map/all_to_all | solution.py:43
  229.7 16.0 %all-to-all-done.6 = bf16[64,2,4096]{2,1,0:T(2,128)(2,1)} async-done(((bf16[64,2,4096]{2,1,0:T(2,128)(2,1)}), bf16[64,2,4096]{2,1,0:T(2,128)(2,1)}, u32[]{:S(2)}, u32[]{:S(2)}) %all-to-all-start.6) | async-done | bytes 1048608 | tf_op jit(solution)/shard_map/all_to_all | solution.py:43
  256.3 4.7 %all-to-all-start.8 = ((bf16[64,2,4096]{2,1,0:T(2,128)(2,1)}), bf16[64,2,4096]{2,1,0:T(2,128)(2,1)S(1)}, u32[]{:S(2)}, u32[]{:S(2)}) async-start(bf16[64,2,4096]{2,1,0:T(2,128)(2,1)} %reshape.142), calls=%async_computation.8 | async-start | bytes 2097152 | tf_op jit(solution)/shard_map/all_to_all | solution.py:43
  263.0 17.5 %all-to-all-done.8 = bf16[64,2,4096]{2,1,0:T(2,128)(2,1)S(1)} async-done(((bf16[64,2,4096]{2,1,0:T(2,128)(2,1)}), bf16[64,2,4096]{2,1,0:T(2,128)(2,1)S(1)}, u32[]{:S(2)}, u32[]{:S(2)}) %all-to-all-start.8) | async-done | bytes 1048608 | tf_op jit(solution)/shard_map/all_to_all | solution.py:43
  (111 shorter events, 56.9 us)
Async XLA Ops:
  5.2 1.4 collective-permute-start
  26.9 16.0 %all-to-all-start.2 = ((bf16[16,4,3456]{2,1,0:T(4,128)(2,1)}), bf16[16,4,3456]{2,1,0:T(4,128)(2,1)S(1)}, u32[]{:S(2)}, u32[]{:S(2)}) async-start(bf16[16,4,3456]{2,1,0:T(4,128)(2,1)} %get-tuple-element.27), calls=%async_computation.2 | async-start | bytes 884736 | tf_op jit(solution)/shard_map/all_to_all | solution.py:43
  33.3 21.9 %collective-permute-start.4 = (bf16[64,3456]{1,0:T(8,128)(2,1)S(1)}, bf16[64,3456]{1,0:T(8,128)(2,1)S(1)}, u32[]{:S(2)}, u32[]{:S(2)}) collective-permute-start(bf16[64,3456]{1,0:T(8,128)(2,1)S(1)} %reshape.131.refs_0_), channel_id=1, source_target_pairs={{0,2},{2,0},{4,6},{6,4},{1,3},{3,1},{5,7},{7,5},{8,10},{10,8},{12,... | collective-permute-start | bytes 1327112 | tf_op jit(solution)/shard_map/ppermute | solution.py:406
  43.0 28.2 %collective-permute-start.7 = (bf16[64,3456]{1,0:T(8,128)(2,1)S(1)}, bf16[64,3456]{1,0:T(8,128)(2,1)S(1)}, u32[]{:S(2)}, u32[]{:S(2)}) collective-permute-start(bf16[64,3456]{1,0:T(8,128)(2,1)S(1)} %reshape.132.refs_0_), channel_id=1, source_target_pairs={{0,16},{16,0},{32,48},{48,32},{1,17},{17,1},{33,49},{49,33},{2,18}... | collective-permute-start | bytes 1327112 | tf_op jit(solution)/shard_map/ppermute | solution.py:406
  43.3 28.1 %collective-permute-start.8 = (bf16[64,3456]{1,0:T(8,128)(2,1)S(1)}, bf16[64,3456]{1,0:T(8,128)(2,1)S(1)}, u32[]{:S(2)}, u32[]{:S(2)}) collective-permute-start(bf16[64,3456]{1,0:T(8,128)(2,1)S(1)} %reshape.132.refs_0_), channel_id=1, source_target_pairs={{0,32},{16,48},{32,0},{48,16},{1,33},{17,49},{33,1},{49,17},{2,34}... | collective-permute-start | bytes 1327112 | tf_op jit(solution)/shard_map/ppermute | solution.py:406
  45.7 28.3 %collective-permute-start.9 = (bf16[64,3456]{1,0:T(8,128)(2,1)S(1)}, bf16[64,3456]{1,0:T(8,128)(2,1)S(1)}, u32[]{:S(2)}, u32[]{:S(2)}) collective-permute-start(bf16[64,3456]{1,0:T(8,128)(2,1)S(1)} %reshape.132.refs_0_), channel_id=1, source_target_pairs={{0,48},{16,32},{32,16},{48,0},{1,49},{17,33},{33,17},{49,1},{2,50}... | collective-permute-start | bytes 1327112 | tf_op jit(solution)/shard_map/ppermute | solution.py:406
  47.8 22.3 %all-to-all-start = ((bf16[16,4,3328]{2,1,0:T(4,128)(2,1)}), bf16[16,4,3328]{2,1,0:T(4,128)(2,1)}, u32[]{:S(2)}, u32[]{:S(2)}) async-start(bf16[16,4,3328]{2,1,0:T(4,128)(2,1)} %get-tuple-element.25), calls=%async_computation | async-start | bytes 851968 | tf_op jit(solution)/shard_map/all_to_all | solution.py:43
  52.0 30.6 %collective-permute-start.5 = (bf16[64,3456]{1,0:T(8,128)(2,1)S(1)}, bf16[64,3456]{1,0:T(8,128)(2,1)S(1)}, u32[]{:S(2)}, u32[]{:S(2)}) collective-permute-start(bf16[64,3456]{1,0:T(8,128)(2,1)S(1)} %reshape.131.refs_0_), channel_id=1, source_target_pairs={{0,4},{2,6},{4,0},{6,2},{1,5},{3,7},{5,1},{7,3},{8,12},{10,14},{12... | collective-permute-start | bytes 1327112 | tf_op jit(solution)/shard_map/ppermute | solution.py:406
  55.3 27.3 %collective-permute-start.6 = (bf16[64,3456]{1,0:T(8,128)(2,1)S(1)}, bf16[64,3456]{1,0:T(8,128)(2,1)}, u32[]{:S(2)}, u32[]{:S(2)}) collective-permute-start(bf16[64,3456]{1,0:T(8,128)(2,1)S(1)} %reshape.131.refs_0_), channel_id=1, source_target_pairs={{0,6},{2,4},{4,2},{6,0},{1,7},{3,5},{5,3},{7,1},{8,14},{10,12},{12... | collective-permute-start | bytes 1327112 | tf_op jit(solution)/shard_map/ppermute | solution.py:406
  71.2 16.6 %collective-permute-start.1 = (bf16[64,3328]{1,0:T(8,128)(2,1)S(1)}, bf16[64,3328]{1,0:T(8,128)(2,1)}, u32[]{:S(2)}, u32[]{:S(2)}) collective-permute-start(bf16[64,3328]{1,0:T(8,128)(2,1)S(1)} %reshape.130.refs_0_), channel_id=1, source_target_pairs={{0,1},{1,0},{8,9},{9,8},{2,3},{3,2},{10,11},{11,10},{4,5},{5,4},{1... | collective-permute-start | bytes 1277960 | tf_op jit(solution)/shard_map/ppermute | solution.py:406
  71.5 16.3 %collective-permute-start.2 = (bf16[64,3328]{1,0:T(8,128)(2,1)S(1)}, bf16[64,3328]{1,0:T(8,128)(2,1)}, u32[]{:S(2)}, u32[]{:S(2)}) collective-permute-start(bf16[64,3328]{1,0:T(8,128)(2,1)S(1)} %reshape.130.refs_0_), channel_id=1, source_target_pairs={{0,8},{1,9},{8,0},{9,1},{2,10},{3,11},{10,2},{11,3},{4,12},{5,13},... | collective-permute-start | bytes 1277960 | tf_op jit(solution)/shard_map/ppermute | solution.py:406
  74.0 16.3 %collective-permute-start.3 = (bf16[64,3328]{1,0:T(8,128)(2,1)S(1)}, bf16[64,3328]{1,0:T(8,128)(2,1)}, u32[]{:S(2)}, u32[]{:S(2)}) collective-permute-start(bf16[64,3328]{1,0:T(8,128)(2,1)S(1)} %reshape.130.refs_0_), channel_id=1, source_target_pairs={{0,9},{1,8},{8,1},{9,0},{2,11},{3,10},{10,3},{11,2},{4,13},{5,12},... | collective-permute-start | bytes 1277960 | tf_op jit(solution)/shard_map/ppermute | solution.py:406
  82.6 21.1 %collective-permute-start.12 = (bf16[256,3456]{1,0:T(8,128)(2,1)}, bf16[256,3456]{1,0:T(8,128)(2,1)S(1)}, u32[]{:S(2)}, u32[]{:S(2)}) collective-permute-start(bf16[256,3456]{1,0:T(8,128)(2,1)} %get-tuple-element.32), channel_id=1, source_target_pairs={{0,64},{64,0},{1,65},{65,1},{2,66},{66,2},{3,67},{67,3},{4,68},{68... | collective-permute-start | bytes 5308424 | tf_op jit(solution)/shard_map/ppermute | solution.py:39
  87.1 23.1 %collective-permute-start.11 = (bf16[256,3456]{1,0:T(8,128)(2,1)}, bf16[256,3456]{1,0:T(8,128)(2,1)}, u32[]{:S(2)}, u32[]{:S(2)}) collective-permute-start(bf16[256,3456]{1,0:T(8,128)(2,1)} %get-tuple-element.31), channel_id=1, source_target_pairs={{0,64},{64,0},{1,65},{65,1},{2,66},{66,2},{3,67},{67,3},{4,68},{68... | collective-permute-start | bytes 5308424 | tf_op jit(solution)/shard_map/ppermute | solution.py:39
  90.3 5.5 %copy-start.14 = (s32[256]{0:T(256)S(1)}, s32[256]{0:T(256)}, u32[]{:S(2)}) copy-start(s32[256]{0:T(256)} %param.18) | copy-start | bytes 3076
  95.8 19.1 %collective-permute-start.10 = (bf16[256,3328]{1,0:T(8,128)(2,1)}, bf16[256,3328]{1,0:T(8,128)(2,1)}, u32[]{:S(2)}, u32[]{:S(2)}) collective-permute-start(bf16[256,3328]{1,0:T(8,128)(2,1)} %get-tuple-element.30), channel_id=1, source_target_pairs={{0,64},{64,0},{1,65},{65,1},{2,66},{66,2},{3,67},{67,3},{4,68},{68... | collective-permute-start | bytes 5111816 | tf_op jit(solution)/shard_map/ppermute | solution.py:39
  100.7 3.0 %copy-start.5 = (f32[501,256]{1,0:T(8,128)S(1)}, f32[501,256]{1,0:T(8,128)}, u32[]{:S(2)}) copy-start(f32[501,256]{1,0:T(8,128)} %copy-done.4) | copy-start | bytes 1539076
  103.1 27.0 %collective-permute-start.14 = (bf16[128,4096]{1,0:T(8,128)(2,1)}, bf16[128,4096]{1,0:T(8,128)(2,1)}, u32[]{:S(2)}, u32[]{:S(2)}) collective-permute-start(bf16[128,4096]{1,0:T(8,128)(2,1)} %slice.9), channel_id=1, source_target_pairs={{0,64},{64,0},{1,65},{65,1},{2,66},{66,2},{3,67},{67,3},{4,68},{68... | collective-permute-start | bytes 3145736 | tf_op jit(solution)/shard_map/ppermute | solution.py:39
  121.6 21.5 %all-to-all-start.3 = ((f32[128,8,128]{2,1,0:T(8,128)}), f32[128,8,128]{2,1,0:T(8,128)S(1)}, u32[]{:S(2)}, u32[]{:S(2)}) async-start(f32[128,8,128]{2,1,0:T(8,128)} %broadcast_in_dim.9), calls=%async_computation.3 | async-start | bytes 1048576 | tf_op jit(solution)/shard_map/all_to_all | solution.py:43
  131.9 17.2 %copy-start.15 = (f32[256]{0:T(256)S(1)}, f32[256]{0:T(256)}, u32[]{:S(2)}) copy-start(f32[256]{0:T(256)} %param.23) | copy-start | bytes 3076
  143.1 24.7 %all-to-all-start.5 = ((bf16[64,2,4096]{2,1,0:T(2,128)(2,1)}), bf16[64,2,4096]{2,1,0:T(2,128)(2,1)}, u32[]{:S(2)}, u32[]{:S(2)}) async-start(bf16[64,2,4096]{2,1,0:T(2,128)(2,1)} %reshape.139), calls=%async_computation.5 | async-start | bytes 2097152 | tf_op jit(solution)/shard_map/all_to_all | solution.py:43
  152.6 3.8 %copy-start.12 = (bf16[4096]{0:T(1024)(128)(2,1)S(1)}, bf16[4096]{0:T(1024)(128)(2,1)}, u32[]{:S(2)}) copy-start(bf16[4096]{0:T(1024)(128)(2,1)} %param.16) | copy-start | bytes 24580
  152.6 3.8 %copy-start.13 = (bf16[4096]{0:T(1024)(128)(2,1)S(1)}, bf16[4096]{0:T(1024)(128)(2,1)}, u32[]{:S(2)}) copy-start(bf16[4096]{0:T(1024)(128)(2,1)} %param.19) | copy-start | bytes 24580
  156.4 13.6 %collective-permute-start.13 = (bf16[128,4096]{1,0:T(8,128)(2,1)}, bf16[128,4096]{1,0:T(8,128)(2,1)}, u32[]{:S(2)}, u32[]{:S(2)}) collective-permute-start(bf16[128,4096]{1,0:T(8,128)(2,1)} %get-tuple-element.41), channel_id=1, source_target_pairs={{0,64},{64,0},{1,65},{65,1},{2,66},{66,2},{3,67},{67,3},{4,68},{68... | collective-permute-start | bytes 3145736 | tf_op jit(solution)/shard_map/ppermute | solution.py:39
  175.0 22.5 %all-to-all-start.4 = ((bf16[64,2,4096]{2,1,0:T(2,128)(2,1)}), bf16[64,2,4096]{2,1,0:T(2,128)(2,1)S(1)}, u32[]{:S(2)}, u32[]{:S(2)}) async-start(bf16[64,2,4096]{2,1,0:T(2,128)(2,1)} %reshape.137), calls=%async_computation.4 | async-start | bytes 2097152 | tf_op jit(solution)/shard_map/all_to_all | solution.py:43
  179.7 25.5 %copy-start.10 = (bf16[2,4096]{1,0:T(2,128)(2,1)S(1)}, bf16[2,4096]{1,0:T(2,128)(2,1)}, u32[]{:S(2)}) copy-start(bf16[2,4096]{1,0:T(2,128)(2,1)} %student_ref.1) | copy-start | bytes 49156
  199.5 22.2 %all-to-all-start.7 = ((bf16[64,2,4096]{2,1,0:T(2,128)(2,1)}), bf16[64,2,4096]{2,1,0:T(2,128)(2,1)S(1)}, u32[]{:S(2)}, u32[]{:S(2)}) async-start(bf16[64,2,4096]{2,1,0:T(2,128)(2,1)} %broadcast_in_dim.11), calls=%async_computation.7 | async-start | bytes 2097152 | tf_op jit(solution)/shard_map/all_to_all | solution.py:43
  223.6 22.0 %all-to-all-start.6 = ((bf16[64,2,4096]{2,1,0:T(2,128)(2,1)}), bf16[64,2,4096]{2,1,0:T(2,128)(2,1)}, u32[]{:S(2)}, u32[]{:S(2)}) async-start(bf16[64,2,4096]{2,1,0:T(2,128)(2,1)} %broadcast_in_dim.10), calls=%async_computation.6 | async-start | bytes 2097152 | tf_op jit(solution)/shard_map/all_to_all | solution.py:43
  229.6 19.3 %collective-permute-start.16 = (bf16[128,4096]{1,0:T(8,128)(2,1)S(1)}, bf16[128,4096]{1,0:T(8,128)(2,1)S(1)}, u32[]{:S(2)}, u32[]{:S(2)}) collective-permute-start(bf16[128,4096]{1,0:T(8,128)(2,1)S(1)} %reshape.141.own_ref), channel_id=1, source_target_pairs={{0,64},{64,0},{1,65},{65,1},{2,66},{66,2},{3,67},{67,3},{4,68},{68... | collective-permute-start | bytes 3145736 | tf_op jit(solution)/shard_map/ppermute | solution.py:39
  247.1 2.9 %collective-permute-start.15 = (bf16[128,4096]{1,0:T(8,128)(2,1)S(1)}, bf16[128,4096]{1,0:T(8,128)(2,1)S(1)}, u32[]{:S(2)}, u32[]{:S(2)}) collective-permute-start(bf16[128,4096]{1,0:T(8,128)(2,1)S(1)} %reshape.140.own_ref), channel_id=1, source_target_pairs={{0,64},{64,0},{1,65},{65,1},{2,66},{66,2},{3,67},{67,3},{4,68},{68... | collective-permute-start | bytes 3145736 | tf_op jit(solution)/shard_map/ppermute | solution.py:39
  251.6 2.9 %collective-permute-start.17 = (bf16[128,4096]{1,0:T(8,128)(2,1)S(1)}, bf16[128,4096]{1,0:T(8,128)(2,1)S(1)}, u32[]{:S(2)}, u32[]{:S(2)}) collective-permute-start(bf16[128,4096]{1,0:T(8,128)(2,1)S(1)} %get-tuple-element.43), channel_id=1, source_target_pairs={{0,64},{64,0},{1,65},{65,1},{2,66},{66,2},{3,67},{67,3},{4,68},{68... | collective-permute-start | bytes 3145736 | tf_op jit(solution)/shard_map/ppermute | solution.py:39
  256.3 24.3 %all-to-all-start.8 = ((bf16[64,2,4096]{2,1,0:T(2,128)(2,1)}), bf16[64,2,4096]{2,1,0:T(2,128)(2,1)S(1)}, u32[]{:S(2)}, u32[]{:S(2)}) async-start(bf16[64,2,4096]{2,1,0:T(2,128)(2,1)} %reshape.142), calls=%async_computation.8 | async-start | bytes 2097152 | tf_op jit(solution)/shard_map/all_to_all | solution.py:43
  (10 other events, 12.8 us)

commit v2 on v1

v2 whole, which is shorter than its diff:
```python
import functools

import jax
import jax.numpy as jnp
from jax import lax
from jax.experimental import pallas as pl
from jax.experimental.pallas import tpu as pltpu
from jax.sharding import Mesh
from jax.sharding import PartitionSpec as P

eps = 1e-05
SHAPE = (2, 4, 2, 4, 2)
AXES = ("core", "x", "yh", "z", "yl")
CHIPS = AXES[1:]
MIB = 1024 * 1024

VMEM = pl.BlockSpec(memory_space=pltpu.VMEM)
SMEM = pl.BlockSpec(memory_space=pltpu.SMEM)
HBM = pl.BlockSpec(memory_space=pltpu.HBM)
ANY = pl.BlockSpec(memory_space=pl.ANY)
SEGMENTS = 8
SEGMENT = 512


def kernel_call(body, name, out_shape, limit=8, flops=0, moved=0, **options):
    return pl.pallas_call(
        body,
        name=name,
        out_shape=out_shape,
        compiler_params=pltpu.CompilerParams(vmem_limit_bytes=limit * MIB),
        cost_estimate=pl.CostEstimate(flops=flops, bytes_accessed=moved, transcendentals=0),
        **options,
    )


def shape_of(shape, dtype=jnp.bfloat16):
    return jax.ShapeDtypeStruct(shape, dtype)


def row_product(left, right):
    return lax.dot_general(
        left, right, (((1,), (1,)), ((), ())), preferred_element_type=jnp.float32
    )


def swap_cores(values):
    return lax.ppermute(values, "core", [(0, 1), (1, 0)])


def line_pieces(block, line):
    return [block] + [lax.ppermute(block, line, [(i, i ^ m) for i in range(4)]) for m in (1, 2, 3)]


def exchange(blocks, axes):
    return lax.all_to_all(blocks, axes, split_axis=0, concat_axis=0, tiled=True)


def rows_kernel(
    core_ref, teacher_ref, teacher_gain, student_ref, student_gain, keep_ref, send_ref, gains
):
    first = student_gain.shape[0]
    gains[:first, :] = student_gain[...].astype(jnp.float32)
    gains[first:, :] = teacher_gain[...].astype(jnp.float32)
    column = 0
    for values, base in ((student_ref, 0), (teacher_ref, first)):
        half = values.shape[1] // 2
        every = values[...].astype(jnp.float32)
        inverse = lax.rsqrt(jnp.mean(every * every, axis=-1, keepdims=True) + eps)
        for part, out in ((core_ref[0], keep_ref), (1 - core_ref[0], send_ref)):
            for k in range(half // 128):
                place = pl.ds(pl.multiple_of(part * half + k * 128, 128), 128)
                rows = values[:, place].astype(jnp.float32) * inverse
                rows = rows * gains[pl.ds(base + part * (half // 128) + k, 1), :]
                out[:, column + k * 128 : column + (k + 1) * 128] = rows.astype(jnp.bfloat16)
        column = column + half


def chip_kernel(core_ref, keep_ref, came_ref, out_ref):
    keep, came = keep_ref[...].astype(jnp.float32), came_ref[...].astype(jnp.float32)
    first = core_ref[0] == 0
    rows = jnp.concatenate([jnp.where(first, keep, came), jnp.where(first, came, keep)], axis=0)
    out_ref[...] = rows.astype(jnp.bfloat16)


def line_kernel(place_ref, *refs):
    pieces = [ref[...].astype(jnp.float32) for ref in refs[:4]]
    rows = []
    for j in range(4):
        m = place_ref[0] ^ j
        low = jnp.where(m == 0, pieces[0], pieces[1])
        high = jnp.where(m == 2, pieces[2], pieces[3])
        rows.append(jnp.where(m < 2, low, high))
    rows = jnp.concatenate(rows, axis=0).astype(jnp.bfloat16)
    column = 0
    for out in refs[4:]:
        out[...] = rows[:, column : column + out.shape[1]]
        column = column + out.shape[1]


def plane_kernel(place_ref, *refs):
    pieces, out, sems = refs[:4], refs[4], refs[5]
    copies = []
    for m, piece in enumerate(pieces):
        tokens = piece.shape[0]
        at = pl.multiple_of((place_ref[0] ^ m) * tokens, tokens)
        copy = pltpu.make_async_copy(piece, out.at[pl.ds(at, tokens), :], sems.at[m])
        copy.start()
        copies.append(copy)
    for copy in copies:
        copy.wait()


def in_line_order(place, pieces):
    tokens, width = pieces[0].shape
    return kernel_call(
        plane_kernel,
        "plane",
        shape_of((4 * tokens, width)),
        limit=2,
        moved=16 * tokens * width,
        in_specs=[SMEM] + [ANY] * 4,
        out_specs=ANY,
        scratch_shapes=[pltpu.SemaphoreType.DMA((4,))],
    )(place, *pieces)


GROUPS = (
    ((0, 0, 2048), (1, 0, 1536), (1, 1536, 1536)),
    ((1, 3072, 1280), (1, 4352, 1280), (1, 5632, 1280), (1, 6912, 1280)),
)
WIDTHS = tuple(sum(p[2] for p in group) for group in GROUPS)


def reordered(values):
    source = lax.broadcasted_iota(jnp.int32, (256, 256), 0)
    place = lax.broadcasted_iota(jnp.int32, (256, 256), 1)
    wanted = (((place >> 4) & 3) << 6) | (((place >> 6) & 3) << 4) | (place & 15)
    moves = (source == wanted).astype(jnp.bfloat16)
    high = values.astype(jnp.bfloat16)
    rest = values - high.astype(jnp.float32)
    middle = rest.astype(jnp.bfloat16)
    low = (rest - middle.astype(jnp.float32)).astype(jnp.bfloat16)
    high, middle, low = (
        jnp.dot(part, moves, preferred_element_type=jnp.float32) for part in (high, middle, low)
    )
    return (high + middle) + low


def softmax_stats(teacher, student, stats_out):
    teacher_peak = jnp.max(teacher, axis=0, keepdims=True)
    student_peak = jnp.max(student, axis=0, keepdims=True)
    teacher_exp = jnp.exp(teacher - teacher_peak)
    teacher_total = jnp.sum(teacher_exp, axis=0, keepdims=True)
    student_total = jnp.sum(jnp.exp(student - student_peak), axis=0, keepdims=True)
    cross = jnp.sum(teacher_exp * (teacher - student), axis=0, keepdims=True)
    stats = (
        teacher_peak + jnp.log(teacher_total),
        student_peak + jnp.log(student_total),
        cross / teacher_total,
    )
    stats_out[...] = jnp.zeros_like(stats_out)
    for i, row in enumerate(stats):
        stats_out[i : i + 1, :] = row[:, :128]
        stats_out[i + 3 : i + 4, :] = row[:, 128:]


def logits_kernel(group, own, place_ref, *refs):
    count = 4 if own else 1
    pieces, heads, refs = refs[:count], refs[count : count + 2], refs[count + 2 :]
    rows, head, row_sems, head_sems = refs[-4:]
    refs = refs[:-4]
    copies = []
    column = 0
    for i, (kind, start, width) in enumerate(GROUPS[group]):
        columns = slice(column, column + width)
        size = heads[kind].shape[1] // 2
        start = pl.multiple_of(place_ref[0] * size + start, 128)
        copy = pltpu.make_async_copy(
            heads[kind].at[:, pl.ds(start, width)], head.at[:, columns], head_sems.at[i]
        )
        copy.start()
        needed = [copy]
        for m, piece in enumerate(pieces):
            tokens = piece.shape[0]
            at = pl.multiple_of((place_ref[1] ^ m) * tokens, tokens)
            copy = pltpu.make_async_copy(
                piece.at[:, columns], rows.at[pl.ds(at, tokens), columns], row_sems.at[i, m]
            )
            copy.start()
            needed.append(copy)
        copies.append((kind, columns, needed))
        column = column + width
    sums = [None, None]
    for kind, columns, needed in copies:
        for copy in needed:
            copy.wait()
        term = row_product(head[:, columns], rows[:, columns])
        sums[kind] = term if sums[kind] is None else sums[kind] + term
    if group == 0:
        student, teacher = sums
        if own:
            student_out, teacher_out = refs
        else:
            student_in, teacher_in, student_out, teacher_out = refs
            student, teacher = student + student_in[...], teacher + teacher_in[...]
        student_out[...] = student
        teacher_out[...] = teacher
    elif own:
        refs[0][...] = sums[1]
    else:
        second_in, student_in, teacher_in, teacher_out, stats_out = refs
        teacher = teacher_in[...] + reordered(sums[1] + second_in[...])
        teacher_out[...] = teacher
        softmax_stats(teacher, student_in[...], stats_out)


def logits_part(group, place, pieces, heads, sums=()):
    vocab, tokens, width = heads[1].shape[0], 256, WIDTHS[group]
    own = len(pieces) > 1
    shape = shape_of((vocab, tokens), jnp.float32)
    out_shape = [shape, shape] if group == 0 else [shape]
    scratch = [
        pltpu.VMEM((vocab, width), jnp.bfloat16),
        pltpu.SemaphoreType.DMA((len(GROUPS[group]), 4)),
        pltpu.SemaphoreType.DMA((len(GROUPS[group]),)),
    ]
    if own:
        out_shape = out_shape + [shape_of((tokens, width))]
    else:
        scratch = [pltpu.VMEM((tokens, width), jnp.bfloat16)] + scratch
        if group == 1:
            out_shape = out_shape + [shape_of((8, 128), jnp.float32)]
    return kernel_call(
        functools.partial(logits_kernel, group, own),
        "logits",
        out_shape,
        limit=20,
        flops=2 * vocab * tokens * width,
        moved=(vocab + tokens) * width * 2,
        in_specs=[SMEM] + [ANY] * len(pieces) + [HBM] * 2 + [VMEM] * len(sums),
        out_specs=[VMEM] * len(out_shape),
        scratch_shapes=scratch,
    )(place, *pieces, *heads, *sums)


def one_hot_rows(core):
    place = lax.broadcasted_iota(jnp.int32, (256, 256), 0)
    column = lax.broadcasted_iota(jnp.int32, (256, 256), 1)
    x, yh, z, yl = (place >> 4) & 3, (place >> 3) & 1, (place >> 1) & 3, place & 1
    source = (x << 6) | (z << 4) | (yh << 3) | (yl << 2)
    source = source | (((place >> 7) ^ core) << 1) | ((place >> 6) & 1)
    return (column == source).astype(jnp.bfloat16)


def row_grad_kernel(
    core_ref, every_ref, weight_ref, teacher_ref, student_ref, head_ref,
    own_ref, send_ref, divergence_ref, grad,
):
    @pl.when(pl.program_id(0) == 0)
    def _():
        every = every_ref[...]
        peak = jnp.max(every, axis=0)
        scaled = jnp.exp(every - peak[None])
        total = jnp.sum(scaled, axis=0)
        lse = peak + jnp.log(total)
        cross = jnp.sum(scaled * pltpu.roll(every, 6, 1), axis=0) / total
        teacher_lse = jnp.concatenate([lse[0:1], lse[3:4]], axis=1)
        student_lse = jnp.concatenate([lse[1:2], lse[4:5]], axis=1)
        divergence_ref[...] = (
            jnp.concatenate([cross[0:1], cross[3:4]], axis=1) - teacher_lse + student_lse
        )
        logit_grad = weight_ref[...] * (
            jnp.exp(student_ref[...] - student_lse) - jnp.exp(teacher_ref[...] - teacher_lse)
        )
        grad[...] = row_product(
            one_hot_rows(core_ref[0]), logit_grad.astype(jnp.bfloat16)
        ).astype(jnp.bfloat16)

    out = jnp.dot(grad[...], head_ref[...], preferred_element_type=jnp.float32)
    own_ref[...] = out[:128]
    send_ref[...] = out[128:].astype(jnp.bfloat16)


def row_grad_part(core, every, weight, teacher, student, student_head_t):
    vocab, width = student_head_t.shape
    tokens, columns = weight.shape[1], 1024
    half = pl.BlockSpec((tokens // 2, columns), lambda i, c: (0, i))
    return kernel_call(
        row_grad_kernel,
        "row_grad",
        [
            shape_of((tokens // 2, width), jnp.float32),
            shape_of((tokens // 2, width)),
            shape_of((1, tokens), jnp.float32),
        ],
        limit=14,
        flops=2 * vocab * tokens * width,
        moved=vocab * width * 2 + tokens * width * 3,
        grid_spec=pltpu.PrefetchScalarGridSpec(
            num_scalar_prefetch=1,
            grid=(width // columns,),
            in_specs=[
                pl.BlockSpec(every.shape, lambda i, c: (0, 0, 0)),
                pl.BlockSpec(weight.shape, lambda i, c: (0, 0)),
                pl.BlockSpec(teacher.shape, lambda i, c: (0, 0)),
                pl.BlockSpec(student.shape, lambda i, c: (0, 0)),
                pl.BlockSpec((vocab, columns), lambda i, c: (0, i)),
            ],
            out_specs=[half, half, pl.BlockSpec((1, tokens), lambda i, c: (0, 0))],
            scratch_shapes=[pltpu.VMEM((tokens, vocab), jnp.bfloat16)],
        ),
    )(core, every, weight, teacher, student, student_head_t)


def pick_kernel(ids_ref, head_ref, own_ref, send_ref):
    tokens, vocab = ids_ref.shape[0], head_ref.shape[0]
    entry = lax.broadcasted_iota(jnp.int32, (tokens, vocab), 1)
    chosen = (ids_ref[...] == entry).astype(jnp.bfloat16)
    out = jnp.dot(chosen, head_ref[...], preferred_element_type=jnp.float32)
    own_ref[...] = out[: tokens // 2].astype(jnp.bfloat16)
    send_ref[...] = out[tokens // 2 :].astype(jnp.bfloat16)


def pick_part(ids, student_head_t):
    vocab, width = student_head_t.shape
    tokens, columns = ids.shape[0], 1024
    half = pl.BlockSpec((tokens // 2, columns), lambda i: (0, i))
    shape = shape_of((tokens // 2, width))
    return kernel_call(
        pick_kernel,
        "pick",
        [shape, shape],
        flops=2 * vocab * tokens * width,
        moved=(vocab + tokens) * width * 2,
        grid=(width // columns,),
        in_specs=[
            pl.BlockSpec(ids.shape, lambda i: (0, 0)),
            pl.BlockSpec((vocab, columns), lambda i: (0, i)),
        ],
        out_specs=[half, half],
    )(ids, student_head_t)


def join_kernel(own_ref, came_ref, out_ref, rows):
    chips = out_ref.shape[0]
    for t in range(2):
        for i in range(SEGMENTS):
            for k in range(SEGMENT // 128):
                part = slice(t * chips, (t + 1) * chips)
                lanes = slice(i * SEGMENT + k * 128, i * SEGMENT + (k + 1) * 128)
                total = own_ref[part, lanes].astype(jnp.float32)
                total = total + came_ref[part, lanes].astype(jnp.float32)
                at = pl.ds(t * SEGMENTS + i, chips, stride=2 * SEGMENTS)
                rows[k, at, :] = total
    for k in range(SEGMENT // 128):
        out_ref[:, :, k * 128 : (k + 1) * 128] = (
            rows[k].reshape(chips, 2 * SEGMENTS, 128).astype(jnp.bfloat16)
        )


def join_part(own, send):
    chips = own.shape[0] // 2
    block = (chips, 2 * SEGMENTS, SEGMENT)
    return kernel_call(
        join_kernel,
        "join",
        shape_of(block),
        limit=10,
        moved=own.size * 8,
        in_specs=[VMEM] * 2,
        out_specs=VMEM,
        scratch_shapes=[pltpu.VMEM((SEGMENT // 128, chips * 2 * SEGMENTS, 128), jnp.float32)],
    )(own, swap_cores(send))


def block_gain(gain_ref):
    gain = gain_ref[...].astype(jnp.float32)
    lanes = SEGMENT // 128
    token = jnp.concatenate(
        [
            jnp.concatenate([gain[lanes * i + k : lanes * i + k + 1] for k in range(lanes)], axis=1)
            for i in range(SEGMENTS)
        ],
        axis=0,
    )
    return jnp.concatenate([token, token], axis=0)


def block_mean(values):
    means = []
    for t in range(2):
        part = values[t * SEGMENTS : (t + 1) * SEGMENTS]
        total = jnp.sum(jnp.sum(part, axis=0, keepdims=True), axis=1, keepdims=True)
        means.append(jnp.broadcast_to(total / (SEGMENTS * SEGMENT), (SEGMENTS, 1)))
    return jnp.concatenate(means, axis=0)


def block_inverse(values):
    return lax.rsqrt(block_mean(values * values) + eps)


def block_back(upstream, values, gain):
    inverse = block_inverse(values)
    gained = upstream * gain
    return inverse * gained - values * inverse**3 * block_mean(gained * values)


def block_sum(blocks_ref):
    return jnp.sum(blocks_ref[...].astype(jnp.float32), axis=0)


def embed_kernel(blocks_ref, gain_ref, embedded_ref, out_ref):
    values = block_sum(blocks_ref)
    embedded_ref[...] = values
    rows = (values * block_inverse(values) * block_gain(gain_ref)).astype(jnp.bfloat16)
    out_ref[...] = jnp.broadcast_to(rows[None], out_ref.shape)


def final_kernel(blocks_ref, states_ref, gain_ref, grad_ref, out_ref, states):
    for i in range(SEGMENTS):
        part = states_ref[:, i * SEGMENT : (i + 1) * SEGMENT].astype(jnp.float32)
        for t in range(2):
            states[t * SEGMENTS + i : t * SEGMENTS + i + 1, :] = part[t : t + 1]
    grad = block_back(block_sum(blocks_ref), states[...], block_gain(gain_ref))
    grad_ref[...] = grad
    out_ref[...] = jnp.broadcast_to(grad.astype(jnp.bfloat16)[None], out_ref.shape)


def state_kernel(blocks_ref, grad_ref, embedded_ref, gain_ref, out_ref):
    back = block_back(block_sum(blocks_ref), embedded_ref[...], block_gain(gain_ref))
    grad = grad_ref[...] + back
    for t in range(2):
        for i in range(SEGMENTS):
            out_ref[t : t + 1, i * SEGMENT : (i + 1) * SEGMENT] = grad[
                t * SEGMENTS + i : t * SEGMENTS + i + 1
            ]


BLOCK = (2 * SEGMENTS, SEGMENT)


def owner_part(body, name, blocks, *others, scratch=()):
    return kernel_call(
        body,
        name,
        [shape_of(BLOCK, jnp.float32), shape_of(blocks.shape)],
        moved=blocks.size * 4,
        in_specs=[VMEM] * (1 + len(others)),
        out_specs=[VMEM] * 2,
        scratch_shapes=list(scratch),
    )(blocks, *others)


def spread_rows(refs, scratches):
    for ref, rows in zip(refs, scratches):
        values = ref[...].astype(jnp.float32)
        values = values.reshape(values.shape[0] * values.shape[1], values.shape[2])
        for k in range(SEGMENT // 128):
            rows[k] = values[:, k * 128 : (k + 1) * 128]


def segment_rows(scratches, segment):
    parts = []
    for rows in scratches:
        chips = rows.shape[1] // (2 * SEGMENTS)
        for t in range(2):
            at = pl.ds(t * SEGMENTS + segment, chips, stride=2 * SEGMENTS)
            parts.append(
                jnp.concatenate([rows[k, at, :] for k in range(SEGMENT // 128)], axis=1)
            )
    return jnp.concatenate(parts, axis=0).astype(jnp.bfloat16)


def gate_kernel(own_ref, other_ref, gate_ref, up_ref, out_ref, *scratches):
    spread_rows((own_ref, other_ref), scratches)
    total = None
    for i in range(SEGMENTS):
        columns = slice(i * SEGMENT, (i + 1) * SEGMENT)
        weight = jnp.concatenate([gate_ref[:, columns], up_ref[:, columns]], axis=0)
        term = row_product(weight, segment_rows(scratches, i))
        total = term if total is None else total + term
    out_ref[...] = total


def ffn_grad_kernel(
    own_ref, other_ref, down_ref, hidden_ref, gate_ref, up_ref, own_out, send_out, *scratches
):
    spread_rows((own_ref, other_ref), scratches)
    units = down_ref.shape[0]
    act_grad = None
    for i in range(SEGMENTS):
        term = row_product(
            down_ref[:, i * SEGMENT : (i + 1) * SEGMENT], segment_rows(scratches, i)
        )
        act_grad = term if act_grad is None else act_grad + term
    gate, upper = hidden_ref[:units, :], hidden_ref[units:, :]
    sigmoid_gate = jax.nn.sigmoid(gate)
    gate_grad = act_grad * upper * sigmoid_gate * (1.0 + gate * (1.0 - sigmoid_gate))
    upper_grad = act_grad * gate * sigmoid_gate
    grads = jnp.concatenate([gate_grad, upper_grad], axis=0).astype(jnp.bfloat16)
    tokens = grads.shape[1]
    same = lax.broadcasted_iota(jnp.int32, (tokens, tokens), 0) == lax.broadcasted_iota(
        jnp.int32, (tokens, tokens), 1
    )
    grads = row_product(same.astype(jnp.bfloat16), grads).astype(jnp.bfloat16)
    for i in range(SEGMENTS):
        columns = slice(i * SEGMENT, (i + 1) * SEGMENT)
        weight = jnp.concatenate([gate_ref[:, columns], up_ref[:, columns]], axis=0)
        out = jnp.dot(grads, weight, preferred_element_type=jnp.float32)
        own_out[:, columns] = out[: tokens // 2]
        send_out[:, columns] = out[tokens // 2 :].astype(jnp.bfloat16)


def ffn_part(body, name, out_shape, blocks, *others):
    rows = blocks.shape[0] * blocks.shape[1]
    scratch = pltpu.VMEM((SEGMENT // 128, rows, 128), jnp.float32)
    return kernel_call(
        body,
        name,
        out_shape,
        limit=18,
        flops=16 * 112 * 256 * 4096 // 2,
        moved=blocks.size * 8,
        in_specs=[VMEM] * (2 + len(others)),
        out_specs=[VMEM] * len(out_shape),
        scratch_shapes=[scratch, scratch],
    )(blocks, swap_cores(blocks), *others)


def shards(
    teacher_states,
    teacher_gain,
    teacher_head,
    student_states,
    student_gain,
    student_head,
    token_ids,
    ffn_gain,
    gate_weight,
    up_weight,
    down_weight,
    token_weight,
):
    core = lax.axis_index("core")
    device = lax.axis_index(AXES)
    own_core = jnp.full((1,), core, jnp.int32)
    x, z, y = (
        jnp.full((1,), lax.axis_index(line), jnp.int32) for line in ("x", "z", ("yh", "yl"))
    )
    teacher_gain, student_gain, ffn_gain = (
        gain.reshape(-1, 128) for gain in (teacher_gain, student_gain, ffn_gain)
    )
    student_head_t, teacher_head_t = student_head.T, teacher_head.T
    heads = (student_head_t, teacher_head_t)
    gate_t, up_t = gate_weight.T, up_weight.T

    width = sum(WIDTHS)
    half_shape = shape_of((2, width))
    keep, send = kernel_call(
        rows_kernel,
        "rows",
        [half_shape, half_shape],
        in_specs=[SMEM] + [VMEM] * 4,
        out_specs=[VMEM] * 2,
        scratch_shapes=[pltpu.VMEM((160, 128), jnp.float32)],
    )(own_core, teacher_states, teacher_gain, student_states, student_gain)
    rows = kernel_call(
        chip_kernel,
        "chip",
        shape_of((4, width)),
        in_specs=[SMEM] + [VMEM] * 2,
        out_specs=VMEM,
    )(own_core, keep, swap_cores(send))
    first, second = kernel_call(
        line_kernel,
        "line",
        [shape_of((16, w)) for w in WIDTHS],
        in_specs=[SMEM] + [VMEM] * 4,
        out_specs=[VMEM] * 2,
    )(y, *line_pieces(rows, ("yh", "yl")))
    first, second = line_pieces(first, "z"), line_pieces(second, "x")
    first, second = in_line_order(z, first), in_line_order(x, second)

    ids = token_ids.reshape(2, 64, 2).transpose(0, 2, 1).reshape(2, 128)
    ids = jnp.where(core == 0, ids, ids[::-1]).reshape(256, 1) - device * student_head.shape[1]
    ids, second = lax.optimization_barrier((ids, second))
    picked = join_part(*pick_part(ids, student_head_t))

    first, second = line_pieces(first, "x"), line_pieces(second, "z")
    first, picked = lax.optimization_barrier((first, picked))
    picked = exchange(picked, CHIPS)
    place = jnp.concatenate([own_core, x])
    student, teacher, first = logits_part(0, place, first, heads)
    place = jnp.concatenate([own_core, z])
    teacher_second, second = logits_part(1, place, second, heads)
    first, second = swap_cores(first), swap_cores(second)
    first, picked = lax.optimization_barrier((first, picked))
    place = jnp.concatenate([1 - own_core, 0 * x])
    student, teacher = logits_part(0, place, [first], heads, (student, teacher))
    teacher, stats = logits_part(
        1, place, [second], heads, (teacher_second, student, teacher)
    )
    every = exchange(jnp.broadcast_to(stats[None], (128,) + stats.shape), AXES)
    embedded, ffn_rows = owner_part(embed_kernel, "embed", picked, ffn_gain)
    ffn_rows = exchange(ffn_rows, CHIPS)

    weight = token_weight.reshape(2, 4, 2, 4, 2, 2).transpose(1, 3, 2, 4, 0, 5).reshape(1, 256)
    own, send, divergence = row_grad_part(
        own_core, every, weight, teacher, student, student_head_t
    )
    divergence = divergence.reshape(4, 4, 2, 2, 2, 2).transpose(4, 0, 2, 1, 3, 5).reshape(256)
    row_grad = join_part(own, send)
    row_grad, ffn_rows = lax.optimization_barrier((row_grad, ffn_rows))
    row_grad = exchange(row_grad, CHIPS)
    (hidden,) = ffn_part(
        gate_kernel, "gate_upper", [shape_of((224, 256), jnp.float32)], ffn_rows, gate_t, up_t
    )
    final_grad, final_half = owner_part(
        final_kernel,
        "final",
        row_grad,
        student_states,
        student_gain,
        scratch=[pltpu.VMEM(BLOCK, jnp.float32)],
    )
    final_half, hidden = lax.optimization_barrier((final_half, hidden))
    final_half = exchange(final_half, CHIPS)
    shape = (128, 4096)
    own, send = ffn_part(
        ffn_grad_kernel,
        "ffn_grad",
        [shape_of(shape, jnp.float32), shape_of(shape)],
        final_half,
        down_weight,
        hidden,
        gate_t,
        up_t,
    )
    ffn_grad = exchange(join_part(own, send), CHIPS)
    state_grad = kernel_call(
        state_kernel,
        "state",
        shape_of((2, 4096), jnp.float32),
        in_specs=[VMEM] * 4,
        out_specs=VMEM,
    )(ffn_grad, final_grad, embedded, ffn_gain)
    return (divergence, state_grad)


def solution(mesh):
    fine = Mesh(mesh.devices.reshape(SHAPE), AXES)
    in_specs = (
        P(AXES, None),
        P(),
        P(None, AXES),
        P(AXES, None),
        P(),
        P(None, AXES),
        P(),
        P(),
        P(None, AXES),
        P(None, AXES),
        P(AXES, None),
        P(),
    )
    out_specs = (P(), P(AXES, None))
    return jax.shard_map(shards, mesh=fine, in_specs=in_specs, out_specs=out_specs, check_vma=False)
```

time: 284 us -> 292 us (1.028)
  blocking collectives: 17.8 us -> 46.4 us
  starting transfers between devices: 62.5 us -> 42.3 us
  other arithmetic: 12.2 us -> 0.89 us
  Pallas kernels: 35.9 us -> 42 us
  local copies, waits for them, and re-layouts: 32.1 us -> 37.9 us
  matrix products: 4.88 us -> 0 us
  waiting for transfers between devices: 116 us -> 120 us
    ppermute x9 -> x15, waiting for transfers between devices: 2.58 us -> 48 us  [line_pieces(): lax.ppermute(block, line, [(i, i ^ m) for i in range(4)])]
    all_to_all x8 -> x4, waiting for transfers between devices: 110 us -> 65.9 us  [exchange(): return lax.all_to_all(blocks, axes, split_axis=0, concat_axis=0, tiled=True)]
    all_to_all x1 -> x2, blocking collectives: 17.8 us -> 46.4 us  [exchange(): return lax.all_to_all(blocks, axes, split_axis=0, concat_axis=0, tiled=True)]
    all_to_all x8 -> x4, starting transfers between devices: 44.7 us -> 20.7 us  [exchange(): return lax.all_to_all(blocks, axes, split_axis=0, concat_axis=0, tiled=True)]
    unnamed x32 -> x62, local copies, waits for them, and re-layouts: 11.6 us -> 34.1 us
    reshape x14 -> x6, local copies, waits for them, and re-layouts: 12.6 us -> 2.08 us  [the longest x2 0.89 us: shards(): ids = token_ids.reshape(2, 64, 2).transpose(0, 2, 1).reshape(2, 128)]
    pallas_call x11 -> x19, Pallas kernels: 35.9 us -> 42 us  [the longest x4 20.3 us: logits_part(): kernel_call(functools.partial(logits_kernel, group, own), 'logits', out_s...]
    ppermute x9 -> x15, starting transfers between devices: 16 us -> 21.2 us  [line_pieces(): lax.ppermute(block, line, [(i, i ^ m) for i in range(4)])]
  transfers between devices with their start and end apart: 26 -> 27, of which waited for: 11 -> 18; matrix products, arithmetic and copies ran while one was open for 8% -> 1% of each run, Pallas kernels for 11% -> 7%
where the time goes in v2:
time: 292 us; the launch traced here: 291 us
  waiting for transfers between devices  120 us (41%)
  blocking collectives  46.4 us (16%)
  starting transfers between devices  42.3 us (14%)
  Pallas kernels  42 us (14%)
  local copies, waits for them, and re-layouts  37.9 us (13%)
    all_to_all x4, waiting for transfers between devices, exchange(): return lax.all_to_all(blocks, axes, split_axis=0, concat_axis=0, tiled=True)  65.9 us
    ppermute x15, waiting for transfers between devices, line_pieces(): lax.ppermute(block, line, [(i, i ^ m) for i in range(4)])  48 us
    all_to_all x2, blocking collectives, exchange(): return lax.all_to_all(blocks, axes, split_axis=0, concat_axis=0, tiled=True)  46.4 us
    unnamed x62, local copies, waits for them, and re-layouts  34.1 us
    ppermute x15, starting transfers between devices, line_pieces(): lax.ppermute(block, line, [(i, i ^ m) for i in range(4)])  21.2 us
    all_to_all x4, starting transfers between devices, exchange(): return lax.all_to_all(blocks, axes, split_axis=0, concat_axis=0, tiled=True)  20.7 us
    pallas_call x4, Pallas kernels, logits_part(): kernel_call(functools.partial(logits_kernel, group, own), 'logits', out_s...  20.3 us
    ppermute x8, waiting for transfers between devices, swap_cores(): return lax.ppermute(values, 'core', [(0, 1), (1, 0)])  6.4 us
  transfers between devices with their start and end apart: 27, of which 18 were waited for; matrix products, arithmetic and copies ran while one was open for 1% of the time, Pallas kernels for 7%

profile of v2, /device:TPU:0, one launch (start us, length us, event | category | flops | bytes accessed | tf_op | source)
XLA Modules:
  0.0 290.8 jit_solution(13035217879696196325)
XLA Ops:
  7.1 2.9 collective-permute-start.2
  11.1 3.2 %collective-permute-done.2.refs_2_ = bf16[4,10240]{1,0:T(4,128)(2,1)S(1)} collective-permute-done((bf16[4,10240]{1,0:T(4,128)(2,1)S(1)}, bf16[4,10240]{1,0:T(4,128)(2,1)S(1)}, u32[]{:S(2)}, u32[]{:S(2)}) %collective-permute-start.2) | collective-permute-done | bytes 81952 | tf_op jit(solution)/shard_map/ppermute | solution.py:51
  17.7 2.7 collective-permute-start.5
  20.9 2.3 collective-permute-done.4.refs_1_
  23.3 4.4 %collective-permute-done.5.refs_2_ = bf16[16,5120]{1,0:T(8,128)(2,1)S(1)} collective-permute-done((bf16[16,5120]{1,0:T(8,128)(2,1)S(1)}, bf16[16,5120]{1,0:T(8,128)(2,1)S(1)}, u32[]{:S(2)}, u32[]{:S(2)}) %collective-permute-start.5) | collective-permute-done | bytes 163872 | tf_op jit(solution)/shard_map/ppermute | solution.py:51
  33.1 2.4 pick.1
  37.6 3.6 %collective-permute-start.12 = (bf16[16,5120]{1,0:T(8,128)(2,1)S(1)}, bf16[16,5120]{1,0:T(8,128)(2,1)S(1)}, u32[]{:S(2)}, u32[]{:S(2)}) collective-permute-start(bf16[16,5120]{1,0:T(8,128)(2,1)S(1)} %get-tuple-element.45.refs_0_), channel_id=1, source_target_pairs={{0,4},{2,6},{4,0},{6,2},{1,5},{3,7},{5,1},{7,3},{8,12},{10,14},{12... | collective-permute-start | bytes 491528 | tf_op jit(solution)/shard_map/ppermute | solution.py:51
  42.6 6.7 %collective-permute-done.12.refs_2_ = bf16[16,5120]{1,0:T(8,128)(2,1)S(1)} collective-permute-done((bf16[16,5120]{1,0:T(8,128)(2,1)S(1)}, bf16[16,5120]{1,0:T(8,128)(2,1)S(1)}, u32[]{:S(2)}, u32[]{:S(2)}) %collective-permute-start.12) | collective-permute-done | bytes 163872 | tf_op jit(solution)/shard_map/ppermute | solution.py:51
  49.3 2.6 collective-permute-done.13.refs_3_
  54.8 2.7 collective-permute-start.16
  57.5 13.0 %collective-permute-done.14.refs_1_ = bf16[64,5120]{1,0:T(8,128)(2,1)S(1)} collective-permute-done((bf16[64,5120]{1,0:T(8,128)(2,1)S(1)}, bf16[64,5120]{1,0:T(8,128)(2,1)S(1)}, u32[]{:S(2)}, u32[]{:S(2)}) %collective-permute-start.14) | collective-permute-done | bytes 655392 | tf_op jit(solution)/shard_map/ppermute | solution.py:51
  74.1 8.8 %collective-permute-done.15.refs_2_ = bf16[64,5120]{1,0:T(8,128)(2,1)S(1)} collective-permute-done((bf16[64,5120]{1,0:T(8,128)(2,1)S(1)}, bf16[64,5120]{1,0:T(8,128)(2,1)S(1)}, u32[]{:S(2)}, u32[]{:S(2)}) %collective-permute-start.15) | collective-permute-done | bytes 655392 | tf_op jit(solution)/shard_map/ppermute | solution.py:51
  86.4 5.7 %copy-done = bf16[16384,501]{0,1:T(8,128)(2,1)S(1)} copy-done((bf16[16384,501]{0,1:T(8,128)(2,1)S(1)}, bf16[16384,501]{0,1:T(8,128)(2,1)}, u32[]{:S(2)}) %copy-start) | copy-done | bytes 16416792
  94.2 4.6 %logits.5 = (f32[501,256]{1,0:T(8,128)S(1)}, f32[501,256]{1,0:T(8,128)S(1)}, bf16[256,5120]{1,0:T(8,128)(2,1)}) custom-call(s32[2]{0:T(128)S(1)} %pad_add_fusion.2.place_ref, bf16[64,5120]{1,0:T(8,128)(2,1)S(1)} %plane.3.refs_0_, bf16[64,5120]{1,0:T(8,128)(2,1)S(1)} %collective-permute-done.14.refs_1_, bf16[64,5120]{1,0:T(8,128)(2,1)S(1)} %copy-done.14, ...), custom_call_target="tpu_custom_call" | custom-call | flops 1313341440 | bytes 7751680 | tf_op jit(solution)/shard_map/logits/pallas_call | solution.py:233
  103.4 5.7 %logits.4 = (f32[501,256]{1,0:T(8,128)S(1)}, bf16[256,5120]{1,0:T(8,128)(2,1)}) custom-call(s32[2]{0:T(128)S(1)} %pad_add_fusion.1.place_ref, bf16[64,5120]{1,0:T(8,128)(2,1)S(1)} %plane.2.refs_0_, bf16[64,5120]{1,0:T(8,128)(2,1)S(1)} %collective-permute-done.7.refs_1_, bf16[64,5120]{1,0:T(8,128)(2,1)S(1)} %collective-permute-done.8.refs_2_, ...), custom_call_target="tpu_custom_call" | custom-call | flops 1313341440 | bytes 7751680 | tf_op jit(solution)/shard_map/logits/pallas_call | solution.py:233
  109.9 5.8 %all-to-all-start = ((bf16[64,16,512]{2,1,0:T(8,128)(2,1)}), bf16[64,16,512]{2,1,0:T(8,128)(2,1)S(1)}, u32[]{:S(2)}, u32[]{:S(2)}) async-start(bf16[64,16,512]{2,1,0:T(8,128)(2,1)} %join.3), calls=%async_computation | async-start | bytes 2097152 | tf_op jit(solution)/shard_map/all_to_all | solution.py:55
  115.8 19.4 %all-to-all-done.blocks_ref = bf16[64,16,512]{2,1,0:T(8,128)(2,1)S(1)} async-done(((bf16[64,16,512]{2,1,0:T(8,128)(2,1)}), bf16[64,16,512]{2,1,0:T(8,128)(2,1)S(1)}, u32[]{:S(2)}, u32[]{:S(2)}) %all-to-all-start) | async-done | bytes 1048608 | tf_op jit(solution)/shard_map/all_to_all | solution.py:55
  135.2 5.7 %copy-done.2 = bf16[16384,501]{0,1:T(8,128)(2,1)S(1)} copy-done((bf16[16384,501]{0,1:T(8,128)(2,1)S(1)}, bf16[16384,501]{0,1:T(8,128)(2,1)}, u32[]{:S(2)}) %copy-start.2) | copy-done | bytes 16416792
  144.1 4.2 %logits.6 = (f32[501,256]{1,0:T(8,128)S(1)}, f32[501,256]{1,0:T(8,128)S(1)}) custom-call(s32[2]{0:T(128)S(1)} %pad_add_fusion.place_ref, bf16[256,5120]{1,0:T(8,128)(2,1)} %collective-permute-done.18.refs_0_, bf16[501,4096]{1,0:T(8,128)(2,1)S(1)} %bitcast.22, bf16[501,16384]{1,0:T(8,128)(2,1)S(1)} %bitcast.17, f32[501,256]{1,0:T(8,128)S(1)} %copy-done.18, ...), custom_call_target="tpu_custom_call" | custom-call | flops 1313341440 | bytes 7751680 | tf_op jit(solution)/shard_map/logits/pallas_call | solution.py:233
  148.3 5.9 %logits.7 = (f32[501,256]{1,0:T(8,128)S(1)}, f32[8,128]{1,0:T(8,128)S(1)}) custom-call(s32[2]{0:T(128)S(1)} %pad_add_fusion.place_ref, bf16[256,5120]{1,0:T(8,128)(2,1)} %collective-permute-done.10.refs_0_, bf16[501,4096]{1,0:T(8,128)(2,1)S(1)} %bitcast.23, bf16[501,16384]{1,0:T(8,128)(2,1)S(1)} %bitcast.18, f32[501,256]{1,0:T(8,128)S(1)} %copy-done.22, ...), custom_call_target="tpu_custom_call" | custom-call | flops 1313341440 | bytes 7751680 | tf_op jit(solution)/shard_map/logits/pallas_call | solution.py:233
  155.1 4.6 %all-to-all-start.1 = ((f32[128,8,128]{2,1,0:T(8,128)}), f32[128,8,128]{2,1,0:T(8,128)S(1)}, u32[]{:S(2)}, u32[]{:S(2)}) async-start(f32[128,8,128]{2,1,0:T(8,128)} %broadcast_in_dim.22), calls=%async_computation.1 | async-start | bytes 1048576 | tf_op jit(solution)/shard_map/all_to_all | solution.py:55
  160.1 12.6 %all-to-all-done.1.every_ref = f32[128,8,128]{2,1,0:T(8,128)S(1)} async-done(((f32[128,8,128]{2,1,0:T(8,128)}), f32[128,8,128]{2,1,0:T(8,128)S(1)}, u32[]{:S(2)}, u32[]{:S(2)}) %all-to-all-start.1) | async-done | bytes 524320 | tf_op jit(solution)/shard_map/all_to_all | solution.py:55
  174.9 3.8 %row_grad.1 = (f32[128,4096]{1,0:T(8,128)S(1)}, bf16[128,4096]{1,0:T(8,128)(2,1)}, f32[1,256]{1,0:T(1,128)S(1)}) custom-call(s32[1]{0:T(128)} %bitcast.core_ref, f32[128,8,128]{2,1,0:T(8,128)S(1)} %all-to-all-done.1.every_ref, f32[1,256]{1,0:T(1,128)S(1)} %reshape.52.weight_ref, f32[501,256]{1,0:T(8,128)S(1)} %get-tuple-element.61.teacher_ref, ...), custom_call_target="tpu_custom_call" | custom-call | flops 1050673152 | bytes 7249920 | tf_op jit(solution)/shard_map/row_grad/pallas_call | solution.py:288
  181.4 5.6 %all-to-all-start.2 = ((bf16[64,16,512]{2,1,0:T(8,128)(2,1)}), bf16[64,16,512]{2,1,0:T(8,128)(2,1)S(1)}, u32[]{:S(2)}, u32[]{:S(2)}) async-start(bf16[64,16,512]{2,1,0:T(8,128)(2,1)} %get-tuple-element.66), calls=%async_computation.2 | async-start | bytes 2097152 | tf_op jit(solution)/shard_map/all_to_all | solution.py:55
  190.0 16.6 %all-to-all-done.2.own_ref = bf16[64,16,512]{2,1,0:T(8,128)(2,1)S(1)} async-done(((bf16[64,16,512]{2,1,0:T(8,128)(2,1)}), bf16[64,16,512]{2,1,0:T(8,128)(2,1)S(1)}, u32[]{:S(2)}, u32[]{:S(2)}) %all-to-all-start.2) | async-done | bytes 1048608 | tf_op jit(solution)/shard_map/all_to_all | solution.py:55
  206.5 23.9 %all_to_all.30.blocks_ref = bf16[64,16,512]{2,1,0:T(8,128)(2,1)S(1)} all-to-all(bf16[64,16,512]{2,1,0:T(8,128)(2,1)S(1)} %join.4), channel_id=1, replica_groups=mesh['core'=2,'x'=4,'yh'=2,'z'=4,'yl'=2] {'x','yh','z','yl'}, dimensions={0} | all-to-all | bytes 2097152 | tf_op jit(solution)/shard_map/all_to_all | solution.py:55
  232.6 22.5 %all_to_all.31.own_ref = bf16[64,16,512]{2,1,0:T(8,128)(2,1)S(1)} all-to-all(bf16[64,16,512]{2,1,0:T(8,128)(2,1)S(1)} %get-tuple-element.70), channel_id=1, replica_groups=mesh['core'=2,'x'=4,'yh'=2,'z'=4,'yl'=2] {'x','yh','z','yl'}, dimensions={0} | all-to-all | bytes 2097152 | tf_op jit(solution)/shard_map/all_to_all | solution.py:55
  255.1 2.7 collective-permute-done.21.other_ref
  257.8 3.0 %ffn_grad.1 = (f32[128,4096]{1,0:T(8,128)S(1)}, bf16[128,4096]{1,0:T(8,128)(2,1)S(1)}) custom-call(bf16[64,16,512]{2,1,0:T(8,128)(2,1)S(1)} %all_to_all.31.own_ref, bf16[64,16,512]{2,1,0:T(8,128)(2,1)S(1)} %collective-permute-done.21.other_ref, bf16[112,4096]{1,0:T(8,128)(2,1)S(1)} %copy-done.12, f32[224,256]{1,0:T(8,128)S(1)} %gate_upper.1.hidden_ref, ...), custom_call_target="tpu_custom_call" | custom-call | flops 939524096 | bytes 4194304 | tf_op jit(solution)/shard_map/ffn_grad/pallas_call | solution.py:517
  261.0 2.5 collective-permute-done.22.came_ref
  265.9 4.7 %all-to-all-start.5 = ((bf16[64,16,512]{2,1,0:T(8,128)(2,1)}), bf16[64,16,512]{2,1,0:T(8,128)(2,1)S(1)}, u32[]{:S(2)}, u32[]{:S(2)}) async-start(bf16[64,16,512]{2,1,0:T(8,128)(2,1)} %join.5), calls=%async_computation.5 | async-start | bytes 2097152 | tf_op jit(solution)/shard_map/all_to_all | solution.py:55
  272.6 17.3 %all-to-all-done.5.blocks_ref = bf16[64,16,512]{2,1,0:T(8,128)(2,1)S(1)} async-done(((bf16[64,16,512]{2,1,0:T(8,128)(2,1)}), bf16[64,16,512]{2,1,0:T(8,128)(2,1)S(1)}, u32[]{:S(2)}, u32[]{:S(2)}) %all-to-all-start.5) | async-done | bytes 1048608 | tf_op jit(solution)/shard_map/all_to_all | solution.py:55
  (123 shorter events, 57.9 us)
Async XLA Ops:
  4.0 1.3 collective-permute-start
  5.3 5.8 %collective-permute-start.1 = (bf16[4,10240]{1,0:T(4,128)(2,1)S(1)}, bf16[4,10240]{1,0:T(4,128)(2,1)S(1)}, u32[]{:S(2)}, u32[]{:S(2)}) collective-permute-start(bf16[4,10240]{1,0:T(4,128)(2,1)S(1)} %chip.1.refs_0_), channel_id=1, source_target_pairs={{0,1},{1,0},{8,9},{9,8},{2,3},{3,2},{10,11},{11,10},{4,5},{5,4},{1... | collective-permute-start | bytes 245768 | tf_op jit(solution)/shard_map/ppermute | solution.py:51
  7.1 7.2 %collective-permute-start.2 = (bf16[4,10240]{1,0:T(4,128)(2,1)S(1)}, bf16[4,10240]{1,0:T(4,128)(2,1)S(1)}, u32[]{:S(2)}, u32[]{:S(2)}) collective-permute-start(bf16[4,10240]{1,0:T(4,128)(2,1)S(1)} %chip.1.refs_0_), channel_id=1, source_target_pairs={{0,8},{1,9},{8,0},{9,1},{2,10},{3,11},{10,2},{11,3},{4,12},{5,13},... | collective-permute-start | bytes 245768 | tf_op jit(solution)/shard_map/ppermute | solution.py:51
  10.0 6.0 %collective-permute-start.3 = (bf16[4,10240]{1,0:T(4,128)(2,1)S(1)}, bf16[4,10240]{1,0:T(4,128)(2,1)S(1)}, u32[]{:S(2)}, u32[]{:S(2)}) collective-permute-start(bf16[4,10240]{1,0:T(4,128)(2,1)S(1)} %chip.1.refs_0_), channel_id=1, source_target_pairs={{0,9},{1,8},{8,1},{9,0},{2,11},{3,10},{10,3},{11,2},{4,13},{5,12},... | collective-permute-start | bytes 245768 | tf_op jit(solution)/shard_map/ppermute | solution.py:51
  16.1 7.1 %collective-permute-start.4 = (bf16[16,5120]{1,0:T(8,128)(2,1)S(1)}, bf16[16,5120]{1,0:T(8,128)(2,1)S(1)}, u32[]{:S(2)}, u32[]{:S(2)}) collective-permute-start(bf16[16,5120]{1,0:T(8,128)(2,1)S(1)} %get-tuple-element.41.refs_0_), channel_id=1, source_target_pairs={{0,16},{16,0},{32,48},{48,32},{1,17},{17,1},{33,49},{49,33},{2,18}... | collective-permute-start | bytes 491528 | tf_op jit(solution)/shard_map/ppermute | solution.py:51
  17.7 10.0 %collective-permute-start.5 = (bf16[16,5120]{1,0:T(8,128)(2,1)S(1)}, bf16[16,5120]{1,0:T(8,128)(2,1)S(1)}, u32[]{:S(2)}, u32[]{:S(2)}) collective-permute-start(bf16[16,5120]{1,0:T(8,128)(2,1)S(1)} %get-tuple-element.41.refs_0_), channel_id=1, source_target_pairs={{0,32},{16,48},{32,0},{48,16},{1,33},{17,49},{33,1},{49,17},{2,34}... | collective-permute-start | bytes 491528 | tf_op jit(solution)/shard_map/ppermute | solution.py:51
  20.4 9.5 %collective-permute-start.6 = (bf16[16,5120]{1,0:T(8,128)(2,1)S(1)}, bf16[16,5120]{1,0:T(8,128)(2,1)S(1)}, u32[]{:S(2)}, u32[]{:S(2)}) collective-permute-start(bf16[16,5120]{1,0:T(8,128)(2,1)S(1)} %get-tuple-element.41.refs_0_), channel_id=1, source_target_pairs={{0,48},{16,32},{32,16},{48,0},{1,49},{17,33},{33,17},{49,1},{2,50}... | collective-permute-start | bytes 491528 | tf_op jit(solution)/shard_map/ppermute | solution.py:51
  35.5 50.9 %copy-start.4 = (bf16[4096,501]{0,1:T(8,128)(2,1)S(1)}, bf16[4096,501]{0,1:T(8,128)(2,1)}, u32[]{:S(2)}) copy-start(bf16[4096,501]{0,1:T(8,128)(2,1)} %param.17) | copy-start | bytes 12312580
  35.5 35.0 %collective-permute-start.17 = (bf16[128,4096]{1,0:T(8,128)(2,1)S(1)}, bf16[128,4096]{1,0:T(8,128)(2,1)S(1)}, u32[]{:S(2)}, u32[]{:S(2)}) collective-permute-start(bf16[128,4096]{1,0:T(8,128)(2,1)S(1)} %get-tuple-element.48), channel_id=1, source_target_pairs={{0,64},{64,0},{1,65},{65,1},{2,66},{66,2},{3,67},{67,3},{4,68},{68... | collective-permute-start | bytes 3145736 | tf_op jit(solution)/shard_map/ppermute | solution.py:47
  35.6 7.1 %collective-permute-start.11 = (bf16[16,5120]{1,0:T(8,128)(2,1)S(1)}, bf16[16,5120]{1,0:T(8,128)(2,1)S(1)}, u32[]{:S(2)}, u32[]{:S(2)}) collective-permute-start(bf16[16,5120]{1,0:T(8,128)(2,1)S(1)} %get-tuple-element.45.refs_0_), channel_id=1, source_target_pairs={{0,2},{2,0},{4,6},{6,4},{1,3},{3,1},{5,7},{7,5},{8,10},{10,8},{12,... | collective-permute-start | bytes 491528 | tf_op jit(solution)/shard_map/ppermute | solution.py:51
  37.6 11.7 %collective-permute-start.12 = (bf16[16,5120]{1,0:T(8,128)(2,1)S(1)}, bf16[16,5120]{1,0:T(8,128)(2,1)S(1)}, u32[]{:S(2)}, u32[]{:S(2)}) collective-permute-start(bf16[16,5120]{1,0:T(8,128)(2,1)S(1)} %get-tuple-element.45.refs_0_), channel_id=1, source_target_pairs={{0,4},{2,6},{4,0},{6,2},{1,5},{3,7},{5,1},{7,3},{8,12},{10,14},{12... | collective-permute-start | bytes 491528 | tf_op jit(solution)/shard_map/ppermute | solution.py:51
  41.2 10.7 %collective-permute-start.13 = (bf16[16,5120]{1,0:T(8,128)(2,1)S(1)}, bf16[16,5120]{1,0:T(8,128)(2,1)S(1)}, u32[]{:S(2)}, u32[]{:S(2)}) collective-permute-start(bf16[16,5120]{1,0:T(8,128)(2,1)S(1)} %get-tuple-element.45.refs_0_), channel_id=1, source_target_pairs={{0,6},{2,4},{4,2},{6,0},{1,7},{3,5},{5,3},{7,1},{8,14},{10,12},{12... | collective-permute-start | bytes 491528 | tf_op jit(solution)/shard_map/ppermute | solution.py:51
  52.7 17.7 %collective-permute-start.14 = (bf16[64,5120]{1,0:T(8,128)(2,1)S(1)}, bf16[64,5120]{1,0:T(8,128)(2,1)S(1)}, u32[]{:S(2)}, u32[]{:S(2)}) collective-permute-start(bf16[64,5120]{1,0:T(8,128)(2,1)S(1)} %plane.3.refs_0_), channel_id=1, source_target_pairs={{0,16},{16,0},{32,48},{48,32},{1,17},{17,1},{33,49},{49,33},{2,18}... | collective-permute-start | bytes 1966088 | tf_op jit(solution)/shard_map/ppermute | solution.py:51
  52.8 30.1 %collective-permute-start.15 = (bf16[64,5120]{1,0:T(8,128)(2,1)S(1)}, bf16[64,5120]{1,0:T(8,128)(2,1)S(1)}, u32[]{:S(2)}, u32[]{:S(2)}) collective-permute-start(bf16[64,5120]{1,0:T(8,128)(2,1)S(1)} %plane.3.refs_0_), channel_id=1, source_target_pairs={{0,32},{16,48},{32,0},{48,16},{1,33},{17,49},{33,1},{49,17},{2,34}... | collective-permute-start | bytes 1966088 | tf_op jit(solution)/shard_map/ppermute | solution.py:51
  54.8 30.7 %collective-permute-start.16 = (bf16[64,5120]{1,0:T(8,128)(2,1)S(1)}, bf16[64,5120]{1,0:T(8,128)(2,1)S(1)}, u32[]{:S(2)}, u32[]{:S(2)}) collective-permute-start(bf16[64,5120]{1,0:T(8,128)(2,1)S(1)} %plane.3.refs_0_), channel_id=1, source_target_pairs={{0,48},{16,32},{32,16},{48,0},{1,49},{17,33},{33,17},{49,1},{2,50}... | collective-permute-start | bytes 1966088 | tf_op jit(solution)/shard_map/ppermute | solution.py:51
  57.5 43.0 %collective-permute-start.7 = (bf16[64,5120]{1,0:T(8,128)(2,1)S(1)}, bf16[64,5120]{1,0:T(8,128)(2,1)S(1)}, u32[]{:S(2)}, u32[]{:S(2)}) collective-permute-start(bf16[64,5120]{1,0:T(8,128)(2,1)S(1)} %plane.2.refs_0_), channel_id=1, source_target_pairs={{0,2},{2,0},{4,6},{6,4},{1,3},{3,1},{5,7},{7,5},{8,10},{10,8},{12,... | collective-permute-start | bytes 1966088 | tf_op jit(solution)/shard_map/ppermute | solution.py:51
  70.5 30.0 %collective-permute-start.8 = (bf16[64,5120]{1,0:T(8,128)(2,1)S(1)}, bf16[64,5120]{1,0:T(8,128)(2,1)S(1)}, u32[]{:S(2)}, u32[]{:S(2)}) collective-permute-start(bf16[64,5120]{1,0:T(8,128)(2,1)S(1)} %plane.2.refs_0_), channel_id=1, source_target_pairs={{0,4},{2,6},{4,0},{6,2},{1,5},{3,7},{5,1},{7,3},{8,12},{10,14},{12... | collective-permute-start | bytes 1966088 | tf_op jit(solution)/shard_map/ppermute | solution.py:51
  70.5 30.0 %collective-permute-start.9 = (bf16[64,5120]{1,0:T(8,128)(2,1)S(1)}, bf16[64,5120]{1,0:T(8,128)(2,1)S(1)}, u32[]{:S(2)}, u32[]{:S(2)}) collective-permute-start(bf16[64,5120]{1,0:T(8,128)(2,1)S(1)} %plane.2.refs_0_), channel_id=1, source_target_pairs={{0,6},{2,4},{4,2},{6,0},{1,7},{3,5},{5,3},{7,1},{8,14},{10,12},{12... | collective-permute-start | bytes 1966088 | tf_op jit(solution)/shard_map/ppermute | solution.py:51
  100.4 34.8 %collective-permute-start.18 = (bf16[256,5120]{1,0:T(8,128)(2,1)}, bf16[256,5120]{1,0:T(8,128)(2,1)}, u32[]{:S(2)}, u32[]{:S(2)}) collective-permute-start(bf16[256,5120]{1,0:T(8,128)(2,1)} %get-tuple-element.53), channel_id=1, source_target_pairs={{0,64},{64,0},{1,65},{65,1},{2,66},{66,2},{3,67},{67,3},{4,68},{68... | collective-permute-start | bytes 7864328 | tf_op jit(solution)/shard_map/ppermute | solution.py:47
  103.4 31.8 %copy-start.18 = (f32[501,256]{1,0:T(8,128)S(1)}, f32[501,256]{1,0:T(8,128)}, u32[]{:S(2)}) copy-start(f32[501,256]{1,0:T(8,128)} %copy-done.17) | copy-start | bytes 1539076
  109.9 38.4 %collective-permute-start.10 = (bf16[256,5120]{1,0:T(8,128)(2,1)}, bf16[256,5120]{1,0:T(8,128)(2,1)}, u32[]{:S(2)}, u32[]{:S(2)}) collective-permute-start(bf16[256,5120]{1,0:T(8,128)(2,1)} %get-tuple-element.43), channel_id=1, source_target_pairs={{0,64},{64,0},{1,65},{65,1},{2,66},{66,2},{3,67},{67,3},{4,68},{68... | collective-permute-start | bytes 7864328 | tf_op jit(solution)/shard_map/ppermute | solution.py:47
  109.9 25.3 %all-to-all-start = ((bf16[64,16,512]{2,1,0:T(8,128)(2,1)}), bf16[64,16,512]{2,1,0:T(8,128)(2,1)S(1)}, u32[]{:S(2)}, u32[]{:S(2)}) async-start(bf16[64,16,512]{2,1,0:T(8,128)(2,1)} %join.3), calls=%async_computation | async-start | bytes 2097152 | tf_op jit(solution)/shard_map/all_to_all | solution.py:55
  155.1 17.7 %all-to-all-start.1 = ((f32[128,8,128]{2,1,0:T(8,128)}), f32[128,8,128]{2,1,0:T(8,128)S(1)}, u32[]{:S(2)}, u32[]{:S(2)}) async-start(f32[128,8,128]{2,1,0:T(8,128)} %broadcast_in_dim.22), calls=%async_computation.1 | async-start | bytes 1048576 | tf_op jit(solution)/shard_map/all_to_all | solution.py:55
  180.1 7.0 %collective-permute-start.19 = (bf16[128,4096]{1,0:T(8,128)(2,1)}, bf16[128,4096]{1,0:T(8,128)(2,1)S(1)}, u32[]{:S(2)}, u32[]{:S(2)}) collective-permute-start(bf16[128,4096]{1,0:T(8,128)(2,1)} %get-tuple-element.64), channel_id=1, source_target_pairs={{0,64},{64,0},{1,65},{65,1},{2,66},{66,2},{3,67},{67,3},{4,68},{68... | collective-permute-start | bytes 3145736 | tf_op jit(solution)/shard_map/ppermute | solution.py:47
  181.4 25.1 %all-to-all-start.2 = ((bf16[64,16,512]{2,1,0:T(8,128)(2,1)}), bf16[64,16,512]{2,1,0:T(8,128)(2,1)S(1)}, u32[]{:S(2)}, u32[]{:S(2)}) async-start(bf16[64,16,512]{2,1,0:T(8,128)(2,1)} %get-tuple-element.66), calls=%async_computation.2 | async-start | bytes 2097152 | tf_op jit(solution)/shard_map/all_to_all | solution.py:55
  188.7 41.8 %copy-start.24 = (bf16[2,4096]{1,0:T(2,128)(2,1)S(1)}, bf16[2,4096]{1,0:T(2,128)(2,1)}, u32[]{:S(2)}) copy-start(bf16[2,4096]{1,0:T(2,128)(2,1)} %states_ref.1) | copy-start | bytes 49156
  188.7 41.8 %copy-start.28 = (bf16[4096]{0:T(1024)(128)(2,1)S(1)}, bf16[4096]{0:T(1024)(128)(2,1)}, u32[]{:S(2)}) copy-start(bf16[4096]{0:T(1024)(128)(2,1)} %param.16) | copy-start | bytes 24580
  190.0 40.9 %copy-start.8 = (bf16[4096,112]{0,1:T(8,128)(2,1)S(1)}, bf16[4096,112]{0,1:T(8,128)(2,1)}, u32[]{:S(2)}) copy-start(bf16[4096,112]{0,1:T(8,128)(2,1)} %param.20) | copy-start | bytes 2752516
  206.5 24.3 %collective-permute-start.20 = (bf16[64,16,512]{2,1,0:T(8,128)(2,1)S(1)}, bf16[64,16,512]{2,1,0:T(8,128)(2,1)S(1)}, u32[]{:S(2)}, u32[]{:S(2)}) collective-permute-start(bf16[64,16,512]{2,1,0:T(8,128)(2,1)S(1)} %all-to-all-done.2.own_ref), channel_id=1, source_target_pairs={{0,64},{64,0},{1,65},{65,1},{2,66},{66,2},{3,67},{67,3},{4,68},{68... | collective-permute-start | bytes 3145736 | tf_op jit(solution)/shard_map/ppermute | solution.py:47
  255.1 2.7 collective-permute-start.21
  260.8 2.7 collective-permute-start.22
  265.9 24.0 %all-to-all-start.5 = ((bf16[64,16,512]{2,1,0:T(8,128)(2,1)}), bf16[64,16,512]{2,1,0:T(8,128)(2,1)S(1)}, u32[]{:S(2)}, u32[]{:S(2)}) async-start(bf16[64,16,512]{2,1,0:T(8,128)(2,1)} %join.5), calls=%async_computation.5 | async-start | bytes 2097152 | tf_op jit(solution)/shard_map/all_to_all | solution.py:55
  (26 other events, 112.4 us)

commit v3 on v2

--- a/solution.py
+++ b/solution.py
@@ -16,19 +16,18 @@
 
 VMEM = pl.BlockSpec(memory_space=pltpu.VMEM)
 SMEM = pl.BlockSpec(memory_space=pltpu.SMEM)
-HBM = pl.BlockSpec(memory_space=pltpu.HBM)
 ANY = pl.BlockSpec(memory_space=pl.ANY)
 SEGMENTS = 8
 SEGMENT = 512
 
 
-def kernel_call(body, name, out_shape, limit=8, flops=0, moved=0, **options):
+def kernel_call(body, name, out_shape, limit=8, **options):
     return pl.pallas_call(
         body,
         name=name,
         out_shape=out_shape,
         compiler_params=pltpu.CompilerParams(vmem_limit_bytes=limit * MIB),
-        cost_estimate=pl.CostEstimate(flops=flops, bytes_accessed=moved, transcendentals=0),
+        cost_estimate=pl.CostEstimate(flops=1, bytes_accessed=1, transcendentals=0),
         **options,
     )
 
@@ -56,11 +55,27 @@
 
 
 def rows_kernel(
-    core_ref, teacher_ref, teacher_gain, student_ref, student_gain, keep_ref, send_ref, gains
+    core_ref, teacher_from, teacher_gain, student_from, student_gain, keep_ref, send_ref,
+    teacher_ref, student_ref, teacher_gains, student_gains, gains, sems,
 ):
+    copies = [
+        pltpu.make_async_copy(source, target, sems.at[i])
+        for i, (source, target) in enumerate(
+            (
+                (student_gain, student_gains),
+                (student_from, student_ref),
+                (teacher_gain, teacher_gains),
+                (teacher_from, teacher_ref),
+            )
+        )
+    ]
+    for copy in copies:
+        copy.start()
+    for copy in copies:
+        copy.wait()
     first = student_gain.shape[0]
-    gains[:first, :] = student_gain[...].astype(jnp.float32)
-    gains[first:, :] = teacher_gain[...].astype(jnp.float32)
+    gains[:first, :] = student_gains[...].astype(jnp.float32)
+    gains[first:, :] = teacher_gains[...].astype(jnp.float32)
     column = 0
     for values, base in ((student_ref, 0), (teacher_ref, first)):
         half = values.shape[1] // 2
@@ -117,7 +132,6 @@
         "plane",
         shape_of((4 * tokens, width)),
         limit=2,
-        moved=16 * tokens * width,
         in_specs=[SMEM] + [ANY] * 4,
         out_specs=ANY,
         scratch_shapes=[pltpu.SemaphoreType.DMA((4,))],
@@ -164,83 +178,71 @@
         stats_out[i + 3 : i + 4, :] = row[:, 128:]
 
 
-def logits_kernel(group, own, place_ref, *refs):
-    count = 4 if own else 1
-    pieces, heads, refs = refs[:count], refs[count : count + 2], refs[count + 2 :]
+def logits_kernel(last, place_ref, *refs):
+    rows_from, heads, refs = refs[:2], refs[2:4], refs[4:]
     rows, head, row_sems, head_sems = refs[-4:]
     refs = refs[:-4]
     copies = []
     column = 0
-    for i, (kind, start, width) in enumerate(GROUPS[group]):
-        columns = slice(column, column + width)
-        size = heads[kind].shape[1] // 2
-        start = pl.multiple_of(place_ref[0] * size + start, 128)
-        copy = pltpu.make_async_copy(
-            heads[kind].at[:, pl.ds(start, width)], head.at[:, columns], head_sems.at[i]
-        )
-        copy.start()
-        needed = [copy]
-        for m, piece in enumerate(pieces):
-            tokens = piece.shape[0]
-            at = pl.multiple_of((place_ref[1] ^ m) * tokens, tokens)
-            copy = pltpu.make_async_copy(
-                piece.at[:, columns], rows.at[pl.ds(at, tokens), columns], row_sems.at[i, m]
+    for group, source in zip(GROUPS, rows_from):
+        base = column
+        for kind, start, width in group:
+            i = len(copies)
+            columns = slice(column, column + width)
+            size = heads[kind].shape[1] // 2
+            start = pl.multiple_of(place_ref[0] * size + start, 128)
+            pair = (
+                pltpu.make_async_copy(
+                    source.at[:, column - base : column - base + width],
+                    rows.at[:, columns],
+                    row_sems.at[i],
+                ),
+                pltpu.make_async_copy(
+                    heads[kind].at[:, pl.ds(start, width)], head.at[:, columns], head_sems.at[i]
+                ),
             )
-            copy.start()
-            needed.append(copy)
-        copies.append((kind, columns, needed))
-        column = column + width
-    sums = [None, None]
-    for kind, columns, needed in copies:
-        for copy in needed:
+            for copy in pair:
+                copy.start()
+            copies.append((kind + (base > 0), columns, pair))
+            column = column + width
+    sums = [None, None, None]
+    for kind, columns, pair in copies:
+        for copy in pair:
             copy.wait()
         term = row_product(head[:, columns], rows[:, columns])
         sums[kind] = term if sums[kind] is None else sums[kind] + term
-    if group == 0:
-        student, teacher = sums
-        if own:
-            student_out, teacher_out = refs
-        else:
-            student_in, teacher_in, student_out, teacher_out = refs
-            student, teacher = student + student_in[...], teacher + teacher_in[...]
+    if last:
+        came, (student_out, teacher_out, stats_out) = refs[:3], refs[3:]
+        student, teacher, second = (total + ref[...] for total, ref in zip(sums, came))
+        teacher = teacher + reordered(second)
         student_out[...] = student
         teacher_out[...] = teacher
-    elif own:
-        refs[0][...] = sums[1]
+        softmax_stats(teacher, student, stats_out)
     else:
-        second_in, student_in, teacher_in, teacher_out, stats_out = refs
-        teacher = teacher_in[...] + reordered(sums[1] + second_in[...])
-        teacher_out[...] = teacher
-        softmax_stats(teacher, student_in[...], stats_out)
-
-
-def logits_part(group, place, pieces, heads, sums=()):
-    vocab, tokens, width = heads[1].shape[0], 256, WIDTHS[group]
-    own = len(pieces) > 1
+        for total, out in zip(sums, refs):
+            out[...] = total
+
+
+def logits_part(place, rows, heads, sums=()):
+    vocab, tokens = heads[1].shape[0], rows[0].shape[0]
     shape = shape_of((vocab, tokens), jnp.float32)
-    out_shape = [shape, shape] if group == 0 else [shape]
-    scratch = [
-        pltpu.VMEM((vocab, width), jnp.bfloat16),
-        pltpu.SemaphoreType.DMA((len(GROUPS[group]), 4)),
-        pltpu.SemaphoreType.DMA((len(GROUPS[group]),)),
-    ]
-    if own:
-        out_shape = out_shape + [shape_of((tokens, width))]
-    else:
-        scratch = [pltpu.VMEM((tokens, width), jnp.bfloat16)] + scratch
-        if group == 1:
-            out_shape = out_shape + [shape_of((8, 128), jnp.float32)]
+    last = len(sums) > 0
+    pieces = sum(len(group) for group in GROUPS)
+    out_shape = [shape, shape, shape_of((8, 128), jnp.float32) if last else shape]
     return kernel_call(
-        functools.partial(logits_kernel, group, own),
+        functools.partial(logits_kernel, last),
         "logits",
         out_shape,
-        limit=20,
-        flops=2 * vocab * tokens * width,
-        moved=(vocab + tokens) * width * 2,
-        in_specs=[SMEM] + [ANY] * len(pieces) + [HBM] * 2 + [VMEM] * len(sums),
-        out_specs=[VMEM] * len(out_shape),
-        scratch_shapes=scratch,
-    )(place, *pieces, *heads, *sums)
+        limit=56,
+        in_specs=[SMEM] + [ANY] * 4 + [VMEM] * len(sums),
+        out_specs=[VMEM] * 3,
+        scratch_shapes=[
+            pltpu.VMEM((tokens, sum(WIDTHS)), jnp.bfloat16),
+            pltpu.VMEM((vocab, sum(WIDTHS)), jnp.bfloat16),
+            pltpu.SemaphoreType.DMA((pieces,)),
+            pltpu.SemaphoreType.DMA((pieces,)),
+        ],
+    )(place, *rows, *heads, *sums)
 
 
 def one_hot_rows(core):
@@ -293,9 +295,7 @@
             shape_of((tokens // 2, width)),
             shape_of((1, tokens), jnp.float32),
         ],
-        limit=14,
-        flops=2 * vocab * tokens * width,
-        moved=vocab * width * 2 + tokens * width * 3,
+        limit=56,
         grid_spec=pltpu.PrefetchScalarGridSpec(
             num_scalar_prefetch=1,
             grid=(width // columns,),
@@ -312,33 +312,45 @@
     )(core, every, weight, teacher, student, student_head_t)
 
 
-def pick_kernel(ids_ref, head_ref, own_ref, send_ref):
-    tokens, vocab = ids_ref.shape[0], head_ref.shape[0]
-    entry = lax.broadcasted_iota(jnp.int32, (tokens, vocab), 1)
-    chosen = (ids_ref[...] == entry).astype(jnp.bfloat16)
-    out = jnp.dot(chosen, head_ref[...], preferred_element_type=jnp.float32)
-    own_ref[...] = out[: tokens // 2].astype(jnp.bfloat16)
-    send_ref[...] = out[tokens // 2 :].astype(jnp.bfloat16)
-
-
-def pick_part(ids, student_head_t):
+def pick_kernel(place_ref, ids_ref, head_ref, own_ref, send_ref, chosen):
+    @pl.when(pl.program_id(0) == 0)
+    def _():
+        vocab, tokens = head_ref.shape[0], ids_ref.shape[1]
+        entry = lax.broadcasted_iota(jnp.int32, (vocab, tokens), 0) + place_ref[1] * vocab
+        place = lax.broadcasted_iota(jnp.int32, (tokens, tokens), 0)
+        column = lax.broadcasted_iota(jnp.int32, (tokens, tokens), 1)
+        source = (((place >> 7) ^ place_ref[0]) << 7) | ((place & 63) << 1) | ((place >> 6) & 1)
+        chosen[...] = row_product(
+            (column == source).astype(jnp.bfloat16), (ids_ref[...] == entry).astype(jnp.bfloat16)
+        ).astype(jnp.bfloat16)
+
+    half = own_ref.shape[0]
+    out = jnp.dot(chosen[...], head_ref[...], preferred_element_type=jnp.float32)
+    own_ref[...] = out[:half].astype(jnp.bfloat16)
+    send_ref[...] = out[half:].astype(jnp.bfloat16)
+
+
+def pick_part(place, ids, student_head_t):
     vocab, width = student_head_t.shape
-    tokens, columns = ids.shape[0], 1024
-    half = pl.BlockSpec((tokens // 2, columns), lambda i: (0, i))
+    tokens, columns = ids.shape[1], 1024
+    half = pl.BlockSpec((tokens // 2, columns), lambda i, p: (0, i))
     shape = shape_of((tokens // 2, width))
     return kernel_call(
         pick_kernel,
         "pick",
         [shape, shape],
-        flops=2 * vocab * tokens * width,
-        moved=(vocab + tokens) * width * 2,
-        grid=(width // columns,),
-        in_specs=[
-            pl.BlockSpec(ids.shape, lambda i: (0, 0)),
-            pl.BlockSpec((vocab, columns), lambda i: (0, i)),
-        ],
-        out_specs=[half, half],
-    )(ids, student_head_t)
+        limit=56,
+        grid_spec=pltpu.PrefetchScalarGridSpec(
+            num_scalar_prefetch=1,
+            grid=(width // columns,),
+            in_specs=[
+                pl.BlockSpec(ids.shape, lambda i, p: (0, 0)),
+                pl.BlockSpec((vocab, columns), lambda i, p: (0, i)),
+            ],
+            out_specs=[half, half],
+            scratch_shapes=[pltpu.VMEM((tokens, vocab), jnp.bfloat16)],
+        ),
+    )(place, ids, student_head_t)
 
 
 def join_kernel(own_ref, came_ref, out_ref, rows):
@@ -366,7 +378,6 @@
         "join",
         shape_of(block),
         limit=10,
-        moved=own.size * 8,
         in_specs=[VMEM] * 2,
         out_specs=VMEM,
         scratch_shapes=[pltpu.VMEM((SEGMENT // 128, chips * 2 * SEGMENTS, 128), jnp.float32)],
@@ -444,7 +455,6 @@
         body,
         name,
         [shape_of(BLOCK, jnp.float32), shape_of(blocks.shape)],
-        moved=blocks.size * 4,
         in_specs=[VMEM] * (1 + len(others)),
         out_specs=[VMEM] * 2,
         scratch_shapes=list(scratch),
@@ -519,8 +529,6 @@
         name,
         out_shape,
         limit=18,
-        flops=16 * 112 * 256 * 4096 // 2,
-        moved=blocks.size * 8,
         in_specs=[VMEM] * (2 + len(others)),
         out_specs=[VMEM] * len(out_shape),
         scratch_shapes=[scratch, scratch],
@@ -560,9 +568,17 @@
         rows_kernel,
         "rows",
         [half_shape, half_shape],
-        in_specs=[SMEM] + [VMEM] * 4,
+        limit=56,
+        in_specs=[SMEM] + [ANY] * 4,
         out_specs=[VMEM] * 2,
-        scratch_shapes=[pltpu.VMEM((160, 128), jnp.float32)],
+        scratch_shapes=[
+            pltpu.VMEM(teacher_states.shape, jnp.bfloat16),
+            pltpu.VMEM(student_states.shape, jnp.bfloat16),
+            pltpu.VMEM(teacher_gain.shape, jnp.bfloat16),
+            pltpu.VMEM(student_gain.shape, jnp.bfloat16),
+            pltpu.VMEM((160, 128), jnp.float32),
+            pltpu.SemaphoreType.DMA((4,)),
+        ],
     )(own_core, teacher_states, teacher_gain, student_states, student_gain)
     rows = kernel_call(
         chip_kernel,
@@ -571,38 +587,32 @@
         in_specs=[SMEM] + [VMEM] * 2,
         out_specs=VMEM,
     )(own_core, keep, swap_cores(send))
+    pieces = line_pieces(rows, ("yh", "yl"))
+
+    place = jnp.stack([core, device]).astype(jnp.int32)
+    picked = join_part(*pick_part(place, token_ids.reshape(1, 256), student_head_t))
+    pieces, picked = lax.optimization_barrier((pieces, picked))
+    picked = exchange(picked, CHIPS)
+
     first, second = kernel_call(
         line_kernel,
         "line",
         [shape_of((16, w)) for w in WIDTHS],
         in_specs=[SMEM] + [VMEM] * 4,
         out_specs=[VMEM] * 2,
-    )(y, *line_pieces(rows, ("yh", "yl")))
+    )(y, *pieces)
     first, second = line_pieces(first, "z"), line_pieces(second, "x")
-    first, second = in_line_order(z, first), in_line_order(x, second)
-
-    ids = token_ids.reshape(2, 64, 2).transpose(0, 2, 1).reshape(2, 128)
-    ids = jnp.where(core == 0, ids, ids[::-1]).reshape(256, 1) - device * student_head.shape[1]
-    ids, second = lax.optimization_barrier((ids, second))
-    picked = join_part(*pick_part(ids, student_head_t))
-
-    first, second = line_pieces(first, "x"), line_pieces(second, "z")
-    first, picked = lax.optimization_barrier((first, picked))
-    picked = exchange(picked, CHIPS)
-    place = jnp.concatenate([own_core, x])
-    student, teacher, first = logits_part(0, place, first, heads)
-    place = jnp.concatenate([own_core, z])
-    teacher_second, second = logits_part(1, place, second, heads)
-    first, second = swap_cores(first), swap_cores(second)
-    first, picked = lax.optimization_barrier((first, picked))
-    place = jnp.concatenate([1 - own_core, 0 * x])
-    student, teacher = logits_part(0, place, [first], heads, (student, teacher))
-    teacher, stats = logits_part(
-        1, place, [second], heads, (teacher_second, student, teacher)
-    )
-    every = exchange(jnp.broadcast_to(stats[None], (128,) + stats.shape), AXES)
+    first, second, picked = lax.optimization_barrier((first, second, picked))
     embedded, ffn_rows = owner_part(embed_kernel, "embed", picked, ffn_gain)
     ffn_rows = exchange(ffn_rows, CHIPS)
+    first, second = in_line_order(z, first), in_line_order(x, second)
+    first, second = line_pieces(first, "x"), line_pieces(second, "z")
+    first, second, ffn_rows = lax.optimization_barrier((first, second, ffn_rows))
+    rows = (in_line_order(x, first), in_line_order(z, second))
+    others = tuple(swap_cores(part) for part in rows)
+    sums = logits_part(own_core, rows, heads)
+    student, teacher, stats = logits_part(1 - own_core, others, heads, sums)
+    every = exchange(jnp.broadcast_to(stats[None], (128,) + stats.shape), AXES)
 
     weight = token_weight.reshape(2, 4, 2, 4, 2, 2).transpose(1, 3, 2, 4, 0, 5).reshape(1, 256)
     own, send, divergence = row_grad_part(
@@ -610,11 +620,11 @@
     )
     divergence = divergence.reshape(4, 4, 2, 2, 2, 2).transpose(4, 0, 2, 1, 3, 5).reshape(256)
     row_grad = join_part(own, send)
-    row_grad, ffn_rows = lax.optimization_barrier((row_grad, ffn_rows))
-    row_grad = exchange(row_grad, CHIPS)
     (hidden,) = ffn_part(
         gate_kernel, "gate_upper", [shape_of((224, 256), jnp.float32)], ffn_rows, gate_t, up_t
     )
+    row_grad, hidden = lax.optimization_barrier((row_grad, hidden))
+    row_grad = exchange(row_grad, CHIPS)
     final_grad, final_half = owner_part(
         final_kernel,
         "final",
@@ -623,7 +633,6 @@
         student_gain,
         scratch=[pltpu.VMEM(BLOCK, jnp.float32)],
     )
-    final_half, hidden = lax.optimization_barrier((final_half, hidden))
     final_half = exchange(final_half, CHIPS)
     shape = (128, 4096)
     own, send = ffn_part(

time: 292 us -> 263 us (0.901)
  waiting for transfers between devices: 120 us -> 82.8 us
  local copies, waits for them, and re-layouts: 37.9 us -> 21.2 us
  starting transfers between devices: 42.3 us -> 56.5 us
  Pallas kernels: 42 us -> 52 us
    all_to_all x4, waiting for transfers between devices: 65.9 us -> 29.4 us  [exchange(): return lax.all_to_all(blocks, axes, split_axis=0, concat_axis=0, tiled=True)]
    unnamed x62 -> x64, local copies, waits for them, and re-layouts: 34.1 us -> 17.3 us
    all_to_all x4, starting transfers between devices: 20.7 us -> 31.8 us  [exchange(): return lax.all_to_all(blocks, axes, split_axis=0, concat_axis=0, tiled=True)]
    pallas_call x11 -> x9, Pallas kernels: 33.6 us -> 39 us  [the longest x2 20.6 us: logits_part(): kernel_call(functools.partial(logits_kernel, last), 'logits', out_shape,...]
  transfers between devices with their start and end apart: 27 -> 27, of which waited for: 18 -> 12; matrix products, arithmetic and copies ran while one was open for 1% -> 1% of each run, Pallas kernels for 7% -> 10%
where the time goes in v3:
time: 263 us; the launch traced here: 262 us
  waiting for transfers between devices  82.8 us (31%)
  starting transfers between devices  56.5 us (21%)
  Pallas kernels  52 us (20%)
  blocking collectives  47.5 us (18%)
  local copies, waits for them, and re-layouts  21.2 us (8%)
    all_to_all x2, blocking collectives, exchange(): return lax.all_to_all(blocks, axes, split_axis=0, concat_axis=0, tiled=True)  47.5 us
    ppermute x15, waiting for transfers between devices, line_pieces(): lax.ppermute(block, line, [(i, i ^ m) for i in range(4)])  46.1 us
    all_to_all x4, starting transfers between devices, exchange(): return lax.all_to_all(blocks, axes, split_axis=0, concat_axis=0, tiled=True)  31.8 us
    all_to_all x4, waiting for transfers between devices, exchange(): return lax.all_to_all(blocks, axes, split_axis=0, concat_axis=0, tiled=True)  29.4 us
    ppermute x15, starting transfers between devices, line_pieces(): lax.ppermute(block, line, [(i, i ^ m) for i in range(4)])  23.5 us
    pallas_call x2, Pallas kernels, logits_part(): kernel_call(functools.partial(logits_kernel, last), 'logits', out_shape,...  20.6 us
    unnamed x64, local copies, waits for them, and re-layouts  17.3 us
    ppermute x8, waiting for transfers between devices, swap_cores(): return lax.ppermute(values, 'core', [(0, 1), (1, 0)])  7.36 us
  transfers between devices with their start and end apart: 27, of which 12 were waited for; matrix products, arithmetic and copies ran while one was open for 1% of the time, Pallas kernels for 10%

profile of v3, /device:TPU:0, one launch (start us, length us, event | category | flops | bytes accessed | tf_op | source)
XLA Modules:
  0.0 262.3 jit_solution(792516708600365031)
XLA Ops:
  1.3 5.9 %pick.1 = (bf16[128,4096]{1,0:T(8,128)(2,1)}, bf16[128,4096]{1,0:T(8,128)(2,1)}) custom-call(s32[2]{0:T(128)} %pad_add_fusion.place_ref, s32[1,256]{1,0:T(1,128)} %bitcast.32, bf16[501,4096]{1,0:T(8,128)(2,1)} %bitcast.25), custom_call_target="tpu_custom_call" | custom-call | flops 1 | bytes 1 | tf_op jit(solution)/shard_map/pick/pallas_call | solution.py:338
  7.3 1.9 rows.1
  11.7 3.2 %collective-permute-start.3 = (bf16[4,10240]{1,0:T(4,128)(2,1)S(1)}, bf16[4,10240]{1,0:T(4,128)(2,1)S(1)}, u32[]{:S(2)}, u32[]{:S(2)}) collective-permute-start(bf16[4,10240]{1,0:T(4,128)(2,1)S(1)} %chip.1.refs_0_), channel_id=1, source_target_pairs={{0,9},{1,8},{8,1},{9,0},{2,11},{3,10},{10,3},{11,2},{4,13},{5,12},... | collective-permute-start | bytes 245768 | tf_op jit(solution)/shard_map/ppermute | solution.py:50
  17.1 2.3 join.3
  19.4 2.3 collective-permute-done.2.refs_2_
  21.6 9.9 %all-to-all-start = ((bf16[64,16,512]{2,1,0:T(8,128)(2,1)}), bf16[64,16,512]{2,1,0:T(8,128)(2,1)S(1)}, u32[]{:S(2)}, u32[]{:S(2)}) async-start(bf16[64,16,512]{2,1,0:T(8,128)(2,1)} %join.3), calls=%async_computation | async-start | bytes 2097152 | tf_op jit(solution)/shard_map/all_to_all | solution.py:54
  31.7 2.9 %collective-permute-start.7 = (bf16[16,5120]{1,0:T(8,128)(2,1)S(1)}, bf16[16,5120]{1,0:T(8,128)(2,1)S(1)}, u32[]{:S(2)}, u32[]{:S(2)}) collective-permute-start(bf16[16,5120]{1,0:T(8,128)(2,1)S(1)} %get-tuple-element.59.refs_0_), channel_id=1, source_target_pairs={{0,6},{2,4},{4,2},{6,0},{1,7},{3,5},{5,3},{7,1},{8,14},{10,12},{12... | collective-permute-start | bytes 491528 | tf_op jit(solution)/shard_map/ppermute | solution.py:50
  36.5 3.0 %collective-permute-start.10 = (bf16[16,5120]{1,0:T(8,128)(2,1)S(1)}, bf16[16,5120]{1,0:T(8,128)(2,1)S(1)}, u32[]{:S(2)}, u32[]{:S(2)}) collective-permute-start(bf16[16,5120]{1,0:T(8,128)(2,1)S(1)} %get-tuple-element.63.refs_0_), channel_id=1, source_target_pairs={{0,48},{16,32},{32,16},{48,0},{1,49},{17,33},{33,17},{49,1},{2,50}... | collective-permute-start | bytes 491528 | tf_op jit(solution)/shard_map/ppermute | solution.py:50
  40.2 12.4 %collective-permute-done.7.refs_3_ = bf16[16,5120]{1,0:T(8,128)(2,1)S(1)} collective-permute-done((bf16[16,5120]{1,0:T(8,128)(2,1)S(1)}, bf16[16,5120]{1,0:T(8,128)(2,1)S(1)}, u32[]{:S(2)}, u32[]{:S(2)}) %collective-permute-start.7) | collective-permute-done | bytes 163872 | tf_op jit(solution)/shard_map/ppermute | solution.py:50
  55.8 2.7 %collective-permute-done.8.refs_1_ = bf16[16,5120]{1,0:T(8,128)(2,1)S(1)} collective-permute-done((bf16[16,5120]{1,0:T(8,128)(2,1)S(1)}, bf16[16,5120]{1,0:T(8,128)(2,1)S(1)}, u32[]{:S(2)}, u32[]{:S(2)}) %collective-permute-start.8) | collective-permute-done | bytes 163872 | tf_op jit(solution)/shard_map/ppermute | solution.py:50
  59.4 2.7 %collective-permute-start.16 = (bf16[64,5120]{1,0:T(8,128)(2,1)S(1)}, bf16[64,5120]{1,0:T(8,128)(2,1)S(1)}, u32[]{:S(2)}, u32[]{:S(2)}) collective-permute-start(bf16[64,5120]{1,0:T(8,128)(2,1)S(1)} %plane.5.refs_0_), channel_id=1, source_target_pairs={{0,6},{2,4},{4,2},{6,0},{1,7},{3,5},{5,3},{7,1},{8,14},{10,12},{12... | collective-permute-start | bytes 1966088 | tf_op jit(solution)/shard_map/ppermute | solution.py:50
  62.1 1.4 embed.1
  63.4 7.9 %all-to-all-start.1 = ((bf16[64,16,512]{2,1,0:T(8,128)(2,1)}), bf16[64,16,512]{2,1,0:T(8,128)(2,1)S(1)}, u32[]{:S(2)}, u32[]{:S(2)}) async-start(bf16[64,16,512]{2,1,0:T(8,128)(2,1)} %get-tuple-element.68), calls=%async_computation.1 | async-start | bytes 2097152 | tf_op jit(solution)/shard_map/all_to_all | solution.py:54
  71.4 3.2 %collective-permute-start.15 = (bf16[64,5120]{1,0:T(8,128)(2,1)S(1)}, bf16[64,5120]{1,0:T(8,128)(2,1)S(1)}, u32[]{:S(2)}, u32[]{:S(2)}) collective-permute-start(bf16[64,5120]{1,0:T(8,128)(2,1)S(1)} %plane.5.refs_0_), channel_id=1, source_target_pairs={{0,4},{2,6},{4,0},{6,2},{1,5},{3,7},{5,1},{7,3},{8,12},{10,14},{12... | collective-permute-start | bytes 1966088 | tf_op jit(solution)/shard_map/ppermute | solution.py:50
  79.6 3.0 %collective-permute-start.13 = (bf16[64,5120]{1,0:T(8,128)(2,1)S(1)}, bf16[64,5120]{1,0:T(8,128)(2,1)S(1)}, u32[]{:S(2)}, u32[]{:S(2)}) collective-permute-start(bf16[64,5120]{1,0:T(8,128)(2,1)S(1)} %plane.4.refs_0_), channel_id=1, source_target_pairs={{0,48},{16,32},{32,16},{48,0},{1,49},{17,33},{33,17},{49,1},{2,50}... | collective-permute-start | bytes 1966088 | tf_op jit(solution)/shard_map/ppermute | solution.py:50
  83.3 17.6 %collective-permute-done.16.refs_3_ = bf16[64,5120]{1,0:T(8,128)(2,1)S(1)} collective-permute-done((bf16[64,5120]{1,0:T(8,128)(2,1)S(1)}, bf16[64,5120]{1,0:T(8,128)(2,1)S(1)}, u32[]{:S(2)}, u32[]{:S(2)}) %collective-permute-start.16) | collective-permute-done | bytes 655392 | tf_op jit(solution)/shard_map/ppermute | solution.py:50
  102.0 11.0 %collective-permute-done.14.refs_1_ = bf16[64,5120]{1,0:T(8,128)(2,1)S(1)} collective-permute-done((bf16[64,5120]{1,0:T(8,128)(2,1)S(1)}, bf16[64,5120]{1,0:T(8,128)(2,1)S(1)}, u32[]{:S(2)}, u32[]{:S(2)}) %collective-permute-start.14) | collective-permute-done | bytes 655392 | tf_op jit(solution)/shard_map/ppermute | solution.py:50
  122.5 9.3 %logits.2 = (f32[501,256]{1,0:T(8,128)}, f32[501,256]{1,0:T(8,128)}, f32[501,256]{1,0:T(8,128)}) custom-call(s32[1]{0:T(128)} %bitcast.core_ref.place_ref, bf16[256,5120]{1,0:T(8,128)(2,1)} %copy-done.1, bf16[256,5120]{1,0:T(8,128)(2,1)} %copy-done, bf16[501,4096]{1,0:T(8,128)(2,1)} %bitcast.26, bf16[501,16384]{1,0:T(8,128)(2,1)} %bitcast.23), custom_call_target="tpu_custom_call" | custom-call | flops 1 | bytes 1 | tf_op jit(solution)/shard_map/logits/pallas_call | solution.py:232
  131.8 11.3 %logits.3 = (f32[501,256]{1,0:T(8,128)}, f32[501,256]{1,0:T(8,128)}, f32[8,128]{1,0:T(8,128)}) custom-call(s32[1]{0:T(128)S(6)} %sub.3.place_ref, bf16[256,5120]{1,0:T(8,128)(2,1)} %collective-permute-done.17.refs_0_, bf16[256,5120]{1,0:T(8,128)(2,1)} %collective-permute-done.18.refs_1_, bf16[501,4096]{1,0:T(8,128)(2,1)} %bitcast.27, ...), custom_call_target="tpu_custom_call" | custom-call | flops 1 | bytes 1 | tf_op jit(solution)/shard_map/logits/pallas_call | solution.py:232
  143.1 1.5 broadcast_in_dim.22
  144.7 9.3 %all-to-all-start.2 = ((f32[128,8,128]{2,1,0:T(8,128)}), f32[128,8,128]{2,1,0:T(8,128)S(1)}, u32[]{:S(2)}, u32[]{:S(2)}) async-start(f32[128,8,128]{2,1,0:T(8,128)} %broadcast_in_dim.22), calls=%async_computation.2 | async-start | bytes 1048576 | tf_op jit(solution)/shard_map/all_to_all | solution.py:54
  155.0 12.1 %all-to-all-done.2.every_ref = f32[128,8,128]{2,1,0:T(8,128)S(1)} async-done(((f32[128,8,128]{2,1,0:T(8,128)}), f32[128,8,128]{2,1,0:T(8,128)S(1)}, u32[]{:S(2)}, u32[]{:S(2)}) %all-to-all-start.2) | async-done | bytes 524320 | tf_op jit(solution)/shard_map/all_to_all | solution.py:54
  167.9 6.6 %row_grad.1 = (f32[128,4096]{1,0:T(8,128)}, bf16[128,4096]{1,0:T(8,128)(2,1)}, f32[1,256]{1,0:T(1,128)}) custom-call(s32[1]{0:T(128)} %bitcast.core_ref.place_ref, f32[128,8,128]{2,1,0:T(8,128)} %copy-done.29, f32[1,256]{1,0:T(1,128)} %reshape.34.weight_ref, f32[501,256]{1,0:T(8,128)} %get-tuple-element.81.teacher_ref, ...), custom_call_target="tpu_custom_call" | custom-call | flops 1 | bytes 1 | tf_op jit(solution)/shard_map/row_grad/pallas_call | solution.py:290
  174.6 1.7 gate_upper.1.hidden_ref
  178.7 24.9 %all_to_all.30.blocks_ref = bf16[64,16,512]{2,1,0:T(8,128)(2,1)S(1)} all-to-all(bf16[64,16,512]{2,1,0:T(8,128)(2,1)S(1)} %join.4), channel_id=1, replica_groups=mesh['core'=2,'x'=4,'yh'=2,'z'=4,'yl'=2] {'x','yh','z','yl'}, dimensions={0} | all-to-all | bytes 2097152 | tf_op jit(solution)/shard_map/all_to_all | solution.py:54
  204.0 22.5 %all_to_all.31.own_ref = bf16[64,16,512]{2,1,0:T(8,128)(2,1)S(1)} all-to-all(bf16[64,16,512]{2,1,0:T(8,128)(2,1)S(1)} %get-tuple-element.88), channel_id=1, replica_groups=mesh['core'=2,'x'=4,'yh'=2,'z'=4,'yl'=2] {'x','yh','z','yl'}, dimensions={0} | all-to-all | bytes 2097152 | tf_op jit(solution)/shard_map/all_to_all | solution.py:54
  226.6 2.7 %collective-permute-done.21.other_ref = bf16[64,16,512]{2,1,0:T(8,128)(2,1)S(1)} collective-permute-done((bf16[64,16,512]{2,1,0:T(8,128)(2,1)S(1)}, bf16[64,16,512]{2,1,0:T(8,128)(2,1)S(1)}, u32[]{:S(2)}, u32[]{:S(2)}) %collective-permute-start.21) | collective-permute-done | bytes 1048608 | tf_op jit(solution)/shard_map/ppermute | solution.py:46
  229.2 3.0 %ffn_grad.1 = (f32[128,4096]{1,0:T(8,128)S(1)}, bf16[128,4096]{1,0:T(8,128)(2,1)S(1)}) custom-call(bf16[64,16,512]{2,1,0:T(8,128)(2,1)S(1)} %all_to_all.31.own_ref, bf16[64,16,512]{2,1,0:T(8,128)(2,1)S(1)} %collective-permute-done.21.other_ref, bf16[112,4096]{1,0:T(8,128)(2,1)S(1)} %copy-done.6, f32[224,256]{1,0:T(8,128)S(1)} %gate_upper.1.hidden_ref, ...), custom_call_target="tpu_custom_call" | custom-call | flops 1 | bytes 1 | tf_op jit(solution)/shard_map/ffn_grad/pallas_call | solution.py:527
  232.5 2.5 collective-permute-done.22.came_ref
  235.0 2.3 join.5
  237.3 4.7 %all-to-all-start.5 = ((bf16[64,16,512]{2,1,0:T(8,128)(2,1)}), bf16[64,16,512]{2,1,0:T(8,128)(2,1)S(1)}, u32[]{:S(2)}, u32[]{:S(2)}) async-start(bf16[64,16,512]{2,1,0:T(8,128)(2,1)} %join.5), calls=%async_computation.5 | async-start | bytes 2097152 | tf_op jit(solution)/shard_map/all_to_all | solution.py:54
  244.1 17.3 %all-to-all-done.5.blocks_ref = bf16[64,16,512]{2,1,0:T(8,128)(2,1)S(1)} async-done(((bf16[64,16,512]{2,1,0:T(8,128)(2,1)}), bf16[64,16,512]{2,1,0:T(8,128)(2,1)S(1)}, u32[]{:S(2)}, u32[]{:S(2)}) %all-to-all-start.5) | async-done | bytes 1048608 | tf_op jit(solution)/shard_map/all_to_all | solution.py:54
  (117 shorter events, 36.5 us)
Async XLA Ops:
  7.3 8.6 %collective-permute-start.4 = (bf16[128,4096]{1,0:T(8,128)(2,1)}, bf16[128,4096]{1,0:T(8,128)(2,1)S(1)}, u32[]{:S(2)}, u32[]{:S(2)}) collective-permute-start(bf16[128,4096]{1,0:T(8,128)(2,1)} %get-tuple-element.51), channel_id=1, source_target_pairs={{0,64},{64,0},{1,65},{65,1},{2,66},{66,2},{3,67},{67,3},{4,68},{68... | collective-permute-start | bytes 3145736 | tf_op jit(solution)/shard_map/ppermute | solution.py:46
  9.1 1.7 collective-permute-start
  11.7 7.7 %collective-permute-start.3 = (bf16[4,10240]{1,0:T(4,128)(2,1)S(1)}, bf16[4,10240]{1,0:T(4,128)(2,1)S(1)}, u32[]{:S(2)}, u32[]{:S(2)}) collective-permute-start(bf16[4,10240]{1,0:T(4,128)(2,1)S(1)} %chip.1.refs_0_), channel_id=1, source_target_pairs={{0,9},{1,8},{8,1},{9,0},{2,11},{3,10},{10,3},{11,2},{4,13},{5,12},... | collective-permute-start | bytes 245768 | tf_op jit(solution)/shard_map/ppermute | solution.py:50
  14.8 6.8 %collective-permute-start.2 = (bf16[4,10240]{1,0:T(4,128)(2,1)S(1)}, bf16[4,10240]{1,0:T(4,128)(2,1)S(1)}, u32[]{:S(2)}, u32[]{:S(2)}) collective-permute-start(bf16[4,10240]{1,0:T(4,128)(2,1)S(1)} %chip.1.refs_0_), channel_id=1, source_target_pairs={{0,8},{1,9},{8,0},{9,1},{2,10},{3,11},{10,2},{11,3},{4,12},{5,13},... | collective-permute-start | bytes 245768 | tf_op jit(solution)/shard_map/ppermute | solution.py:50
  15.5 6.2 %collective-permute-start.1 = (bf16[4,10240]{1,0:T(4,128)(2,1)S(1)}, bf16[4,10240]{1,0:T(4,128)(2,1)S(1)}, u32[]{:S(2)}, u32[]{:S(2)}) collective-permute-start(bf16[4,10240]{1,0:T(4,128)(2,1)S(1)} %chip.1.refs_0_), channel_id=1, source_target_pairs={{0,1},{1,0},{8,9},{9,8},{2,3},{3,2},{10,11},{11,10},{4,5},{5,4},{1... | collective-permute-start | bytes 245768 | tf_op jit(solution)/shard_map/ppermute | solution.py:50
  19.4 42.7 %copy-start.27 = (bf16[4096]{0:T(1024)(128)(2,1)S(1)}, bf16[4096]{0:T(1024)(128)(2,1)}, u32[]{:S(2)}) copy-start(bf16[4096]{0:T(1024)(128)(2,1)} %param.19) | copy-start | bytes 24580
  21.6 36.9 %all-to-all-start = ((bf16[64,16,512]{2,1,0:T(8,128)(2,1)}), bf16[64,16,512]{2,1,0:T(8,128)(2,1)S(1)}, u32[]{:S(2)}, u32[]{:S(2)}) async-start(bf16[64,16,512]{2,1,0:T(8,128)(2,1)} %join.3), calls=%async_computation | async-start | bytes 2097152 | tf_op jit(solution)/shard_map/all_to_all | solution.py:54
  31.7 20.8 %collective-permute-start.7 = (bf16[16,5120]{1,0:T(8,128)(2,1)S(1)}, bf16[16,5120]{1,0:T(8,128)(2,1)S(1)}, u32[]{:S(2)}, u32[]{:S(2)}) collective-permute-start(bf16[16,5120]{1,0:T(8,128)(2,1)S(1)} %get-tuple-element.59.refs_0_), channel_id=1, source_target_pairs={{0,6},{2,4},{4,2},{6,0},{1,7},{3,5},{5,3},{7,1},{8,14},{10,12},{12... | collective-permute-start | bytes 491528 | tf_op jit(solution)/shard_map/ppermute | solution.py:50
  34.5 19.9 %collective-permute-start.6 = (bf16[16,5120]{1,0:T(8,128)(2,1)S(1)}, bf16[16,5120]{1,0:T(8,128)(2,1)S(1)}, u32[]{:S(2)}, u32[]{:S(2)}) collective-permute-start(bf16[16,5120]{1,0:T(8,128)(2,1)S(1)} %get-tuple-element.59.refs_0_), channel_id=1, source_target_pairs={{0,4},{2,6},{4,0},{6,2},{1,5},{3,7},{5,1},{7,3},{8,12},{10,14},{12... | collective-permute-start | bytes 491528 | tf_op jit(solution)/shard_map/ppermute | solution.py:50
  35.4 19.8 %collective-permute-start.5 = (bf16[16,5120]{1,0:T(8,128)(2,1)S(1)}, bf16[16,5120]{1,0:T(8,128)(2,1)S(1)}, u32[]{:S(2)}, u32[]{:S(2)}) collective-permute-start(bf16[16,5120]{1,0:T(8,128)(2,1)S(1)} %get-tuple-element.59.refs_0_), channel_id=1, source_target_pairs={{0,2},{2,0},{4,6},{6,4},{1,3},{3,1},{5,7},{7,5},{8,10},{10,8},{12,... | collective-permute-start | bytes 491528 | tf_op jit(solution)/shard_map/ppermute | solution.py:50
  36.5 19.3 %collective-permute-start.10 = (bf16[16,5120]{1,0:T(8,128)(2,1)S(1)}, bf16[16,5120]{1,0:T(8,128)(2,1)S(1)}, u32[]{:S(2)}, u32[]{:S(2)}) collective-permute-start(bf16[16,5120]{1,0:T(8,128)(2,1)S(1)} %get-tuple-element.63.refs_0_), channel_id=1, source_target_pairs={{0,48},{16,32},{32,16},{48,0},{1,49},{17,33},{33,17},{49,1},{2,50}... | collective-permute-start | bytes 491528 | tf_op jit(solution)/shard_map/ppermute | solution.py:50
  39.5 16.3 %collective-permute-start.9 = (bf16[16,5120]{1,0:T(8,128)(2,1)S(1)}, bf16[16,5120]{1,0:T(8,128)(2,1)S(1)}, u32[]{:S(2)}, u32[]{:S(2)}) collective-permute-start(bf16[16,5120]{1,0:T(8,128)(2,1)S(1)} %get-tuple-element.63.refs_0_), channel_id=1, source_target_pairs={{0,32},{16,48},{32,0},{48,16},{1,33},{17,49},{33,1},{49,17},{2,34}... | collective-permute-start | bytes 491528 | tf_op jit(solution)/shard_map/ppermute | solution.py:50
  53.2 5.3 %collective-permute-start.8 = (bf16[16,5120]{1,0:T(8,128)(2,1)S(1)}, bf16[16,5120]{1,0:T(8,128)(2,1)S(1)}, u32[]{:S(2)}, u32[]{:S(2)}) collective-permute-start(bf16[16,5120]{1,0:T(8,128)(2,1)S(1)} %get-tuple-element.63.refs_0_), channel_id=1, source_target_pairs={{0,16},{16,0},{32,48},{48,32},{1,17},{17,1},{33,49},{49,33},{2,18}... | collective-permute-start | bytes 491528 | tf_op jit(solution)/shard_map/ppermute | solution.py:50
  59.4 41.5 %collective-permute-start.16 = (bf16[64,5120]{1,0:T(8,128)(2,1)S(1)}, bf16[64,5120]{1,0:T(8,128)(2,1)S(1)}, u32[]{:S(2)}, u32[]{:S(2)}) collective-permute-start(bf16[64,5120]{1,0:T(8,128)(2,1)S(1)} %plane.5.refs_0_), channel_id=1, source_target_pairs={{0,6},{2,4},{4,2},{6,0},{1,7},{3,5},{5,3},{7,1},{8,14},{10,12},{12... | collective-permute-start | bytes 1966088 | tf_op jit(solution)/shard_map/ppermute | solution.py:50
  63.4 53.0 %all-to-all-start.1 = ((bf16[64,16,512]{2,1,0:T(8,128)(2,1)}), bf16[64,16,512]{2,1,0:T(8,128)(2,1)S(1)}, u32[]{:S(2)}, u32[]{:S(2)}) async-start(bf16[64,16,512]{2,1,0:T(8,128)(2,1)} %get-tuple-element.68), calls=%async_computation.1 | async-start | bytes 2097152 | tf_op jit(solution)/shard_map/all_to_all | solution.py:54
  71.4 29.8 %collective-permute-start.15 = (bf16[64,5120]{1,0:T(8,128)(2,1)S(1)}, bf16[64,5120]{1,0:T(8,128)(2,1)S(1)}, u32[]{:S(2)}, u32[]{:S(2)}) collective-permute-start(bf16[64,5120]{1,0:T(8,128)(2,1)S(1)} %plane.5.refs_0_), channel_id=1, source_target_pairs={{0,4},{2,6},{4,0},{6,2},{1,5},{3,7},{5,1},{7,3},{8,12},{10,14},{12... | collective-permute-start | bytes 1966088 | tf_op jit(solution)/shard_map/ppermute | solution.py:50
  74.5 38.5 %collective-permute-start.14 = (bf16[64,5120]{1,0:T(8,128)(2,1)S(1)}, bf16[64,5120]{1,0:T(8,128)(2,1)S(1)}, u32[]{:S(2)}, u32[]{:S(2)}) collective-permute-start(bf16[64,5120]{1,0:T(8,128)(2,1)S(1)} %plane.5.refs_0_), channel_id=1, source_target_pairs={{0,2},{2,0},{4,6},{6,4},{1,3},{3,1},{5,7},{7,5},{8,10},{10,8},{12,... | collective-permute-start | bytes 1966088 | tf_op jit(solution)/shard_map/ppermute | solution.py:50
  79.6 34.3 %collective-permute-start.13 = (bf16[64,5120]{1,0:T(8,128)(2,1)S(1)}, bf16[64,5120]{1,0:T(8,128)(2,1)S(1)}, u32[]{:S(2)}, u32[]{:S(2)}) collective-permute-start(bf16[64,5120]{1,0:T(8,128)(2,1)S(1)} %plane.4.refs_0_), channel_id=1, source_target_pairs={{0,48},{16,32},{32,16},{48,0},{1,49},{17,33},{33,17},{49,1},{2,50}... | collective-permute-start | bytes 1966088 | tf_op jit(solution)/shard_map/ppermute | solution.py:50
  82.6 32.1 %collective-permute-start.12 = (bf16[64,5120]{1,0:T(8,128)(2,1)S(1)}, bf16[64,5120]{1,0:T(8,128)(2,1)S(1)}, u32[]{:S(2)}, u32[]{:S(2)}) collective-permute-start(bf16[64,5120]{1,0:T(8,128)(2,1)S(1)} %plane.4.refs_0_), channel_id=1, source_target_pairs={{0,32},{16,48},{32,0},{48,16},{1,33},{17,49},{33,1},{49,17},{2,34}... | collective-permute-start | bytes 1966088 | tf_op jit(solution)/shard_map/ppermute | solution.py:50
  100.9 14.7 %collective-permute-start.11 = (bf16[64,5120]{1,0:T(8,128)(2,1)S(1)}, bf16[64,5120]{1,0:T(8,128)(2,1)S(1)}, u32[]{:S(2)}, u32[]{:S(2)}) collective-permute-start(bf16[64,5120]{1,0:T(8,128)(2,1)S(1)} %plane.4.refs_0_), channel_id=1, source_target_pairs={{0,16},{16,0},{32,48},{48,32},{1,17},{17,1},{33,49},{49,33},{2,18}... | collective-permute-start | bytes 1966088 | tf_op jit(solution)/shard_map/ppermute | solution.py:50
  119.5 12.3 %collective-permute-start.18 = (bf16[256,5120]{1,0:T(8,128)(2,1)S(1)}, bf16[256,5120]{1,0:T(8,128)(2,1)}, u32[]{:S(2)}, u32[]{:S(2)}) collective-permute-start(bf16[256,5120]{1,0:T(8,128)(2,1)S(1)} %plane.7.refs_1_), channel_id=1, source_target_pairs={{0,64},{64,0},{1,65},{65,1},{2,66},{66,2},{3,67},{67,3},{4,68},{68... | collective-permute-start | bytes 7864328 | tf_op jit(solution)/shard_map/ppermute | solution.py:46
  121.0 10.8 %collective-permute-start.17 = (bf16[256,5120]{1,0:T(8,128)(2,1)S(1)}, bf16[256,5120]{1,0:T(8,128)(2,1)}, u32[]{:S(2)}, u32[]{:S(2)}) collective-permute-start(bf16[256,5120]{1,0:T(8,128)(2,1)S(1)} %plane.6.refs_0_), channel_id=1, source_target_pairs={{0,64},{64,0},{1,65},{65,1},{2,66},{66,2},{3,67},{67,3},{4,68},{68... | collective-permute-start | bytes 7864328 | tf_op jit(solution)/shard_map/ppermute | solution.py:46
  131.8 22.2 %copy-start.30 = (f32[256]{0:T(256)S(1)}, f32[256]{0:T(256)}, u32[]{:S(2)}) copy-start(f32[256]{0:T(256)} %param.23) | copy-start | bytes 3076
  144.7 22.4 %all-to-all-start.2 = ((f32[128,8,128]{2,1,0:T(8,128)}), f32[128,8,128]{2,1,0:T(8,128)S(1)}, u32[]{:S(2)}, u32[]{:S(2)}) async-start(f32[128,8,128]{2,1,0:T(8,128)} %broadcast_in_dim.22), calls=%async_computation.2 | async-start | bytes 1048576 | tf_op jit(solution)/shard_map/all_to_all | solution.py:54
  155.0 19.6 %collective-permute-start.20 = (bf16[64,16,512]{2,1,0:T(8,128)(2,1)S(1)}, bf16[64,16,512]{2,1,0:T(8,128)(2,1)S(1)}, u32[]{:S(2)}, u32[]{:S(2)}) collective-permute-start(bf16[64,16,512]{2,1,0:T(8,128)(2,1)S(1)} %all-to-all-done.1.own_ref), channel_id=1, source_target_pairs={{0,64},{64,0},{1,65},{65,1},{2,66},{66,2},{3,67},{67,3},{4,68},{68... | collective-permute-start | bytes 3145736 | tf_op jit(solution)/shard_map/ppermute | solution.py:46
  174.5 2.9 %collective-permute-start.19 = (bf16[128,4096]{1,0:T(8,128)(2,1)}, bf16[128,4096]{1,0:T(8,128)(2,1)S(1)}, u32[]{:S(2)}, u32[]{:S(2)}) collective-permute-start(bf16[128,4096]{1,0:T(8,128)(2,1)} %get-tuple-element.85), channel_id=1, source_target_pairs={{0,64},{64,0},{1,65},{65,1},{2,66},{66,2},{3,67},{67,3},{4,68},{68... | collective-permute-start | bytes 3145736 | tf_op jit(solution)/shard_map/ppermute | solution.py:46
  177.4 26.3 %copy-start.25 = (bf16[2,4096]{1,0:T(2,128)(2,1)S(1)}, bf16[2,4096]{1,0:T(2,128)(2,1)}, u32[]{:S(2)}) copy-start(bf16[2,4096]{1,0:T(2,128)(2,1)} %states_ref.1) | copy-start | bytes 49156
  177.4 26.3 %copy-start.28 = (bf16[4096]{0:T(1024)(128)(2,1)S(1)}, bf16[4096]{0:T(1024)(128)(2,1)}, u32[]{:S(2)}) copy-start(bf16[4096]{0:T(1024)(128)(2,1)} %param.16) | copy-start | bytes 24580
  178.7 50.5 %copy-start.6 = (bf16[112,4096]{1,0:T(8,128)(2,1)S(1)}, bf16[112,4096]{1,0:T(8,128)(2,1)}, u32[]{:S(2)}) copy-start(bf16[112,4096]{1,0:T(8,128)(2,1)} %down_ref.1) | copy-start | bytes 2752516
  226.6 2.7 %collective-permute-start.21 = (bf16[64,16,512]{2,1,0:T(8,128)(2,1)S(1)}, bf16[64,16,512]{2,1,0:T(8,128)(2,1)S(1)}, u32[]{:S(2)}, u32[]{:S(2)}) collective-permute-start(bf16[64,16,512]{2,1,0:T(8,128)(2,1)S(1)} %all_to_all.31.own_ref), channel_id=1, source_target_pairs={{0,64},{64,0},{1,65},{65,1},{2,66},{66,2},{3,67},{67,3},{4,68},{68... | collective-permute-start | bytes 3145736 | tf_op jit(solution)/shard_map/ppermute | solution.py:46
  232.3 2.7 %collective-permute-start.22 = (bf16[128,4096]{1,0:T(8,128)(2,1)S(1)}, bf16[128,4096]{1,0:T(8,128)(2,1)S(1)}, u32[]{:S(2)}, u32[]{:S(2)}) collective-permute-start(bf16[128,4096]{1,0:T(8,128)(2,1)S(1)} %get-tuple-element.91), channel_id=1, source_target_pairs={{0,64},{64,0},{1,65},{65,1},{2,66},{66,2},{3,67},{67,3},{4,68},{68... | collective-permute-start | bytes 3145736 | tf_op jit(solution)/shard_map/ppermute | solution.py:46
  237.3 24.0 %all-to-all-start.5 = ((bf16[64,16,512]{2,1,0:T(8,128)(2,1)}), bf16[64,16,512]{2,1,0:T(8,128)(2,1)S(1)}, u32[]{:S(2)}, u32[]{:S(2)}) async-start(bf16[64,16,512]{2,1,0:T(8,128)(2,1)} %join.5), calls=%async_computation.5 | async-start | bytes 2097152 | tf_op jit(solution)/shard_map/all_to_all | solution.py:54
  (27 other events, 46.2 us)

commit v4 on v3

--- a/solution.py
+++ b/solution.py
@@ -138,9 +138,65 @@
     )(place, *pieces)
 
 
+def halves_kernel(*refs):
+    count = (len(refs) - 1) // 2
+    copies = []
+    for i, (piece, out) in enumerate(zip(refs[:count], refs[count:])):
+        rows = out.shape[0]
+        copy = pltpu.make_async_copy(piece.at[pl.ds((i % 2) * rows, rows), :], out, refs[-1].at[i])
+        copy.start()
+        copies.append(copy)
+    for copy in copies:
+        copy.wait()
+
+
+def halves_of(pieces):
+    return kernel_call(
+        halves_kernel,
+        "halves",
+        [shape_of((p.shape[0] // 2, p.shape[1])) for p in pieces],
+        limit=2,
+        in_specs=[ANY] * len(pieces),
+        out_specs=[ANY] * len(pieces),
+        scratch_shapes=[pltpu.SemaphoreType.DMA((len(pieces),))],
+    )(*pieces)
+
+
+def along(block, line, mask):
+    return lax.ppermute(block, line, [(i, i ^ mask) for i in range(4)])
+
+
+def whole_kernel(place_ref, *refs):
+    pieces, out, sems = refs[:5], refs[5], refs[6]
+    tokens = pieces[0].shape[0]
+    copies = []
+    for i, (mask, half) in enumerate(((0, 0), (1, 0), (3, 0), (2, 0), (2, 1))):
+        at = (place_ref[0] ^ mask) * tokens + half * (tokens // 2)
+        at = pl.multiple_of(at, tokens // 2)
+        rows = pieces[i].shape[0]
+        copy = pltpu.make_async_copy(pieces[i], out.at[pl.ds(at, rows), :], sems.at[i])
+        copy.start()
+        copies.append(copy)
+    for copy in copies:
+        copy.wait()
+
+
+def whole_rows(place, pieces):
+    tokens, width = pieces[0].shape
+    return kernel_call(
+        whole_kernel,
+        "whole",
+        shape_of((4 * tokens, width)),
+        limit=2,
+        in_specs=[SMEM] + [ANY] * 5,
+        out_specs=ANY,
+        scratch_shapes=[pltpu.SemaphoreType.DMA((5,))],
+    )(place, *pieces)
+
+
 GROUPS = (
-    ((0, 0, 2048), (1, 0, 1536), (1, 1536, 1536)),
-    ((1, 3072, 1280), (1, 4352, 1280), (1, 5632, 1280), (1, 6912, 1280)),
+    tuple((0, i * 1024, 1024) for i in range(2)) + tuple((1, i * 1024, 1024) for i in range(3)),
+    tuple((1, i * 1024, 1024) for i in range(3, 8)),
 )
 WIDTHS = tuple(sum(p[2] for p in group) for group in GROUPS)
 
@@ -172,10 +228,9 @@
         student_peak + jnp.log(student_total),
         cross / teacher_total,
     )
-    stats_out[...] = jnp.zeros_like(stats_out)
-    for i, row in enumerate(stats):
-        stats_out[i : i + 1, :] = row[:, :128]
-        stats_out[i + 3 : i + 4, :] = row[:, 128:]
+    rows = [row[:, :128] for row in stats] + [row[:, 128:] for row in stats]
+    rows = jnp.concatenate(rows + [jnp.zeros((2, 128), jnp.float32)], axis=0)
+    stats_out[...] = jnp.broadcast_to(rows[None], stats_out.shape)
 
 
 def logits_kernel(last, place_ref, *refs):
@@ -201,14 +256,19 @@
                     heads[kind].at[:, pl.ds(start, width)], head.at[:, columns], head_sems.at[i]
                 ),
             )
-            for copy in pair:
-                copy.start()
             copies.append((kind + (base > 0), columns, pair))
             column = column + width
+    ahead = 3
+    for _, _, pair in copies[:ahead]:
+        for copy in pair:
+            copy.start()
     sums = [None, None, None]
-    for kind, columns, pair in copies:
+    for i, (kind, columns, pair) in enumerate(copies):
         for copy in pair:
             copy.wait()
+        if i + ahead < len(copies):
+            for copy in copies[i + ahead][2]:
+                copy.start()
         term = row_product(head[:, columns], rows[:, columns])
         sums[kind] = term if sums[kind] is None else sums[kind] + term
     if last:
@@ -228,12 +288,12 @@
     shape = shape_of((vocab, tokens), jnp.float32)
     last = len(sums) > 0
     pieces = sum(len(group) for group in GROUPS)
-    out_shape = [shape, shape, shape_of((8, 128), jnp.float32) if last else shape]
+    out_shape = [shape, shape, shape_of((128, 8, 128), jnp.float32) if last else shape]
     return kernel_call(
         functools.partial(logits_kernel, last),
         "logits",
         out_shape,
-        limit=56,
+        limit=48,
         in_specs=[SMEM] + [ANY] * 4 + [VMEM] * len(sums),
         out_specs=[VMEM] * 3,
         scratch_shapes=[
@@ -254,39 +314,50 @@
     return (column == source).astype(jnp.bfloat16)
 
 
+def head_copies(source, head, sems):
+    columns = head.shape[1] // sems.shape[0]
+    parts = [slice(i * columns, (i + 1) * columns) for i in range(sems.shape[0])]
+    copies = [
+        pltpu.make_async_copy(source.at[:, part], head.at[:, part], sems.at[i])
+        for i, part in enumerate(parts)
+    ]
+    for copy in copies:
+        copy.start()
+    return list(zip(parts, copies))
+
+
 def row_grad_kernel(
-    core_ref, every_ref, weight_ref, teacher_ref, student_ref, head_ref,
-    own_ref, send_ref, divergence_ref, grad,
+    core_ref, every_ref, weight_ref, teacher_ref, student_ref, head_from,
+    own_ref, send_ref, divergence_ref, head, sems,
 ):
-    @pl.when(pl.program_id(0) == 0)
-    def _():
-        every = every_ref[...]
-        peak = jnp.max(every, axis=0)
-        scaled = jnp.exp(every - peak[None])
-        total = jnp.sum(scaled, axis=0)
-        lse = peak + jnp.log(total)
-        cross = jnp.sum(scaled * pltpu.roll(every, 6, 1), axis=0) / total
-        teacher_lse = jnp.concatenate([lse[0:1], lse[3:4]], axis=1)
-        student_lse = jnp.concatenate([lse[1:2], lse[4:5]], axis=1)
-        divergence_ref[...] = (
-            jnp.concatenate([cross[0:1], cross[3:4]], axis=1) - teacher_lse + student_lse
-        )
-        logit_grad = weight_ref[...] * (
-            jnp.exp(student_ref[...] - student_lse) - jnp.exp(teacher_ref[...] - teacher_lse)
-        )
-        grad[...] = row_product(
-            one_hot_rows(core_ref[0]), logit_grad.astype(jnp.bfloat16)
-        ).astype(jnp.bfloat16)
-
-    out = jnp.dot(grad[...], head_ref[...], preferred_element_type=jnp.float32)
-    own_ref[...] = out[:128]
-    send_ref[...] = out[128:].astype(jnp.bfloat16)
+    copies = head_copies(head_from, head, sems)
+    every = every_ref[...]
+    peak = jnp.max(every, axis=0)
+    scaled = jnp.exp(every - peak[None])
+    total = jnp.sum(scaled, axis=0)
+    lse = peak + jnp.log(total)
+    cross = jnp.sum(scaled * pltpu.roll(every, 6, 1), axis=0) / total
+    teacher_lse = jnp.concatenate([lse[0:1], lse[3:4]], axis=1)
+    student_lse = jnp.concatenate([lse[1:2], lse[4:5]], axis=1)
+    divergence_ref[...] = (
+        jnp.concatenate([cross[0:1], cross[3:4]], axis=1) - teacher_lse + student_lse
+    )
+    logit_grad = weight_ref[...] * (
+        jnp.exp(student_ref[...] - student_lse) - jnp.exp(teacher_ref[...] - teacher_lse)
+    )
+    grad = row_product(one_hot_rows(core_ref[0]), logit_grad.astype(jnp.bfloat16))
+    grad = grad.astype(jnp.bfloat16)
+    half = own_ref.shape[0]
+    for columns, copy in copies:
+        copy.wait()
+        out = jnp.dot(grad, head[:, columns], preferred_element_type=jnp.float32)
+        own_ref[:, columns] = out[:half]
+        send_ref[:, columns] = out[half:].astype(jnp.bfloat16)
 
 
 def row_grad_part(core, every, weight, teacher, student, student_head_t):
     vocab, width = student_head_t.shape
-    tokens, columns = weight.shape[1], 1024
-    half = pl.BlockSpec((tokens // 2, columns), lambda i, c: (0, i))
+    tokens = weight.shape[1]
     return kernel_call(
         row_grad_kernel,
         "row_grad",
@@ -295,93 +366,82 @@
             shape_of((tokens // 2, width)),
             shape_of((1, tokens), jnp.float32),
         ],
-        limit=56,
-        grid_spec=pltpu.PrefetchScalarGridSpec(
-            num_scalar_prefetch=1,
-            grid=(width // columns,),
-            in_specs=[
-                pl.BlockSpec(every.shape, lambda i, c: (0, 0, 0)),
-                pl.BlockSpec(weight.shape, lambda i, c: (0, 0)),
-                pl.BlockSpec(teacher.shape, lambda i, c: (0, 0)),
-                pl.BlockSpec(student.shape, lambda i, c: (0, 0)),
-                pl.BlockSpec((vocab, columns), lambda i, c: (0, i)),
-            ],
-            out_specs=[half, half, pl.BlockSpec((1, tokens), lambda i, c: (0, 0))],
-            scratch_shapes=[pltpu.VMEM((tokens, vocab), jnp.bfloat16)],
-        ),
+        limit=48,
+        in_specs=[SMEM] + [VMEM] * 4 + [ANY],
+        out_specs=[VMEM] * 3,
+        scratch_shapes=[
+            pltpu.VMEM((vocab, width), jnp.bfloat16),
+            pltpu.SemaphoreType.DMA((4,)),
+        ],
     )(core, every, weight, teacher, student, student_head_t)
 
 
-def pick_kernel(place_ref, ids_ref, head_ref, own_ref, send_ref, chosen):
-    @pl.when(pl.program_id(0) == 0)
-    def _():
-        vocab, tokens = head_ref.shape[0], ids_ref.shape[1]
-        entry = lax.broadcasted_iota(jnp.int32, (vocab, tokens), 0) + place_ref[1] * vocab
-        place = lax.broadcasted_iota(jnp.int32, (tokens, tokens), 0)
-        column = lax.broadcasted_iota(jnp.int32, (tokens, tokens), 1)
-        source = (((place >> 7) ^ place_ref[0]) << 7) | ((place & 63) << 1) | ((place >> 6) & 1)
-        chosen[...] = row_product(
-            (column == source).astype(jnp.bfloat16), (ids_ref[...] == entry).astype(jnp.bfloat16)
-        ).astype(jnp.bfloat16)
-
+def pick_kernel(place_ref, ids_ref, head_from, own_ref, send_ref, head, sems):
+    copies = head_copies(head_from, head, sems)
+    vocab, tokens = head.shape[0], ids_ref.shape[1]
+    entry = lax.broadcasted_iota(jnp.int32, (vocab, tokens), 0) + place_ref[1] * vocab
+    place = lax.broadcasted_iota(jnp.int32, (tokens, tokens), 0)
+    column = lax.broadcasted_iota(jnp.int32, (tokens, tokens), 1)
+    source = (((place >> 7) ^ place_ref[0]) << 7) | ((place & 63) << 1) | ((place >> 6) & 1)
+    chosen = row_product(
+        (column == source).astype(jnp.bfloat16), (ids_ref[...] == entry).astype(jnp.bfloat16)
+    ).astype(jnp.bfloat16)
     half = own_ref.shape[0]
-    out = jnp.dot(chosen[...], head_ref[...], preferred_element_type=jnp.float32)
-    own_ref[...] = out[:half].astype(jnp.bfloat16)
-    send_ref[...] = out[half:].astype(jnp.bfloat16)
+    for columns, copy in copies:
+        copy.wait()
+        out = jnp.dot(chosen, head[:, columns], preferred_element_type=jnp.float32)
+        own_ref[:, columns] = out[:half].astype(jnp.bfloat16)
+        send_ref[:, columns] = out[half:].astype(jnp.bfloat16)
 
 
 def pick_part(place, ids, student_head_t):
     vocab, width = student_head_t.shape
-    tokens, columns = ids.shape[1], 1024
-    half = pl.BlockSpec((tokens // 2, columns), lambda i, p: (0, i))
-    shape = shape_of((tokens // 2, width))
+    shape = shape_of((ids.shape[1] // 2, width))
     return kernel_call(
         pick_kernel,
         "pick",
         [shape, shape],
-        limit=56,
-        grid_spec=pltpu.PrefetchScalarGridSpec(
-            num_scalar_prefetch=1,
-            grid=(width // columns,),
-            in_specs=[
-                pl.BlockSpec(ids.shape, lambda i, p: (0, 0)),
-                pl.BlockSpec((vocab, columns), lambda i, p: (0, i)),
-            ],
-            out_specs=[half, half],
-            scratch_shapes=[pltpu.VMEM((tokens, vocab), jnp.bfloat16)],
-        ),
+        limit=48,
+        in_specs=[SMEM, VMEM, ANY],
+        out_specs=[VMEM] * 2,
+        scratch_shapes=[
+            pltpu.VMEM((vocab, width), jnp.bfloat16),
+            pltpu.SemaphoreType.DMA((4,)),
+        ],
     )(place, ids, student_head_t)
 
 
-def join_kernel(own_ref, came_ref, out_ref, rows):
-    chips = out_ref.shape[0]
-    for t in range(2):
-        for i in range(SEGMENTS):
-            for k in range(SEGMENT // 128):
-                part = slice(t * chips, (t + 1) * chips)
-                lanes = slice(i * SEGMENT + k * 128, i * SEGMENT + (k + 1) * 128)
-                total = own_ref[part, lanes].astype(jnp.float32)
-                total = total + came_ref[part, lanes].astype(jnp.float32)
-                at = pl.ds(t * SEGMENTS + i, chips, stride=2 * SEGMENTS)
-                rows[k, at, :] = total
-    for k in range(SEGMENT // 128):
-        out_ref[:, :, k * 128 : (k + 1) * 128] = (
-            rows[k].reshape(chips, 2 * SEGMENTS, 128).astype(jnp.bfloat16)
-        )
-
-
-def join_part(own, send):
-    chips = own.shape[0] // 2
-    block = (chips, 2 * SEGMENTS, SEGMENT)
+def join_kernel(*refs):
+    pairs, out_ref, rows = refs[:-2], refs[-2], refs[-1]
+    chips, height = out_ref.shape[0], 2 * SEGMENTS
+    for base, (own_ref, came_ref) in enumerate(zip(pairs[::2], pairs[1::2])):
+        for t in range(2):
+            for i in range(SEGMENTS):
+                for k in range(SEGMENT // 128):
+                    part = slice(t * chips, (t + 1) * chips)
+                    lanes = slice(i * SEGMENT + k * 128, i * SEGMENT + (k + 1) * 128)
+                    total = own_ref[part, lanes].astype(jnp.float32)
+                    total = total + came_ref[part, lanes].astype(jnp.float32)
+                    at = pl.ds(t * SEGMENTS + i, chips, stride=height)
+                    rows[k, at, :] = total
+        for k in range(SEGMENT // 128):
+            out_ref[:, base * height : (base + 1) * height, k * 128 : (k + 1) * 128] = (
+                rows[k].reshape(chips, height, 128).astype(jnp.bfloat16)
+            )
+
+
+def join_part(*pairs):
+    chips = pairs[0].shape[0] // 2
+    height = 2 * SEGMENTS
     return kernel_call(
         join_kernel,
         "join",
-        shape_of(block),
-        limit=10,
-        in_specs=[VMEM] * 2,
+        shape_of((chips, height * len(pairs) // 2, SEGMENT)),
+        limit=14,
+        in_specs=[VMEM] * len(pairs),
         out_specs=VMEM,
-        scratch_shapes=[pltpu.VMEM((SEGMENT // 128, chips * 2 * SEGMENTS, 128), jnp.float32)],
-    )(own, swap_cores(send))
+        scratch_shapes=[pltpu.VMEM((SEGMENT // 128, chips * height, 128), jnp.float32)],
+    )(*pairs)
 
 
 def block_gain(gain_ref):
@@ -420,21 +480,22 @@
     return jnp.sum(blocks_ref[...].astype(jnp.float32), axis=0)
 
 
-def embed_kernel(blocks_ref, gain_ref, embedded_ref, out_ref):
-    values = block_sum(blocks_ref)
-    embedded_ref[...] = values
-    rows = (values * block_inverse(values) * block_gain(gain_ref)).astype(jnp.bfloat16)
-    out_ref[...] = jnp.broadcast_to(rows[None], out_ref.shape)
-
-
-def final_kernel(blocks_ref, states_ref, gain_ref, grad_ref, out_ref, states):
+def final_kernel(
+    blocks_ref, states_ref, student_gain, ffn_gain, grad_ref, embedded_ref, out_ref, states
+):
+    height = 2 * SEGMENTS
+    total = block_sum(blocks_ref)
+    embedded = total[height:]
+    embedded_ref[...] = embedded
+    rows = embedded * block_inverse(embedded) * block_gain(ffn_gain)
     for i in range(SEGMENTS):
         part = states_ref[:, i * SEGMENT : (i + 1) * SEGMENT].astype(jnp.float32)
         for t in range(2):
             states[t * SEGMENTS + i : t * SEGMENTS + i + 1, :] = part[t : t + 1]
-    grad = block_back(block_sum(blocks_ref), states[...], block_gain(gain_ref))
+    grad = block_back(total[:height], states[...], block_gain(student_gain))
     grad_ref[...] = grad
-    out_ref[...] = jnp.broadcast_to(grad.astype(jnp.bfloat16)[None], out_ref.shape)
+    rows = jnp.concatenate([grad, rows], axis=0).astype(jnp.bfloat16)
+    out_ref[...] = jnp.broadcast_to(rows[None], out_ref.shape)
 
 
 def state_kernel(blocks_ref, grad_ref, embedded_ref, gain_ref, out_ref):
@@ -450,17 +511,6 @@
 BLOCK = (2 * SEGMENTS, SEGMENT)
 
 
-def owner_part(body, name, blocks, *others, scratch=()):
-    return kernel_call(
-        body,
-        name,
-        [shape_of(BLOCK, jnp.float32), shape_of(blocks.shape)],
-        in_specs=[VMEM] * (1 + len(others)),
-        out_specs=[VMEM] * 2,
-        scratch_shapes=list(scratch),
-    )(blocks, *others)
-
-
 def spread_rows(refs, scratches):
     for ref, rows in zip(refs, scratches):
         values = ref[...].astype(jnp.float32)
@@ -469,41 +519,32 @@
             rows[k] = values[:, k * 128 : (k + 1) * 128]
 
 
-def segment_rows(scratches, segment):
+def segment_rows(scratches, first):
     parts = []
     for rows in scratches:
-        chips = rows.shape[1] // (2 * SEGMENTS)
+        height = 4 * SEGMENTS
         for t in range(2):
-            at = pl.ds(t * SEGMENTS + segment, chips, stride=2 * SEGMENTS)
+            at = pl.ds(first + t * SEGMENTS, rows.shape[1] // height, stride=height)
             parts.append(
                 jnp.concatenate([rows[k, at, :] for k in range(SEGMENT // 128)], axis=1)
             )
     return jnp.concatenate(parts, axis=0).astype(jnp.bfloat16)
 
 
-def gate_kernel(own_ref, other_ref, gate_ref, up_ref, out_ref, *scratches):
+def ffn_grad_kernel(
+    own_ref, other_ref, down_ref, gate_ref, up_ref, own_out, send_out, *scratches
+):
     spread_rows((own_ref, other_ref), scratches)
-    total = None
+    units = down_ref.shape[0]
+    hidden, act_grad = None, None
     for i in range(SEGMENTS):
         columns = slice(i * SEGMENT, (i + 1) * SEGMENT)
         weight = jnp.concatenate([gate_ref[:, columns], up_ref[:, columns]], axis=0)
-        term = row_product(weight, segment_rows(scratches, i))
-        total = term if total is None else total + term
-    out_ref[...] = total
-
-
-def ffn_grad_kernel(
-    own_ref, other_ref, down_ref, hidden_ref, gate_ref, up_ref, own_out, send_out, *scratches
-):
-    spread_rows((own_ref, other_ref), scratches)
-    units = down_ref.shape[0]
-    act_grad = None
-    for i in range(SEGMENTS):
-        term = row_product(
-            down_ref[:, i * SEGMENT : (i + 1) * SEGMENT], segment_rows(scratches, i)
-        )
+        term = row_product(weight, segment_rows(scratches, 2 * SEGMENTS + i))
+        hidden = term if hidden is None else hidden + term
+        term = row_product(down_ref[:, columns], segment_rows(scratches, i))
         act_grad = term if act_grad is None else act_grad + term
-    gate, upper = hidden_ref[:units, :], hidden_ref[units:, :]
+    gate, upper = hidden[:units, :], hidden[units:, :]
     sigmoid_gate = jax.nn.sigmoid(gate)
     gate_grad = act_grad * upper * sigmoid_gate * (1.0 + gate * (1.0 - sigmoid_gate))
     upper_grad = act_grad * gate * sigmoid_gate
@@ -528,7 +569,7 @@
         body,
         name,
         out_shape,
-        limit=18,
+        limit=30,
         in_specs=[VMEM] * (2 + len(others)),
         out_specs=[VMEM] * len(out_shape),
         scratch_shapes=[scratch, scratch],
@@ -588,12 +629,10 @@
         out_specs=VMEM,
     )(own_core, keep, swap_cores(send))
     pieces = line_pieces(rows, ("yh", "yl"))
-
     place = jnp.stack([core, device]).astype(jnp.int32)
-    picked = join_part(*pick_part(place, token_ids.reshape(1, 256), student_head_t))
+    picked = pick_part(place, token_ids.reshape(1, 256), student_head_t)
     pieces, picked = lax.optimization_barrier((pieces, picked))
-    picked = exchange(picked, CHIPS)
-
+    picked = (picked[0], swap_cores(picked[1]))
     first, second = kernel_call(
         line_kernel,
         "line",
@@ -603,49 +642,51 @@
     )(y, *pieces)
     first, second = line_pieces(first, "z"), line_pieces(second, "x")
     first, second, picked = lax.optimization_barrier((first, second, picked))
-    embedded, ffn_rows = owner_part(embed_kernel, "embed", picked, ffn_gain)
-    ffn_rows = exchange(ffn_rows, CHIPS)
     first, second = in_line_order(z, first), in_line_order(x, second)
-    first, second = line_pieces(first, "x"), line_pieces(second, "z")
-    first, second, ffn_rows = lax.optimization_barrier((first, second, ffn_rows))
-    rows = (in_line_order(x, first), in_line_order(z, second))
+    came = [along(first, "x", 1), along(first, "x", 3), along(second, "z", 1), along(second, "z", 3)]
+    came = lax.optimization_barrier(came)
+    halves = halves_of(came)
+    far = [
+        along(half, line, mask)
+        for half, line, mask in zip(halves, ("x", "x", "z", "z"), (3, 1, 3, 1))
+    ]
+    far = lax.optimization_barrier(far)
+    rows = (
+        whole_rows(x, [first] + came[:2] + far[:2]),
+        whole_rows(z, [second] + came[2:] + far[2:]),
+    )
     others = tuple(swap_cores(part) for part in rows)
     sums = logits_part(own_core, rows, heads)
     student, teacher, stats = logits_part(1 - own_core, others, heads, sums)
-    every = exchange(jnp.broadcast_to(stats[None], (128,) + stats.shape), AXES)
+    every = exchange(stats, AXES)
 
     weight = token_weight.reshape(2, 4, 2, 4, 2, 2).transpose(1, 3, 2, 4, 0, 5).reshape(1, 256)
     own, send, divergence = row_grad_part(
         own_core, every, weight, teacher, student, student_head_t
     )
     divergence = divergence.reshape(4, 4, 2, 2, 2, 2).transpose(4, 0, 2, 1, 3, 5).reshape(256)
-    row_grad = join_part(own, send)
-    (hidden,) = ffn_part(
-        gate_kernel, "gate_upper", [shape_of((224, 256), jnp.float32)], ffn_rows, gate_t, up_t
-    )
-    row_grad, hidden = lax.optimization_barrier((row_grad, hidden))
-    row_grad = exchange(row_grad, CHIPS)
-    final_grad, final_half = owner_part(
+    blocks = exchange(join_part(own, swap_cores(send), *picked), CHIPS)
+    final_grad, embedded, blocks = kernel_call(
         final_kernel,
         "final",
-        row_grad,
-        student_states,
-        student_gain,
-        scratch=[pltpu.VMEM(BLOCK, jnp.float32)],
-    )
-    final_half = exchange(final_half, CHIPS)
+        [shape_of(BLOCK, jnp.float32), shape_of(BLOCK, jnp.float32), shape_of(blocks.shape)],
+        limit=14,
+        in_specs=[VMEM] * 4,
+        out_specs=[VMEM] * 3,
+        scratch_shapes=[pltpu.VMEM(BLOCK, jnp.float32)],
+    )(blocks, student_states, student_gain, ffn_gain)
+    blocks = exchange(blocks, CHIPS)
     shape = (128, 4096)
     own, send = ffn_part(
         ffn_grad_kernel,
         "ffn_grad",
         [shape_of(shape, jnp.float32), shape_of(shape)],
-        final_half,
+        blocks,
         down_weight,
-        hidden,
         gate_t,
         up_t,
     )
-    ffn_grad = exchange(join_part(own, send), CHIPS)
+    ffn_grad = exchange(join_part(own, swap_cores(send)), CHIPS)
     state_grad = kernel_call(
         state_kernel,
         "state",

time: 263 us -> 238 us (0.905)
  blocking collectives: 47.5 us -> 71.7 us
  starting transfers between devices: 56.5 us -> 39.8 us
  local copies, waits for them, and re-layouts: 21.2 us -> 7.07 us
  waiting for transfers between devices: 82.8 us -> 71.2 us
  Pallas kernels: 52 us -> 45.4 us
    ppermute x15 -> x9, waiting for transfers between devices: 46.1 us -> 8.5 us  [line_pieces(): lax.ppermute(block, line, [(i, i ^ m) for i in range(4)])]
    all_to_all x2, blocking collectives: 47.5 us -> 71.7 us  [exchange(): return lax.all_to_all(blocks, axes, split_axis=0, concat_axis=0, tiled=True)]
    ppermute x0 -> x8, waiting for transfers between devices: none -> 22.4 us  [along(): return lax.ppermute(block, line, [(i, i ^ mask) for i in range(4)])]
    all_to_all x4 -> x2, starting transfers between devices: 31.8 us -> 13 us  [exchange(): return lax.all_to_all(blocks, axes, split_axis=0, concat_axis=0, tiled=True)]
    unnamed x64 -> x26, local copies, waits for them, and re-layouts: 17.3 us -> 5.27 us
    ppermute x0 -> x8, starting transfers between devices: none -> 8.36 us  [along(): return lax.ppermute(block, line, [(i, i ^ mask) for i in range(4)])]
    ppermute x15 -> x9, starting transfers between devices: 23.5 us -> 17.6 us  [line_pieces(): lax.ppermute(block, line, [(i, i ^ m) for i in range(4)])]
    ppermute x8 -> x7, waiting for transfers between devices: 7.36 us -> 10.7 us  [swap_cores(): return lax.ppermute(values, 'core', [(0, 1), (1, 0)])]
  transfers between devices with their start and end apart: 27 -> 26, of which waited for: 12 -> 18; matrix products, arithmetic and copies ran while one was open for 1% -> 1% of each run, Pallas kernels for 10% -> 6%
where the time goes in v4:
time: 238 us; the launch traced here: 237 us
  blocking collectives  71.7 us (30%)
  waiting for transfers between devices  71.2 us (30%)
  Pallas kernels  45.4 us (19%)
  starting transfers between devices  39.8 us (17%)
  local copies, waits for them, and re-layouts  7.07 us (3%)
    all_to_all x2, blocking collectives, exchange(): return lax.all_to_all(blocks, axes, split_axis=0, concat_axis=0, tiled=True)  71.7 us
    all_to_all x2, waiting for transfers between devices, exchange(): return lax.all_to_all(blocks, axes, split_axis=0, concat_axis=0, tiled=True)  29.6 us
    ppermute x8, waiting for transfers between devices, along(): return lax.ppermute(block, line, [(i, i ^ mask) for i in range(4)])  22.4 us
    pallas_call x2, Pallas kernels, logits_part(): kernel_call(functools.partial(logits_kernel, last), 'logits', out_shape,...  18.2 us
    ppermute x9, starting transfers between devices, line_pieces(): lax.ppermute(block, line, [(i, i ^ m) for i in range(4)])  17.6 us
    all_to_all x2, starting transfers between devices, exchange(): return lax.all_to_all(blocks, axes, split_axis=0, concat_axis=0, tiled=True)  13 us
    ppermute x7, waiting for transfers between devices, swap_cores(): return lax.ppermute(values, 'core', [(0, 1), (1, 0)])  10.7 us
    ppermute x9, waiting for transfers between devices, line_pieces(): lax.ppermute(block, line, [(i, i ^ m) for i in range(4)])  8.5 us
  transfers between devices with their start and end apart: 26, of which 18 were waited for; matrix products, arithmetic and copies ran while one was open for 1% of the time, Pallas kernels for 6%

profile of v4, /device:TPU:0, one launch (start us, length us, event | category | flops | bytes accessed | tf_op | source)
XLA Modules:
  0.0 236.9 jit_solution(313073807219952522)
XLA Ops:
  0.6 1.9 rows.1
  4.9 1.7 collective-permute-start.1
  6.6 2.9 %collective-permute-start.2 = (bf16[4,10240]{1,0:T(4,128)(2,1)S(1)}, bf16[4,10240]{1,0:T(4,128)(2,1)S(1)}, u32[]{:S(2)}, u32[]{:S(2)}) collective-permute-start(bf16[4,10240]{1,0:T(4,128)(2,1)S(1)} %chip.1.refs_0_), channel_id=1, source_target_pairs={{0,8},{1,9},{8,0},{9,1},{2,10},{3,11},{10,2},{11,3},{4,12},{5,13},... | collective-permute-start | bytes 245768 | tf_op jit(solution)/shard_map/ppermute | solution.py:50
  10.4 4.6 %pick.1 = (bf16[128,4096]{1,0:T(8,128)(2,1)S(1)}, bf16[128,4096]{1,0:T(8,128)(2,1)}) custom-call(s32[2]{0:T(128)S(1)} %pad_add_fusion.place_ref, s32[1,256]{1,0:T(1,128)S(1)} %bitcast.21, bf16[501,4096]{1,0:T(8,128)(2,1)} %bitcast.24), custom_call_target="tpu_custom_call" | custom-call | flops 1 | bytes 1 | tf_op jit(solution)/shard_map/pick/pallas_call | solution.py:400
  15.7 2.0 collective-permute-start.4
  17.7 3.6 %collective-permute-start.5 = (bf16[16,5120]{1,0:T(8,128)(2,1)S(1)}, bf16[16,5120]{1,0:T(8,128)(2,1)S(1)}, u32[]{:S(2)}, u32[]{:S(2)}) collective-permute-start(bf16[16,5120]{1,0:T(8,128)(2,1)S(1)} %get-tuple-element.62.refs_0_), channel_id=1, source_target_pairs={{0,4},{2,6},{4,0},{6,2},{1,5},{3,7},{5,1},{7,3},{8,12},{10,14},{12... | collective-permute-start | bytes 491528 | tf_op jit(solution)/shard_map/ppermute | solution.py:50
  21.2 1.5 collective-permute-start.7
  22.8 3.0 %collective-permute-start.8 = (bf16[16,5120]{1,0:T(8,128)(2,1)S(1)}, bf16[16,5120]{1,0:T(8,128)(2,1)S(1)}, u32[]{:S(2)}, u32[]{:S(2)}) collective-permute-start(bf16[16,5120]{1,0:T(8,128)(2,1)S(1)} %get-tuple-element.66.refs_0_), channel_id=1, source_target_pairs={{0,32},{16,48},{32,0},{48,16},{1,33},{17,49},{33,1},{49,17},{2,34}... | collective-permute-start | bytes 491528 | tf_op jit(solution)/shard_map/ppermute | solution.py:50
  25.8 3.6 %collective-permute-done.5.refs_2_ = bf16[16,5120]{1,0:T(8,128)(2,1)S(1)} collective-permute-done((bf16[16,5120]{1,0:T(8,128)(2,1)S(1)}, bf16[16,5120]{1,0:T(8,128)(2,1)S(1)}, u32[]{:S(2)}, u32[]{:S(2)}) %collective-permute-start.5) | collective-permute-done | bytes 163872 | tf_op jit(solution)/shard_map/ppermute | solution.py:50
  29.4 2.8 %collective-permute-start.9 = (bf16[16,5120]{1,0:T(8,128)(2,1)S(1)}, bf16[16,5120]{1,0:T(8,128)(2,1)S(1)}, u32[]{:S(2)}, u32[]{:S(2)}) collective-permute-start(bf16[16,5120]{1,0:T(8,128)(2,1)S(1)} %get-tuple-element.66.refs_0_), channel_id=1, source_target_pairs={{0,48},{16,32},{32,16},{48,0},{1,49},{17,33},{33,17},{49,1},{2,50}... | collective-permute-start | bytes 491528 | tf_op jit(solution)/shard_map/ppermute | solution.py:50
  33.0 3.5 %collective-permute-done.9.refs_3_ = bf16[16,5120]{1,0:T(8,128)(2,1)S(1)} collective-permute-done((bf16[16,5120]{1,0:T(8,128)(2,1)S(1)}, bf16[16,5120]{1,0:T(8,128)(2,1)S(1)}, u32[]{:S(2)}, u32[]{:S(2)}) %collective-permute-start.9) | collective-permute-done | bytes 163872 | tf_op jit(solution)/shard_map/ppermute | solution.py:50
  37.5 2.5 %collective-permute-start.14 = (bf16[64,5120]{1,0:T(8,128)(2,1)S(1)}, bf16[64,5120]{1,0:T(8,128)(2,1)S(1)}, u32[]{:S(2)}, u32[]{:S(2)}) collective-permute-start(bf16[64,5120]{1,0:T(8,128)(2,1)S(1)} %plane.3.refs_0_), channel_id=1, source_target_pairs={{0,6},{2,4},{4,2},{6,0},{1,7},{3,5},{5,3},{7,1},{8,14},{10,12},{12... | collective-permute-start | bytes 1966088 | tf_op jit(solution)/shard_map/ppermute | solution.py:166
  41.2 1.9 collective-permute-start.12
  43.2 9.8 %collective-permute-done.13.refs_2_.refs_1_ = bf16[64,5120]{1,0:T(8,128)(2,1)S(1)} collective-permute-done((bf16[64,5120]{1,0:T(8,128)(2,1)S(1)}, bf16[64,5120]{1,0:T(8,128)(2,1)S(1)}, u32[]{:S(2)}, u32[]{:S(2)}) %collective-permute-start.13) | collective-permute-done | bytes 655392 | tf_op jit(solution)/shard_map/ppermute | solution.py:166
  54.3 2.4 %collective-permute-done.11.refs_0_.refs_1_ = bf16[64,5120]{1,0:T(8,128)(2,1)S(1)} collective-permute-done((bf16[64,5120]{1,0:T(8,128)(2,1)S(1)}, bf16[64,5120]{1,0:T(8,128)(2,1)S(1)}, u32[]{:S(2)}, u32[]{:S(2)}) %collective-permute-start.11) | collective-permute-done | bytes 655392 | tf_op jit(solution)/shard_map/ppermute | solution.py:166
  58.5 2.2 collective-permute-start.15
  62.0 5.5 %collective-permute-done.15.refs_3_ = bf16[32,5120]{1,0:T(8,128)(2,1)S(1)} collective-permute-done((bf16[32,5120]{1,0:T(8,128)(2,1)S(1)}, bf16[32,5120]{1,0:T(8,128)(2,1)S(1)}, u32[]{:S(2)}, u32[]{:S(2)}) %collective-permute-start.15) | collective-permute-done | bytes 327712 | tf_op jit(solution)/shard_map/ppermute | solution.py:166
  72.2 8.4 %logits.2 = (f32[501,256]{1,0:T(8,128)S(1)}, f32[501,256]{1,0:T(8,128)S(1)}, f32[501,256]{1,0:T(8,128)S(1)}) custom-call(s32[1]{0:T(128)} %bitcast.core_ref.place_ref, bf16[256,5120]{1,0:T(8,128)(2,1)S(1)} %whole.2.refs_0_, bf16[256,5120]{1,0:T(8,128)(2,1)} %copy-done, bf16[501,4096]{1,0:T(8,128)(2,1)} %bitcast.25, bf16[501,16384]{1,0:T(8,128)(2,1)} %bitcast.22), custom_call_target="tpu_custom_call" | custom-call | flops 1 | bytes 1 | tf_op jit(solution)/shard_map/logits/pallas_call | solution.py:292
  82.1 9.8 %logits.3 = (f32[501,256]{1,0:T(8,128)S(1)}, f32[501,256]{1,0:T(8,128)S(1)}, f32[128,8,128]{2,1,0:T(8,128)}) custom-call(s32[1]{0:T(128)S(6)} %sub.3.place_ref, bf16[256,5120]{1,0:T(8,128)(2,1)S(1)} %collective-permute-done.19.refs_0_, bf16[256,5120]{1,0:T(8,128)(2,1)} %copy-done.11, bf16[501,4096]{1,0:T(8,128)(2,1)} %bitcast.26, ...), custom_call_target="tpu_custom_call" | custom-call | flops 1 | bytes 1 | tf_op jit(solution)/shard_map/logits/pallas_call | solution.py:292
  92.7 7.6 %all-to-all-start = ((f32[128,8,128]{2,1,0:T(8,128)}), f32[128,8,128]{2,1,0:T(8,128)S(1)}, u32[]{:S(2)}, u32[]{:S(2)}) async-start(f32[128,8,128]{2,1,0:T(8,128)} %get-tuple-element.85), calls=%async_computation | async-start | bytes 1048576 | tf_op jit(solution)/shard_map/all_to_all | solution.py:54
  100.6 12.6 %all-to-all-done.every_ref = f32[128,8,128]{2,1,0:T(8,128)S(1)} async-done(((f32[128,8,128]{2,1,0:T(8,128)}), f32[128,8,128]{2,1,0:T(8,128)S(1)}, u32[]{:S(2)}, u32[]{:S(2)}) %all-to-all-start) | async-done | bytes 524320 | tf_op jit(solution)/shard_map/all_to_all | solution.py:54
  114.3 3.7 %row_grad.1 = (f32[128,4096]{1,0:T(8,128)S(1)}, bf16[128,4096]{1,0:T(8,128)(2,1)S(1)}, f32[1,256]{1,0:T(1,128)S(1)}) custom-call(s32[1]{0:T(128)} %bitcast.core_ref.place_ref, f32[128,8,128]{2,1,0:T(8,128)S(1)} %all-to-all-done.every_ref, f32[1,256]{1,0:T(1,128)S(1)} %reshape.32.weight_ref, f32[501,256]{1,0:T(8,128)S(1)} %copy-done.5, ...), custom_call_target="tpu_custom_call" | custom-call | flops 1 | bytes 1 | tf_op jit(solution)/shard_map/row_grad/pallas_call | solution.py:361
  118.2 2.6 %collective-permute-done.21.refs_1_ = bf16[128,4096]{1,0:T(8,128)(2,1)S(1)} collective-permute-done((bf16[128,4096]{1,0:T(8,128)(2,1)S(1)}, bf16[128,4096]{1,0:T(8,128)(2,1)S(1)}, u32[]{:S(2)}, u32[]{:S(2)}) %collective-permute-start.21) | collective-permute-done | bytes 1048608 | tf_op jit(solution)/shard_map/ppermute | solution.py:46
  120.7 2.6 %join.2 = bf16[64,32,512]{2,1,0:T(8,128)(2,1)S(1)} custom-call(f32[128,4096]{1,0:T(8,128)S(1)} %get-tuple-element.89.refs_0_, bf16[128,4096]{1,0:T(8,128)(2,1)S(1)} %collective-permute-done.21.refs_1_, bf16[128,4096]{1,0:T(8,128)(2,1)S(1)} %get-tuple-element.91.refs_2_, bf16[128,4096]{1,0:T(8,128)(2,1)S(1)} %collective-permute-done.10.refs_3_), custom_call_target="tpu_custom_call" | custom-call | flops 1 | bytes 1 | tf_op jit(solution)/shard_map/join/pallas_call | solution.py:436
  123.4 36.1 %all_to_all.20.blocks_ref = bf16[64,32,512]{2,1,0:T(8,128)(2,1)S(1)} all-to-all(bf16[64,32,512]{2,1,0:T(8,128)(2,1)S(1)} %join.2), channel_id=1, replica_groups=mesh['core'=2,'x'=4,'yh'=2,'z'=4,'yl'=2] {'x','yh','z','yl'}, dimensions={0} | all-to-all | bytes 4194304 | tf_op jit(solution)/shard_map/all_to_all | solution.py:54
  160.1 35.6 %all_to_all.21.own_ref = bf16[64,32,512]{2,1,0:T(8,128)(2,1)S(1)} all-to-all(bf16[64,32,512]{2,1,0:T(8,128)(2,1)S(1)} %get-tuple-element.93), channel_id=1, replica_groups=mesh['core'=2,'x'=4,'yh'=2,'z'=4,'yl'=2] {'x','yh','z','yl'}, dimensions={0} | all-to-all | bytes 4194304 | tf_op jit(solution)/shard_map/all_to_all | solution.py:54
  195.7 4.2 %collective-permute-done.22.other_ref = bf16[64,32,512]{2,1,0:T(8,128)(2,1)S(1)} collective-permute-done((bf16[64,32,512]{2,1,0:T(8,128)(2,1)S(1)}, bf16[64,32,512]{2,1,0:T(8,128)(2,1)S(1)}, u32[]{:S(2)}, u32[]{:S(2)}) %collective-permute-start.22) | collective-permute-done | bytes 2097184 | tf_op jit(solution)/shard_map/ppermute | solution.py:46
  199.8 6.5 %ffn_grad.1 = (f32[128,4096]{1,0:T(8,128)S(1)}, bf16[128,4096]{1,0:T(8,128)(2,1)S(1)}) custom-call(bf16[64,32,512]{2,1,0:T(8,128)(2,1)S(1)} %all_to_all.21.own_ref, bf16[64,32,512]{2,1,0:T(8,128)(2,1)S(1)} %collective-permute-done.22.other_ref, bf16[112,4096]{1,0:T(8,128)(2,1)S(1)} %copy-done.1, bf16[112,4096]{1,0:T(8,128)(2,1)S(1)} %bitcast.15, ...), custom_call_target="tpu_custom_call" | custom-call | flops 1 | bytes 1 | tf_op jit(solution)/shard_map/ffn_grad/pallas_call | solution.py:568
  206.6 2.5 %collective-permute-done.23.refs_1_ = bf16[128,4096]{1,0:T(8,128)(2,1)S(1)} collective-permute-done((bf16[128,4096]{1,0:T(8,128)(2,1)S(1)}, bf16[128,4096]{1,0:T(8,128)(2,1)S(1)}, u32[]{:S(2)}, u32[]{:S(2)}) %collective-permute-start.23) | collective-permute-done | bytes 1048608 | tf_op jit(solution)/shard_map/ppermute | solution.py:46
  209.1 2.3 join.3
  211.4 5.4 %all-to-all-start.3 = ((bf16[64,16,512]{2,1,0:T(8,128)(2,1)}), bf16[64,16,512]{2,1,0:T(8,128)(2,1)S(1)}, u32[]{:S(2)}, u32[]{:S(2)}) async-start(bf16[64,16,512]{2,1,0:T(8,128)(2,1)} %join.3), calls=%async_computation.3 | async-start | bytes 2097152 | tf_op jit(solution)/shard_map/all_to_all | solution.py:54
  218.9 17.0 %all-to-all-done.3.blocks_ref = bf16[64,16,512]{2,1,0:T(8,128)(2,1)S(1)} async-done(((bf16[64,16,512]{2,1,0:T(8,128)(2,1)}), bf16[64,16,512]{2,1,0:T(8,128)(2,1)S(1)}, u32[]{:S(2)}, u32[]{:S(2)}) %all-to-all-start.3) | async-done | bytes 1048608 | tf_op jit(solution)/shard_map/all_to_all | solution.py:54
  (74 shorter events, 23.8 us)
Async XLA Ops:
  2.5 1.5 collective-permute-start
  4.9 10.1 %collective-permute-start.1 = (bf16[4,10240]{1,0:T(4,128)(2,1)S(1)}, bf16[4,10240]{1,0:T(4,128)(2,1)S(1)}, u32[]{:S(2)}, u32[]{:S(2)}) collective-permute-start(bf16[4,10240]{1,0:T(4,128)(2,1)S(1)} %chip.1.refs_0_), channel_id=1, source_target_pairs={{0,1},{1,0},{8,9},{9,8},{2,3},{3,2},{10,11},{11,10},{4,5},{5,4},{1... | collective-permute-start | bytes 245768 | tf_op jit(solution)/shard_map/ppermute | solution.py:50
  6.6 8.4 %collective-permute-start.2 = (bf16[4,10240]{1,0:T(4,128)(2,1)S(1)}, bf16[4,10240]{1,0:T(4,128)(2,1)S(1)}, u32[]{:S(2)}, u32[]{:S(2)}) collective-permute-start(bf16[4,10240]{1,0:T(4,128)(2,1)S(1)} %chip.1.refs_0_), channel_id=1, source_target_pairs={{0,8},{1,9},{8,0},{9,1},{2,10},{3,11},{10,2},{11,3},{4,12},{5,13},... | collective-permute-start | bytes 245768 | tf_op jit(solution)/shard_map/ppermute | solution.py:50
  9.5 6.0 %collective-permute-start.3 = (bf16[4,10240]{1,0:T(4,128)(2,1)S(1)}, bf16[4,10240]{1,0:T(4,128)(2,1)S(1)}, u32[]{:S(2)}, u32[]{:S(2)}) collective-permute-start(bf16[4,10240]{1,0:T(4,128)(2,1)S(1)} %chip.1.refs_0_), channel_id=1, source_target_pairs={{0,9},{1,8},{8,1},{9,0},{2,11},{3,10},{10,3},{11,2},{4,13},{5,12},... | collective-permute-start | bytes 245768 | tf_op jit(solution)/shard_map/ppermute | solution.py:50
  15.5 21.0 %collective-permute-start.10 = (bf16[128,4096]{1,0:T(8,128)(2,1)}, bf16[128,4096]{1,0:T(8,128)(2,1)S(1)}, u32[]{:S(2)}, u32[]{:S(2)}) collective-permute-start(bf16[128,4096]{1,0:T(8,128)(2,1)} %get-tuple-element.61), channel_id=1, source_target_pairs={{0,64},{64,0},{1,65},{65,1},{2,66},{66,2},{3,67},{67,3},{4,68},{68... | collective-permute-start | bytes 3145736 | tf_op jit(solution)/shard_map/ppermute | solution.py:46
  15.7 7.2 %collective-permute-start.4 = (bf16[16,5120]{1,0:T(8,128)(2,1)S(1)}, bf16[16,5120]{1,0:T(8,128)(2,1)S(1)}, u32[]{:S(2)}, u32[]{:S(2)}) collective-permute-start(bf16[16,5120]{1,0:T(8,128)(2,1)S(1)} %get-tuple-element.62.refs_0_), channel_id=1, source_target_pairs={{0,2},{2,0},{4,6},{6,4},{1,3},{3,1},{5,7},{7,5},{8,10},{10,8},{12,... | collective-permute-start | bytes 491528 | tf_op jit(solution)/shard_map/ppermute | solution.py:50
  17.7 11.8 %collective-permute-start.5 = (bf16[16,5120]{1,0:T(8,128)(2,1)S(1)}, bf16[16,5120]{1,0:T(8,128)(2,1)S(1)}, u32[]{:S(2)}, u32[]{:S(2)}) collective-permute-start(bf16[16,5120]{1,0:T(8,128)(2,1)S(1)} %get-tuple-element.62.refs_0_), channel_id=1, source_target_pairs={{0,4},{2,6},{4,0},{6,2},{1,5},{3,7},{5,1},{7,3},{8,12},{10,14},{12... | collective-permute-start | bytes 491528 | tf_op jit(solution)/shard_map/ppermute | solution.py:50
  21.2 11.0 %collective-permute-start.6 = (bf16[16,5120]{1,0:T(8,128)(2,1)S(1)}, bf16[16,5120]{1,0:T(8,128)(2,1)S(1)}, u32[]{:S(2)}, u32[]{:S(2)}) collective-permute-start(bf16[16,5120]{1,0:T(8,128)(2,1)S(1)} %get-tuple-element.62.refs_0_), channel_id=1, source_target_pairs={{0,6},{2,4},{4,2},{6,0},{1,7},{3,5},{5,3},{7,1},{8,14},{10,12},{12... | collective-permute-start | bytes 491528 | tf_op jit(solution)/shard_map/ppermute | solution.py:50
  21.2 11.0 %collective-permute-start.7 = (bf16[16,5120]{1,0:T(8,128)(2,1)S(1)}, bf16[16,5120]{1,0:T(8,128)(2,1)S(1)}, u32[]{:S(2)}, u32[]{:S(2)}) collective-permute-start(bf16[16,5120]{1,0:T(8,128)(2,1)S(1)} %get-tuple-element.66.refs_0_), channel_id=1, source_target_pairs={{0,16},{16,0},{32,48},{48,32},{1,17},{17,1},{33,49},{49,33},{2,18}... | collective-permute-start | bytes 491528 | tf_op jit(solution)/shard_map/ppermute | solution.py:50
  22.8 10.2 %collective-permute-start.8 = (bf16[16,5120]{1,0:T(8,128)(2,1)S(1)}, bf16[16,5120]{1,0:T(8,128)(2,1)S(1)}, u32[]{:S(2)}, u32[]{:S(2)}) collective-permute-start(bf16[16,5120]{1,0:T(8,128)(2,1)S(1)} %get-tuple-element.66.refs_0_), channel_id=1, source_target_pairs={{0,32},{16,48},{32,0},{48,16},{1,33},{17,49},{33,1},{49,17},{2,34}... | collective-permute-start | bytes 491528 | tf_op jit(solution)/shard_map/ppermute | solution.py:50
  29.4 7.1 %collective-permute-start.9 = (bf16[16,5120]{1,0:T(8,128)(2,1)S(1)}, bf16[16,5120]{1,0:T(8,128)(2,1)S(1)}, u32[]{:S(2)}, u32[]{:S(2)}) collective-permute-start(bf16[16,5120]{1,0:T(8,128)(2,1)S(1)} %get-tuple-element.66.refs_0_), channel_id=1, source_target_pairs={{0,48},{16,32},{32,16},{48,0},{1,49},{17,33},{33,17},{49,1},{2,50}... | collective-permute-start | bytes 491528 | tf_op jit(solution)/shard_map/ppermute | solution.py:50
  37.4 15.6 %collective-permute-start.13 = (bf16[64,5120]{1,0:T(8,128)(2,1)S(1)}, bf16[64,5120]{1,0:T(8,128)(2,1)S(1)}, u32[]{:S(2)}, u32[]{:S(2)}) collective-permute-start(bf16[64,5120]{1,0:T(8,128)(2,1)S(1)} %plane.3.refs_0_), channel_id=1, source_target_pairs={{0,2},{2,0},{4,6},{6,4},{1,3},{3,1},{5,7},{7,5},{8,10},{10,8},{12,... | collective-permute-start | bytes 1966088 | tf_op jit(solution)/shard_map/ppermute | solution.py:166
  37.5 16.8 %collective-permute-start.14 = (bf16[64,5120]{1,0:T(8,128)(2,1)S(1)}, bf16[64,5120]{1,0:T(8,128)(2,1)S(1)}, u32[]{:S(2)}, u32[]{:S(2)}) collective-permute-start(bf16[64,5120]{1,0:T(8,128)(2,1)S(1)} %plane.3.refs_0_), channel_id=1, source_target_pairs={{0,6},{2,4},{4,2},{6,0},{1,7},{3,5},{5,3},{7,1},{8,14},{10,12},{12... | collective-permute-start | bytes 1966088 | tf_op jit(solution)/shard_map/ppermute | solution.py:166
  40.8 15.8 %collective-permute-start.11 = (bf16[64,5120]{1,0:T(8,128)(2,1)S(1)}, bf16[64,5120]{1,0:T(8,128)(2,1)S(1)}, u32[]{:S(2)}, u32[]{:S(2)}) collective-permute-start(bf16[64,5120]{1,0:T(8,128)(2,1)S(1)} %plane.2.refs_0_), channel_id=1, source_target_pairs={{0,16},{16,0},{32,48},{48,32},{1,17},{17,1},{33,49},{49,33},{2,18}... | collective-permute-start | bytes 1966088 | tf_op jit(solution)/shard_map/ppermute | solution.py:166
  41.2 16.8 %collective-permute-start.12 = (bf16[64,5120]{1,0:T(8,128)(2,1)S(1)}, bf16[64,5120]{1,0:T(8,128)(2,1)S(1)}, u32[]{:S(2)}, u32[]{:S(2)}) collective-permute-start(bf16[64,5120]{1,0:T(8,128)(2,1)S(1)} %plane.2.refs_0_), channel_id=1, source_target_pairs={{0,48},{16,32},{32,16},{48,0},{1,49},{17,33},{33,17},{49,1},{2,50}... | collective-permute-start | bytes 1966088 | tf_op jit(solution)/shard_map/ppermute | solution.py:166
  58.5 9.0 %collective-permute-start.15 = (bf16[32,5120]{1,0:T(8,128)(2,1)S(1)}, bf16[32,5120]{1,0:T(8,128)(2,1)S(1)}, u32[]{:S(2)}, u32[]{:S(2)}) collective-permute-start(bf16[32,5120]{1,0:T(8,128)(2,1)S(1)} %get-tuple-element.74), channel_id=1, source_target_pairs={{0,48},{16,32},{32,16},{48,0},{1,49},{17,33},{33,17},{49,1},{2,50}... | collective-permute-start | bytes 983048 | tf_op jit(solution)/shard_map/ppermute | solution.py:166
  60.7 7.6 %collective-permute-start.16 = (bf16[32,5120]{1,0:T(8,128)(2,1)S(1)}, bf16[32,5120]{1,0:T(8,128)(2,1)S(1)}, u32[]{:S(2)}, u32[]{:S(2)}) collective-permute-start(bf16[32,5120]{1,0:T(8,128)(2,1)S(1)} %get-tuple-element.75), channel_id=1, source_target_pairs={{0,16},{16,0},{32,48},{48,32},{1,17},{17,1},{33,49},{49,33},{2,18}... | collective-permute-start | bytes 983048 | tf_op jit(solution)/shard_map/ppermute | solution.py:166
  60.7 8.8 %collective-permute-start.17 = (bf16[32,5120]{1,0:T(8,128)(2,1)S(1)}, bf16[32,5120]{1,0:T(8,128)(2,1)S(1)}, u32[]{:S(2)}, u32[]{:S(2)}) collective-permute-start(bf16[32,5120]{1,0:T(8,128)(2,1)S(1)} %get-tuple-element.76), channel_id=1, source_target_pairs={{0,6},{2,4},{4,2},{6,0},{1,7},{3,5},{5,3},{7,1},{8,14},{10,12},{12... | collective-permute-start | bytes 983048 | tf_op jit(solution)/shard_map/ppermute | solution.py:166
  61.4 8.1 %collective-permute-start.18 = (bf16[32,5120]{1,0:T(8,128)(2,1)S(1)}, bf16[32,5120]{1,0:T(8,128)(2,1)S(1)}, u32[]{:S(2)}, u32[]{:S(2)}) collective-permute-start(bf16[32,5120]{1,0:T(8,128)(2,1)S(1)} %get-tuple-element.77), channel_id=1, source_target_pairs={{0,2},{2,0},{4,6},{6,4},{1,3},{3,1},{5,7},{7,5},{8,10},{10,8},{12,... | collective-permute-start | bytes 983048 | tf_op jit(solution)/shard_map/ppermute | solution.py:166
  70.4 10.1 %collective-permute-start.20 = (bf16[256,5120]{1,0:T(8,128)(2,1)S(1)}, bf16[256,5120]{1,0:T(8,128)(2,1)S(1)}, u32[]{:S(2)}, u32[]{:S(2)}) collective-permute-start(bf16[256,5120]{1,0:T(8,128)(2,1)S(1)} %whole.3.refs_1_), channel_id=1, source_target_pairs={{0,64},{64,0},{1,65},{65,1},{2,66},{66,2},{3,67},{67,3},{4,68},{68... | collective-permute-start | bytes 7864328 | tf_op jit(solution)/shard_map/ppermute | solution.py:46
  71.9 8.7 %collective-permute-start.19 = (bf16[256,5120]{1,0:T(8,128)(2,1)S(1)}, bf16[256,5120]{1,0:T(8,128)(2,1)S(1)}, u32[]{:S(2)}, u32[]{:S(2)}) collective-permute-start(bf16[256,5120]{1,0:T(8,128)(2,1)S(1)} %whole.2.refs_0_), channel_id=1, source_target_pairs={{0,64},{64,0},{1,65},{65,1},{2,66},{66,2},{3,67},{67,3},{4,68},{68... | collective-permute-start | bytes 7864328 | tf_op jit(solution)/shard_map/ppermute | solution.py:46
  92.7 20.6 %all-to-all-start = ((f32[128,8,128]{2,1,0:T(8,128)}), f32[128,8,128]{2,1,0:T(8,128)S(1)}, u32[]{:S(2)}, u32[]{:S(2)}) async-start(f32[128,8,128]{2,1,0:T(8,128)} %get-tuple-element.85), calls=%async_computation | async-start | bytes 1048576 | tf_op jit(solution)/shard_map/all_to_all | solution.py:54
  118.0 2.7 %collective-permute-start.21 = (bf16[128,4096]{1,0:T(8,128)(2,1)S(1)}, bf16[128,4096]{1,0:T(8,128)(2,1)S(1)}, u32[]{:S(2)}, u32[]{:S(2)}) collective-permute-start(bf16[128,4096]{1,0:T(8,128)(2,1)S(1)} %get-tuple-element.90), channel_id=1, source_target_pairs={{0,64},{64,0},{1,65},{65,1},{2,66},{66,2},{3,67},{67,3},{4,68},{68... | collective-permute-start | bytes 3145736 | tf_op jit(solution)/shard_map/ppermute | solution.py:46
  123.4 36.1 %copy-start.6 = (bf16[2,4096]{1,0:T(2,128)(2,1)S(1)}, bf16[2,4096]{1,0:T(2,128)(2,1)}, u32[]{:S(2)}) copy-start(bf16[2,4096]{1,0:T(2,128)(2,1)} %states_ref.1) | copy-start | bytes 49156
  123.4 36.1 %copy-start.8 = (bf16[4096]{0:T(1024)(128)(2,1)S(1)}, bf16[4096]{0:T(1024)(128)(2,1)}, u32[]{:S(2)}) copy-start(bf16[4096]{0:T(1024)(128)(2,1)} %param.19) | copy-start | bytes 24580
  123.4 36.1 %copy-start.9 = (bf16[4096]{0:T(1024)(128)(2,1)S(1)}, bf16[4096]{0:T(1024)(128)(2,1)}, u32[]{:S(2)}) copy-start(bf16[4096]{0:T(1024)(128)(2,1)} %param.16) | copy-start | bytes 24580
  160.0 39.8 %copy-start.1 = (bf16[112,4096]{1,0:T(8,128)(2,1)S(1)}, bf16[112,4096]{1,0:T(8,128)(2,1)}, u32[]{:S(2)}) copy-start(bf16[112,4096]{1,0:T(8,128)(2,1)} %down_ref.1) | copy-start | bytes 2752516
  160.0 39.8 %copy-start.2 = (bf16[4096,112]{0,1:T(8,128)(2,1)S(1)}, bf16[4096,112]{0,1:T(8,128)(2,1)}, u32[]{:S(2)}) copy-start(bf16[4096,112]{0,1:T(8,128)(2,1)} %param.20) | copy-start | bytes 2752516
  160.1 39.8 %copy-start.3 = (bf16[4096,112]{0,1:T(8,128)(2,1)S(1)}, bf16[4096,112]{0,1:T(8,128)(2,1)}, u32[]{:S(2)}) copy-start(bf16[4096,112]{0,1:T(8,128)(2,1)} %param.21) | copy-start | bytes 2752516
  195.7 4.2 %collective-permute-start.22 = (bf16[64,32,512]{2,1,0:T(8,128)(2,1)S(1)}, bf16[64,32,512]{2,1,0:T(8,128)(2,1)S(1)}, u32[]{:S(2)}, u32[]{:S(2)}) collective-permute-start(bf16[64,32,512]{2,1,0:T(8,128)(2,1)S(1)} %all_to_all.21.own_ref), channel_id=1, source_target_pairs={{0,64},{64,0},{1,65},{65,1},{2,66},{66,2},{3,67},{67,3},{4,68},{68... | collective-permute-start | bytes 6291464 | tf_op jit(solution)/shard_map/ppermute | solution.py:46
  206.4 2.7 %collective-permute-start.23 = (bf16[128,4096]{1,0:T(8,128)(2,1)S(1)}, bf16[128,4096]{1,0:T(8,128)(2,1)S(1)}, u32[]{:S(2)}, u32[]{:S(2)}) collective-permute-start(bf16[128,4096]{1,0:T(8,128)(2,1)S(1)} %get-tuple-element.95), channel_id=1, source_target_pairs={{0,64},{64,0},{1,65},{65,1},{2,66},{66,2},{3,67},{67,3},{4,68},{68... | collective-permute-start | bytes 3145736 | tf_op jit(solution)/shard_map/ppermute | solution.py:46
  211.4 24.5 %all-to-all-start.3 = ((bf16[64,16,512]{2,1,0:T(8,128)(2,1)}), bf16[64,16,512]{2,1,0:T(8,128)(2,1)S(1)}, u32[]{:S(2)}, u32[]{:S(2)}) async-start(bf16[64,16,512]{2,1,0:T(8,128)(2,1)} %join.3), calls=%async_computation.3 | async-start | bytes 2097152 | tf_op jit(solution)/shard_map/all_to_all | solution.py:54
  (7 other events, 24.5 us)

commit v5 on v4

--- a/solution.py
+++ b/solution.py
@@ -44,10 +44,6 @@
 
 def swap_cores(values):
     return lax.ppermute(values, "core", [(0, 1), (1, 0)])
-
-
-def line_pieces(block, line):
-    return [block] + [lax.ppermute(block, line, [(i, i ^ m) for i in range(4)]) for m in (1, 2, 3)]
 
 
 def exchange(blocks, axes):
@@ -90,52 +86,55 @@
         column = column + half
 
 
-def chip_kernel(core_ref, keep_ref, came_ref, out_ref):
-    keep, came = keep_ref[...].astype(jnp.float32), came_ref[...].astype(jnp.float32)
-    first = core_ref[0] == 0
-    rows = jnp.concatenate([jnp.where(first, keep, came), jnp.where(first, came, keep)], axis=0)
-    out_ref[...] = rows.astype(jnp.bfloat16)
-
-
-def line_kernel(place_ref, *refs):
-    pieces = [ref[...].astype(jnp.float32) for ref in refs[:4]]
-    rows = []
-    for j in range(4):
-        m = place_ref[0] ^ j
-        low = jnp.where(m == 0, pieces[0], pieces[1])
-        high = jnp.where(m == 2, pieces[2], pieces[3])
-        rows.append(jnp.where(m < 2, low, high))
-    rows = jnp.concatenate(rows, axis=0).astype(jnp.bfloat16)
+def pair_kernel(place_ref, own_ref, came_ref, *out_refs):
+    own, came = own_ref[...].astype(jnp.float32), came_ref[...].astype(jnp.float32)
+    first = place_ref[0] == 0
+    rows = jnp.concatenate([jnp.where(first, own, came), jnp.where(first, came, own)], axis=0)
+    rows = rows.astype(jnp.bfloat16)
     column = 0
-    for out in refs[4:]:
+    for out in out_refs:
         out[...] = rows[:, column : column + out.shape[1]]
         column = column + out.shape[1]
 
 
-def plane_kernel(place_ref, *refs):
-    pieces, out, sems = refs[:4], refs[4], refs[5]
+def in_pair(bit, own, came, widths):
+    tokens = 2 * own.shape[0]
+    return kernel_call(
+        pair_kernel,
+        "pair",
+        [shape_of((tokens, w)) for w in widths],
+        in_specs=[SMEM] + [VMEM] * 2,
+        out_specs=[VMEM] * len(widths),
+    )(bit, own, came)
+
+
+def groups_kernel(place_ref, *refs):
+    count = (len(refs) - 1) // 3
+    sources, outs, sems = refs[: 2 * count], refs[2 * count : -1], refs[-1]
     copies = []
-    for m, piece in enumerate(pieces):
-        tokens = piece.shape[0]
-        at = pl.multiple_of((place_ref[0] ^ m) * tokens, tokens)
-        copy = pltpu.make_async_copy(piece, out.at[pl.ds(at, tokens), :], sems.at[m])
-        copy.start()
-        copies.append(copy)
+    for g, out in enumerate(outs):
+        for i in range(2):
+            source = sources[2 * g + i]
+            tokens = source.shape[0]
+            at = pl.multiple_of((place_ref[g] ^ i) * tokens, tokens)
+            copy = pltpu.make_async_copy(source, out.at[pl.ds(at, tokens), :], sems.at[2 * g + i])
+            copy.start()
+            copies.append(copy)
     for copy in copies:
         copy.wait()
 
 
-def in_line_order(place, pieces):
-    tokens, width = pieces[0].shape
-    return kernel_call(
-        plane_kernel,
-        "plane",
-        shape_of((4 * tokens, width)),
+def in_pairs(bits, parts):
+    tokens = 2 * parts[0].shape[0]
+    return kernel_call(
+        groups_kernel,
+        "pairs",
+        [shape_of((tokens, part.shape[1])) for part in parts[::2]],
         limit=2,
-        in_specs=[SMEM] + [ANY] * 4,
-        out_specs=ANY,
-        scratch_shapes=[pltpu.SemaphoreType.DMA((4,))],
-    )(place, *pieces)
+        in_specs=[SMEM] + [ANY] * len(parts),
+        out_specs=[ANY] * (len(parts) // 2),
+        scratch_shapes=[pltpu.SemaphoreType.DMA((len(parts),))],
+    )(bits, *parts)
 
 
 def halves_kernel(*refs):
@@ -195,8 +194,8 @@
 
 
 GROUPS = (
-    tuple((0, i * 1024, 1024) for i in range(2)) + tuple((1, i * 1024, 1024) for i in range(3)),
-    tuple((1, i * 1024, 1024) for i in range(3, 8)),
+    ((0, 0, 2048), (1, 0, 3072)),
+    ((1, 3072, 2560), (1, 5632, 2560)),
 )
 WIDTHS = tuple(sum(p[2] for p in group) for group in GROUPS)
 
@@ -229,8 +228,7 @@
         cross / teacher_total,
     )
     rows = [row[:, :128] for row in stats] + [row[:, 128:] for row in stats]
-    rows = jnp.concatenate(rows + [jnp.zeros((2, 128), jnp.float32)], axis=0)
-    stats_out[...] = jnp.broadcast_to(rows[None], stats_out.shape)
+    stats_out[...] = jnp.concatenate(rows + [jnp.zeros((2, 128), jnp.float32)], axis=0)
 
 
 def logits_kernel(last, place_ref, *refs):
@@ -258,7 +256,7 @@
             )
             copies.append((kind + (base > 0), columns, pair))
             column = column + width
-    ahead = 3
+    ahead = 2
     for _, _, pair in copies[:ahead]:
         for copy in pair:
             copy.start()
@@ -288,7 +286,7 @@
     shape = shape_of((vocab, tokens), jnp.float32)
     last = len(sums) > 0
     pieces = sum(len(group) for group in GROUPS)
-    out_shape = [shape, shape, shape_of((128, 8, 128), jnp.float32) if last else shape]
+    out_shape = [shape, shape, shape_of((8, 128), jnp.float32) if last else shape]
     return kernel_call(
         functools.partial(logits_kernel, last),
         "logits",
@@ -326,17 +324,27 @@
     return list(zip(parts, copies))
 
 
+def merged_stats(every):
+    peak = jnp.max(every, axis=0)
+    scaled = jnp.exp(every - peak[None])
+    total = jnp.sum(scaled, axis=0)
+    cross = jnp.sum(scaled * pltpu.roll(every, 6, 1), axis=0) / total
+    return peak + jnp.log(total), cross
+
+
+def chip_stats_kernel(own_ref, came_ref, out_ref):
+    lse, cross = merged_stats(jnp.concatenate([own_ref[...][None], came_ref[...][None]], axis=0))
+    row = lax.broadcasted_iota(jnp.int32, lse.shape, 0)
+    merged = jnp.where((row == 2) | (row == 5), pltpu.roll(cross, 2, 0), lse)
+    out_ref[...] = jnp.broadcast_to(merged[None], out_ref.shape)
+
+
 def row_grad_kernel(
     core_ref, every_ref, weight_ref, teacher_ref, student_ref, head_from,
     own_ref, send_ref, divergence_ref, head, sems,
 ):
     copies = head_copies(head_from, head, sems)
-    every = every_ref[...]
-    peak = jnp.max(every, axis=0)
-    scaled = jnp.exp(every - peak[None])
-    total = jnp.sum(scaled, axis=0)
-    lse = peak + jnp.log(total)
-    cross = jnp.sum(scaled * pltpu.roll(every, 6, 1), axis=0) / total
+    lse, cross = merged_stats(every_ref[...])
     teacher_lse = jnp.concatenate([lse[0:1], lse[3:4]], axis=1)
     student_lse = jnp.concatenate([lse[1:2], lse[4:5]], axis=1)
     divergence_ref[...] = (
@@ -480,22 +488,21 @@
     return jnp.sum(blocks_ref[...].astype(jnp.float32), axis=0)
 
 
-def final_kernel(
-    blocks_ref, states_ref, student_gain, ffn_gain, grad_ref, embedded_ref, out_ref, states
-):
-    height = 2 * SEGMENTS
-    total = block_sum(blocks_ref)
-    embedded = total[height:]
-    embedded_ref[...] = embedded
-    rows = embedded * block_inverse(embedded) * block_gain(ffn_gain)
+def embed_kernel(blocks_ref, gain_ref, embedded_ref, out_ref):
+    values = block_sum(blocks_ref)
+    embedded_ref[...] = values
+    rows = (values * block_inverse(values) * block_gain(gain_ref)).astype(jnp.bfloat16)
+    out_ref[...] = jnp.broadcast_to(rows[None], out_ref.shape)
+
+
+def final_kernel(blocks_ref, states_ref, gain_ref, grad_ref, out_ref, states):
     for i in range(SEGMENTS):
         part = states_ref[:, i * SEGMENT : (i + 1) * SEGMENT].astype(jnp.float32)
         for t in range(2):
             states[t * SEGMENTS + i : t * SEGMENTS + i + 1, :] = part[t : t + 1]
-    grad = block_back(total[:height], states[...], block_gain(student_gain))
+    grad = block_back(block_sum(blocks_ref), states[...], block_gain(gain_ref))
     grad_ref[...] = grad
-    rows = jnp.concatenate([grad, rows], axis=0).astype(jnp.bfloat16)
-    out_ref[...] = jnp.broadcast_to(rows[None], out_ref.shape)
+    out_ref[...] = jnp.broadcast_to(grad.astype(jnp.bfloat16)[None], out_ref.shape)
 
 
 def state_kernel(blocks_ref, grad_ref, embedded_ref, gain_ref, out_ref):
@@ -519,29 +526,37 @@
             rows[k] = values[:, k * 128 : (k + 1) * 128]
 
 
-def segment_rows(scratches, first):
+def segment_rows(scratches, segment):
     parts = []
     for rows in scratches:
-        height = 4 * SEGMENTS
+        height = 2 * SEGMENTS
         for t in range(2):
-            at = pl.ds(first + t * SEGMENTS, rows.shape[1] // height, stride=height)
+            at = pl.ds(t * SEGMENTS + segment, rows.shape[1] // height, stride=height)
             parts.append(
                 jnp.concatenate([rows[k, at, :] for k in range(SEGMENT // 128)], axis=1)
             )
     return jnp.concatenate(parts, axis=0).astype(jnp.bfloat16)
 
 
+def gate_kernel(own_ref, other_ref, gate_ref, up_ref, out_ref, *scratches):
+    spread_rows((own_ref, other_ref), scratches)
+    total = None
+    for i in range(SEGMENTS):
+        columns = slice(i * SEGMENT, (i + 1) * SEGMENT)
+        weight = jnp.concatenate([gate_ref[:, columns], up_ref[:, columns]], axis=0)
+        term = row_product(weight, segment_rows(scratches, i))
+        total = term if total is None else total + term
+    out_ref[...] = total
+
+
 def ffn_grad_kernel(
-    own_ref, other_ref, down_ref, gate_ref, up_ref, own_out, send_out, *scratches
+    own_ref, other_ref, down_ref, hidden_ref, gate_ref, up_ref, own_out, send_out, *scratches
 ):
     spread_rows((own_ref, other_ref), scratches)
     units = down_ref.shape[0]
-    hidden, act_grad = None, None
+    hidden, act_grad = hidden_ref[...], None
     for i in range(SEGMENTS):
         columns = slice(i * SEGMENT, (i + 1) * SEGMENT)
-        weight = jnp.concatenate([gate_ref[:, columns], up_ref[:, columns]], axis=0)
-        term = row_product(weight, segment_rows(scratches, 2 * SEGMENTS + i))
-        hidden = term if hidden is None else hidden + term
         term = row_product(down_ref[:, columns], segment_rows(scratches, i))
         act_grad = term if act_grad is None else act_grad + term
     gate, upper = hidden[:units, :], hidden[units:, :]
@@ -569,7 +584,7 @@
         body,
         name,
         out_shape,
-        limit=30,
+        limit=20,
         in_specs=[VMEM] * (2 + len(others)),
         out_specs=[VMEM] * len(out_shape),
         scratch_shapes=[scratch, scratch],
@@ -593,9 +608,7 @@
     core = lax.axis_index("core")
     device = lax.axis_index(AXES)
     own_core = jnp.full((1,), core, jnp.int32)
-    x, z, y = (
-        jnp.full((1,), lax.axis_index(line), jnp.int32) for line in ("x", "z", ("yh", "yl"))
-    )
+    x, z, y = (lax.axis_index(line).astype(jnp.int32) for line in ("x", "z", ("yh", "yl")))
     teacher_gain, student_gain, ffn_gain = (
         gain.reshape(-1, 128) for gain in (teacher_gain, student_gain, ffn_gain)
     )
@@ -621,30 +634,18 @@
             pltpu.SemaphoreType.DMA((4,)),
         ],
     )(own_core, teacher_states, teacher_gain, student_states, student_gain)
-    rows = kernel_call(
-        chip_kernel,
-        "chip",
-        shape_of((4, width)),
-        in_specs=[SMEM] + [VMEM] * 2,
-        out_specs=VMEM,
-    )(own_core, keep, swap_cores(send))
-    pieces = line_pieces(rows, ("yh", "yl"))
+    (rows,) = in_pair(own_core, keep, swap_cores(send), (width,))
+
+    (rows,) = in_pair((y & 1).reshape(1), rows, along(rows, ("yh", "yl"), 1), (width,))
+    first, second = in_pair((y >> 1).reshape(1), rows, along(rows, ("yh", "yl"), 3), WIDTHS)
+    for bit, mask in ((0, 1), (1, 3)):
+        came = (along(first, "z", mask), along(second, "x", mask))
+        bits = (jnp.stack([z, x]) >> bit) & 1
+        first, second = in_pairs(bits, (first, came[0], second, came[1]))
+    came = [along(first, "x", 1), along(first, "x", 3), along(second, "z", 1), along(second, "z", 3)]
     place = jnp.stack([core, device]).astype(jnp.int32)
-    picked = pick_part(place, token_ids.reshape(1, 256), student_head_t)
-    pieces, picked = lax.optimization_barrier((pieces, picked))
-    picked = (picked[0], swap_cores(picked[1]))
-    first, second = kernel_call(
-        line_kernel,
-        "line",
-        [shape_of((16, w)) for w in WIDTHS],
-        in_specs=[SMEM] + [VMEM] * 4,
-        out_specs=[VMEM] * 2,
-    )(y, *pieces)
-    first, second = line_pieces(first, "z"), line_pieces(second, "x")
-    first, second, picked = lax.optimization_barrier((first, second, picked))
-    first, second = in_line_order(z, first), in_line_order(x, second)
-    came = [along(first, "x", 1), along(first, "x", 3), along(second, "z", 1), along(second, "z", 3)]
-    came = lax.optimization_barrier(came)
+    own, send = pick_part(place, token_ids.reshape(1, 256), student_head_t)
+    came, picked = lax.optimization_barrier((came, join_part(own, swap_cores(send))))
     halves = halves_of(came)
     far = [
         along(half, line, mask)
@@ -652,30 +653,52 @@
     ]
     far = lax.optimization_barrier(far)
     rows = (
-        whole_rows(x, [first] + came[:2] + far[:2]),
-        whole_rows(z, [second] + came[2:] + far[2:]),
+        whole_rows(x.reshape(1), [first] + came[:2] + far[:2]),
+        whole_rows(z.reshape(1), [second] + came[2:] + far[2:]),
     )
     others = tuple(swap_cores(part) for part in rows)
     sums = logits_part(own_core, rows, heads)
     student, teacher, stats = logits_part(1 - own_core, others, heads, sums)
-    every = exchange(stats, AXES)
+    stats = kernel_call(
+        chip_stats_kernel,
+        "chip_stats",
+        shape_of((64, 8, 128), jnp.float32),
+        limit=2,
+        in_specs=[VMEM] * 2,
+        out_specs=VMEM,
+    )(stats, swap_cores(stats))
+    stats, picked = lax.optimization_barrier((stats, picked))
+    every = exchange(stats, CHIPS)
+    picked = exchange(picked, CHIPS)
 
     weight = token_weight.reshape(2, 4, 2, 4, 2, 2).transpose(1, 3, 2, 4, 0, 5).reshape(1, 256)
     own, send, divergence = row_grad_part(
         own_core, every, weight, teacher, student, student_head_t
     )
     divergence = divergence.reshape(4, 4, 2, 2, 2, 2).transpose(4, 0, 2, 1, 3, 5).reshape(256)
-    blocks = exchange(join_part(own, swap_cores(send), *picked), CHIPS)
-    final_grad, embedded, blocks = kernel_call(
+    embedded, ffn_rows = kernel_call(
+        embed_kernel,
+        "embed",
+        [shape_of(BLOCK, jnp.float32), shape_of(picked.shape)],
+        in_specs=[VMEM] * 2,
+        out_specs=[VMEM] * 2,
+    )(picked, ffn_gain)
+    blocks = join_part(own, swap_cores(send))
+    blocks, ffn_rows = lax.optimization_barrier((blocks, ffn_rows))
+    blocks = exchange(blocks, CHIPS)
+    ffn_rows = exchange(ffn_rows, CHIPS)
+    final_grad, blocks = kernel_call(
         final_kernel,
         "final",
-        [shape_of(BLOCK, jnp.float32), shape_of(BLOCK, jnp.float32), shape_of(blocks.shape)],
-        limit=14,
-        in_specs=[VMEM] * 4,
-        out_specs=[VMEM] * 3,
+        [shape_of(BLOCK, jnp.float32), shape_of(blocks.shape)],
+        in_specs=[VMEM] * 3,
+        out_specs=[VMEM] * 2,
         scratch_shapes=[pltpu.VMEM(BLOCK, jnp.float32)],
-    )(blocks, student_states, student_gain, ffn_gain)
+    )(blocks, student_states, student_gain)
     blocks = exchange(blocks, CHIPS)
+    (hidden,) = ffn_part(
+        gate_kernel, "gate_upper", [shape_of((224, 256), jnp.float32)], ffn_rows, gate_t, up_t
+    )
     shape = (128, 4096)
     own, send = ffn_part(
         ffn_grad_kernel,
@@ -683,6 +706,7 @@
         [shape_of(shape, jnp.float32), shape_of(shape)],
         blocks,
         down_weight,
+        hidden,
         gate_t,
         up_t,
     )

time: 238 us -> 248 us (1.042)
  waiting for transfers between devices: 71.2 us -> 103 us
  blocking collectives: 71.7 us -> 46.5 us
  starting transfers between devices: 39.8 us -> 44.6 us
    all_to_all x2 -> x4, waiting for transfers between devices: 29.6 us -> 61.4 us  [exchange(): return lax.all_to_all(blocks, axes, split_axis=0, concat_axis=0, tiled=True)]
    all_to_all x2, blocking collectives: 71.7 us -> 46.5 us  [exchange(): return lax.all_to_all(blocks, axes, split_axis=0, concat_axis=0, tiled=True)]
    ppermute x9 -> x0, starting transfers between devices: 17.6 us -> none  [line_pieces(): lax.ppermute(block, line, [(i, i ^ m) for i in range(4)])]
    ppermute x8 -> x14, waiting for transfers between devices: 22.4 us -> 36.7 us  [along(): return lax.ppermute(block, line, [(i, i ^ mask) for i in range(4)])]
    ppermute x8 -> x14, starting transfers between devices: 8.36 us -> 20.2 us  [along(): return lax.ppermute(block, line, [(i, i ^ mask) for i in range(4)])]
    all_to_all x2 -> x4, starting transfers between devices: 13 us -> 22.7 us  [exchange(): return lax.all_to_all(blocks, axes, split_axis=0, concat_axis=0, tiled=True)]
    ppermute x9 -> x0, waiting for transfers between devices: 8.5 us -> none  [line_pieces(): lax.ppermute(block, line, [(i, i ^ m) for i in range(4)])]
    ppermute x7 -> x9, waiting for transfers between devices: 10.7 us -> 4.61 us  [swap_cores(): return lax.ppermute(values, 'core', [(0, 1), (1, 0)])]
  transfers between devices with their start and end apart: 26 -> 27, of which waited for: 18 -> 18; matrix products, arithmetic and copies ran while one was open for 1% -> 1% of each run, Pallas kernels for 6% -> 8%
where the time goes in v5:
time: 248 us; the launch traced here: 247 us
  waiting for transfers between devices  103 us (42%)
  blocking collectives  46.5 us (19%)
  starting transfers between devices  44.6 us (18%)
  Pallas kernels  44 us (18%)
  local copies, waits for them, and re-layouts  6.94 us (3%)
    all_to_all x4, waiting for transfers between devices, exchange(): return lax.all_to_all(blocks, axes, split_axis=0, concat_axis=0, tiled=True)  61.4 us
    all_to_all x2, blocking collectives, exchange(): return lax.all_to_all(blocks, axes, split_axis=0, concat_axis=0, tiled=True)  46.5 us
    ppermute x14, waiting for transfers between devices, along(): return lax.ppermute(block, line, [(i, i ^ mask) for i in range(4)])  36.7 us
    all_to_all x4, starting transfers between devices, exchange(): return lax.all_to_all(blocks, axes, split_axis=0, concat_axis=0, tiled=True)  22.7 us
    ppermute x14, starting transfers between devices, along(): return lax.ppermute(block, line, [(i, i ^ mask) for i in range(4)])  20.2 us
    pallas_call x2, Pallas kernels, logits_part(): kernel_call(functools.partial(logits_kernel, last), 'logits', out_shape,...  17 us
    pallas_call x2, Pallas kernels, ffn_part(): kernel_call(body, name, out_shape, limit=20, in_specs=[VMEM] * (2 + len(o...  6.03 us
    unnamed x24, local copies, waits for them, and re-layouts  5.15 us
  transfers between devices with their start and end apart: 27, of which 18 were waited for; matrix products, arithmetic and copies ran while one was open for 1% of the time, Pallas kernels for 8%

profile of v5, /device:TPU:0, one launch (start us, length us, event | category | flops | bytes accessed | tf_op | source)
XLA Modules:
  0.0 246.6 jit_solution(7527806724812539717)
XLA Ops:
  0.6 1.9 rows.1
  4.9 1.7 collective-permute-start.1
  6.6 2.9 %collective-permute-done.1.came_ref = bf16[4,10240]{1,0:T(4,128)(2,1)S(1)} collective-permute-done((bf16[4,10240]{1,0:T(4,128)(2,1)S(1)}, bf16[4,10240]{1,0:T(4,128)(2,1)S(1)}, u32[]{:S(2)}, u32[]{:S(2)}) %collective-permute-start.1) | collective-permute-done | bytes 81952 | tf_op jit(solution)/shard_map/ppermute | solution.py:165
  9.5 3.2 %collective-permute-start.2 = (bf16[8,10240]{1,0:T(8,128)(2,1)S(1)}, bf16[8,10240]{1,0:T(8,128)(2,1)S(1)}, u32[]{:S(2)}, u32[]{:S(2)}) collective-permute-start(bf16[8,10240]{1,0:T(8,128)(2,1)S(1)} %pair.4.own_ref), channel_id=1, source_target_pairs={{0,9},{1,8},{8,1},{9,0},{2,11},{3,10},{10,3},{11,2},{4,13},{5,12},... | collective-permute-start | bytes 491528 | tf_op jit(solution)/shard_map/ppermute | solution.py:165
  12.7 3.7 %collective-permute-done.2.came_ref = bf16[8,10240]{1,0:T(8,128)(2,1)S(1)} collective-permute-done((bf16[8,10240]{1,0:T(8,128)(2,1)S(1)}, bf16[8,10240]{1,0:T(8,128)(2,1)S(1)}, u32[]{:S(2)}, u32[]{:S(2)}) %collective-permute-start.2) | collective-permute-done | bytes 163872 | tf_op jit(solution)/shard_map/ppermute | solution.py:165
  16.5 2.0 collective-permute-start.3
  20.7 3.6 %pick.1 = (bf16[128,4096]{1,0:T(8,128)(2,1)S(1)}, bf16[128,4096]{1,0:T(8,128)(2,1)S(1)}) custom-call(s32[2]{0:T(128)S(1)} %pad_add_fusion.1.place_ref, s32[1,256]{1,0:T(1,128)S(1)} %bitcast.24, bf16[501,4096]{1,0:T(8,128)(2,1)} %bitcast.27), custom_call_target="tpu_custom_call" | custom-call | flops 1 | bytes 1 | tf_op jit(solution)/shard_map/pick/pallas_call | solution.py:408
  25.9 2.6 %collective-permute-start.5 = (bf16[32,5120]{1,0:T(8,128)(2,1)S(1)}, bf16[32,5120]{1,0:T(8,128)(2,1)S(1)}, u32[]{:S(2)}, u32[]{:S(2)}) collective-permute-start(bf16[32,5120]{1,0:T(8,128)(2,1)S(1)} %get-tuple-element.48.refs_0_), channel_id=1, source_target_pairs={{0,6},{2,4},{4,2},{6,0},{1,7},{3,5},{5,3},{7,1},{8,14},{10,12},{12... | collective-permute-start | bytes 983048 | tf_op jit(solution)/shard_map/ppermute | solution.py:165
  28.5 2.1 collective-permute-start.6
  30.7 6.6 %collective-permute-done.5.refs_1_ = bf16[32,5120]{1,0:T(8,128)(2,1)S(1)} collective-permute-done((bf16[32,5120]{1,0:T(8,128)(2,1)S(1)}, bf16[32,5120]{1,0:T(8,128)(2,1)S(1)}, u32[]{:S(2)}, u32[]{:S(2)}) %collective-permute-start.5) | collective-permute-done | bytes 327712 | tf_op jit(solution)/shard_map/ppermute | solution.py:165
  37.3 2.2 collective-permute-done.6.refs_3_
  41.5 2.8 %collective-permute-start.8 = (bf16[64,5120]{1,0:T(8,128)(2,1)S(1)}, bf16[64,5120]{1,0:T(8,128)(2,1)S(1)}, u32[]{:S(2)}, u32[]{:S(2)}) collective-permute-start(bf16[64,5120]{1,0:T(8,128)(2,1)S(1)} %get-tuple-element.50.refs_0_), channel_id=1, source_target_pairs={{0,48},{16,32},{32,16},{48,0},{1,49},{17,33},{33,17},{49,1},{2,50}... | collective-permute-start | bytes 1966088 | tf_op jit(solution)/shard_map/ppermute | solution.py:165
  45.5 12.4 %collective-permute-done.10.refs_3_.refs_2_ = bf16[64,5120]{1,0:T(8,128)(2,1)S(1)} collective-permute-done((bf16[64,5120]{1,0:T(8,128)(2,1)S(1)}, bf16[64,5120]{1,0:T(8,128)(2,1)S(1)}, u32[]{:S(2)}, u32[]{:S(2)}) %collective-permute-start.10) | collective-permute-done | bytes 655392 | tf_op jit(solution)/shard_map/ppermute | solution.py:165
  61.8 1.9 collective-permute-start.14
  63.7 5.4 %collective-permute-done.12.refs_3_ = bf16[32,5120]{1,0:T(8,128)(2,1)S(1)} collective-permute-done((bf16[32,5120]{1,0:T(8,128)(2,1)S(1)}, bf16[32,5120]{1,0:T(8,128)(2,1)S(1)}, u32[]{:S(2)}, u32[]{:S(2)}) %collective-permute-start.12) | collective-permute-done | bytes 327712 | tf_op jit(solution)/shard_map/ppermute | solution.py:165
  73.4 8.3 %logits.2 = (f32[501,256]{1,0:T(8,128)S(1)}, f32[501,256]{1,0:T(8,128)S(1)}, f32[501,256]{1,0:T(8,128)S(1)}) custom-call(s32[1]{0:T(128)} %bitcast.core_ref.place_ref, bf16[256,5120]{1,0:T(8,128)(2,1)S(1)} %whole.2.refs_0_, bf16[256,5120]{1,0:T(8,128)(2,1)} %copy-done, bf16[501,4096]{1,0:T(8,128)(2,1)} %bitcast.28, bf16[501,16384]{1,0:T(8,128)(2,1)} %bitcast.25), custom_call_target="tpu_custom_call" | custom-call | flops 1 | bytes 1 | tf_op jit(solution)/shard_map/logits/pallas_call | solution.py:290
  81.8 8.7 %logits.3 = (f32[501,256]{1,0:T(8,128)S(1)}, f32[501,256]{1,0:T(8,128)S(1)}, f32[8,128]{1,0:T(8,128)S(1)}) custom-call(s32[1]{0:T(128)S(6)} %sub.3.place_ref, bf16[256,5120]{1,0:T(8,128)(2,1)S(1)} %collective-permute-done.16.refs_0_, bf16[256,5120]{1,0:T(8,128)(2,1)} %collective-permute-done.17.refs_1_, bf16[501,4096]{1,0:T(8,128)(2,1)} %bitcast.29, ...), custom_call_target="tpu_custom_call" | custom-call | flops 1 | bytes 1 | tf_op jit(solution)/shard_map/logits/pallas_call | solution.py:290
  92.5 8.7 %all-to-all-start = ((f32[64,8,128]{2,1,0:T(8,128)}), f32[64,8,128]{2,1,0:T(8,128)S(1)}, u32[]{:S(2)}, u32[]{:S(2)}) async-start(f32[64,8,128]{2,1,0:T(8,128)} %chip_stats.1), calls=%async_computation | async-start | bytes 524288 | tf_op jit(solution)/shard_map/all_to_all | solution.py:50
  101.5 10.6 %all-to-all-done.every_ref = f32[64,8,128]{2,1,0:T(8,128)S(1)} async-done(((f32[64,8,128]{2,1,0:T(8,128)}), f32[64,8,128]{2,1,0:T(8,128)S(1)}, u32[]{:S(2)}, u32[]{:S(2)}) %all-to-all-start) | async-done | bytes 262176 | tf_op jit(solution)/shard_map/all_to_all | solution.py:50
  112.1 3.4 %row_grad.1 = (f32[128,4096]{1,0:T(8,128)S(1)}, bf16[128,4096]{1,0:T(8,128)(2,1)S(1)}, f32[1,256]{1,0:T(1,128)S(1)}) custom-call(s32[1]{0:T(128)} %bitcast.core_ref.place_ref, f32[64,8,128]{2,1,0:T(8,128)S(1)} %all-to-all-done.every_ref, f32[1,256]{1,0:T(1,128)S(1)} %reshape.45.weight_ref, f32[501,256]{1,0:T(8,128)S(1)} %get-tuple-element.72.teacher_ref, ...), custom_call_target="tpu_custom_call" | custom-call | flops 1 | bytes 1 | tf_op jit(solution)/shard_map/row_grad/pallas_call | solution.py:369
  115.6 24.0 %all_to_all.30.blocks_ref = bf16[64,16,512]{2,1,0:T(8,128)(2,1)S(1)} all-to-all(bf16[64,16,512]{2,1,0:T(8,128)(2,1)S(1)} %join.3), channel_id=1, replica_groups=mesh['core'=2,'x'=4,'yh'=2,'z'=4,'yl'=2] {'x','yh','z','yl'}, dimensions={0} | all-to-all | bytes 2097152 | tf_op jit(solution)/shard_map/all_to_all | solution.py:50
  142.2 22.5 %all_to_all.31.blocks_ref = bf16[64,16,512]{2,1,0:T(8,128)(2,1)S(1)} all-to-all(bf16[64,16,512]{2,1,0:T(8,128)(2,1)S(1)} %join.4), channel_id=1, replica_groups=mesh['core'=2,'x'=4,'yh'=2,'z'=4,'yl'=2] {'x','yh','z','yl'}, dimensions={0} | all-to-all | bytes 2097152 | tf_op jit(solution)/shard_map/all_to_all | solution.py:50
  164.7 4.8 %all-to-all-start.4 = ((bf16[64,16,512]{2,1,0:T(8,128)(2,1)}), bf16[64,16,512]{2,1,0:T(8,128)(2,1)S(1)}, u32[]{:S(2)}, u32[]{:S(2)}) async-start(bf16[64,16,512]{2,1,0:T(8,128)(2,1)} %copy-done.3), calls=%async_computation.4 | async-start | bytes 2097152 | tf_op jit(solution)/shard_map/all_to_all | solution.py:50
  170.9 16.2 %all-to-all-done.4.own_ref = bf16[64,16,512]{2,1,0:T(8,128)(2,1)S(1)} async-done(((bf16[64,16,512]{2,1,0:T(8,128)(2,1)}), bf16[64,16,512]{2,1,0:T(8,128)(2,1)S(1)}, u32[]{:S(2)}, u32[]{:S(2)}) %all-to-all-start.4) | async-done | bytes 1048608 | tf_op jit(solution)/shard_map/all_to_all | solution.py:50
  187.0 4.7 %all-to-all-start.3 = ((bf16[64,16,512]{2,1,0:T(8,128)(2,1)}), bf16[64,16,512]{2,1,0:T(8,128)(2,1)S(1)}, u32[]{:S(2)}, u32[]{:S(2)}) async-start(bf16[64,16,512]{2,1,0:T(8,128)(2,1)} %copy-done.4), calls=%async_computation.3 | async-start | bytes 2097152 | tf_op jit(solution)/shard_map/all_to_all | solution.py:50
  191.8 17.2 %all-to-all-done.3.own_ref = bf16[64,16,512]{2,1,0:T(8,128)(2,1)S(1)} async-done(((bf16[64,16,512]{2,1,0:T(8,128)(2,1)}), bf16[64,16,512]{2,1,0:T(8,128)(2,1)S(1)}, u32[]{:S(2)}, u32[]{:S(2)}) %all-to-all-start.3) | async-done | bytes 1048608 | tf_op jit(solution)/shard_map/all_to_all | solution.py:50
  210.2 3.0 %gate_upper.1.hidden_ref = f32[224,256]{1,0:T(8,128)S(1)} custom-call(bf16[64,16,512]{2,1,0:T(8,128)(2,1)S(1)} %all-to-all-done.4.own_ref, bf16[64,16,512]{2,1,0:T(8,128)(2,1)} %collective-permute-done.21.other_ref, bf16[112,4096]{1,0:T(8,128)(2,1)S(1)} %bitcast.16, bf16[112,4096]{1,0:T(8,128)(2,1)S(1)} %bitcast.18), custom_call_target="tpu_custom_call" | custom-call | flops 1 | bytes 1 | tf_op jit(solution)/shard_map/gate_upper/pallas_call | solution.py:583
  213.2 3.0 %ffn_grad.1 = (f32[128,4096]{1,0:T(8,128)S(1)}, bf16[128,4096]{1,0:T(8,128)(2,1)S(1)}) custom-call(bf16[64,16,512]{2,1,0:T(8,128)(2,1)S(1)} %all-to-all-done.3.own_ref, bf16[64,16,512]{2,1,0:T(8,128)(2,1)S(1)} %collective-permute-done.20.other_ref, bf16[112,4096]{1,0:T(8,128)(2,1)S(1)} %copy-done.5, f32[224,256]{1,0:T(8,128)S(1)} %gate_upper.1.hidden_ref, ...), custom_call_target="tpu_custom_call" | custom-call | flops 1 | bytes 1 | tf_op jit(solution)/shard_map/ffn_grad/pallas_call | solution.py:583
  216.8 2.3 collective-permute-done.22.refs_1_
  219.1 2.3 join.5
  221.4 4.7 %all-to-all-start.5 = ((bf16[64,16,512]{2,1,0:T(8,128)(2,1)}), bf16[64,16,512]{2,1,0:T(8,128)(2,1)S(1)}, u32[]{:S(2)}, u32[]{:S(2)}) async-start(bf16[64,16,512]{2,1,0:T(8,128)(2,1)} %join.5), calls=%async_computation.5 | async-start | bytes 2097152 | tf_op jit(solution)/shard_map/all_to_all | solution.py:50
  228.2 17.5 %all-to-all-done.5.blocks_ref = bf16[64,16,512]{2,1,0:T(8,128)(2,1)S(1)} async-done(((bf16[64,16,512]{2,1,0:T(8,128)(2,1)}), bf16[64,16,512]{2,1,0:T(8,128)(2,1)S(1)}, u32[]{:S(2)}, u32[]{:S(2)}) %all-to-all-start.5) | async-done | bytes 1048608 | tf_op jit(solution)/shard_map/all_to_all | solution.py:50
  (81 shorter events, 29.1 us)
Async XLA Ops:
  2.5 1.5 collective-permute-start
  4.9 4.6 %collective-permute-start.1 = (bf16[4,10240]{1,0:T(4,128)(2,1)S(1)}, bf16[4,10240]{1,0:T(4,128)(2,1)S(1)}, u32[]{:S(2)}, u32[]{:S(2)}) collective-permute-start(bf16[4,10240]{1,0:T(4,128)(2,1)S(1)} %pair.3.own_ref), channel_id=1, source_target_pairs={{0,1},{1,0},{8,9},{9,8},{2,3},{3,2},{10,11},{11,10},{4,5},{5,4},{1... | collective-permute-start | bytes 245768 | tf_op jit(solution)/shard_map/ppermute | solution.py:165
  9.5 6.9 %collective-permute-start.2 = (bf16[8,10240]{1,0:T(8,128)(2,1)S(1)}, bf16[8,10240]{1,0:T(8,128)(2,1)S(1)}, u32[]{:S(2)}, u32[]{:S(2)}) collective-permute-start(bf16[8,10240]{1,0:T(8,128)(2,1)S(1)} %pair.4.own_ref), channel_id=1, source_target_pairs={{0,9},{1,8},{8,1},{9,0},{2,11},{3,10},{10,3},{11,2},{4,13},{5,12},... | collective-permute-start | bytes 491528 | tf_op jit(solution)/shard_map/ppermute | solution.py:165
  16.5 8.0 %collective-permute-start.3 = (bf16[16,5120]{1,0:T(8,128)(2,1)S(1)}, bf16[16,5120]{1,0:T(8,128)(2,1)S(1)}, u32[]{:S(2)}, u32[]{:S(2)}) collective-permute-start(bf16[16,5120]{1,0:T(8,128)(2,1)S(1)} %get-tuple-element.46.refs_0_), channel_id=1, source_target_pairs={{0,2},{2,0},{4,6},{6,4},{1,3},{3,1},{5,7},{7,5},{8,10},{10,8},{12,... | collective-permute-start | bytes 491528 | tf_op jit(solution)/shard_map/ppermute | solution.py:165
  18.5 6.0 %collective-permute-start.4 = (bf16[16,5120]{1,0:T(8,128)(2,1)S(1)}, bf16[16,5120]{1,0:T(8,128)(2,1)S(1)}, u32[]{:S(2)}, u32[]{:S(2)}) collective-permute-start(bf16[16,5120]{1,0:T(8,128)(2,1)S(1)} %get-tuple-element.47.refs_2_), channel_id=1, source_target_pairs={{0,16},{16,0},{32,48},{48,32},{1,17},{17,1},{33,49},{49,33},{2,18}... | collective-permute-start | bytes 491528 | tf_op jit(solution)/shard_map/ppermute | solution.py:165
  24.3 20.0 %collective-permute-start.11 = (bf16[128,4096]{1,0:T(8,128)(2,1)S(1)}, bf16[128,4096]{1,0:T(8,128)(2,1)S(1)}, u32[]{:S(2)}, u32[]{:S(2)}) collective-permute-start(bf16[128,4096]{1,0:T(8,128)(2,1)S(1)} %get-tuple-element.53), channel_id=1, source_target_pairs={{0,64},{64,0},{1,65},{65,1},{2,66},{66,2},{3,67},{67,3},{4,68},{68... | collective-permute-start | bytes 3145736 | tf_op jit(solution)/shard_map/ppermute | solution.py:46
  25.9 11.4 %collective-permute-start.5 = (bf16[32,5120]{1,0:T(8,128)(2,1)S(1)}, bf16[32,5120]{1,0:T(8,128)(2,1)S(1)}, u32[]{:S(2)}, u32[]{:S(2)}) collective-permute-start(bf16[32,5120]{1,0:T(8,128)(2,1)S(1)} %get-tuple-element.48.refs_0_), channel_id=1, source_target_pairs={{0,6},{2,4},{4,2},{6,0},{1,7},{3,5},{5,3},{7,1},{8,14},{10,12},{12... | collective-permute-start | bytes 983048 | tf_op jit(solution)/shard_map/ppermute | solution.py:165
  28.5 11.0 %collective-permute-start.6 = (bf16[32,5120]{1,0:T(8,128)(2,1)S(1)}, bf16[32,5120]{1,0:T(8,128)(2,1)S(1)}, u32[]{:S(2)}, u32[]{:S(2)}) collective-permute-start(bf16[32,5120]{1,0:T(8,128)(2,1)S(1)} %get-tuple-element.49.refs_2_), channel_id=1, source_target_pairs={{0,48},{16,32},{32,16},{48,0},{1,49},{17,33},{33,17},{49,1},{2,50}... | collective-permute-start | bytes 983048 | tf_op jit(solution)/shard_map/ppermute | solution.py:165
  40.6 17.3 %collective-permute-start.10 = (bf16[64,5120]{1,0:T(8,128)(2,1)S(1)}, bf16[64,5120]{1,0:T(8,128)(2,1)S(1)}, u32[]{:S(2)}, u32[]{:S(2)}) collective-permute-start(bf16[64,5120]{1,0:T(8,128)(2,1)S(1)} %get-tuple-element.51.refs_0_), channel_id=1, source_target_pairs={{0,6},{2,4},{4,2},{6,0},{1,7},{3,5},{5,3},{7,1},{8,14},{10,12},{12... | collective-permute-start | bytes 1966088 | tf_op jit(solution)/shard_map/ppermute | solution.py:165
  41.4 16.5 %collective-permute-start.7 = (bf16[64,5120]{1,0:T(8,128)(2,1)S(1)}, bf16[64,5120]{1,0:T(8,128)(2,1)S(1)}, u32[]{:S(2)}, u32[]{:S(2)}) collective-permute-start(bf16[64,5120]{1,0:T(8,128)(2,1)S(1)} %get-tuple-element.50.refs_0_), channel_id=1, source_target_pairs={{0,16},{16,0},{32,48},{48,32},{1,17},{17,1},{33,49},{49,33},{2,18}... | collective-permute-start | bytes 1966088 | tf_op jit(solution)/shard_map/ppermute | solution.py:165
  41.5 16.9 %collective-permute-start.8 = (bf16[64,5120]{1,0:T(8,128)(2,1)S(1)}, bf16[64,5120]{1,0:T(8,128)(2,1)S(1)}, u32[]{:S(2)}, u32[]{:S(2)}) collective-permute-start(bf16[64,5120]{1,0:T(8,128)(2,1)S(1)} %get-tuple-element.50.refs_0_), channel_id=1, source_target_pairs={{0,48},{16,32},{32,16},{48,0},{1,49},{17,33},{33,17},{49,1},{2,50}... | collective-permute-start | bytes 1966088 | tf_op jit(solution)/shard_map/ppermute | solution.py:165
  44.2 15.5 %collective-permute-start.9 = (bf16[64,5120]{1,0:T(8,128)(2,1)S(1)}, bf16[64,5120]{1,0:T(8,128)(2,1)S(1)}, u32[]{:S(2)}, u32[]{:S(2)}) collective-permute-start(bf16[64,5120]{1,0:T(8,128)(2,1)S(1)} %get-tuple-element.51.refs_0_), channel_id=1, source_target_pairs={{0,2},{2,0},{4,6},{6,4},{1,3},{3,1},{5,7},{7,5},{8,10},{10,8},{12,... | collective-permute-start | bytes 1966088 | tf_op jit(solution)/shard_map/ppermute | solution.py:165
  60.2 8.9 %collective-permute-start.12 = (bf16[32,5120]{1,0:T(8,128)(2,1)S(1)}, bf16[32,5120]{1,0:T(8,128)(2,1)S(1)}, u32[]{:S(2)}, u32[]{:S(2)}) collective-permute-start(bf16[32,5120]{1,0:T(8,128)(2,1)S(1)} %get-tuple-element.58), channel_id=1, source_target_pairs={{0,48},{16,32},{32,16},{48,0},{1,49},{17,33},{33,17},{49,1},{2,50}... | collective-permute-start | bytes 983048 | tf_op jit(solution)/shard_map/ppermute | solution.py:165
  61.8 7.6 %collective-permute-start.13 = (bf16[32,5120]{1,0:T(8,128)(2,1)S(1)}, bf16[32,5120]{1,0:T(8,128)(2,1)S(1)}, u32[]{:S(2)}, u32[]{:S(2)}) collective-permute-start(bf16[32,5120]{1,0:T(8,128)(2,1)S(1)} %get-tuple-element.59), channel_id=1, source_target_pairs={{0,16},{16,0},{32,48},{48,32},{1,17},{17,1},{33,49},{49,33},{2,18}... | collective-permute-start | bytes 983048 | tf_op jit(solution)/shard_map/ppermute | solution.py:165
  61.8 8.8 %collective-permute-start.14 = (bf16[32,5120]{1,0:T(8,128)(2,1)S(1)}, bf16[32,5120]{1,0:T(8,128)(2,1)S(1)}, u32[]{:S(2)}, u32[]{:S(2)}) collective-permute-start(bf16[32,5120]{1,0:T(8,128)(2,1)S(1)} %get-tuple-element.60), channel_id=1, source_target_pairs={{0,6},{2,4},{4,2},{6,0},{1,7},{3,5},{5,3},{7,1},{8,14},{10,12},{12... | collective-permute-start | bytes 983048 | tf_op jit(solution)/shard_map/ppermute | solution.py:165
  63.7 7.1 %collective-permute-start.15 = (bf16[32,5120]{1,0:T(8,128)(2,1)S(1)}, bf16[32,5120]{1,0:T(8,128)(2,1)S(1)}, u32[]{:S(2)}, u32[]{:S(2)}) collective-permute-start(bf16[32,5120]{1,0:T(8,128)(2,1)S(1)} %get-tuple-element.61), channel_id=1, source_target_pairs={{0,2},{2,0},{4,6},{6,4},{1,3},{3,1},{5,7},{7,5},{8,10},{10,8},{12,... | collective-permute-start | bytes 983048 | tf_op jit(solution)/shard_map/ppermute | solution.py:165
  71.7 10.0 %collective-permute-start.17 = (bf16[256,5120]{1,0:T(8,128)(2,1)S(1)}, bf16[256,5120]{1,0:T(8,128)(2,1)}, u32[]{:S(2)}, u32[]{:S(2)}) collective-permute-start(bf16[256,5120]{1,0:T(8,128)(2,1)S(1)} %whole.3.refs_1_), channel_id=1, source_target_pairs={{0,64},{64,0},{1,65},{65,1},{2,66},{66,2},{3,67},{67,3},{4,68},{68... | collective-permute-start | bytes 7864328 | tf_op jit(solution)/shard_map/ppermute | solution.py:46
  73.2 8.5 %collective-permute-start.16 = (bf16[256,5120]{1,0:T(8,128)(2,1)S(1)}, bf16[256,5120]{1,0:T(8,128)(2,1)S(1)}, u32[]{:S(2)}, u32[]{:S(2)}) collective-permute-start(bf16[256,5120]{1,0:T(8,128)(2,1)S(1)} %whole.2.refs_0_), channel_id=1, source_target_pairs={{0,64},{64,0},{1,65},{65,1},{2,66},{66,2},{3,67},{67,3},{4,68},{68... | collective-permute-start | bytes 7864328 | tf_op jit(solution)/shard_map/ppermute | solution.py:46
  81.7 19.4 %copy-start.11 = (f32[256]{0:T(256)S(1)}, f32[256]{0:T(256)}, u32[]{:S(2)}) copy-start(f32[256]{0:T(256)} %param.23) | copy-start | bytes 3076
  90.5 1.2 collective-permute-start.18
  92.5 19.6 %all-to-all-start = ((f32[64,8,128]{2,1,0:T(8,128)}), f32[64,8,128]{2,1,0:T(8,128)S(1)}, u32[]{:S(2)}, u32[]{:S(2)}) async-start(f32[64,8,128]{2,1,0:T(8,128)} %chip_stats.1), calls=%async_computation | async-start | bytes 524288 | tf_op jit(solution)/shard_map/all_to_all | solution.py:50
  112.1 27.5 %copy-start.8 = (bf16[4096]{0:T(1024)(128)(2,1)S(1)}, bf16[4096]{0:T(1024)(128)(2,1)}, u32[]{:S(2)}) copy-start(bf16[4096]{0:T(1024)(128)(2,1)} %param.19) | copy-start | bytes 24580
  115.5 25.4 %collective-permute-start.19 = (bf16[128,4096]{1,0:T(8,128)(2,1)S(1)}, bf16[128,4096]{1,0:T(8,128)(2,1)S(1)}, u32[]{:S(2)}, u32[]{:S(2)}) collective-permute-start(bf16[128,4096]{1,0:T(8,128)(2,1)S(1)} %get-tuple-element.76), channel_id=1, source_target_pairs={{0,64},{64,0},{1,65},{65,1},{2,66},{66,2},{3,67},{67,3},{4,68},{68... | collective-permute-start | bytes 3145736 | tf_op jit(solution)/shard_map/ppermute | solution.py:46
  142.2 27.3 %copy-start.6 = (bf16[2,4096]{1,0:T(2,128)(2,1)S(1)}, bf16[2,4096]{1,0:T(2,128)(2,1)}, u32[]{:S(2)}) copy-start(bf16[2,4096]{1,0:T(2,128)(2,1)} %states_ref.1) | copy-start | bytes 49156
  142.2 27.3 %copy-start.9 = (bf16[4096]{0:T(1024)(128)(2,1)S(1)}, bf16[4096]{0:T(1024)(128)(2,1)}, u32[]{:S(2)}) copy-start(bf16[4096]{0:T(1024)(128)(2,1)} %param.16) | copy-start | bytes 24580
  164.7 44.3 %copy-start.1 = (bf16[4096,112]{0,1:T(8,128)(2,1)S(1)}, bf16[4096,112]{0,1:T(8,128)(2,1)}, u32[]{:S(2)}) copy-start(bf16[4096,112]{0,1:T(8,128)(2,1)} %param.20) | copy-start | bytes 2752516
  164.7 22.4 %all-to-all-start.4 = ((bf16[64,16,512]{2,1,0:T(8,128)(2,1)}), bf16[64,16,512]{2,1,0:T(8,128)(2,1)S(1)}, u32[]{:S(2)}, u32[]{:S(2)}) async-start(bf16[64,16,512]{2,1,0:T(8,128)(2,1)} %copy-done.3), calls=%async_computation.4 | async-start | bytes 2097152 | tf_op jit(solution)/shard_map/all_to_all | solution.py:50
  187.0 21.9 %all-to-all-start.3 = ((bf16[64,16,512]{2,1,0:T(8,128)(2,1)}), bf16[64,16,512]{2,1,0:T(8,128)(2,1)S(1)}, u32[]{:S(2)}, u32[]{:S(2)}) async-start(bf16[64,16,512]{2,1,0:T(8,128)(2,1)} %copy-done.4), calls=%async_computation.3 | async-start | bytes 2097152 | tf_op jit(solution)/shard_map/all_to_all | solution.py:50
  191.7 17.3 %collective-permute-start.21 = (bf16[64,16,512]{2,1,0:T(8,128)(2,1)S(1)}, bf16[64,16,512]{2,1,0:T(8,128)(2,1)}, u32[]{:S(2)}, u32[]{:S(2)}) collective-permute-start(bf16[64,16,512]{2,1,0:T(8,128)(2,1)S(1)} %all-to-all-done.4.own_ref), channel_id=1, source_target_pairs={{0,64},{64,0},{1,65},{65,1},{2,66},{66,2},{3,67},{67,3},{4,68},{68... | collective-permute-start | bytes 3145736 | tf_op jit(solution)/shard_map/ppermute | solution.py:46
  209.0 4.2 %collective-permute-start.20 = (bf16[64,16,512]{2,1,0:T(8,128)(2,1)S(1)}, bf16[64,16,512]{2,1,0:T(8,128)(2,1)S(1)}, u32[]{:S(2)}, u32[]{:S(2)}) collective-permute-start(bf16[64,16,512]{2,1,0:T(8,128)(2,1)S(1)} %all-to-all-done.3.own_ref), channel_id=1, source_target_pairs={{0,64},{64,0},{1,65},{65,1},{2,66},{66,2},{3,67},{67,3},{4,68},{68... | collective-permute-start | bytes 3145736 | tf_op jit(solution)/shard_map/ppermute | solution.py:46
  216.2 2.9 %collective-permute-start.22 = (bf16[128,4096]{1,0:T(8,128)(2,1)S(1)}, bf16[128,4096]{1,0:T(8,128)(2,1)S(1)}, u32[]{:S(2)}, u32[]{:S(2)}) collective-permute-start(bf16[128,4096]{1,0:T(8,128)(2,1)S(1)} %get-tuple-element.83), channel_id=1, source_target_pairs={{0,64},{64,0},{1,65},{65,1},{2,66},{66,2},{3,67},{67,3},{4,68},{68... | collective-permute-start | bytes 3145736 | tf_op jit(solution)/shard_map/ppermute | solution.py:46
  221.4 24.3 %all-to-all-start.5 = ((bf16[64,16,512]{2,1,0:T(8,128)(2,1)}), bf16[64,16,512]{2,1,0:T(8,128)(2,1)S(1)}, u32[]{:S(2)}, u32[]{:S(2)}) async-start(bf16[64,16,512]{2,1,0:T(8,128)(2,1)} %join.5), calls=%async_computation.5 | async-start | bytes 2097152 | tf_op jit(solution)/shard_map/all_to_all | solution.py:50
  (7 other events, 9.2 us)

commit v6 on v5

--- a/solution.py
+++ b/solution.py
@@ -636,16 +636,19 @@
     )(own_core, teacher_states, teacher_gain, student_states, student_gain)
     (rows,) = in_pair(own_core, keep, swap_cores(send), (width,))
 
+    place = jnp.stack([core, device]).astype(jnp.int32)
+    own, send = pick_part(place, token_ids.reshape(1, 256), student_head_t)
     (rows,) = in_pair((y & 1).reshape(1), rows, along(rows, ("yh", "yl"), 1), (width,))
-    first, second = in_pair((y >> 1).reshape(1), rows, along(rows, ("yh", "yl"), 3), WIDTHS)
+    came = along(rows, ("yh", "yl"), 3)
+    came, picked = lax.optimization_barrier((came, join_part(own, swap_cores(send))))
+    picked = exchange(picked, CHIPS)
+    first, second = in_pair((y >> 1).reshape(1), rows, came, WIDTHS)
     for bit, mask in ((0, 1), (1, 3)):
         came = (along(first, "z", mask), along(second, "x", mask))
         bits = (jnp.stack([z, x]) >> bit) & 1
         first, second = in_pairs(bits, (first, came[0], second, came[1]))
     came = [along(first, "x", 1), along(first, "x", 3), along(second, "z", 1), along(second, "z", 3)]
-    place = jnp.stack([core, device]).astype(jnp.int32)
-    own, send = pick_part(place, token_ids.reshape(1, 256), student_head_t)
-    came, picked = lax.optimization_barrier((came, join_part(own, swap_cores(send))))
+    came, picked = lax.optimization_barrier((came, picked))
     halves = halves_of(came)
     far = [
         along(half, line, mask)
@@ -656,6 +659,15 @@
         whole_rows(x.reshape(1), [first] + came[:2] + far[:2]),
         whole_rows(z.reshape(1), [second] + came[2:] + far[2:]),
     )
+    embedded, ffn_rows = kernel_call(
+        embed_kernel,
+        "embed",
+        [shape_of(BLOCK, jnp.float32), shape_of(picked.shape)],
+        in_specs=[VMEM] * 2,
+        out_specs=[VMEM] * 2,
+    )(picked, ffn_gain)
+    rows, ffn_rows = lax.optimization_barrier((rows, ffn_rows))
+    ffn_rows = exchange(ffn_rows, CHIPS)
     others = tuple(swap_cores(part) for part in rows)
     sums = logits_part(own_core, rows, heads)
     student, teacher, stats = logits_part(1 - own_core, others, heads, sums)
@@ -667,26 +679,19 @@
         in_specs=[VMEM] * 2,
         out_specs=VMEM,
     )(stats, swap_cores(stats))
-    stats, picked = lax.optimization_barrier((stats, picked))
     every = exchange(stats, CHIPS)
-    picked = exchange(picked, CHIPS)
 
     weight = token_weight.reshape(2, 4, 2, 4, 2, 2).transpose(1, 3, 2, 4, 0, 5).reshape(1, 256)
     own, send, divergence = row_grad_part(
         own_core, every, weight, teacher, student, student_head_t
     )
     divergence = divergence.reshape(4, 4, 2, 2, 2, 2).transpose(4, 0, 2, 1, 3, 5).reshape(256)
-    embedded, ffn_rows = kernel_call(
-        embed_kernel,
-        "embed",
-        [shape_of(BLOCK, jnp.float32), shape_of(picked.shape)],
-        in_specs=[VMEM] * 2,
-        out_specs=[VMEM] * 2,
-    )(picked, ffn_gain)
     blocks = join_part(own, swap_cores(send))
-    blocks, ffn_rows = lax.optimization_barrier((blocks, ffn_rows))
+    (hidden,) = ffn_part(
+        gate_kernel, "gate_upper", [shape_of((224, 256), jnp.float32)], ffn_rows, gate_t, up_t
+    )
+    blocks, hidden = lax.optimization_barrier((blocks, hidden))
     blocks = exchange(blocks, CHIPS)
-    ffn_rows = exchange(ffn_rows, CHIPS)
     final_grad, blocks = kernel_call(
         final_kernel,
         "final",
@@ -696,9 +701,6 @@
         scratch_shapes=[pltpu.VMEM(BLOCK, jnp.float32)],
     )(blocks, student_states, student_gain)
     blocks = exchange(blocks, CHIPS)
-    (hidden,) = ffn_part(
-        gate_kernel, "gate_upper", [shape_of((224, 256), jnp.float32)], ffn_rows, gate_t, up_t
-    )
     shape = (128, 4096)
     own, send = ffn_part(
         ffn_grad_kernel,

time: 248 us -> 275 us (1.11)
  Pallas kernels: 44 us -> 87.8 us
  waiting for transfers between devices: 103 us -> 74.9 us
  starting transfers between devices: 44.6 us -> 58.5 us
    pallas_call x2, Pallas kernels: 1.79 us -> 42.1 us  [whole_rows(): kernel_call(whole_kernel, 'whole', shape_of((4 * tokens, width)), limit=2...]
    all_to_all x4, waiting for transfers between devices: 61.4 us -> 27.7 us  [exchange(): return lax.all_to_all(blocks, axes, split_axis=0, concat_axis=0, tiled=True)]
    all_to_all x4, starting transfers between devices: 22.7 us -> 33.6 us  [exchange(): return lax.all_to_all(blocks, axes, split_axis=0, concat_axis=0, tiled=True)]
    ppermute x14, waiting for transfers between devices: 36.7 us -> 39.8 us  [along(): return lax.ppermute(block, line, [(i, i ^ mask) for i in range(4)])]
    ppermute x9, waiting for transfers between devices: 4.61 us -> 7.43 us  [swap_cores(): return lax.ppermute(values, 'core', [(0, 1), (1, 0)])]
    ppermute x14, starting transfers between devices: 20.2 us -> 23 us  [along(): return lax.ppermute(block, line, [(i, i ^ mask) for i in range(4)])]
  transfers between devices with their start and end apart: 27 -> 27, of which waited for: 18 -> 15; matrix products, arithmetic and copies ran while one was open for 1% -> 1% of each run, Pallas kernels for 8% -> 12%
where the time goes in v6:
time: 275 us; the launch traced here: 274 us
  Pallas kernels  87.8 us (32%)
  waiting for transfers between devices  74.9 us (27%)
  starting transfers between devices  58.5 us (21%)
  blocking collectives  46.6 us (17%)
  local copies, waits for them, and re-layouts  4.46 us (2%)
    all_to_all x2, blocking collectives, exchange(): return lax.all_to_all(blocks, axes, split_axis=0, concat_axis=0, tiled=True)  46.6 us
    pallas_call x2, Pallas kernels, whole_rows(): kernel_call(whole_kernel, 'whole', shape_of((4 * tokens, width)), limit=2...  42.1 us
    ppermute x14, waiting for transfers between devices, along(): return lax.ppermute(block, line, [(i, i ^ mask) for i in range(4)])  39.8 us
    all_to_all x4, starting transfers between devices, exchange(): return lax.all_to_all(blocks, axes, split_axis=0, concat_axis=0, tiled=True)  33.6 us
    all_to_all x4, waiting for transfers between devices, exchange(): return lax.all_to_all(blocks, axes, split_axis=0, concat_axis=0, tiled=True)  27.7 us
    ppermute x14, starting transfers between devices, along(): return lax.ppermute(block, line, [(i, i ^ mask) for i in range(4)])  23 us
    pallas_call x2, Pallas kernels, logits_part(): kernel_call(functools.partial(logits_kernel, last), 'logits', out_shape,...  18.1 us
    ppermute x9, waiting for transfers between devices, swap_cores(): return lax.ppermute(values, 'core', [(0, 1), (1, 0)])  7.43 us
  transfers between devices with their start and end apart: 27, of which 15 were waited for; matrix products, arithmetic and copies ran while one was open for 1% of the time, Pallas kernels for 12%

profile of v6, /device:TPU:0, one launch (start us, length us, event | category | flops | bytes accessed | tf_op | source)
XLA Modules:
  0.0 274.3 jit_solution(13146931409498240684)
XLA Ops:
  1.4 3.6 %pick.1 = (bf16[128,4096]{1,0:T(8,128)(2,1)S(1)}, bf16[128,4096]{1,0:T(8,128)(2,1)S(1)}) custom-call(s32[2]{0:T(128)S(1)} %pad_add_fusion.1.place_ref, s32[1,256]{1,0:T(1,128)S(1)} %bitcast.24, bf16[501,4096]{1,0:T(8,128)(2,1)} %bitcast.27), custom_call_target="tpu_custom_call" | custom-call | flops 1 | bytes 1 | tf_op jit(solution)/shard_map/pick/pallas_call | solution.py:408
  5.1 1.9 rows.1
  11.2 3.0 %collective-permute-done.1.came_ref = bf16[4,10240]{1,0:T(4,128)(2,1)S(1)} collective-permute-done((bf16[4,10240]{1,0:T(4,128)(2,1)S(1)}, bf16[4,10240]{1,0:T(4,128)(2,1)S(1)}, u32[]{:S(2)}, u32[]{:S(2)}) %collective-permute-start.1) | collective-permute-done | bytes 81952 | tf_op jit(solution)/shard_map/ppermute | solution.py:165
  14.3 3.2 %collective-permute-start.2 = (bf16[8,10240]{1,0:T(8,128)(2,1)S(1)}, bf16[8,10240]{1,0:T(8,128)(2,1)S(1)}, u32[]{:S(2)}, u32[]{:S(2)}) collective-permute-start(bf16[8,10240]{1,0:T(8,128)(2,1)S(1)} %pair.4.own_ref), channel_id=1, source_target_pairs={{0,9},{1,8},{8,1},{9,0},{2,11},{3,10},{10,3},{11,2},{4,13},{5,12},... | collective-permute-start | bytes 491528 | tf_op jit(solution)/shard_map/ppermute | solution.py:165
  17.5 2.3 join.3
  21.5 2.0 collective-permute-start.4
  24.9 10.4 %all-to-all-start = ((bf16[64,16,512]{2,1,0:T(8,128)(2,1)}), bf16[64,16,512]{2,1,0:T(8,128)(2,1)S(1)}, u32[]{:S(2)}, u32[]{:S(2)}) async-start(bf16[64,16,512]{2,1,0:T(8,128)(2,1)} %join.3), calls=%async_computation | async-start | bytes 2097152 | tf_op jit(solution)/shard_map/all_to_all | solution.py:50
  36.9 2.9 %collective-permute-start.6 = (bf16[32,5120]{1,0:T(8,128)(2,1)S(1)}, bf16[32,5120]{1,0:T(8,128)(2,1)S(1)}, u32[]{:S(2)}, u32[]{:S(2)}) collective-permute-start(bf16[32,5120]{1,0:T(8,128)(2,1)S(1)} %get-tuple-element.54.refs_0_), channel_id=1, source_target_pairs={{0,6},{2,4},{4,2},{6,0},{1,7},{3,5},{5,3},{7,1},{8,14},{10,12},{12... | collective-permute-start | bytes 983048 | tf_op jit(solution)/shard_map/ppermute | solution.py:165
  39.8 2.9 %collective-permute-start.7 = (bf16[32,5120]{1,0:T(8,128)(2,1)S(1)}, bf16[32,5120]{1,0:T(8,128)(2,1)S(1)}, u32[]{:S(2)}, u32[]{:S(2)}) collective-permute-start(bf16[32,5120]{1,0:T(8,128)(2,1)S(1)} %get-tuple-element.55.refs_2_), channel_id=1, source_target_pairs={{0,48},{16,32},{32,16},{48,0},{1,49},{17,33},{33,17},{49,1},{2,50}... | collective-permute-start | bytes 983048 | tf_op jit(solution)/shard_map/ppermute | solution.py:165
  42.8 13.5 %collective-permute-done.6.refs_1_ = bf16[32,5120]{1,0:T(8,128)(2,1)S(1)} collective-permute-done((bf16[32,5120]{1,0:T(8,128)(2,1)S(1)}, bf16[32,5120]{1,0:T(8,128)(2,1)S(1)}, u32[]{:S(2)}, u32[]{:S(2)}) %collective-permute-start.6) | collective-permute-done | bytes 327712 | tf_op jit(solution)/shard_map/ppermute | solution.py:165
  58.0 2.1 collective-permute-start.11
  61.0 1.8 collective-permute-start.9
  62.8 11.5 %collective-permute-done.10.refs_2_.refs_1_ = bf16[64,5120]{1,0:T(8,128)(2,1)S(1)} collective-permute-done((bf16[64,5120]{1,0:T(8,128)(2,1)}, bf16[64,5120]{1,0:T(8,128)(2,1)S(1)}, u32[]{:S(2)}, u32[]{:S(2)}) %collective-permute-start.10) | collective-permute-done | bytes 655392 | tf_op jit(solution)/shard_map/ppermute | solution.py:165
  75.6 2.6 collective-permute-done.9.refs_1_.refs_2_
  81.0 1.8 collective-permute-start.14
  83.6 4.9 %collective-permute-done.12.refs_3_ = bf16[32,5120]{1,0:T(8,128)(2,1)S(1)} collective-permute-done((bf16[32,5120]{1,0:T(8,128)(2,1)S(1)}, bf16[32,5120]{1,0:T(8,128)(2,1)S(1)}, u32[]{:S(2)}, u32[]{:S(2)}) %collective-permute-start.12) | collective-permute-done | bytes 327712 | tf_op jit(solution)/shard_map/ppermute | solution.py:165
  92.3 40.9 %whole.2.refs_0_ = bf16[256,5120]{1,0:T(8,128)(2,1)} custom-call(s32[1]{0:T(128)} %bitcast.1.place_ref, bf16[64,5120]{1,0:T(8,128)(2,1)} %get-tuple-element.56.refs_0_, bf16[64,5120]{1,0:T(8,128)(2,1)S(1)} %copy-done.4, bf16[64,5120]{1,0:T(8,128)(2,1)} %collective-permute-done.9.refs_1_.refs_2_, bf16[32,5120]{1,0:T(8,128)(2,1)S(1)} %collective-permute-done.12.refs_3_, ...), custom_call_target="tpu_custom_call" | custom-call | flops 1 | bytes 1 | tf_op jit(solution)/shard_map/whole/pallas_call | solution.py:185
  133.7 8.5 %all-to-all-start.2 = ((bf16[64,16,512]{2,1,0:T(8,128)(2,1)}), bf16[64,16,512]{2,1,0:T(8,128)(2,1)}, u32[]{:S(2)}, u32[]{:S(2)}) async-start(bf16[64,16,512]{2,1,0:T(8,128)(2,1)} %copy-done.7), calls=%async_computation.2 | async-start | bytes 2097152 | tf_op jit(solution)/shard_map/all_to_all | solution.py:50
  142.2 8.7 %logits.2 = (f32[501,256]{1,0:T(8,128)S(1)}, f32[501,256]{1,0:T(8,128)S(1)}, f32[501,256]{1,0:T(8,128)S(1)}) custom-call(s32[1]{0:T(128)} %bitcast.core_ref.place_ref, bf16[256,5120]{1,0:T(8,128)(2,1)} %whole.2.refs_0_, bf16[256,5120]{1,0:T(8,128)(2,1)} %copy-done, bf16[501,4096]{1,0:T(8,128)(2,1)} %bitcast.28, bf16[501,16384]{1,0:T(8,128)(2,1)} %bitcast.25), custom_call_target="tpu_custom_call" | custom-call | flops 1 | bytes 1 | tf_op jit(solution)/shard_map/logits/pallas_call | solution.py:290
  151.0 9.4 %logits.3 = (f32[501,256]{1,0:T(8,128)S(1)}, f32[501,256]{1,0:T(8,128)S(1)}, f32[8,128]{1,0:T(8,128)S(1)}) custom-call(s32[1]{0:T(128)S(6)} %sub.3.place_ref, bf16[256,5120]{1,0:T(8,128)(2,1)} %collective-permute-done.16.refs_0_, bf16[256,5120]{1,0:T(8,128)(2,1)} %collective-permute-done.17.refs_1_, bf16[501,4096]{1,0:T(8,128)(2,1)} %bitcast.29, ...), custom_call_target="tpu_custom_call" | custom-call | flops 1 | bytes 1 | tf_op jit(solution)/shard_map/logits/pallas_call | solution.py:290
  162.3 10.1 %all-to-all-start.1 = ((f32[64,8,128]{2,1,0:T(8,128)}), f32[64,8,128]{2,1,0:T(8,128)S(1)}, u32[]{:S(2)}, u32[]{:S(2)}) async-start(f32[64,8,128]{2,1,0:T(8,128)} %chip_stats.1), calls=%async_computation.1 | async-start | bytes 524288 | tf_op jit(solution)/shard_map/all_to_all | solution.py:50
  172.9 10.4 %all-to-all-done.1.every_ref = f32[64,8,128]{2,1,0:T(8,128)S(1)} async-done(((f32[64,8,128]{2,1,0:T(8,128)}), f32[64,8,128]{2,1,0:T(8,128)S(1)}, u32[]{:S(2)}, u32[]{:S(2)}) %all-to-all-start.1) | async-done | bytes 262176 | tf_op jit(solution)/shard_map/all_to_all | solution.py:50
  183.3 3.6 %row_grad.1 = (f32[128,4096]{1,0:T(8,128)S(1)}, bf16[128,4096]{1,0:T(8,128)(2,1)S(1)}, f32[1,256]{1,0:T(1,128)S(1)}) custom-call(s32[1]{0:T(128)} %bitcast.core_ref.place_ref, f32[64,8,128]{2,1,0:T(8,128)S(1)} %all-to-all-done.1.every_ref, f32[1,256]{1,0:T(1,128)S(1)} %reshape.46.weight_ref, f32[501,256]{1,0:T(8,128)S(1)} %get-tuple-element.79.teacher_ref, ...), custom_call_target="tpu_custom_call" | custom-call | flops 1 | bytes 1 | tf_op jit(solution)/shard_map/row_grad/pallas_call | solution.py:369
  187.2 3.0 %gate_upper.1.hidden_ref = f32[224,256]{1,0:T(8,128)S(1)} custom-call(bf16[64,16,512]{2,1,0:T(8,128)(2,1)} %all-to-all-done.2.own_ref, bf16[64,16,512]{2,1,0:T(8,128)(2,1)S(1)} %collective-permute-done.20.other_ref, bf16[112,4096]{1,0:T(8,128)(2,1)S(1)} %bitcast.16, bf16[112,4096]{1,0:T(8,128)(2,1)S(1)} %bitcast.18), custom_call_target="tpu_custom_call" | custom-call | flops 1 | bytes 1 | tf_op jit(solution)/shard_map/gate_upper/pallas_call | solution.py:583
  191.6 24.1 %all_to_all.30.blocks_ref = bf16[64,16,512]{2,1,0:T(8,128)(2,1)S(1)} all-to-all(bf16[64,16,512]{2,1,0:T(8,128)(2,1)S(1)} %join.4), channel_id=1, replica_groups=mesh['core'=2,'x'=4,'yh'=2,'z'=4,'yl'=2] {'x','yh','z','yl'}, dimensions={0} | all-to-all | bytes 2097152 | tf_op jit(solution)/shard_map/all_to_all | solution.py:50
  216.1 22.5 %all_to_all.31.own_ref = bf16[64,16,512]{2,1,0:T(8,128)(2,1)S(1)} all-to-all(bf16[64,16,512]{2,1,0:T(8,128)(2,1)S(1)} %get-tuple-element.86), channel_id=1, replica_groups=mesh['core'=2,'x'=4,'yh'=2,'z'=4,'yl'=2] {'x','yh','z','yl'}, dimensions={0} | all-to-all | bytes 2097152 | tf_op jit(solution)/shard_map/all_to_all | solution.py:50
  238.5 2.7 collective-permute-done.21.other_ref
  241.2 3.0 %ffn_grad.1 = (f32[128,4096]{1,0:T(8,128)S(1)}, bf16[128,4096]{1,0:T(8,128)(2,1)S(1)}) custom-call(bf16[64,16,512]{2,1,0:T(8,128)(2,1)S(1)} %all_to_all.31.own_ref, bf16[64,16,512]{2,1,0:T(8,128)(2,1)S(1)} %collective-permute-done.21.other_ref, bf16[112,4096]{1,0:T(8,128)(2,1)S(1)} %copy-done.8, f32[224,256]{1,0:T(8,128)S(1)} %gate_upper.1.hidden_ref, ...), custom_call_target="tpu_custom_call" | custom-call | flops 1 | bytes 1 | tf_op jit(solution)/shard_map/ffn_grad/pallas_call | solution.py:583
  244.5 2.5 collective-permute-done.22.refs_1_
  247.0 2.3 join.5
  249.3 4.7 %all-to-all-start.5 = ((bf16[64,16,512]{2,1,0:T(8,128)(2,1)}), bf16[64,16,512]{2,1,0:T(8,128)(2,1)S(1)}, u32[]{:S(2)}, u32[]{:S(2)}) async-start(bf16[64,16,512]{2,1,0:T(8,128)(2,1)} %join.5), calls=%async_computation.5 | async-start | bytes 2097152 | tf_op jit(solution)/shard_map/all_to_all | solution.py:50
  256.0 17.3 %all-to-all-done.5.blocks_ref = bf16[64,16,512]{2,1,0:T(8,128)(2,1)S(1)} async-done(((bf16[64,16,512]{2,1,0:T(8,128)(2,1)}), bf16[64,16,512]{2,1,0:T(8,128)(2,1)S(1)}, u32[]{:S(2)}, u32[]{:S(2)}) %all-to-all-start.5) | async-done | bytes 1048608 | tf_op jit(solution)/shard_map/all_to_all | solution.py:50
  (87 shorter events, 29.5 us)
Async XLA Ops:
  5.0 12.5 %collective-permute-start.3 = (bf16[128,4096]{1,0:T(8,128)(2,1)S(1)}, bf16[128,4096]{1,0:T(8,128)(2,1)S(1)}, u32[]{:S(2)}, u32[]{:S(2)}) collective-permute-start(bf16[128,4096]{1,0:T(8,128)(2,1)S(1)} %get-tuple-element.50), channel_id=1, source_target_pairs={{0,64},{64,0},{1,65},{65,1},{2,66},{66,2},{3,67},{67,3},{4,68},{68... | collective-permute-start | bytes 3145736 | tf_op jit(solution)/shard_map/ppermute | solution.py:46
  7.0 1.7 collective-permute-start
  9.5 4.8 %collective-permute-start.1 = (bf16[4,10240]{1,0:T(4,128)(2,1)S(1)}, bf16[4,10240]{1,0:T(4,128)(2,1)S(1)}, u32[]{:S(2)}, u32[]{:S(2)}) collective-permute-start(bf16[4,10240]{1,0:T(4,128)(2,1)S(1)} %pair.3.own_ref), channel_id=1, source_target_pairs={{0,1},{1,0},{8,9},{9,8},{2,3},{3,2},{10,11},{11,10},{4,5},{5,4},{1... | collective-permute-start | bytes 245768 | tf_op jit(solution)/shard_map/ppermute | solution.py:165
  14.3 7.1 %collective-permute-start.2 = (bf16[8,10240]{1,0:T(8,128)(2,1)S(1)}, bf16[8,10240]{1,0:T(8,128)(2,1)S(1)}, u32[]{:S(2)}, u32[]{:S(2)}) collective-permute-start(bf16[8,10240]{1,0:T(8,128)(2,1)S(1)} %pair.4.own_ref), channel_id=1, source_target_pairs={{0,9},{1,8},{8,1},{9,0},{2,11},{3,10},{10,3},{11,2},{4,13},{5,12},... | collective-permute-start | bytes 491528 | tf_op jit(solution)/shard_map/ppermute | solution.py:165
  21.5 14.0 %collective-permute-start.4 = (bf16[16,5120]{1,0:T(8,128)(2,1)S(1)}, bf16[16,5120]{1,0:T(8,128)(2,1)S(1)}, u32[]{:S(2)}, u32[]{:S(2)}) collective-permute-start(bf16[16,5120]{1,0:T(8,128)(2,1)S(1)} %get-tuple-element.52.refs_0_), channel_id=1, source_target_pairs={{0,2},{2,0},{4,6},{6,4},{1,3},{3,1},{5,7},{7,5},{8,10},{10,8},{12,... | collective-permute-start | bytes 491528 | tf_op jit(solution)/shard_map/ppermute | solution.py:165
  23.5 12.0 %collective-permute-start.5 = (bf16[16,5120]{1,0:T(8,128)(2,1)S(1)}, bf16[16,5120]{1,0:T(8,128)(2,1)S(1)}, u32[]{:S(2)}, u32[]{:S(2)}) collective-permute-start(bf16[16,5120]{1,0:T(8,128)(2,1)S(1)} %get-tuple-element.53.refs_2_), channel_id=1, source_target_pairs={{0,16},{16,0},{32,48},{48,32},{1,17},{17,1},{33,49},{49,33},{2,18}... | collective-permute-start | bytes 491528 | tf_op jit(solution)/shard_map/ppermute | solution.py:165
  24.9 37.9 %all-to-all-start = ((bf16[64,16,512]{2,1,0:T(8,128)(2,1)}), bf16[64,16,512]{2,1,0:T(8,128)(2,1)S(1)}, u32[]{:S(2)}, u32[]{:S(2)}) async-start(bf16[64,16,512]{2,1,0:T(8,128)(2,1)} %join.3), calls=%async_computation | async-start | bytes 2097152 | tf_op jit(solution)/shard_map/all_to_all | solution.py:50
  35.4 47.9 %copy-start.11 = (bf16[4096]{0:T(1024)(128)(2,1)S(1)}, bf16[4096]{0:T(1024)(128)(2,1)}, u32[]{:S(2)}) copy-start(bf16[4096]{0:T(1024)(128)(2,1)} %param.19) | copy-start | bytes 24580
  36.9 19.3 %collective-permute-start.6 = (bf16[32,5120]{1,0:T(8,128)(2,1)S(1)}, bf16[32,5120]{1,0:T(8,128)(2,1)S(1)}, u32[]{:S(2)}, u32[]{:S(2)}) collective-permute-start(bf16[32,5120]{1,0:T(8,128)(2,1)S(1)} %get-tuple-element.54.refs_0_), channel_id=1, source_target_pairs={{0,6},{2,4},{4,2},{6,0},{1,7},{3,5},{5,3},{7,1},{8,14},{10,12},{12... | collective-permute-start | bytes 983048 | tf_op jit(solution)/shard_map/ppermute | solution.py:165
  39.8 16.5 %collective-permute-start.7 = (bf16[32,5120]{1,0:T(8,128)(2,1)S(1)}, bf16[32,5120]{1,0:T(8,128)(2,1)S(1)}, u32[]{:S(2)}, u32[]{:S(2)}) collective-permute-start(bf16[32,5120]{1,0:T(8,128)(2,1)S(1)} %get-tuple-element.55.refs_2_), channel_id=1, source_target_pairs={{0,48},{16,32},{32,16},{48,0},{1,49},{17,33},{33,17},{49,1},{2,50}... | collective-permute-start | bytes 983048 | tf_op jit(solution)/shard_map/ppermute | solution.py:165
  57.9 16.4 %collective-permute-start.10 = (bf16[64,5120]{1,0:T(8,128)(2,1)}, bf16[64,5120]{1,0:T(8,128)(2,1)S(1)}, u32[]{:S(2)}, u32[]{:S(2)}) collective-permute-start(bf16[64,5120]{1,0:T(8,128)(2,1)} %get-tuple-element.57.refs_0_), channel_id=1, source_target_pairs={{0,2},{2,0},{4,6},{6,4},{1,3},{3,1},{5,7},{7,5},{8,10},{10,8},{12,... | collective-permute-start | bytes 1966088 | tf_op jit(solution)/shard_map/ppermute | solution.py:165
  58.0 17.6 %collective-permute-start.11 = (bf16[64,5120]{1,0:T(8,128)(2,1)}, bf16[64,5120]{1,0:T(8,128)(2,1)S(1)}, u32[]{:S(2)}, u32[]{:S(2)}) collective-permute-start(bf16[64,5120]{1,0:T(8,128)(2,1)} %get-tuple-element.57.refs_0_), channel_id=1, source_target_pairs={{0,6},{2,4},{4,2},{6,0},{1,7},{3,5},{5,3},{7,1},{8,14},{10,12},{12... | collective-permute-start | bytes 1966088 | tf_op jit(solution)/shard_map/ppermute | solution.py:165
  60.1 15.5 %collective-permute-start.8 = (bf16[64,5120]{1,0:T(8,128)(2,1)}, bf16[64,5120]{1,0:T(8,128)(2,1)S(1)}, u32[]{:S(2)}, u32[]{:S(2)}) collective-permute-start(bf16[64,5120]{1,0:T(8,128)(2,1)} %get-tuple-element.56.refs_0_), channel_id=1, source_target_pairs={{0,16},{16,0},{32,48},{48,32},{1,17},{17,1},{33,49},{49,33},{2,18}... | collective-permute-start | bytes 1966088 | tf_op jit(solution)/shard_map/ppermute | solution.py:165
  61.0 17.3 %collective-permute-start.9 = (bf16[64,5120]{1,0:T(8,128)(2,1)}, bf16[64,5120]{1,0:T(8,128)(2,1)}, u32[]{:S(2)}, u32[]{:S(2)}) collective-permute-start(bf16[64,5120]{1,0:T(8,128)(2,1)} %get-tuple-element.56.refs_0_), channel_id=1, source_target_pairs={{0,48},{16,32},{32,16},{48,0},{1,49},{17,33},{33,17},{49,1},{2,50}... | collective-permute-start | bytes 1966088 | tf_op jit(solution)/shard_map/ppermute | solution.py:165
  79.4 9.1 %collective-permute-start.12 = (bf16[32,5120]{1,0:T(8,128)(2,1)S(1)}, bf16[32,5120]{1,0:T(8,128)(2,1)S(1)}, u32[]{:S(2)}, u32[]{:S(2)}) collective-permute-start(bf16[32,5120]{1,0:T(8,128)(2,1)S(1)} %get-tuple-element.63), channel_id=1, source_target_pairs={{0,48},{16,32},{32,16},{48,0},{1,49},{17,33},{33,17},{49,1},{2,50}... | collective-permute-start | bytes 983048 | tf_op jit(solution)/shard_map/ppermute | solution.py:165
  81.0 7.5 %collective-permute-start.13 = (bf16[32,5120]{1,0:T(8,128)(2,1)S(1)}, bf16[32,5120]{1,0:T(8,128)(2,1)S(1)}, u32[]{:S(2)}, u32[]{:S(2)}) collective-permute-start(bf16[32,5120]{1,0:T(8,128)(2,1)S(1)} %get-tuple-element.64), channel_id=1, source_target_pairs={{0,16},{16,0},{32,48},{48,32},{1,17},{17,1},{33,49},{49,33},{2,18}... | collective-permute-start | bytes 983048 | tf_op jit(solution)/shard_map/ppermute | solution.py:165
  81.0 8.5 %collective-permute-start.14 = (bf16[32,5120]{1,0:T(8,128)(2,1)S(1)}, bf16[32,5120]{1,0:T(8,128)(2,1)S(1)}, u32[]{:S(2)}, u32[]{:S(2)}) collective-permute-start(bf16[32,5120]{1,0:T(8,128)(2,1)S(1)} %get-tuple-element.65), channel_id=1, source_target_pairs={{0,6},{2,4},{4,2},{6,0},{1,7},{3,5},{5,3},{7,1},{8,14},{10,12},{12... | collective-permute-start | bytes 983048 | tf_op jit(solution)/shard_map/ppermute | solution.py:165
  82.8 7.1 %collective-permute-start.15 = (bf16[32,5120]{1,0:T(8,128)(2,1)S(1)}, bf16[32,5120]{1,0:T(8,128)(2,1)S(1)}, u32[]{:S(2)}, u32[]{:S(2)}) collective-permute-start(bf16[32,5120]{1,0:T(8,128)(2,1)S(1)} %get-tuple-element.66), channel_id=1, source_target_pairs={{0,2},{2,0},{4,6},{6,4},{1,3},{3,1},{5,7},{7,5},{8,10},{10,8},{12,... | collective-permute-start | bytes 983048 | tf_op jit(solution)/shard_map/ppermute | solution.py:165
  83.6 49.6 %copy-start.7 = (bf16[64,16,512]{2,1,0:T(8,128)(2,1)}, bf16[64,16,512]{2,1,0:T(8,128)(2,1)S(1)}, u32[]{:S(2)}) copy-start(bf16[64,16,512]{2,1,0:T(8,128)(2,1)S(1)} %get-tuple-element.84) | copy-start | bytes 3145732
  92.3 41.0 %copy-start = (bf16[256,5120]{1,0:T(8,128)(2,1)}, bf16[256,5120]{1,0:T(8,128)(2,1)S(1)}, u32[]{:S(2)}) copy-start(bf16[256,5120]{1,0:T(8,128)(2,1)S(1)} %whole.3.refs_1_) | copy-start | bytes 7864324
  133.2 17.8 %collective-permute-start.16 = (bf16[256,5120]{1,0:T(8,128)(2,1)}, bf16[256,5120]{1,0:T(8,128)(2,1)}, u32[]{:S(2)}, u32[]{:S(2)}) collective-permute-start(bf16[256,5120]{1,0:T(8,128)(2,1)} %whole.2.refs_0_), channel_id=1, source_target_pairs={{0,64},{64,0},{1,65},{65,1},{2,66},{66,2},{3,67},{67,3},{4,68},{68... | collective-permute-start | bytes 7864328 | tf_op jit(solution)/shard_map/ppermute | solution.py:46
  133.3 17.7 %collective-permute-start.17 = (bf16[256,5120]{1,0:T(8,128)(2,1)S(1)}, bf16[256,5120]{1,0:T(8,128)(2,1)}, u32[]{:S(2)}, u32[]{:S(2)}) collective-permute-start(bf16[256,5120]{1,0:T(8,128)(2,1)S(1)} %whole.3.refs_1_), channel_id=1, source_target_pairs={{0,64},{64,0},{1,65},{65,1},{2,66},{66,2},{3,67},{67,3},{4,68},{68... | collective-permute-start | bytes 7864328 | tf_op jit(solution)/shard_map/ppermute | solution.py:46
  133.7 28.6 %all-to-all-start.2 = ((bf16[64,16,512]{2,1,0:T(8,128)(2,1)}), bf16[64,16,512]{2,1,0:T(8,128)(2,1)}, u32[]{:S(2)}, u32[]{:S(2)}) async-start(bf16[64,16,512]{2,1,0:T(8,128)(2,1)} %copy-done.7), calls=%async_computation.2 | async-start | bytes 2097152 | tf_op jit(solution)/shard_map/all_to_all | solution.py:50
  160.3 1.2 collective-permute-start.18
  162.3 21.0 %all-to-all-start.1 = ((f32[64,8,128]{2,1,0:T(8,128)}), f32[64,8,128]{2,1,0:T(8,128)S(1)}, u32[]{:S(2)}, u32[]{:S(2)}) async-start(f32[64,8,128]{2,1,0:T(8,128)} %chip_stats.1), calls=%async_computation.1 | async-start | bytes 524288 | tf_op jit(solution)/shard_map/all_to_all | solution.py:50
  172.8 14.4 %collective-permute-start.20 = (bf16[64,16,512]{2,1,0:T(8,128)(2,1)}, bf16[64,16,512]{2,1,0:T(8,128)(2,1)S(1)}, u32[]{:S(2)}, u32[]{:S(2)}) collective-permute-start(bf16[64,16,512]{2,1,0:T(8,128)(2,1)} %all-to-all-done.2.own_ref), channel_id=1, source_target_pairs={{0,64},{64,0},{1,65},{65,1},{2,66},{66,2},{3,67},{67,3},{4,68},{68... | collective-permute-start | bytes 3145736 | tf_op jit(solution)/shard_map/ppermute | solution.py:46
  186.9 3.4 %collective-permute-start.19 = (bf16[128,4096]{1,0:T(8,128)(2,1)S(1)}, bf16[128,4096]{1,0:T(8,128)(2,1)S(1)}, u32[]{:S(2)}, u32[]{:S(2)}) collective-permute-start(bf16[128,4096]{1,0:T(8,128)(2,1)S(1)} %get-tuple-element.83), channel_id=1, source_target_pairs={{0,64},{64,0},{1,65},{65,1},{2,66},{66,2},{3,67},{67,3},{4,68},{68... | collective-permute-start | bytes 3145736 | tf_op jit(solution)/shard_map/ppermute | solution.py:46
  190.2 25.4 %copy-start.9 = (bf16[2,4096]{1,0:T(2,128)(2,1)S(1)}, bf16[2,4096]{1,0:T(2,128)(2,1)}, u32[]{:S(2)}) copy-start(bf16[2,4096]{1,0:T(2,128)(2,1)} %states_ref.1) | copy-start | bytes 49156
  191.6 49.6 %copy-start.8 = (bf16[112,4096]{1,0:T(8,128)(2,1)S(1)}, bf16[112,4096]{1,0:T(8,128)(2,1)}, u32[]{:S(2)}) copy-start(bf16[112,4096]{1,0:T(8,128)(2,1)} %down_ref.1) | copy-start | bytes 2752516
  238.5 2.7 collective-permute-start.21
  244.2 2.7 collective-permute-start.22
  249.3 24.0 %all-to-all-start.5 = ((bf16[64,16,512]{2,1,0:T(8,128)(2,1)}), bf16[64,16,512]{2,1,0:T(8,128)(2,1)S(1)}, u32[]{:S(2)}, u32[]{:S(2)}) async-start(bf16[64,16,512]{2,1,0:T(8,128)(2,1)} %join.5), calls=%async_computation.5 | async-start | bytes 2097152 | tf_op jit(solution)/shard_map/all_to_all | solution.py:50
  (10 other events, 86.4 us)

commit v7 on v5

--- a/solution.py
+++ b/solution.py
@@ -130,9 +130,9 @@
         groups_kernel,
         "pairs",
         [shape_of((tokens, part.shape[1])) for part in parts[::2]],
-        limit=2,
+        limit=4,
         in_specs=[SMEM] + [ANY] * len(parts),
-        out_specs=[ANY] * (len(parts) // 2),
+        out_specs=[VMEM] * (len(parts) // 2),
         scratch_shapes=[pltpu.SemaphoreType.DMA((len(parts),))],
     )(bits, *parts)
 
@@ -154,9 +154,9 @@
         halves_kernel,
         "halves",
         [shape_of((p.shape[0] // 2, p.shape[1])) for p in pieces],
-        limit=2,
+        limit=4,
         in_specs=[ANY] * len(pieces),
-        out_specs=[ANY] * len(pieces),
+        out_specs=[VMEM] * len(pieces),
         scratch_shapes=[pltpu.SemaphoreType.DMA((len(pieces),))],
     )(*pieces)
 
@@ -186,9 +186,9 @@
         whole_kernel,
         "whole",
         shape_of((4 * tokens, width)),
-        limit=2,
+        limit=6,
         in_specs=[SMEM] + [ANY] * 5,
-        out_specs=ANY,
+        out_specs=VMEM,
         scratch_shapes=[pltpu.SemaphoreType.DMA((5,))],
     )(place, *pieces)
 
@@ -384,39 +384,37 @@
     )(core, every, weight, teacher, student, student_head_t)
 
 
-def pick_kernel(place_ref, ids_ref, head_from, own_ref, send_ref, head, sems):
+def pick_kernel(device_ref, ids_ref, head_from, out_ref, head, sems):
     copies = head_copies(head_from, head, sems)
     vocab, tokens = head.shape[0], ids_ref.shape[1]
-    entry = lax.broadcasted_iota(jnp.int32, (vocab, tokens), 0) + place_ref[1] * vocab
+    entry = lax.broadcasted_iota(jnp.int32, (vocab, tokens), 0) + device_ref[0] * vocab
     place = lax.broadcasted_iota(jnp.int32, (tokens, tokens), 0)
     column = lax.broadcasted_iota(jnp.int32, (tokens, tokens), 1)
-    source = (((place >> 7) ^ place_ref[0]) << 7) | ((place & 63) << 1) | ((place >> 6) & 1)
+    source = (place & 128) | ((place & 63) << 1) | ((place >> 6) & 1)
     chosen = row_product(
         (column == source).astype(jnp.bfloat16), (ids_ref[...] == entry).astype(jnp.bfloat16)
     ).astype(jnp.bfloat16)
-    half = own_ref.shape[0]
     for columns, copy in copies:
         copy.wait()
-        out = jnp.dot(chosen, head[:, columns], preferred_element_type=jnp.float32)
-        own_ref[:, columns] = out[:half].astype(jnp.bfloat16)
-        send_ref[:, columns] = out[half:].astype(jnp.bfloat16)
-
-
-def pick_part(place, ids, student_head_t):
+        out_ref[:, columns] = jnp.dot(
+            chosen, head[:, columns], preferred_element_type=jnp.float32
+        )
+
+
+def pick_part(device, ids, student_head_t):
     vocab, width = student_head_t.shape
-    shape = shape_of((ids.shape[1] // 2, width))
     return kernel_call(
         pick_kernel,
         "pick",
-        [shape, shape],
+        shape_of((ids.shape[1], width), jnp.float32),
         limit=48,
         in_specs=[SMEM, VMEM, ANY],
-        out_specs=[VMEM] * 2,
+        out_specs=VMEM,
         scratch_shapes=[
             pltpu.VMEM((vocab, width), jnp.bfloat16),
             pltpu.SemaphoreType.DMA((4,)),
         ],
-    )(place, ids, student_head_t)
+    )(device, ids, student_head_t)
 
 
 def join_kernel(*refs):
@@ -488,13 +486,6 @@
     return jnp.sum(blocks_ref[...].astype(jnp.float32), axis=0)
 
 
-def embed_kernel(blocks_ref, gain_ref, embedded_ref, out_ref):
-    values = block_sum(blocks_ref)
-    embedded_ref[...] = values
-    rows = (values * block_inverse(values) * block_gain(gain_ref)).astype(jnp.bfloat16)
-    out_ref[...] = jnp.broadcast_to(rows[None], out_ref.shape)
-
-
 def final_kernel(blocks_ref, states_ref, gain_ref, grad_ref, out_ref, states):
     for i in range(SEGMENTS):
         part = states_ref[:, i * SEGMENT : (i + 1) * SEGMENT].astype(jnp.float32)
@@ -538,15 +529,32 @@
     return jnp.concatenate(parts, axis=0).astype(jnp.bfloat16)
 
 
-def gate_kernel(own_ref, other_ref, gate_ref, up_ref, out_ref, *scratches):
-    spread_rows((own_ref, other_ref), scratches)
-    total = None
+def gate_kernel(place_ref, embedded_ref, gain_ref, gate_ref, up_ref, hidden_ref, own_ref):
+    core, chip = place_ref[0], place_ref[1]
+    embedded = embedded_ref[...]
+    inverse = lax.rsqrt(jnp.mean(embedded * embedded, axis=1, keepdims=True) + eps)
+    gain = gain_ref[...].astype(jnp.float32)
+    lanes = SEGMENT // 128
+    hidden = None
     for i in range(SEGMENTS):
+        part = [gain[lanes * i + k : lanes * i + k + 1] for k in range(lanes)]
         columns = slice(i * SEGMENT, (i + 1) * SEGMENT)
+        rows = embedded_ref[:, columns] * inverse * jnp.concatenate(part, axis=1)
         weight = jnp.concatenate([gate_ref[:, columns], up_ref[:, columns]], axis=0)
-        term = row_product(weight, segment_rows(scratches, i))
-        total = term if total is None else total + term
-    out_ref[...] = total
+        term = row_product(weight, rows.astype(jnp.bfloat16))
+        hidden = term if hidden is None else hidden + term
+    low, high = hidden[:, :128], hidden[:, 128:]
+    hidden_ref[:, :128] = jnp.where(core == 0, low, high)
+    hidden_ref[:, 128:] = jnp.where(core == 0, high, low)
+    for t in range(2):
+        base = pl.multiple_of(core * 128 + t * 64 + (chip >> 3) * 8, 8)
+        rows = embedded_ref[pl.ds(base, 8), :]
+        mine = lax.broadcasted_iota(jnp.int32, rows.shape, 0) == (chip & 7)
+        row = jnp.sum(jnp.where(mine, rows, 0.0), axis=0, keepdims=True)
+        for i in range(SEGMENTS):
+            own_ref[t * SEGMENTS + i : t * SEGMENTS + i + 1, :] = row[
+                :, i * SEGMENT : (i + 1) * SEGMENT
+            ]
 
 
 def ffn_grad_kernel(
@@ -636,6 +644,11 @@
     )(own_core, teacher_states, teacher_gain, student_states, student_gain)
     (rows,) = in_pair(own_core, keep, swap_cores(send), (width,))
 
+    ids = token_ids.reshape(1, 256)
+    picked = pick_part(device.reshape(1).astype(jnp.int32), ids, student_head_t)
+    rows, picked = lax.optimization_barrier((rows, picked))
+    embedded = lax.psum(picked, AXES)
+
     (rows,) = in_pair((y & 1).reshape(1), rows, along(rows, ("yh", "yl"), 1), (width,))
     first, second = in_pair((y >> 1).reshape(1), rows, along(rows, ("yh", "yl"), 3), WIDTHS)
     for bit, mask in ((0, 1), (1, 3)):
@@ -643,9 +656,7 @@
         bits = (jnp.stack([z, x]) >> bit) & 1
         first, second = in_pairs(bits, (first, came[0], second, came[1]))
     came = [along(first, "x", 1), along(first, "x", 3), along(second, "z", 1), along(second, "z", 3)]
-    place = jnp.stack([core, device]).astype(jnp.int32)
-    own, send = pick_part(place, token_ids.reshape(1, 256), student_head_t)
-    came, picked = lax.optimization_barrier((came, join_part(own, swap_cores(send))))
+    came = lax.optimization_barrier(came)
     halves = halves_of(came)
     far = [
         along(half, line, mask)
@@ -667,26 +678,15 @@
         in_specs=[VMEM] * 2,
         out_specs=VMEM,
     )(stats, swap_cores(stats))
-    stats, picked = lax.optimization_barrier((stats, picked))
     every = exchange(stats, CHIPS)
-    picked = exchange(picked, CHIPS)
 
     weight = token_weight.reshape(2, 4, 2, 4, 2, 2).transpose(1, 3, 2, 4, 0, 5).reshape(1, 256)
     own, send, divergence = row_grad_part(
         own_core, every, weight, teacher, student, student_head_t
     )
     divergence = divergence.reshape(4, 4, 2, 2, 2, 2).transpose(4, 0, 2, 1, 3, 5).reshape(256)
-    embedded, ffn_rows = kernel_call(
-        embed_kernel,
-        "embed",
-        [shape_of(BLOCK, jnp.float32), shape_of(picked.shape)],
-        in_specs=[VMEM] * 2,
-        out_specs=[VMEM] * 2,
-    )(picked, ffn_gain)
     blocks = join_part(own, swap_cores(send))
-    blocks, ffn_rows = lax.optimization_barrier((blocks, ffn_rows))
     blocks = exchange(blocks, CHIPS)
-    ffn_rows = exchange(ffn_rows, CHIPS)
     final_grad, blocks = kernel_call(
         final_kernel,
         "final",
@@ -696,9 +696,15 @@
         scratch_shapes=[pltpu.VMEM(BLOCK, jnp.float32)],
     )(blocks, student_states, student_gain)
     blocks = exchange(blocks, CHIPS)
-    (hidden,) = ffn_part(
-        gate_kernel, "gate_upper", [shape_of((224, 256), jnp.float32)], ffn_rows, gate_t, up_t
-    )
+    place = jnp.stack([core, lax.axis_index(CHIPS)]).astype(jnp.int32)
+    hidden, embedded = kernel_call(
+        gate_kernel,
+        "gate_upper",
+        [shape_of((2 * gate_t.shape[0], 256), jnp.float32), shape_of(BLOCK, jnp.float32)],
+        limit=24,
+        in_specs=[SMEM] + [VMEM] * 4,
+        out_specs=[VMEM] * 2,
+    )(place, embedded, ffn_gain, gate_t, up_t)
     shape = (128, 4096)
     own, send = ffn_part(
         ffn_grad_kernel,

time: 248 us -> 352 us (1.42)
  waiting for transfers between devices: 103 us -> 215 us
  blocking collectives: 46.5 us -> 24.2 us
  between operations: 1.02 us -> 14.4 us
    psum x0 -> x1, waiting for transfers between devices: none -> 126 us  [shards(): embedded = lax.psum(picked, AXES)]
    all_to_all x2 -> x1, blocking collectives: 46.5 us -> 24.2 us  [exchange(): return lax.all_to_all(blocks, axes, split_axis=0, concat_axis=0, tiled=True)]
    all_to_all x4 -> x3, waiting for transfers between devices: 61.4 us -> 46.4 us  [exchange(): return lax.all_to_all(blocks, axes, split_axis=0, concat_axis=0, tiled=True)]
    all_to_all x4 -> x3, starting transfers between devices: 22.7 us -> 20.3 us  [exchange(): return lax.all_to_all(blocks, axes, split_axis=0, concat_axis=0, tiled=True)]
    unnamed x24 -> x26, local copies, waits for them, and re-layouts: 5.15 us -> 7.1 us
  transfers between devices with their start and end apart: 27 -> 25, of which waited for: 18 -> 19; matrix products, arithmetic and copies ran while one was open for 1% -> 1% of each run, Pallas kernels for 8% -> 5%
where the time goes in v7:
time: 352 us; the launch traced here: 351 us
  waiting for transfers between devices  215 us (61%)
  Pallas kernels  44.4 us (13%)
  starting transfers between devices  43.3 us (12%)
  blocking collectives  24.2 us (7%)
  between operations  14.4 us (4%)
  local copies, waits for them, and re-layouts  8.89 us (3%)
    psum x1, waiting for transfers between devices, shards(): embedded = lax.psum(picked, AXES)  126 us
    all_to_all x3, waiting for transfers between devices, exchange(): return lax.all_to_all(blocks, axes, split_axis=0, concat_axis=0, tiled=True)  46.4 us
    ppermute x14, waiting for transfers between devices, along(): return lax.ppermute(block, line, [(i, i ^ mask) for i in range(4)])  36 us
    all_to_all x1, blocking collectives, exchange(): return lax.all_to_all(blocks, axes, split_axis=0, concat_axis=0, tiled=True)  24.2 us
    ppermute x14, starting transfers between devices, along(): return lax.ppermute(block, line, [(i, i ^ mask) for i in range(4)])  21.8 us
    all_to_all x3, starting transfers between devices, exchange(): return lax.all_to_all(blocks, axes, split_axis=0, concat_axis=0, tiled=True)  20.3 us
    pallas_call x2, Pallas kernels, logits_part(): kernel_call(functools.partial(logits_kernel, last), 'logits', out_shape,...  17 us
    unnamed x26, local copies, waits for them, and re-layouts  7.1 us
  transfers between devices with their start and end apart: 25, of which 19 were waited for; matrix products, arithmetic and copies ran while one was open for 1% of the time, Pallas kernels for 5%

profile of v7, /device:TPU:0, one launch (start us, length us, event | category | flops | bytes accessed | tf_op | source)
XLA Modules:
  0.0 351.4 jit_solution(2339714541308911023)
XLA Ops:
  9.2 2.2 copy-done
  12.0 4.5 %pick.1 = f32[256,4096]{1,0:T(8,128)} custom-call(s32[1]{0:T(128)} %bitcast.7.device_ref, s32[1,256]{1,0:T(1,128)S(1)} %bitcast.29, bf16[501,4096]{1,0:T(8,128)(2,1)S(1)} %bitcast.20), custom_call_target="tpu_custom_call" | custom-call | flops 1 | bytes 1 | tf_op jit(solution)/shard_map/pick/pallas_call | solution.py:406
  18.4 3.2 collective-permute-done.1.came_ref
  21.6 3.2 collective-permute-start.2
  24.8 4.0 %collective-permute-done.2.came_ref = bf16[8,10240]{1,0:T(8,128)(2,1)S(1)} collective-permute-done((bf16[8,10240]{1,0:T(8,128)(2,1)S(1)}, bf16[8,10240]{1,0:T(8,128)(2,1)S(1)}, u32[]{:S(2)}, u32[]{:S(2)}) %collective-permute-start.2) | collective-permute-done | bytes 163872 | tf_op jit(solution)/shard_map/ppermute | solution.py:165
  28.9 2.0 collective-permute-start.3
  34.3 1.9 collective-permute-done.4.refs_3_
  37.7 2.6 collective-permute-start.5
  40.3 2.8 collective-permute-start.6
  43.2 3.2 collective-permute-done.5.refs_1_
  46.3 2.3 collective-permute-done.6.refs_3_
  49.6 2.8 collective-permute-start.8
  53.8 10.0 %collective-permute-done.8.refs_1_.refs_2_ = bf16[64,5120]{1,0:T(8,128)(2,1)S(1)} collective-permute-done((bf16[64,5120]{1,0:T(8,128)(2,1)S(1)}, bf16[64,5120]{1,0:T(8,128)(2,1)S(1)}, u32[]{:S(2)}, u32[]{:S(2)}) %collective-permute-start.8) | collective-permute-done | bytes 655392 | tf_op jit(solution)/shard_map/ppermute | solution.py:165
  70.7 4.5 %collective-permute-done.11.refs_3_ = bf16[32,5120]{1,0:T(8,128)(2,1)S(1)} collective-permute-done((bf16[32,5120]{1,0:T(8,128)(2,1)S(1)}, bf16[32,5120]{1,0:T(8,128)(2,1)S(1)}, u32[]{:S(2)}, u32[]{:S(2)}) %collective-permute-start.11) | collective-permute-done | bytes 327712 | tf_op jit(solution)/shard_map/ppermute | solution.py:165
  75.2 2.0 collective-permute-done.13.refs_3_
  80.4 8.3 %logits.2 = (f32[501,256]{1,0:T(8,128)S(1)}, f32[501,256]{1,0:T(8,128)S(1)}, f32[501,256]{1,0:T(8,128)S(1)}) custom-call(s32[1]{0:T(128)} %bitcast.core_ref.place_ref, bf16[256,5120]{1,0:T(8,128)(2,1)S(1)} %whole.2.refs_0_, bf16[256,5120]{1,0:T(8,128)(2,1)} %copy-done.1, bf16[501,4096]{1,0:T(8,128)(2,1)} %bitcast.17, bf16[501,16384]{1,0:T(8,128)(2,1)} %bitcast.30), custom_call_target="tpu_custom_call" | custom-call | flops 1 | bytes 1 | tf_op jit(solution)/shard_map/logits/pallas_call | solution.py:290
  90.2 8.7 %logits.3 = (f32[501,256]{1,0:T(8,128)S(1)}, f32[501,256]{1,0:T(8,128)S(1)}, f32[8,128]{1,0:T(8,128)S(1)}) custom-call(s32[1]{0:T(128)S(6)} %sub.3.place_ref, bf16[256,5120]{1,0:T(8,128)(2,1)S(1)} %collective-permute-done.15.refs_0_, bf16[256,5120]{1,0:T(8,128)(2,1)} %copy-done.11, bf16[501,4096]{1,0:T(8,128)(2,1)} %bitcast.18, bf16[501,16384]{1,0:T(8,128)(2,1)} %bitcast.31, ...), custom_call_target="tpu_custom_call" | custom-call | flops 1 | bytes 1 | tf_op jit(solution)/shard_map/logits/pallas_call | solution.py:290
  100.9 8.2 %all-to-all-start = ((f32[64,8,128]{2,1,0:T(8,128)}), f32[64,8,128]{2,1,0:T(8,128)S(1)}, u32[]{:S(2)}, u32[]{:S(2)}) async-start(f32[64,8,128]{2,1,0:T(8,128)} %chip_stats.1), calls=%async_computation | async-start | bytes 524288 | tf_op jit(solution)/shard_map/all_to_all | solution.py:50
  109.5 10.6 %all-to-all-done.every_ref = f32[64,8,128]{2,1,0:T(8,128)S(1)} async-done(((f32[64,8,128]{2,1,0:T(8,128)}), f32[64,8,128]{2,1,0:T(8,128)S(1)}, u32[]{:S(2)}, u32[]{:S(2)}) %all-to-all-start) | async-done | bytes 262176 | tf_op jit(solution)/shard_map/all_to_all | solution.py:50
  120.1 3.4 row_grad.1
  123.6 2.6 collective-permute-done.18.refs_1_
  126.2 2.3 join.2
  128.6 4.7 %all-to-all-start.1 = ((bf16[64,16,512]{2,1,0:T(8,128)(2,1)}), bf16[64,16,512]{2,1,0:T(8,128)(2,1)S(1)}, u32[]{:S(2)}, u32[]{:S(2)}) async-start(bf16[64,16,512]{2,1,0:T(8,128)(2,1)} %join.2), calls=%async_computation.1 | async-start | bytes 2097152 | tf_op jit(solution)/shard_map/all_to_all | solution.py:50
  134.1 18.6 %all-to-all-done.1.blocks_ref = bf16[64,16,512]{2,1,0:T(8,128)(2,1)S(1)} async-done(((bf16[64,16,512]{2,1,0:T(8,128)(2,1)}), bf16[64,16,512]{2,1,0:T(8,128)(2,1)S(1)}, u32[]{:S(2)}, u32[]{:S(2)}) %all-to-all-start.1) | async-done | bytes 1048608 | tf_op jit(solution)/shard_map/all_to_all | solution.py:50
  153.1 24.2 %all_to_all.20.own_ref = bf16[64,16,512]{2,1,0:T(8,128)(2,1)S(1)} all-to-all(bf16[64,16,512]{2,1,0:T(8,128)(2,1)S(1)} %get-tuple-element.69), channel_id=1, replica_groups=mesh['core'=2,'x'=4,'yh'=2,'z'=4,'yl'=2] {'x','yh','z','yl'}, dimensions={0} | all-to-all | bytes 2097152 | tf_op jit(solution)/shard_map/all_to_all | solution.py:50
  177.4 126.2 %all-reduce.2.cloned.1.call-done.embedded_ref = f32[256,4096]{1,0:T(8,128)} async-done(((f32[256,4096]{1,0:T(8,128)}), f32[256,4096]{1,0:T(8,128)}) %all-reduce.2.cloned.1.call-update) | async-done | bytes 4194320 | tf_op jit(solution)/shard_map/psum | solution.py:650
  303.6 2.2 copy-done.2
  307.5 4.3 %ffn_grad.1 = (f32[128,4096]{1,0:T(8,128)S(1)}, bf16[128,4096]{1,0:T(8,128)(2,1)S(1)}) custom-call(bf16[64,16,512]{2,1,0:T(8,128)(2,1)S(1)} %all_to_all.20.own_ref, bf16[64,16,512]{2,1,0:T(8,128)(2,1)} %collective-permute-done.19.other_ref, bf16[112,4096]{1,0:T(8,128)(2,1)S(1)} %copy-done.5, f32[224,256]{1,0:T(8,128)S(1)} %get-tuple-element.71.hidden_ref, ...), custom_call_target="tpu_custom_call" | custom-call | flops 1 | bytes 1 | tf_op jit(solution)/shard_map/ffn_grad/pallas_call | solution.py:591
  311.9 2.6 collective-permute-done.20.refs_1_
  314.6 2.3 join.3
  316.9 7.4 %all-to-all-start.3 = ((bf16[64,16,512]{2,1,0:T(8,128)(2,1)}), bf16[64,16,512]{2,1,0:T(8,128)(2,1)S(1)}, u32[]{:S(2)}, u32[]{:S(2)}) async-start(bf16[64,16,512]{2,1,0:T(8,128)(2,1)} %join.3), calls=%async_computation.3 | async-start | bytes 2097152 | tf_op jit(solution)/shard_map/all_to_all | solution.py:50
  326.4 17.2 %all-to-all-done.3.blocks_ref = bf16[64,16,512]{2,1,0:T(8,128)(2,1)S(1)} async-done(((bf16[64,16,512]{2,1,0:T(8,128)(2,1)}), bf16[64,16,512]{2,1,0:T(8,128)(2,1)S(1)}, u32[]{:S(2)}, u32[]{:S(2)}) %all-to-all-start.3) | async-done | bytes 1048608 | tf_op jit(solution)/shard_map/all_to_all | solution.py:50
  (77 shorter events, 31.9 us)
Async XLA Ops:
  9.1 7.5 %collective-permute-start = (bf16[2,10240]{1,0:T(2,128)(2,1)}, bf16[2,10240]{1,0:T(2,128)(2,1)S(1)}, u32[]{:S(2)}, u32[]{:S(2)}) collective-permute-start(bf16[2,10240]{1,0:T(2,128)(2,1)} %get-tuple-element.40), channel_id=1, source_target_pairs={{0,64},{64,0},{1,65},{65,1},{2,66},{66,2},{3,67},{67,3},{4,68},{68... | collective-permute-start | bytes 122888 | tf_op jit(solution)/shard_map/ppermute | solution.py:46
  12.0 4.6 %copy-start.7 = (bf16[2,10240]{1,0:T(2,128)(2,1)S(1)}, bf16[2,10240]{1,0:T(2,128)(2,1)}, u32[]{:S(2)}) copy-start(bf16[2,10240]{1,0:T(2,128)(2,1)} %get-tuple-element.39.own_ref) | copy-start | bytes 122884
  16.7 4.9 %collective-permute-start.1 = (bf16[4,10240]{1,0:T(4,128)(2,1)S(1)}, bf16[4,10240]{1,0:T(4,128)(2,1)S(1)}, u32[]{:S(2)}, u32[]{:S(2)}) collective-permute-start(bf16[4,10240]{1,0:T(4,128)(2,1)S(1)} %pair.3.own_ref), channel_id=1, source_target_pairs={{0,1},{1,0},{8,9},{9,8},{2,3},{3,2},{10,11},{11,10},{4,5},{5,4},{1... | collective-permute-start | bytes 245768 | tf_op jit(solution)/shard_map/ppermute | solution.py:165
  21.6 7.2 %collective-permute-start.2 = (bf16[8,10240]{1,0:T(8,128)(2,1)S(1)}, bf16[8,10240]{1,0:T(8,128)(2,1)S(1)}, u32[]{:S(2)}, u32[]{:S(2)}) collective-permute-start(bf16[8,10240]{1,0:T(8,128)(2,1)S(1)} %pair.4.own_ref), channel_id=1, source_target_pairs={{0,9},{1,8},{8,1},{9,0},{2,11},{3,10},{10,3},{11,2},{4,13},{5,12},... | collective-permute-start | bytes 491528 | tf_op jit(solution)/shard_map/ppermute | solution.py:165
  28.9 5.4 %collective-permute-start.3 = (bf16[16,5120]{1,0:T(8,128)(2,1)S(1)}, bf16[16,5120]{1,0:T(8,128)(2,1)S(1)}, u32[]{:S(2)}, u32[]{:S(2)}) collective-permute-start(bf16[16,5120]{1,0:T(8,128)(2,1)S(1)} %get-tuple-element.42.refs_0_), channel_id=1, source_target_pairs={{0,2},{2,0},{4,6},{6,4},{1,3},{3,1},{5,7},{7,5},{8,10},{10,8},{12,... | collective-permute-start | bytes 491528 | tf_op jit(solution)/shard_map/ppermute | solution.py:165
  30.9 5.3 %collective-permute-start.4 = (bf16[16,5120]{1,0:T(8,128)(2,1)S(1)}, bf16[16,5120]{1,0:T(8,128)(2,1)S(1)}, u32[]{:S(2)}, u32[]{:S(2)}) collective-permute-start(bf16[16,5120]{1,0:T(8,128)(2,1)S(1)} %get-tuple-element.43.refs_2_), channel_id=1, source_target_pairs={{0,16},{16,0},{32,48},{48,32},{1,17},{17,1},{33,49},{49,33},{2,18}... | collective-permute-start | bytes 491528 | tf_op jit(solution)/shard_map/ppermute | solution.py:165
  37.7 8.6 %collective-permute-start.5 = (bf16[32,5120]{1,0:T(8,128)(2,1)S(1)}, bf16[32,5120]{1,0:T(8,128)(2,1)S(1)}, u32[]{:S(2)}, u32[]{:S(2)}) collective-permute-start(bf16[32,5120]{1,0:T(8,128)(2,1)S(1)} %get-tuple-element.44.refs_0_), channel_id=1, source_target_pairs={{0,6},{2,4},{4,2},{6,0},{1,7},{3,5},{5,3},{7,1},{8,14},{10,12},{12... | collective-permute-start | bytes 983048 | tf_op jit(solution)/shard_map/ppermute | solution.py:165
  40.3 8.3 %collective-permute-start.6 = (bf16[32,5120]{1,0:T(8,128)(2,1)S(1)}, bf16[32,5120]{1,0:T(8,128)(2,1)S(1)}, u32[]{:S(2)}, u32[]{:S(2)}) collective-permute-start(bf16[32,5120]{1,0:T(8,128)(2,1)S(1)} %get-tuple-element.45.refs_2_), channel_id=1, source_target_pairs={{0,48},{16,32},{32,16},{48,0},{1,49},{17,33},{33,17},{49,1},{2,50}... | collective-permute-start | bytes 983048 | tf_op jit(solution)/shard_map/ppermute | solution.py:165
  49.6 14.2 %collective-permute-start.8 = (bf16[64,5120]{1,0:T(8,128)(2,1)S(1)}, bf16[64,5120]{1,0:T(8,128)(2,1)S(1)}, u32[]{:S(2)}, u32[]{:S(2)}) collective-permute-start(bf16[64,5120]{1,0:T(8,128)(2,1)S(1)} %get-tuple-element.46.refs_0_), channel_id=1, source_target_pairs={{0,48},{16,32},{32,16},{48,0},{1,49},{17,33},{33,17},{49,1},{2,50}... | collective-permute-start | bytes 1966088 | tf_op jit(solution)/shard_map/ppermute | solution.py:165
  52.5 12.9 %collective-permute-start.7 = (bf16[64,5120]{1,0:T(8,128)(2,1)S(1)}, bf16[64,5120]{1,0:T(8,128)(2,1)S(1)}, u32[]{:S(2)}, u32[]{:S(2)}) collective-permute-start(bf16[64,5120]{1,0:T(8,128)(2,1)S(1)} %get-tuple-element.46.refs_0_), channel_id=1, source_target_pairs={{0,16},{16,0},{32,48},{48,32},{1,17},{17,1},{33,49},{49,33},{2,18}... | collective-permute-start | bytes 1966088 | tf_op jit(solution)/shard_map/ppermute | solution.py:165
  52.5 13.9 %collective-permute-start.10 = (bf16[64,5120]{1,0:T(8,128)(2,1)S(1)}, bf16[64,5120]{1,0:T(8,128)(2,1)S(1)}, u32[]{:S(2)}, u32[]{:S(2)}) collective-permute-start(bf16[64,5120]{1,0:T(8,128)(2,1)S(1)} %get-tuple-element.47.refs_0_), channel_id=1, source_target_pairs={{0,6},{2,4},{4,2},{6,0},{1,7},{3,5},{5,3},{7,1},{8,14},{10,12},{12... | collective-permute-start | bytes 1966088 | tf_op jit(solution)/shard_map/ppermute | solution.py:165
  53.2 13.2 %collective-permute-start.9 = (bf16[64,5120]{1,0:T(8,128)(2,1)S(1)}, bf16[64,5120]{1,0:T(8,128)(2,1)S(1)}, u32[]{:S(2)}, u32[]{:S(2)}) collective-permute-start(bf16[64,5120]{1,0:T(8,128)(2,1)S(1)} %get-tuple-element.47.refs_0_), channel_id=1, source_target_pairs={{0,2},{2,0},{4,6},{6,4},{1,3},{3,1},{5,7},{7,5},{8,10},{10,8},{12,... | collective-permute-start | bytes 1966088 | tf_op jit(solution)/shard_map/ppermute | solution.py:165
  66.8 8.4 %collective-permute-start.11 = (bf16[32,5120]{1,0:T(8,128)(2,1)S(1)}, bf16[32,5120]{1,0:T(8,128)(2,1)S(1)}, u32[]{:S(2)}, u32[]{:S(2)}) collective-permute-start(bf16[32,5120]{1,0:T(8,128)(2,1)S(1)} %get-tuple-element.52), channel_id=1, source_target_pairs={{0,48},{16,32},{32,16},{48,0},{1,49},{17,33},{33,17},{49,1},{2,50}... | collective-permute-start | bytes 983048 | tf_op jit(solution)/shard_map/ppermute | solution.py:165
  67.4 7.8 %collective-permute-start.12 = (bf16[32,5120]{1,0:T(8,128)(2,1)S(1)}, bf16[32,5120]{1,0:T(8,128)(2,1)S(1)}, u32[]{:S(2)}, u32[]{:S(2)}) collective-permute-start(bf16[32,5120]{1,0:T(8,128)(2,1)S(1)} %get-tuple-element.53), channel_id=1, source_target_pairs={{0,16},{16,0},{32,48},{48,32},{1,17},{17,1},{33,49},{49,33},{2,18}... | collective-permute-start | bytes 983048 | tf_op jit(solution)/shard_map/ppermute | solution.py:165
  68.9 8.3 %collective-permute-start.13 = (bf16[32,5120]{1,0:T(8,128)(2,1)S(1)}, bf16[32,5120]{1,0:T(8,128)(2,1)S(1)}, u32[]{:S(2)}, u32[]{:S(2)}) collective-permute-start(bf16[32,5120]{1,0:T(8,128)(2,1)S(1)} %get-tuple-element.54), channel_id=1, source_target_pairs={{0,6},{2,4},{4,2},{6,0},{1,7},{3,5},{5,3},{7,1},{8,14},{10,12},{12... | collective-permute-start | bytes 983048 | tf_op jit(solution)/shard_map/ppermute | solution.py:165
  70.6 7.1 %collective-permute-start.14 = (bf16[32,5120]{1,0:T(8,128)(2,1)S(1)}, bf16[32,5120]{1,0:T(8,128)(2,1)S(1)}, u32[]{:S(2)}, u32[]{:S(2)}) collective-permute-start(bf16[32,5120]{1,0:T(8,128)(2,1)S(1)} %get-tuple-element.55), channel_id=1, source_target_pairs={{0,2},{2,0},{4,6},{6,4},{1,3},{3,1},{5,7},{7,5},{8,10},{10,8},{12,... | collective-permute-start | bytes 983048 | tf_op jit(solution)/shard_map/ppermute | solution.py:165
  78.6 10.0 %collective-permute-start.16 = (bf16[256,5120]{1,0:T(8,128)(2,1)S(1)}, bf16[256,5120]{1,0:T(8,128)(2,1)S(1)}, u32[]{:S(2)}, u32[]{:S(2)}) collective-permute-start(bf16[256,5120]{1,0:T(8,128)(2,1)S(1)} %whole.3.refs_1_), channel_id=1, source_target_pairs={{0,64},{64,0},{1,65},{65,1},{2,66},{66,2},{3,67},{67,3},{4,68},{68... | collective-permute-start | bytes 7864328 | tf_op jit(solution)/shard_map/ppermute | solution.py:46
  80.1 8.6 %collective-permute-start.15 = (bf16[256,5120]{1,0:T(8,128)(2,1)S(1)}, bf16[256,5120]{1,0:T(8,128)(2,1)S(1)}, u32[]{:S(2)}, u32[]{:S(2)}) collective-permute-start(bf16[256,5120]{1,0:T(8,128)(2,1)S(1)} %whole.2.refs_0_), channel_id=1, source_target_pairs={{0,64},{64,0},{1,65},{65,1},{2,66},{66,2},{3,67},{67,3},{4,68},{68... | collective-permute-start | bytes 7864328 | tf_op jit(solution)/shard_map/ppermute | solution.py:46
  90.2 18.9 %copy-start.12 = (f32[256]{0:T(256)S(1)}, f32[256]{0:T(256)}, u32[]{:S(2)}) copy-start(f32[256]{0:T(256)} %param.23) | copy-start | bytes 3076
  98.9 1.2 collective-permute-start.17
  100.9 19.2 %all-to-all-start = ((f32[64,8,128]{2,1,0:T(8,128)}), f32[64,8,128]{2,1,0:T(8,128)S(1)}, u32[]{:S(2)}, u32[]{:S(2)}) async-start(f32[64,8,128]{2,1,0:T(8,128)} %chip_stats.1), calls=%async_computation | async-start | bytes 524288 | tf_op jit(solution)/shard_map/all_to_all | solution.py:50
  123.5 2.7 collective-permute-start.18
  128.6 24.2 %all-to-all-start.1 = ((bf16[64,16,512]{2,1,0:T(8,128)(2,1)}), bf16[64,16,512]{2,1,0:T(8,128)(2,1)S(1)}, u32[]{:S(2)}, u32[]{:S(2)}) async-start(bf16[64,16,512]{2,1,0:T(8,128)(2,1)} %join.2), calls=%async_computation.1 | async-start | bytes 2097152 | tf_op jit(solution)/shard_map/all_to_all | solution.py:50
  133.3 19.4 %copy-start.6 = (bf16[2,4096]{1,0:T(2,128)(2,1)S(1)}, bf16[2,4096]{1,0:T(2,128)(2,1)}, u32[]{:S(2)}) copy-start(bf16[2,4096]{1,0:T(2,128)(2,1)} %states_ref.1) | copy-start | bytes 49156
  133.3 19.4 %copy-start.9 = (bf16[4096]{0:T(1024)(128)(2,1)S(1)}, bf16[4096]{0:T(1024)(128)(2,1)}, u32[]{:S(2)}) copy-start(bf16[4096]{0:T(1024)(128)(2,1)} %param.16) | copy-start | bytes 24580
  133.3 170.2 %all-reduce.2.cloned.1.call-start = ((), (), s32[]{:S(2)}) async-start(), calls=%async_computation.4 | async-start | bytes 8388608 | tf_op jit(solution)/shard_map/psum | solution.py:650
  134.1 169.5 %copy-start.3 = (bf16[4096,112]{0,1:T(8,128)(2,1)S(1)}, bf16[4096,112]{0,1:T(8,128)(2,1)}, u32[]{:S(2)}) copy-start(bf16[4096,112]{0,1:T(8,128)(2,1)} %param.20) | copy-start | bytes 2752516
  134.1 169.5 %copy-start.4 = (bf16[4096,112]{0,1:T(8,128)(2,1)S(1)}, bf16[4096,112]{0,1:T(8,128)(2,1)}, u32[]{:S(2)}) copy-start(bf16[4096,112]{0,1:T(8,128)(2,1)} %param.21) | copy-start | bytes 2752516
  134.1 169.5 %copy-start.8 = (bf16[4096]{0:T(1024)(128)(2,1)S(1)}, bf16[4096]{0:T(1024)(128)(2,1)}, u32[]{:S(2)}) copy-start(bf16[4096]{0:T(1024)(128)(2,1)} %param.19) | copy-start | bytes 24580
  177.3 130.2 %collective-permute-start.19 = (bf16[64,16,512]{2,1,0:T(8,128)(2,1)S(1)}, bf16[64,16,512]{2,1,0:T(8,128)(2,1)}, u32[]{:S(2)}, u32[]{:S(2)}) collective-permute-start(bf16[64,16,512]{2,1,0:T(8,128)(2,1)S(1)} %all_to_all.20.own_ref), channel_id=1, source_target_pairs={{0,64},{64,0},{1,65},{65,1},{2,66},{66,2},{3,67},{67,3},{4,68},{68... | collective-permute-start | bytes 3145736 | tf_op jit(solution)/shard_map/ppermute | solution.py:46
  311.8 2.7 collective-permute-start.20
  316.9 26.7 %all-to-all-start.3 = ((bf16[64,16,512]{2,1,0:T(8,128)(2,1)}), bf16[64,16,512]{2,1,0:T(8,128)(2,1)S(1)}, u32[]{:S(2)}, u32[]{:S(2)}) async-start(bf16[64,16,512]{2,1,0:T(8,128)(2,1)} %join.3), calls=%async_computation.3 | async-start | bytes 2097152 | tf_op jit(solution)/shard_map/all_to_all | solution.py:50
  (6 other events, 9.8 us)
Sparse Core Ops, SparseCore 0:
  139.1 164.4 all-reduce.1

commit v8 on v6

--- a/solution.py
+++ b/solution.py
@@ -130,9 +130,9 @@
         groups_kernel,
         "pairs",
         [shape_of((tokens, part.shape[1])) for part in parts[::2]],
-        limit=2,
+        limit=4,
         in_specs=[SMEM] + [ANY] * len(parts),
-        out_specs=[ANY] * (len(parts) // 2),
+        out_specs=[VMEM] * (len(parts) // 2),
         scratch_shapes=[pltpu.SemaphoreType.DMA((len(parts),))],
     )(bits, *parts)
 
@@ -154,9 +154,9 @@
         halves_kernel,
         "halves",
         [shape_of((p.shape[0] // 2, p.shape[1])) for p in pieces],
-        limit=2,
+        limit=4,
         in_specs=[ANY] * len(pieces),
-        out_specs=[ANY] * len(pieces),
+        out_specs=[VMEM] * len(pieces),
         scratch_shapes=[pltpu.SemaphoreType.DMA((len(pieces),))],
     )(*pieces)
 
@@ -186,9 +186,9 @@
         whole_kernel,
         "whole",
         shape_of((4 * tokens, width)),
-        limit=2,
+        limit=6,
         in_specs=[SMEM] + [ANY] * 5,
-        out_specs=ANY,
+        out_specs=VMEM,
         scratch_shapes=[pltpu.SemaphoreType.DMA((5,))],
     )(place, *pieces)
 
@@ -488,21 +488,24 @@
     return jnp.sum(blocks_ref[...].astype(jnp.float32), axis=0)
 
 
-def embed_kernel(blocks_ref, gain_ref, embedded_ref, out_ref):
+def embed_kernel(blocks_ref, gain_ref, embedded_ref, rows_ref):
     values = block_sum(blocks_ref)
     embedded_ref[...] = values
-    rows = (values * block_inverse(values) * block_gain(gain_ref)).astype(jnp.bfloat16)
-    out_ref[...] = jnp.broadcast_to(rows[None], out_ref.shape)
-
-
-def final_kernel(blocks_ref, states_ref, gain_ref, grad_ref, out_ref, states):
+    rows = values * block_inverse(values) * block_gain(gain_ref)
+    rows_ref[...] = rows.astype(jnp.bfloat16)
+
+
+def final_kernel(blocks_ref, states_ref, gain_ref, rows_ref, grad_ref, out_ref, states):
     for i in range(SEGMENTS):
         part = states_ref[:, i * SEGMENT : (i + 1) * SEGMENT].astype(jnp.float32)
         for t in range(2):
             states[t * SEGMENTS + i : t * SEGMENTS + i + 1, :] = part[t : t + 1]
     grad = block_back(block_sum(blocks_ref), states[...], block_gain(gain_ref))
     grad_ref[...] = grad
-    out_ref[...] = jnp.broadcast_to(grad.astype(jnp.bfloat16)[None], out_ref.shape)
+    height = 2 * SEGMENTS
+    half = (out_ref.shape[0], height, SEGMENT)
+    out_ref[:, :height, :] = jnp.broadcast_to(grad.astype(jnp.bfloat16)[None], half)
+    out_ref[:, height:, :] = jnp.broadcast_to(rows_ref[...][None], half)
 
 
 def state_kernel(blocks_ref, grad_ref, embedded_ref, gain_ref, out_ref):
@@ -518,46 +521,28 @@
 BLOCK = (2 * SEGMENTS, SEGMENT)
 
 
-def spread_rows(refs, scratches):
-    for ref, rows in zip(refs, scratches):
-        values = ref[...].astype(jnp.float32)
-        values = values.reshape(values.shape[0] * values.shape[1], values.shape[2])
-        for k in range(SEGMENT // 128):
-            rows[k] = values[:, k * 128 : (k + 1) * 128]
-
-
-def segment_rows(scratches, segment):
+def segment_rows(rows, first):
+    height = 4 * SEGMENTS
     parts = []
-    for rows in scratches:
-        height = 2 * SEGMENTS
-        for t in range(2):
-            at = pl.ds(t * SEGMENTS + segment, rows.shape[1] // height, stride=height)
-            parts.append(
-                jnp.concatenate([rows[k, at, :] for k in range(SEGMENT // 128)], axis=1)
-            )
+    for t in range(2):
+        at = pl.ds(first + t * SEGMENTS, rows.shape[1] // height, stride=height)
+        parts.append(jnp.concatenate([rows[k, at, :] for k in range(SEGMENT // 128)], axis=1))
     return jnp.concatenate(parts, axis=0).astype(jnp.bfloat16)
 
 
-def gate_kernel(own_ref, other_ref, gate_ref, up_ref, out_ref, *scratches):
-    spread_rows((own_ref, other_ref), scratches)
-    total = None
+def ffn_grad_kernel(blocks_ref, down_ref, gate_ref, up_ref, out_ref, rows):
+    values = blocks_ref[...].astype(jnp.float32)
+    values = values.reshape(values.shape[0] * values.shape[1], values.shape[2])
+    for k in range(SEGMENT // 128):
+        rows[k] = values[:, k * 128 : (k + 1) * 128]
+    units = down_ref.shape[0]
+    hidden, act_grad = None, None
     for i in range(SEGMENTS):
         columns = slice(i * SEGMENT, (i + 1) * SEGMENT)
         weight = jnp.concatenate([gate_ref[:, columns], up_ref[:, columns]], axis=0)
-        term = row_product(weight, segment_rows(scratches, i))
-        total = term if total is None else total + term
-    out_ref[...] = total
-
-
-def ffn_grad_kernel(
-    own_ref, other_ref, down_ref, hidden_ref, gate_ref, up_ref, own_out, send_out, *scratches
-):
-    spread_rows((own_ref, other_ref), scratches)
-    units = down_ref.shape[0]
-    hidden, act_grad = hidden_ref[...], None
-    for i in range(SEGMENTS):
-        columns = slice(i * SEGMENT, (i + 1) * SEGMENT)
-        term = row_product(down_ref[:, columns], segment_rows(scratches, i))
+        term = row_product(weight, segment_rows(rows, 2 * SEGMENTS + i))
+        hidden = term if hidden is None else hidden + term
+        term = row_product(down_ref[:, columns], segment_rows(rows, i))
         act_grad = term if act_grad is None else act_grad + term
     gate, upper = hidden[:units, :], hidden[units:, :]
     sigmoid_gate = jax.nn.sigmoid(gate)
@@ -573,22 +558,20 @@
         columns = slice(i * SEGMENT, (i + 1) * SEGMENT)
         weight = jnp.concatenate([gate_ref[:, columns], up_ref[:, columns]], axis=0)
         out = jnp.dot(grads, weight, preferred_element_type=jnp.float32)
-        own_out[:, columns] = out[: tokens // 2]
-        send_out[:, columns] = out[tokens // 2 :].astype(jnp.bfloat16)
-
-
-def ffn_part(body, name, out_shape, blocks, *others):
-    rows = blocks.shape[0] * blocks.shape[1]
-    scratch = pltpu.VMEM((SEGMENT // 128, rows, 128), jnp.float32)
-    return kernel_call(
-        body,
-        name,
-        out_shape,
+        out_ref[:, columns] = out.astype(out_ref.dtype)
+
+
+def ffn_grad_part(blocks, dtype, *weights):
+    chips, height, _ = blocks.shape
+    return kernel_call(
+        ffn_grad_kernel,
+        "ffn_grad",
+        shape_of((2 * chips, SEGMENTS * SEGMENT), dtype),
         limit=20,
-        in_specs=[VMEM] * (2 + len(others)),
-        out_specs=[VMEM] * len(out_shape),
-        scratch_shapes=[scratch, scratch],
-    )(blocks, swap_cores(blocks), *others)
+        in_specs=[VMEM] * (1 + len(weights)),
+        out_specs=VMEM,
+        scratch_shapes=[pltpu.VMEM((SEGMENT // 128, chips * height, 128), jnp.float32)],
+    )(blocks, *weights)
 
 
 def shards(
@@ -636,19 +619,16 @@
     )(own_core, teacher_states, teacher_gain, student_states, student_gain)
     (rows,) = in_pair(own_core, keep, swap_cores(send), (width,))
 
-    place = jnp.stack([core, device]).astype(jnp.int32)
-    own, send = pick_part(place, token_ids.reshape(1, 256), student_head_t)
     (rows,) = in_pair((y & 1).reshape(1), rows, along(rows, ("yh", "yl"), 1), (width,))
-    came = along(rows, ("yh", "yl"), 3)
-    came, picked = lax.optimization_barrier((came, join_part(own, swap_cores(send))))
-    picked = exchange(picked, CHIPS)
-    first, second = in_pair((y >> 1).reshape(1), rows, came, WIDTHS)
+    first, second = in_pair((y >> 1).reshape(1), rows, along(rows, ("yh", "yl"), 3), WIDTHS)
     for bit, mask in ((0, 1), (1, 3)):
         came = (along(first, "z", mask), along(second, "x", mask))
         bits = (jnp.stack([z, x]) >> bit) & 1
         first, second = in_pairs(bits, (first, came[0], second, came[1]))
     came = [along(first, "x", 1), along(first, "x", 3), along(second, "z", 1), along(second, "z", 3)]
-    came, picked = lax.optimization_barrier((came, picked))
+    place = jnp.stack([core, device]).astype(jnp.int32)
+    own, send = pick_part(place, token_ids.reshape(1, 256), student_head_t)
+    came, picked = lax.optimization_barrier((came, join_part(own, swap_cores(send))))
     halves = halves_of(came)
     far = [
         along(half, line, mask)
@@ -659,15 +639,14 @@
         whole_rows(x.reshape(1), [first] + came[:2] + far[:2]),
         whole_rows(z.reshape(1), [second] + came[2:] + far[2:]),
     )
+    rows, picked = lax.optimization_barrier((rows, picked))
     embedded, ffn_rows = kernel_call(
         embed_kernel,
         "embed",
-        [shape_of(BLOCK, jnp.float32), shape_of(picked.shape)],
+        [shape_of(BLOCK, jnp.float32), shape_of(BLOCK)],
         in_specs=[VMEM] * 2,
         out_specs=[VMEM] * 2,
-    )(picked, ffn_gain)
-    rows, ffn_rows = lax.optimization_barrier((rows, ffn_rows))
-    ffn_rows = exchange(ffn_rows, CHIPS)
+    )(exchange(picked, CHIPS), ffn_gain)
     others = tuple(swap_cores(part) for part in rows)
     sums = logits_part(own_core, rows, heads)
     student, teacher, stats = logits_part(1 - own_core, others, heads, sums)
@@ -686,32 +665,21 @@
         own_core, every, weight, teacher, student, student_head_t
     )
     divergence = divergence.reshape(4, 4, 2, 2, 2, 2).transpose(4, 0, 2, 1, 3, 5).reshape(256)
-    blocks = join_part(own, swap_cores(send))
-    (hidden,) = ffn_part(
-        gate_kernel, "gate_upper", [shape_of((224, 256), jnp.float32)], ffn_rows, gate_t, up_t
-    )
-    blocks, hidden = lax.optimization_barrier((blocks, hidden))
-    blocks = exchange(blocks, CHIPS)
+    blocks = exchange(join_part(own, swap_cores(send)), CHIPS)
     final_grad, blocks = kernel_call(
         final_kernel,
         "final",
-        [shape_of(BLOCK, jnp.float32), shape_of(blocks.shape)],
-        in_specs=[VMEM] * 3,
+        [shape_of(BLOCK, jnp.float32), shape_of((64, 2 * BLOCK[0], BLOCK[1]))],
+        limit=12,
+        in_specs=[VMEM] * 4,
         out_specs=[VMEM] * 2,
         scratch_shapes=[pltpu.VMEM(BLOCK, jnp.float32)],
-    )(blocks, student_states, student_gain)
+    )(blocks, student_states, student_gain, ffn_rows)
     blocks = exchange(blocks, CHIPS)
-    shape = (128, 4096)
-    own, send = ffn_part(
-        ffn_grad_kernel,
-        "ffn_grad",
-        [shape_of(shape, jnp.float32), shape_of(shape)],
-        blocks,
-        down_weight,
-        hidden,
-        gate_t,
-        up_t,
-    )
+    weights = (down_weight, gate_t, up_t)
+    others = swap_cores(blocks)
+    own = ffn_grad_part(blocks, jnp.float32, *weights)
+    send = ffn_grad_part(others, jnp.bfloat16, *weights)
     ffn_grad = exchange(join_part(own, swap_cores(send)), CHIPS)
     state_grad = kernel_call(
         state_kernel,

time: 275 us -> 244 us (0.89)
  Pallas kernels: 87.8 us -> 50.7 us
  waiting for transfers between devices: 74.9 us -> 105 us
  starting transfers between devices: 58.5 us -> 45.3 us
  blocking collectives: 46.6 us -> 33.6 us
  local copies, waits for them, and re-layouts: 4.46 us -> 7.47 us
    pallas_call x4, Pallas kernels: 48.1 us -> 10.4 us  [the longest x2 8.62 us: ffn_grad_part(): kernel_call(ffn_grad_kernel, 'ffn_grad', shape_of((2 * chips, SEGMENTS *...]
    all_to_all x4, waiting for transfers between devices: 27.7 us -> 62.1 us  [exchange(): return lax.all_to_all(blocks, axes, split_axis=0, concat_axis=0, tiled=True)]
    all_to_all x2 -> x1, blocking collectives: 46.6 us -> 33.6 us  [exchange(): return lax.all_to_all(blocks, axes, split_axis=0, concat_axis=0, tiled=True)]
    all_to_all x4, starting transfers between devices: 33.6 us -> 23.5 us  [exchange(): return lax.all_to_all(blocks, axes, split_axis=0, concat_axis=0, tiled=True)]
    ppermute x14, waiting for transfers between devices: 39.8 us -> 35.8 us  [along(): return lax.ppermute(block, line, [(i, i ^ mask) for i in range(4)])]
    unnamed x30 -> x26, local copies, waits for them, and re-layouts: 2.67 us -> 5.68 us
    ppermute x9 -> x8, waiting for transfers between devices: 7.43 us -> 6.75 us  [swap_cores(): return lax.ppermute(values, 'core', [(0, 1), (1, 0)])]
  transfers between devices with their start and end apart: 27 -> 26, of which waited for: 15 -> 17; matrix products, arithmetic and copies ran while one was open for 1% -> 1% of each run, Pallas kernels for 12% -> 10%
where the time goes in v8:
time: 244 us
  waiting for transfers between devices  105 us (43%)
  Pallas kernels  50.7 us (21%)
  starting transfers between devices  45.3 us (19%)
  blocking collectives  33.6 us (14%)
  local copies, waits for them, and re-layouts  7.47 us (3%)
    all_to_all x4, waiting for transfers between devices, exchange(): return lax.all_to_all(blocks, axes, split_axis=0, concat_axis=0, tiled=True)  62.1 us
    ppermute x14, waiting for transfers between devices, along(): return lax.ppermute(block, line, [(i, i ^ mask) for i in range(4)])  35.8 us
    all_to_all x1, blocking collectives, exchange(): return lax.all_to_all(blocks, axes, split_axis=0, concat_axis=0, tiled=True)  33.6 us
    all_to_all x4, starting transfers between devices, exchange(): return lax.all_to_all(blocks, axes, split_axis=0, concat_axis=0, tiled=True)  23.5 us
    ppermute x14, starting transfers between devices, along(): return lax.ppermute(block, line, [(i, i ^ mask) for i in range(4)])  20.8 us
    pallas_call x2, Pallas kernels, logits_part(): kernel_call(functools.partial(logits_kernel, last), 'logits', out_shape,...  17 us
    pallas_call x2, Pallas kernels, ffn_grad_part(): kernel_call(ffn_grad_kernel, 'ffn_grad', shape_of((2 * chips, SEGMENTS *...  8.62 us
    pallas_call x3, Pallas kernels, join_part(): kernel_call(join_kernel, 'join', shape_of((chips, height * len(pairs) //...  8.06 us
  transfers between devices with their start and end apart: 26, of which 17 were waited for; matrix products, arithmetic and copies ran while one was open for 1% of the time, Pallas kernels for 10%

profile of v8, /device:TPU:0, one launch (start us, length us, event | category | flops | bytes accessed | tf_op | source)
XLA Modules:
  0.0 243.7 jit_solution(4220323018050128290)
XLA Ops:
  0.6 1.9 rows.1
  6.6 2.9 %collective-permute-done.1.came_ref = bf16[4,10240]{1,0:T(4,128)(2,1)S(1)} collective-permute-done((bf16[4,10240]{1,0:T(4,128)(2,1)S(1)}, bf16[4,10240]{1,0:T(4,128)(2,1)S(1)}, u32[]{:S(2)}, u32[]{:S(2)}) %collective-permute-start.1) | collective-permute-done | bytes 81952 | tf_op jit(solution)/shard_map/ppermute | solution.py:165
  9.5 3.2 %collective-permute-start.2 = (bf16[8,10240]{1,0:T(8,128)(2,1)S(1)}, bf16[8,10240]{1,0:T(8,128)(2,1)S(1)}, u32[]{:S(2)}, u32[]{:S(2)}) collective-permute-start(bf16[8,10240]{1,0:T(8,128)(2,1)S(1)} %pair.4.own_ref), channel_id=1, source_target_pairs={{0,9},{1,8},{8,1},{9,0},{2,11},{3,10},{10,3},{11,2},{4,13},{5,12},... | collective-permute-start | bytes 491528 | tf_op jit(solution)/shard_map/ppermute | solution.py:165
  12.7 3.7 %collective-permute-done.2.came_ref = bf16[8,10240]{1,0:T(8,128)(2,1)S(1)} collective-permute-done((bf16[8,10240]{1,0:T(8,128)(2,1)S(1)}, bf16[8,10240]{1,0:T(8,128)(2,1)S(1)}, u32[]{:S(2)}, u32[]{:S(2)}) %collective-permute-start.2) | collective-permute-done | bytes 163872 | tf_op jit(solution)/shard_map/ppermute | solution.py:165
  16.5 2.0 collective-permute-start.3
  20.7 3.6 %pick.1 = (bf16[128,4096]{1,0:T(8,128)(2,1)S(1)}, bf16[128,4096]{1,0:T(8,128)(2,1)S(1)}) custom-call(s32[2]{0:T(128)S(1)} %pad_add_fusion.1.place_ref, s32[1,256]{1,0:T(1,128)S(1)} %bitcast.24, bf16[501,4096]{1,0:T(8,128)(2,1)} %bitcast.27), custom_call_target="tpu_custom_call" | custom-call | flops 1 | bytes 1 | tf_op jit(solution)/shard_map/pick/pallas_call | solution.py:408
  25.9 2.6 %collective-permute-start.5 = (bf16[32,5120]{1,0:T(8,128)(2,1)S(1)}, bf16[32,5120]{1,0:T(8,128)(2,1)S(1)}, u32[]{:S(2)}, u32[]{:S(2)}) collective-permute-start(bf16[32,5120]{1,0:T(8,128)(2,1)S(1)} %get-tuple-element.45.refs_0_), channel_id=1, source_target_pairs={{0,6},{2,4},{4,2},{6,0},{1,7},{3,5},{5,3},{7,1},{8,14},{10,12},{12... | collective-permute-start | bytes 983048 | tf_op jit(solution)/shard_map/ppermute | solution.py:165
  28.5 2.1 collective-permute-start.6
  30.7 6.6 %collective-permute-done.5.refs_1_ = bf16[32,5120]{1,0:T(8,128)(2,1)S(1)} collective-permute-done((bf16[32,5120]{1,0:T(8,128)(2,1)S(1)}, bf16[32,5120]{1,0:T(8,128)(2,1)S(1)}, u32[]{:S(2)}, u32[]{:S(2)}) %collective-permute-start.5) | collective-permute-done | bytes 327712 | tf_op jit(solution)/shard_map/ppermute | solution.py:165
  37.3 2.2 collective-permute-done.6.refs_3_
  40.6 2.2 collective-permute-start.8
  44.2 2.3 join.3
  46.4 11.5 %collective-permute-done.8.refs_1_.refs_2_ = bf16[64,5120]{1,0:T(8,128)(2,1)S(1)} collective-permute-done((bf16[64,5120]{1,0:T(8,128)(2,1)S(1)}, bf16[64,5120]{1,0:T(8,128)(2,1)S(1)}, u32[]{:S(2)}, u32[]{:S(2)}) %collective-permute-start.8) | collective-permute-done | bytes 655392 | tf_op jit(solution)/shard_map/ppermute | solution.py:165
  62.6 1.7 collective-permute-start.14
  64.3 5.0 %collective-permute-done.12.refs_3_ = bf16[32,5120]{1,0:T(8,128)(2,1)S(1)} collective-permute-done((bf16[32,5120]{1,0:T(8,128)(2,1)S(1)}, bf16[32,5120]{1,0:T(8,128)(2,1)S(1)}, u32[]{:S(2)}, u32[]{:S(2)}) %collective-permute-start.12) | collective-permute-done | bytes 327712 | tf_op jit(solution)/shard_map/ppermute | solution.py:165
  74.7 8.3 %logits.2 = (f32[501,256]{1,0:T(8,128)S(1)}, f32[501,256]{1,0:T(8,128)S(1)}, f32[501,256]{1,0:T(8,128)S(1)}) custom-call(s32[1]{0:T(128)} %bitcast.core_ref.place_ref, bf16[256,5120]{1,0:T(8,128)(2,1)S(1)} %whole.2.refs_0_, bf16[256,5120]{1,0:T(8,128)(2,1)} %copy-done, bf16[501,4096]{1,0:T(8,128)(2,1)} %bitcast.28, bf16[501,16384]{1,0:T(8,128)(2,1)} %bitcast.25), custom_call_target="tpu_custom_call" | custom-call | flops 1 | bytes 1 | tf_op jit(solution)/shard_map/logits/pallas_call | solution.py:290
  84.5 8.7 %logits.3 = (f32[501,256]{1,0:T(8,128)S(1)}, f32[501,256]{1,0:T(8,128)S(1)}, f32[8,128]{1,0:T(8,128)S(1)}) custom-call(s32[1]{0:T(128)S(6)} %sub.3.place_ref, bf16[256,5120]{1,0:T(8,128)(2,1)S(1)} %collective-permute-done.16.refs_0_, bf16[256,5120]{1,0:T(8,128)(2,1)} %copy-done.11, bf16[501,4096]{1,0:T(8,128)(2,1)} %bitcast.29, bf16[501,16384]{1,0:T(8,128)(2,1)} %bitcast.26, ...), custom_call_target="tpu_custom_call" | custom-call | flops 1 | bytes 1 | tf_op jit(solution)/shard_map/logits/pallas_call | solution.py:290
  95.9 8.0 %all-to-all-start = ((f32[64,8,128]{2,1,0:T(8,128)}), f32[64,8,128]{2,1,0:T(8,128)S(1)}, u32[]{:S(2)}, u32[]{:S(2)}) async-start(f32[64,8,128]{2,1,0:T(8,128)} %chip_stats.1), calls=%async_computation | async-start | bytes 524288 | tf_op jit(solution)/shard_map/all_to_all | solution.py:50
  104.3 10.5 %all-to-all-done.every_ref = f32[64,8,128]{2,1,0:T(8,128)S(1)} async-done(((f32[64,8,128]{2,1,0:T(8,128)}), f32[64,8,128]{2,1,0:T(8,128)S(1)}, u32[]{:S(2)}, u32[]{:S(2)}) %all-to-all-start) | async-done | bytes 262176 | tf_op jit(solution)/shard_map/all_to_all | solution.py:50
  115.8 4.4 %row_grad.1 = (f32[128,4096]{1,0:T(8,128)S(1)}, bf16[128,4096]{1,0:T(8,128)(2,1)}, f32[1,256]{1,0:T(1,128)S(1)}) custom-call(s32[1]{0:T(128)} %bitcast.core_ref.place_ref, f32[64,8,128]{2,1,0:T(8,128)S(1)} %all-to-all-done.every_ref, f32[1,256]{1,0:T(1,128)S(1)} %reshape.45.weight_ref, f32[501,256]{1,0:T(8,128)S(1)} %copy-done.5, ...), custom_call_target="tpu_custom_call" | custom-call | flops 1 | bytes 1 | tf_op jit(solution)/shard_map/row_grad/pallas_call | solution.py:369
  120.3 4.7 %all-to-all-start.2 = ((bf16[64,16,512]{2,1,0:T(8,128)(2,1)}), bf16[64,16,512]{2,1,0:T(8,128)(2,1)S(1)}, u32[]{:S(2)}, u32[]{:S(2)}) async-start(bf16[64,16,512]{2,1,0:T(8,128)(2,1)} %join.3), calls=%async_computation.2 | async-start | bytes 2097152 | tf_op jit(solution)/shard_map/all_to_all | solution.py:50
  125.1 3.5 %join.4 = bf16[64,16,512]{2,1,0:T(8,128)(2,1)} custom-call(f32[128,4096]{1,0:T(8,128)S(1)} %get-tuple-element.73.refs_0_, bf16[128,4096]{1,0:T(8,128)(2,1)} %collective-permute-done.19.refs_1_), custom_call_target="tpu_custom_call" | custom-call | flops 1 | bytes 1 | tf_op jit(solution)/shard_map/join/pallas_call | solution.py:444
  128.6 16.1 %all-to-all-done.2.blocks_ref = bf16[64,16,512]{2,1,0:T(8,128)(2,1)S(1)} async-done(((bf16[64,16,512]{2,1,0:T(8,128)(2,1)}), bf16[64,16,512]{2,1,0:T(8,128)(2,1)S(1)}, u32[]{:S(2)}, u32[]{:S(2)}) %all-to-all-start.2) | async-done | bytes 1048608 | tf_op jit(solution)/shard_map/all_to_all | solution.py:50
  144.7 4.9 %all-to-all-start.1 = ((bf16[64,16,512]{2,1,0:T(8,128)(2,1)}), bf16[64,16,512]{2,1,0:T(8,128)(2,1)S(1)}, u32[]{:S(2)}, u32[]{:S(2)}) async-start(bf16[64,16,512]{2,1,0:T(8,128)(2,1)} %join.4), calls=%async_computation.1 | async-start | bytes 2097152 | tf_op jit(solution)/shard_map/all_to_all | solution.py:50
  149.9 18.3 %all-to-all-done.1.blocks_ref = bf16[64,16,512]{2,1,0:T(8,128)(2,1)S(1)} async-done(((bf16[64,16,512]{2,1,0:T(8,128)(2,1)}), bf16[64,16,512]{2,1,0:T(8,128)(2,1)S(1)}, u32[]{:S(2)}, u32[]{:S(2)}) %all-to-all-start.1) | async-done | bytes 1048608 | tf_op jit(solution)/shard_map/all_to_all | solution.py:50
  168.6 33.6 %all_to_all.25.blocks_ref = bf16[64,32,512]{2,1,0:T(8,128)(2,1)S(1)} all-to-all(bf16[64,32,512]{2,1,0:T(8,128)(2,1)S(1)} %get-tuple-element.77), channel_id=1, replica_groups=mesh['core'=2,'x'=4,'yh'=2,'z'=4,'yl'=2] {'x','yh','z','yl'}, dimensions={0} | all-to-all | bytes 4194304 | tf_op jit(solution)/shard_map/all_to_all | solution.py:50
  202.2 4.2 %collective-permute-done.20.blocks_ref = bf16[64,32,512]{2,1,0:T(8,128)(2,1)S(1)} collective-permute-done((bf16[64,32,512]{2,1,0:T(8,128)(2,1)S(1)}, bf16[64,32,512]{2,1,0:T(8,128)(2,1)S(1)}, u32[]{:S(2)}, u32[]{:S(2)}) %collective-permute-start.20) | collective-permute-done | bytes 2097184 | tf_op jit(solution)/shard_map/ppermute | solution.py:46
  206.4 4.3 %ffn_grad.3 = bf16[128,4096]{1,0:T(8,128)(2,1)S(1)} custom-call(bf16[64,32,512]{2,1,0:T(8,128)(2,1)S(1)} %collective-permute-done.20.blocks_ref, bf16[112,4096]{1,0:T(8,128)(2,1)S(1)} %copy-done.1, bf16[112,4096]{1,0:T(8,128)(2,1)S(1)} %bitcast.16, bf16[112,4096]{1,0:T(8,128)(2,1)S(1)} %bitcast.18), custom_call_target="tpu_custom_call" | custom-call | flops 1 | bytes 1 | tf_op jit(solution)/shard_map/ffn_grad/pallas_call | solution.py:566
  210.9 4.3 %ffn_grad.2.refs_0_ = f32[128,4096]{1,0:T(8,128)S(1)} custom-call(bf16[64,32,512]{2,1,0:T(8,128)(2,1)S(1)} %all_to_all.25.blocks_ref, bf16[112,4096]{1,0:T(8,128)(2,1)S(1)} %copy-done.1, bf16[112,4096]{1,0:T(8,128)(2,1)S(1)} %bitcast.17, bf16[112,4096]{1,0:T(8,128)(2,1)S(1)} %bitcast.19), custom_call_target="tpu_custom_call" | custom-call | flops 1 | bytes 1 | tf_op jit(solution)/shard_map/ffn_grad/pallas_call | solution.py:566
  215.2 2.3 join.5
  217.5 5.9 %all-to-all-start.4 = ((bf16[64,16,512]{2,1,0:T(8,128)(2,1)}), bf16[64,16,512]{2,1,0:T(8,128)(2,1)S(1)}, u32[]{:S(2)}, u32[]{:S(2)}) async-start(bf16[64,16,512]{2,1,0:T(8,128)(2,1)} %join.5), calls=%async_computation.4 | async-start | bytes 2097152 | tf_op jit(solution)/shard_map/all_to_all | solution.py:50
  225.5 17.2 %all-to-all-done.4.blocks_ref = bf16[64,16,512]{2,1,0:T(8,128)(2,1)S(1)} async-done(((bf16[64,16,512]{2,1,0:T(8,128)(2,1)}), bf16[64,16,512]{2,1,0:T(8,128)(2,1)S(1)}, u32[]{:S(2)}, u32[]{:S(2)}) %all-to-all-start.4) | async-done | bytes 1048608 | tf_op jit(solution)/shard_map/all_to_all | solution.py:50
  (80 shorter events, 30.2 us)
Async XLA Ops:
  2.5 1.5 collective-permute-start
  4.9 4.6 %collective-permute-start.1 = (bf16[4,10240]{1,0:T(4,128)(2,1)S(1)}, bf16[4,10240]{1,0:T(4,128)(2,1)S(1)}, u32[]{:S(2)}, u32[]{:S(2)}) collective-permute-start(bf16[4,10240]{1,0:T(4,128)(2,1)S(1)} %pair.3.own_ref), channel_id=1, source_target_pairs={{0,1},{1,0},{8,9},{9,8},{2,3},{3,2},{10,11},{11,10},{4,5},{5,4},{1... | collective-permute-start | bytes 245768 | tf_op jit(solution)/shard_map/ppermute | solution.py:165
  9.5 6.9 %collective-permute-start.2 = (bf16[8,10240]{1,0:T(8,128)(2,1)S(1)}, bf16[8,10240]{1,0:T(8,128)(2,1)S(1)}, u32[]{:S(2)}, u32[]{:S(2)}) collective-permute-start(bf16[8,10240]{1,0:T(8,128)(2,1)S(1)} %pair.4.own_ref), channel_id=1, source_target_pairs={{0,9},{1,8},{8,1},{9,0},{2,11},{3,10},{10,3},{11,2},{4,13},{5,12},... | collective-permute-start | bytes 491528 | tf_op jit(solution)/shard_map/ppermute | solution.py:165
  16.5 8.0 %collective-permute-start.3 = (bf16[16,5120]{1,0:T(8,128)(2,1)S(1)}, bf16[16,5120]{1,0:T(8,128)(2,1)S(1)}, u32[]{:S(2)}, u32[]{:S(2)}) collective-permute-start(bf16[16,5120]{1,0:T(8,128)(2,1)S(1)} %get-tuple-element.43.refs_0_), channel_id=1, source_target_pairs={{0,2},{2,0},{4,6},{6,4},{1,3},{3,1},{5,7},{7,5},{8,10},{10,8},{12,... | collective-permute-start | bytes 491528 | tf_op jit(solution)/shard_map/ppermute | solution.py:165
  18.5 6.0 %collective-permute-start.4 = (bf16[16,5120]{1,0:T(8,128)(2,1)S(1)}, bf16[16,5120]{1,0:T(8,128)(2,1)S(1)}, u32[]{:S(2)}, u32[]{:S(2)}) collective-permute-start(bf16[16,5120]{1,0:T(8,128)(2,1)S(1)} %get-tuple-element.44.refs_2_), channel_id=1, source_target_pairs={{0,16},{16,0},{32,48},{48,32},{1,17},{17,1},{33,49},{49,33},{2,18}... | collective-permute-start | bytes 491528 | tf_op jit(solution)/shard_map/ppermute | solution.py:165
  24.3 19.9 %collective-permute-start.11 = (bf16[128,4096]{1,0:T(8,128)(2,1)S(1)}, bf16[128,4096]{1,0:T(8,128)(2,1)S(1)}, u32[]{:S(2)}, u32[]{:S(2)}) collective-permute-start(bf16[128,4096]{1,0:T(8,128)(2,1)S(1)} %get-tuple-element.50), channel_id=1, source_target_pairs={{0,64},{64,0},{1,65},{65,1},{2,66},{66,2},{3,67},{67,3},{4,68},{68... | collective-permute-start | bytes 3145736 | tf_op jit(solution)/shard_map/ppermute | solution.py:46
  25.9 11.4 %collective-permute-start.5 = (bf16[32,5120]{1,0:T(8,128)(2,1)S(1)}, bf16[32,5120]{1,0:T(8,128)(2,1)S(1)}, u32[]{:S(2)}, u32[]{:S(2)}) collective-permute-start(bf16[32,5120]{1,0:T(8,128)(2,1)S(1)} %get-tuple-element.45.refs_0_), channel_id=1, source_target_pairs={{0,6},{2,4},{4,2},{6,0},{1,7},{3,5},{5,3},{7,1},{8,14},{10,12},{12... | collective-permute-start | bytes 983048 | tf_op jit(solution)/shard_map/ppermute | solution.py:165
  28.5 11.0 %collective-permute-start.6 = (bf16[32,5120]{1,0:T(8,128)(2,1)S(1)}, bf16[32,5120]{1,0:T(8,128)(2,1)S(1)}, u32[]{:S(2)}, u32[]{:S(2)}) collective-permute-start(bf16[32,5120]{1,0:T(8,128)(2,1)S(1)} %get-tuple-element.46.refs_2_), channel_id=1, source_target_pairs={{0,48},{16,32},{32,16},{48,0},{1,49},{17,33},{33,17},{49,1},{2,50}... | collective-permute-start | bytes 983048 | tf_op jit(solution)/shard_map/ppermute | solution.py:165
  40.6 17.3 %collective-permute-start.8 = (bf16[64,5120]{1,0:T(8,128)(2,1)S(1)}, bf16[64,5120]{1,0:T(8,128)(2,1)S(1)}, u32[]{:S(2)}, u32[]{:S(2)}) collective-permute-start(bf16[64,5120]{1,0:T(8,128)(2,1)S(1)} %get-tuple-element.47.refs_0_), channel_id=1, source_target_pairs={{0,48},{16,32},{32,16},{48,0},{1,49},{17,33},{33,17},{49,1},{2,50}... | collective-permute-start | bytes 1966088 | tf_op jit(solution)/shard_map/ppermute | solution.py:165
  42.8 15.8 %collective-permute-start.7 = (bf16[64,5120]{1,0:T(8,128)(2,1)S(1)}, bf16[64,5120]{1,0:T(8,128)(2,1)S(1)}, u32[]{:S(2)}, u32[]{:S(2)}) collective-permute-start(bf16[64,5120]{1,0:T(8,128)(2,1)S(1)} %get-tuple-element.47.refs_0_), channel_id=1, source_target_pairs={{0,16},{16,0},{32,48},{48,32},{1,17},{17,1},{33,49},{49,33},{2,18}... | collective-permute-start | bytes 1966088 | tf_op jit(solution)/shard_map/ppermute | solution.py:165
  42.8 17.0 %collective-permute-start.10 = (bf16[64,5120]{1,0:T(8,128)(2,1)S(1)}, bf16[64,5120]{1,0:T(8,128)(2,1)S(1)}, u32[]{:S(2)}, u32[]{:S(2)}) collective-permute-start(bf16[64,5120]{1,0:T(8,128)(2,1)S(1)} %get-tuple-element.48.refs_0_), channel_id=1, source_target_pairs={{0,6},{2,4},{4,2},{6,0},{1,7},{3,5},{5,3},{7,1},{8,14},{10,12},{12... | collective-permute-start | bytes 1966088 | tf_op jit(solution)/shard_map/ppermute | solution.py:165
  43.6 16.1 %collective-permute-start.9 = (bf16[64,5120]{1,0:T(8,128)(2,1)S(1)}, bf16[64,5120]{1,0:T(8,128)(2,1)S(1)}, u32[]{:S(2)}, u32[]{:S(2)}) collective-permute-start(bf16[64,5120]{1,0:T(8,128)(2,1)S(1)} %get-tuple-element.48.refs_0_), channel_id=1, source_target_pairs={{0,2},{2,0},{4,6},{6,4},{1,3},{3,1},{5,7},{7,5},{8,10},{10,8},{12,... | collective-permute-start | bytes 1966088 | tf_op jit(solution)/shard_map/ppermute | solution.py:165
  60.2 9.1 %collective-permute-start.12 = (bf16[32,5120]{1,0:T(8,128)(2,1)S(1)}, bf16[32,5120]{1,0:T(8,128)(2,1)S(1)}, u32[]{:S(2)}, u32[]{:S(2)}) collective-permute-start(bf16[32,5120]{1,0:T(8,128)(2,1)S(1)} %get-tuple-element.55), channel_id=1, source_target_pairs={{0,48},{16,32},{32,16},{48,0},{1,49},{17,33},{33,17},{49,1},{2,50}... | collective-permute-start | bytes 983048 | tf_op jit(solution)/shard_map/ppermute | solution.py:165
  61.4 7.9 %collective-permute-start.13 = (bf16[32,5120]{1,0:T(8,128)(2,1)S(1)}, bf16[32,5120]{1,0:T(8,128)(2,1)S(1)}, u32[]{:S(2)}, u32[]{:S(2)}) collective-permute-start(bf16[32,5120]{1,0:T(8,128)(2,1)S(1)} %get-tuple-element.56), channel_id=1, source_target_pairs={{0,16},{16,0},{32,48},{48,32},{1,17},{17,1},{33,49},{49,33},{2,18}... | collective-permute-start | bytes 983048 | tf_op jit(solution)/shard_map/ppermute | solution.py:165
  62.6 8.3 %collective-permute-start.14 = (bf16[32,5120]{1,0:T(8,128)(2,1)S(1)}, bf16[32,5120]{1,0:T(8,128)(2,1)S(1)}, u32[]{:S(2)}, u32[]{:S(2)}) collective-permute-start(bf16[32,5120]{1,0:T(8,128)(2,1)S(1)} %get-tuple-element.57), channel_id=1, source_target_pairs={{0,6},{2,4},{4,2},{6,0},{1,7},{3,5},{5,3},{7,1},{8,14},{10,12},{12... | collective-permute-start | bytes 983048 | tf_op jit(solution)/shard_map/ppermute | solution.py:165
  64.3 7.1 %collective-permute-start.15 = (bf16[32,5120]{1,0:T(8,128)(2,1)S(1)}, bf16[32,5120]{1,0:T(8,128)(2,1)S(1)}, u32[]{:S(2)}, u32[]{:S(2)}) collective-permute-start(bf16[32,5120]{1,0:T(8,128)(2,1)S(1)} %get-tuple-element.58), channel_id=1, source_target_pairs={{0,2},{2,0},{4,6},{6,4},{1,3},{3,1},{5,7},{7,5},{8,10},{10,8},{12,... | collective-permute-start | bytes 983048 | tf_op jit(solution)/shard_map/ppermute | solution.py:165
  73.2 9.8 %collective-permute-start.16 = (bf16[256,5120]{1,0:T(8,128)(2,1)S(1)}, bf16[256,5120]{1,0:T(8,128)(2,1)S(1)}, u32[]{:S(2)}, u32[]{:S(2)}) collective-permute-start(bf16[256,5120]{1,0:T(8,128)(2,1)S(1)} %whole.2.refs_0_), channel_id=1, source_target_pairs={{0,64},{64,0},{1,65},{65,1},{2,66},{66,2},{3,67},{67,3},{4,68},{68... | collective-permute-start | bytes 7864328 | tf_op jit(solution)/shard_map/ppermute | solution.py:46
  73.3 9.7 %collective-permute-start.17 = (bf16[256,5120]{1,0:T(8,128)(2,1)S(1)}, bf16[256,5120]{1,0:T(8,128)(2,1)S(1)}, u32[]{:S(2)}, u32[]{:S(2)}) collective-permute-start(bf16[256,5120]{1,0:T(8,128)(2,1)S(1)} %whole.3.refs_1_), channel_id=1, source_target_pairs={{0,64},{64,0},{1,65},{65,1},{2,66},{66,2},{3,67},{67,3},{4,68},{68... | collective-permute-start | bytes 7864328 | tf_op jit(solution)/shard_map/ppermute | solution.py:46
  94.0 1.2 collective-permute-start.18
  95.9 18.9 %all-to-all-start = ((f32[64,8,128]{2,1,0:T(8,128)}), f32[64,8,128]{2,1,0:T(8,128)S(1)}, u32[]{:S(2)}, u32[]{:S(2)}) async-start(f32[64,8,128]{2,1,0:T(8,128)} %chip_stats.1), calls=%async_computation | async-start | bytes 524288 | tf_op jit(solution)/shard_map/all_to_all | solution.py:50
  120.2 4.8 %collective-permute-start.19 = (bf16[128,4096]{1,0:T(8,128)(2,1)}, bf16[128,4096]{1,0:T(8,128)(2,1)}, u32[]{:S(2)}, u32[]{:S(2)}) collective-permute-start(bf16[128,4096]{1,0:T(8,128)(2,1)} %get-tuple-element.74), channel_id=1, source_target_pairs={{0,64},{64,0},{1,65},{65,1},{2,66},{66,2},{3,67},{67,3},{4,68},{68... | collective-permute-start | bytes 3145736 | tf_op jit(solution)/shard_map/ppermute | solution.py:46
  120.3 24.4 %all-to-all-start.2 = ((bf16[64,16,512]{2,1,0:T(8,128)(2,1)}), bf16[64,16,512]{2,1,0:T(8,128)(2,1)S(1)}, u32[]{:S(2)}, u32[]{:S(2)}) async-start(bf16[64,16,512]{2,1,0:T(8,128)(2,1)} %join.3), calls=%async_computation.2 | async-start | bytes 2097152 | tf_op jit(solution)/shard_map/all_to_all | solution.py:50
  125.0 24.5 %copy-start.8 = (bf16[4096]{0:T(1024)(128)(2,1)S(1)}, bf16[4096]{0:T(1024)(128)(2,1)}, u32[]{:S(2)}) copy-start(bf16[4096]{0:T(1024)(128)(2,1)} %param.19) | copy-start | bytes 24580
  128.6 39.6 %copy-start.6 = (bf16[2,4096]{1,0:T(2,128)(2,1)S(1)}, bf16[2,4096]{1,0:T(2,128)(2,1)}, u32[]{:S(2)}) copy-start(bf16[2,4096]{1,0:T(2,128)(2,1)} %states_ref.1) | copy-start | bytes 49156
  128.6 39.6 %copy-start.9 = (bf16[4096]{0:T(1024)(128)(2,1)S(1)}, bf16[4096]{0:T(1024)(128)(2,1)}, u32[]{:S(2)}) copy-start(bf16[4096]{0:T(1024)(128)(2,1)} %param.16) | copy-start | bytes 24580
  144.7 23.5 %all-to-all-start.1 = ((bf16[64,16,512]{2,1,0:T(8,128)(2,1)}), bf16[64,16,512]{2,1,0:T(8,128)(2,1)S(1)}, u32[]{:S(2)}, u32[]{:S(2)}) async-start(bf16[64,16,512]{2,1,0:T(8,128)(2,1)} %join.4), calls=%async_computation.1 | async-start | bytes 2097152 | tf_op jit(solution)/shard_map/all_to_all | solution.py:50
  168.2 38.2 %copy-start.1 = (bf16[112,4096]{1,0:T(8,128)(2,1)S(1)}, bf16[112,4096]{1,0:T(8,128)(2,1)}, u32[]{:S(2)}) copy-start(bf16[112,4096]{1,0:T(8,128)(2,1)} %down_ref.3) | copy-start | bytes 2752516
  168.2 38.2 %copy-start.2 = (bf16[4096,112]{0,1:T(8,128)(2,1)S(1)}, bf16[4096,112]{0,1:T(8,128)(2,1)}, u32[]{:S(2)}) copy-start(bf16[4096,112]{0,1:T(8,128)(2,1)} %param.20) | copy-start | bytes 2752516
  168.2 38.2 %copy-start.3 = (bf16[4096,112]{0,1:T(8,128)(2,1)S(1)}, bf16[4096,112]{0,1:T(8,128)(2,1)}, u32[]{:S(2)}) copy-start(bf16[4096,112]{0,1:T(8,128)(2,1)} %param.21) | copy-start | bytes 2752516
  202.2 4.2 %collective-permute-start.20 = (bf16[64,32,512]{2,1,0:T(8,128)(2,1)S(1)}, bf16[64,32,512]{2,1,0:T(8,128)(2,1)S(1)}, u32[]{:S(2)}, u32[]{:S(2)}) collective-permute-start(bf16[64,32,512]{2,1,0:T(8,128)(2,1)S(1)} %all_to_all.25.blocks_ref), channel_id=1, source_target_pairs={{0,64},{64,0},{1,65},{65,1},{2,66},{66,2},{3,67},{67,3},{4,68},{68... | collective-permute-start | bytes 6291464 | tf_op jit(solution)/shard_map/ppermute | solution.py:46
  210.7 4.5 %collective-permute-start.21 = (bf16[128,4096]{1,0:T(8,128)(2,1)S(1)}, bf16[128,4096]{1,0:T(8,128)(2,1)S(1)}, u32[]{:S(2)}, u32[]{:S(2)}) collective-permute-start(bf16[128,4096]{1,0:T(8,128)(2,1)S(1)} %ffn_grad.3), channel_id=1, source_target_pairs={{0,64},{64,0},{1,65},{65,1},{2,66},{66,2},{3,67},{67,3},{4,68},{68... | collective-permute-start | bytes 3145736 | tf_op jit(solution)/shard_map/ppermute | solution.py:46
  217.5 25.2 %all-to-all-start.4 = ((bf16[64,16,512]{2,1,0:T(8,128)(2,1)}), bf16[64,16,512]{2,1,0:T(8,128)(2,1)S(1)}, u32[]{:S(2)}, u32[]{:S(2)}) async-start(bf16[64,16,512]{2,1,0:T(8,128)(2,1)} %join.5), calls=%async_computation.4 | async-start | bytes 2097152 | tf_op jit(solution)/shard_map/all_to_all | solution.py:50
  (7 other events, 25.7 us)

commit v9 on v6

--- a/solution.py
+++ b/solution.py
@@ -130,9 +130,9 @@
         groups_kernel,
         "pairs",
         [shape_of((tokens, part.shape[1])) for part in parts[::2]],
-        limit=2,
+        limit=4,
         in_specs=[SMEM] + [ANY] * len(parts),
-        out_specs=[ANY] * (len(parts) // 2),
+        out_specs=[VMEM] * (len(parts) // 2),
         scratch_shapes=[pltpu.SemaphoreType.DMA((len(parts),))],
     )(bits, *parts)
 
@@ -154,9 +154,9 @@
         halves_kernel,
         "halves",
         [shape_of((p.shape[0] // 2, p.shape[1])) for p in pieces],
-        limit=2,
+        limit=4,
         in_specs=[ANY] * len(pieces),
-        out_specs=[ANY] * len(pieces),
+        out_specs=[VMEM] * len(pieces),
         scratch_shapes=[pltpu.SemaphoreType.DMA((len(pieces),))],
     )(*pieces)
 
@@ -186,9 +186,9 @@
         whole_kernel,
         "whole",
         shape_of((4 * tokens, width)),
-        limit=2,
+        limit=6,
         in_specs=[SMEM] + [ANY] * 5,
-        out_specs=ANY,
+        out_specs=VMEM,
         scratch_shapes=[pltpu.SemaphoreType.DMA((5,))],
     )(place, *pieces)
 
@@ -636,25 +636,25 @@
     )(own_core, teacher_states, teacher_gain, student_states, student_gain)
     (rows,) = in_pair(own_core, keep, swap_cores(send), (width,))
 
+    (rows,) = in_pair((y & 1).reshape(1), rows, along(rows, ("yh", "yl"), 1), (width,))
+    first, second = in_pair((y >> 1).reshape(1), rows, along(rows, ("yh", "yl"), 3), WIDTHS)
+    bits = jnp.stack([z, x])
+    came = (along(first, "z", 1), along(second, "x", 1))
+    first, second = in_pairs(bits & 1, (first, came[0], second, came[1]))
+    came = (along(first, "z", 3), along(second, "x", 3))
     place = jnp.stack([core, device]).astype(jnp.int32)
     own, send = pick_part(place, token_ids.reshape(1, 256), student_head_t)
-    (rows,) = in_pair((y & 1).reshape(1), rows, along(rows, ("yh", "yl"), 1), (width,))
-    came = along(rows, ("yh", "yl"), 3)
     came, picked = lax.optimization_barrier((came, join_part(own, swap_cores(send))))
+    first, second = in_pairs(bits >> 1, (first, came[0], second, came[1]))
+    came = [along(first, "x", 1), along(first, "x", 3), along(second, "z", 1), along(second, "z", 3)]
     picked = exchange(picked, CHIPS)
-    first, second = in_pair((y >> 1).reshape(1), rows, came, WIDTHS)
-    for bit, mask in ((0, 1), (1, 3)):
-        came = (along(first, "z", mask), along(second, "x", mask))
-        bits = (jnp.stack([z, x]) >> bit) & 1
-        first, second = in_pairs(bits, (first, came[0], second, came[1]))
-    came = [along(first, "x", 1), along(first, "x", 3), along(second, "z", 1), along(second, "z", 3)]
-    came, picked = lax.optimization_barrier((came, picked))
+    came = lax.optimization_barrier(came)
     halves = halves_of(came)
     far = [
         along(half, line, mask)
         for half, line, mask in zip(halves, ("x", "x", "z", "z"), (3, 1, 3, 1))
     ]
-    far = lax.optimization_barrier(far)
+    far, picked = lax.optimization_barrier((far, picked))
     rows = (
         whole_rows(x.reshape(1), [first] + came[:2] + far[:2]),
         whole_rows(z.reshape(1), [second] + came[2:] + far[2:]),

time: 275 us -> 243 us (0.88)
  Pallas kernels: 87.8 us -> 48.8 us
  local copies, waits for them, and re-layouts: 4.46 us -> 15.5 us
    pallas_call x2, Pallas kernels: 42.1 us -> 3.26 us  [whole_rows(): kernel_call(whole_kernel, 'whole', shape_of((4 * tokens, width)), limit=6...]
    unnamed x30 -> x66, local copies, waits for them, and re-layouts: 2.67 us -> 13.7 us
    all_to_all x4, starting transfers between devices: 33.6 us -> 29.8 us  [exchange(): return lax.all_to_all(blocks, axes, split_axis=0, concat_axis=0, tiled=True)]
  transfers between devices with their start and end apart: 27 -> 27, of which waited for: 15 -> 17; matrix products, arithmetic and copies ran while one was open for 1% -> 1% of each run, Pallas kernels for 12% -> 14%
where the time goes in v9:
time: 243 us; the launch traced here: 242 us
  waiting for transfers between devices  72.3 us (30%)
  starting transfers between devices  56.4 us (23%)
  Pallas kernels  48.8 us (20%)
  blocking collectives  46.6 us (19%)
  local copies, waits for them, and re-layouts  15.5 us (6%)
    all_to_all x2, blocking collectives, exchange(): return lax.all_to_all(blocks, axes, split_axis=0, concat_axis=0, tiled=True)  46.6 us
    ppermute x14, waiting for transfers between devices, along(): return lax.ppermute(block, line, [(i, i ^ mask) for i in range(4)])  37.4 us
    all_to_all x4, starting transfers between devices, exchange(): return lax.all_to_all(blocks, axes, split_axis=0, concat_axis=0, tiled=True)  29.8 us
    all_to_all x4, waiting for transfers between devices, exchange(): return lax.all_to_all(blocks, axes, split_axis=0, concat_axis=0, tiled=True)  27.7 us
    ppermute x14, starting transfers between devices, along(): return lax.ppermute(block, line, [(i, i ^ mask) for i in range(4)])  25 us
    pallas_call x2, Pallas kernels, logits_part(): kernel_call(functools.partial(logits_kernel, last), 'logits', out_shape,...  18.1 us
    unnamed x66, local copies, waits for them, and re-layouts  13.7 us
    ppermute x9, waiting for transfers between devices, swap_cores(): return lax.ppermute(values, 'core', [(0, 1), (1, 0)])  7.22 us
  transfers between devices with their start and end apart: 27, of which 17 were waited for; matrix products, arithmetic and copies ran while one was open for 1% of the time, Pallas kernels for 14%

profile of v9, /device:TPU:0, one launch (start us, length us, event | category | flops | bytes accessed | tf_op | source)
XLA Modules:
  0.0 241.6 jit_solution(635551839445886991)
XLA Ops:
  1.4 4.6 %pick.1 = (bf16[128,4096]{1,0:T(8,128)(2,1)S(1)}, bf16[128,4096]{1,0:T(8,128)(2,1)}) custom-call(s32[2]{0:T(128)S(1)} %pad_add_fusion.1.place_ref, s32[1,256]{1,0:T(1,128)S(1)} %bitcast.24, bf16[501,4096]{1,0:T(8,128)(2,1)} %bitcast.27), custom_call_target="tpu_custom_call" | custom-call | flops 1 | bytes 1 | tf_op jit(solution)/shard_map/pick/pallas_call | solution.py:408
  12.2 3.0 %collective-permute-done.1.came_ref = bf16[4,10240]{1,0:T(4,128)(2,1)S(1)} collective-permute-done((bf16[4,10240]{1,0:T(4,128)(2,1)S(1)}, bf16[4,10240]{1,0:T(4,128)(2,1)S(1)}, u32[]{:S(2)}, u32[]{:S(2)}) %collective-permute-start.1) | collective-permute-done | bytes 81952 | tf_op jit(solution)/shard_map/ppermute | solution.py:165
  15.3 3.2 %collective-permute-start.2 = (bf16[8,10240]{1,0:T(8,128)(2,1)S(1)}, bf16[8,10240]{1,0:T(8,128)(2,1)S(1)}, u32[]{:S(2)}, u32[]{:S(2)}) collective-permute-start(bf16[8,10240]{1,0:T(8,128)(2,1)S(1)} %pair.4.own_ref), channel_id=1, source_target_pairs={{0,9},{1,8},{8,1},{9,0},{2,11},{3,10},{10,3},{11,2},{4,13},{5,12},... | collective-permute-start | bytes 491528 | tf_op jit(solution)/shard_map/ppermute | solution.py:165
  18.5 3.9 %collective-permute-done.2.came_ref = bf16[8,10240]{1,0:T(8,128)(2,1)S(1)} collective-permute-done((bf16[8,10240]{1,0:T(8,128)(2,1)S(1)}, bf16[8,10240]{1,0:T(8,128)(2,1)S(1)}, u32[]{:S(2)}, u32[]{:S(2)}) %collective-permute-start.2) | collective-permute-done | bytes 163872 | tf_op jit(solution)/shard_map/ppermute | solution.py:165
  22.5 2.0 collective-permute-start.3
  31.2 2.6 %collective-permute-start.5 = (bf16[32,5120]{1,0:T(8,128)(2,1)S(1)}, bf16[32,5120]{1,0:T(8,128)(2,1)S(1)}, u32[]{:S(2)}, u32[]{:S(2)}) collective-permute-start(bf16[32,5120]{1,0:T(8,128)(2,1)S(1)} %get-tuple-element.52.refs_0_), channel_id=1, source_target_pairs={{0,6},{2,4},{4,2},{6,0},{1,7},{3,5},{5,3},{7,1},{8,14},{10,12},{12... | collective-permute-start | bytes 983048 | tf_op jit(solution)/shard_map/ppermute | solution.py:165
  33.8 2.8 %collective-permute-start.6 = (bf16[32,5120]{1,0:T(8,128)(2,1)S(1)}, bf16[32,5120]{1,0:T(8,128)(2,1)S(1)}, u32[]{:S(2)}, u32[]{:S(2)}) collective-permute-start(bf16[32,5120]{1,0:T(8,128)(2,1)S(1)} %get-tuple-element.53.refs_2_), channel_id=1, source_target_pairs={{0,48},{16,32},{32,16},{48,0},{1,49},{17,33},{33,17},{49,1},{2,50}... | collective-permute-start | bytes 983048 | tf_op jit(solution)/shard_map/ppermute | solution.py:165
  36.6 2.3 join.3
  39.7 2.4 %collective-permute-done.6.refs_3_ = bf16[32,5120]{1,0:T(8,128)(2,1)S(1)} collective-permute-done((bf16[32,5120]{1,0:T(8,128)(2,1)S(1)}, bf16[32,5120]{1,0:T(8,128)(2,1)S(1)}, u32[]{:S(2)}, u32[]{:S(2)}) %collective-permute-start.6) | collective-permute-done | bytes 327712 | tf_op jit(solution)/shard_map/ppermute | solution.py:165
  42.9 8.1 %all-to-all-start = ((bf16[64,16,512]{2,1,0:T(8,128)(2,1)}), bf16[64,16,512]{2,1,0:T(8,128)(2,1)S(1)}, u32[]{:S(2)}, u32[]{:S(2)}) async-start(bf16[64,16,512]{2,1,0:T(8,128)(2,1)} %join.3), calls=%async_computation | async-start | bytes 2097152 | tf_op jit(solution)/shard_map/all_to_all | solution.py:50
  54.7 2.1 collective-permute-start.11
  59.0 2.2 collective-permute-start.9
  61.2 14.2 %collective-permute-done.10.refs_2_.refs_1_ = bf16[64,5120]{1,0:T(8,128)(2,1)S(1)} collective-permute-done((bf16[64,5120]{1,0:T(8,128)(2,1)S(1)}, bf16[64,5120]{1,0:T(8,128)(2,1)S(1)}, u32[]{:S(2)}, u32[]{:S(2)}) %collective-permute-start.10) | collective-permute-done | bytes 655392 | tf_op jit(solution)/shard_map/ppermute | solution.py:165
  75.5 2.1 collective-permute-done.11.refs_3_.refs_2_
  78.0 2.2 collective-permute-start.12
  81.9 6.0 %collective-permute-done.12.refs_3_ = bf16[32,5120]{1,0:T(8,128)(2,1)S(1)} collective-permute-done((bf16[32,5120]{1,0:T(8,128)(2,1)S(1)}, bf16[32,5120]{1,0:T(8,128)(2,1)S(1)}, u32[]{:S(2)}, u32[]{:S(2)}) %collective-permute-start.12) | collective-permute-done | bytes 327712 | tf_op jit(solution)/shard_map/ppermute | solution.py:165
  98.8 2.4 whole.2.refs_0_
  102.5 6.9 %all-to-all-start.2 = ((bf16[64,16,512]{2,1,0:T(8,128)(2,1)}), bf16[64,16,512]{2,1,0:T(8,128)(2,1)}, u32[]{:S(2)}, u32[]{:S(2)}) async-start(bf16[64,16,512]{2,1,0:T(8,128)(2,1)} %copy-done.11), calls=%async_computation.2 | async-start | bytes 2097152 | tf_op jit(solution)/shard_map/all_to_all | solution.py:50
  109.5 8.7 %logits.2 = (f32[501,256]{1,0:T(8,128)S(1)}, f32[501,256]{1,0:T(8,128)S(1)}, f32[501,256]{1,0:T(8,128)S(1)}) custom-call(s32[1]{0:T(128)} %bitcast.core_ref.place_ref, bf16[256,5120]{1,0:T(8,128)(2,1)} %whole.2.refs_0_, bf16[256,5120]{1,0:T(8,128)(2,1)} %copy-done, bf16[501,4096]{1,0:T(8,128)(2,1)} %bitcast.28, bf16[501,16384]{1,0:T(8,128)(2,1)} %bitcast.25), custom_call_target="tpu_custom_call" | custom-call | flops 1 | bytes 1 | tf_op jit(solution)/shard_map/logits/pallas_call | solution.py:290
  118.3 9.4 %logits.3 = (f32[501,256]{1,0:T(8,128)S(1)}, f32[501,256]{1,0:T(8,128)S(1)}, f32[8,128]{1,0:T(8,128)S(1)}) custom-call(s32[1]{0:T(128)S(6)} %sub.3.place_ref, bf16[256,5120]{1,0:T(8,128)(2,1)} %collective-permute-done.16.refs_0_, bf16[256,5120]{1,0:T(8,128)(2,1)} %collective-permute-done.17.refs_1_, bf16[501,4096]{1,0:T(8,128)(2,1)} %bitcast.29, ...), custom_call_target="tpu_custom_call" | custom-call | flops 1 | bytes 1 | tf_op jit(solution)/shard_map/logits/pallas_call | solution.py:290
  129.6 10.1 %all-to-all-start.1 = ((f32[64,8,128]{2,1,0:T(8,128)}), f32[64,8,128]{2,1,0:T(8,128)S(1)}, u32[]{:S(2)}, u32[]{:S(2)}) async-start(f32[64,8,128]{2,1,0:T(8,128)} %chip_stats.1), calls=%async_computation.1 | async-start | bytes 524288 | tf_op jit(solution)/shard_map/all_to_all | solution.py:50
  140.2 10.4 %all-to-all-done.1.every_ref = f32[64,8,128]{2,1,0:T(8,128)S(1)} async-done(((f32[64,8,128]{2,1,0:T(8,128)}), f32[64,8,128]{2,1,0:T(8,128)S(1)}, u32[]{:S(2)}, u32[]{:S(2)}) %all-to-all-start.1) | async-done | bytes 262176 | tf_op jit(solution)/shard_map/all_to_all | solution.py:50
  150.6 3.6 %row_grad.1 = (f32[128,4096]{1,0:T(8,128)S(1)}, bf16[128,4096]{1,0:T(8,128)(2,1)S(1)}, f32[1,256]{1,0:T(1,128)S(1)}) custom-call(s32[1]{0:T(128)} %bitcast.core_ref.place_ref, f32[64,8,128]{2,1,0:T(8,128)S(1)} %all-to-all-done.1.every_ref, f32[1,256]{1,0:T(1,128)S(1)} %reshape.46.weight_ref, f32[501,256]{1,0:T(8,128)S(1)} %get-tuple-element.81.teacher_ref, ...), custom_call_target="tpu_custom_call" | custom-call | flops 1 | bytes 1 | tf_op jit(solution)/shard_map/row_grad/pallas_call | solution.py:369
  154.5 3.0 %gate_upper.1.hidden_ref = f32[224,256]{1,0:T(8,128)S(1)} custom-call(bf16[64,16,512]{2,1,0:T(8,128)(2,1)} %all-to-all-done.2.own_ref, bf16[64,16,512]{2,1,0:T(8,128)(2,1)S(1)} %collective-permute-done.20.other_ref, bf16[112,4096]{1,0:T(8,128)(2,1)S(1)} %bitcast.16, bf16[112,4096]{1,0:T(8,128)(2,1)S(1)} %bitcast.18), custom_call_target="tpu_custom_call" | custom-call | flops 1 | bytes 1 | tf_op jit(solution)/shard_map/gate_upper/pallas_call | solution.py:583
  158.9 24.1 %all_to_all.30.blocks_ref = bf16[64,16,512]{2,1,0:T(8,128)(2,1)S(1)} all-to-all(bf16[64,16,512]{2,1,0:T(8,128)(2,1)S(1)} %join.4), channel_id=1, replica_groups=mesh['core'=2,'x'=4,'yh'=2,'z'=4,'yl'=2] {'x','yh','z','yl'}, dimensions={0} | all-to-all | bytes 2097152 | tf_op jit(solution)/shard_map/all_to_all | solution.py:50
  183.4 22.5 %all_to_all.31.own_ref = bf16[64,16,512]{2,1,0:T(8,128)(2,1)S(1)} all-to-all(bf16[64,16,512]{2,1,0:T(8,128)(2,1)S(1)} %get-tuple-element.88), channel_id=1, replica_groups=mesh['core'=2,'x'=4,'yh'=2,'z'=4,'yl'=2] {'x','yh','z','yl'}, dimensions={0} | all-to-all | bytes 2097152 | tf_op jit(solution)/shard_map/all_to_all | solution.py:50
  205.8 2.7 %collective-permute-done.21.other_ref = bf16[64,16,512]{2,1,0:T(8,128)(2,1)S(1)} collective-permute-done((bf16[64,16,512]{2,1,0:T(8,128)(2,1)S(1)}, bf16[64,16,512]{2,1,0:T(8,128)(2,1)S(1)}, u32[]{:S(2)}, u32[]{:S(2)}) %collective-permute-start.21) | collective-permute-done | bytes 1048608 | tf_op jit(solution)/shard_map/ppermute | solution.py:46
  208.5 3.0 %ffn_grad.1 = (f32[128,4096]{1,0:T(8,128)S(1)}, bf16[128,4096]{1,0:T(8,128)(2,1)S(1)}) custom-call(bf16[64,16,512]{2,1,0:T(8,128)(2,1)S(1)} %all_to_all.31.own_ref, bf16[64,16,512]{2,1,0:T(8,128)(2,1)S(1)} %collective-permute-done.21.other_ref, bf16[112,4096]{1,0:T(8,128)(2,1)S(1)} %copy-done.12, f32[224,256]{1,0:T(8,128)S(1)} %gate_upper.1.hidden_ref, ...), custom_call_target="tpu_custom_call" | custom-call | flops 1 | bytes 1 | tf_op jit(solution)/shard_map/ffn_grad/pallas_call | solution.py:583
  211.8 2.5 %collective-permute-done.22.refs_1_ = bf16[128,4096]{1,0:T(8,128)(2,1)S(1)} collective-permute-done((bf16[128,4096]{1,0:T(8,128)(2,1)S(1)}, bf16[128,4096]{1,0:T(8,128)(2,1)S(1)}, u32[]{:S(2)}, u32[]{:S(2)}) %collective-permute-start.22) | collective-permute-done | bytes 1048608 | tf_op jit(solution)/shard_map/ppermute | solution.py:46
  214.3 2.3 join.5
  216.6 4.7 %all-to-all-start.5 = ((bf16[64,16,512]{2,1,0:T(8,128)(2,1)}), bf16[64,16,512]{2,1,0:T(8,128)(2,1)S(1)}, u32[]{:S(2)}, u32[]{:S(2)}) async-start(bf16[64,16,512]{2,1,0:T(8,128)(2,1)} %join.5), calls=%async_computation.5 | async-start | bytes 2097152 | tf_op jit(solution)/shard_map/all_to_all | solution.py:50
  223.4 17.3 %all-to-all-done.5.blocks_ref = bf16[64,16,512]{2,1,0:T(8,128)(2,1)S(1)} async-done(((bf16[64,16,512]{2,1,0:T(8,128)(2,1)}), bf16[64,16,512]{2,1,0:T(8,128)(2,1)S(1)}, u32[]{:S(2)}, u32[]{:S(2)}) %all-to-all-start.5) | async-done | bytes 1048608 | tf_op jit(solution)/shard_map/all_to_all | solution.py:50
  (123 shorter events, 43.4 us)
Async XLA Ops:
  6.0 30.6 %collective-permute-start.7 = (bf16[128,4096]{1,0:T(8,128)(2,1)}, bf16[128,4096]{1,0:T(8,128)(2,1)S(1)}, u32[]{:S(2)}, u32[]{:S(2)}) collective-permute-start(bf16[128,4096]{1,0:T(8,128)(2,1)} %get-tuple-element.55), channel_id=1, source_target_pairs={{0,64},{64,0},{1,65},{65,1},{2,66},{66,2},{3,67},{67,3},{4,68},{68... | collective-permute-start | bytes 3145736 | tf_op jit(solution)/shard_map/ppermute | solution.py:46
  8.0 1.7 collective-permute-start
  10.5 4.8 %collective-permute-start.1 = (bf16[4,10240]{1,0:T(4,128)(2,1)S(1)}, bf16[4,10240]{1,0:T(4,128)(2,1)S(1)}, u32[]{:S(2)}, u32[]{:S(2)}) collective-permute-start(bf16[4,10240]{1,0:T(4,128)(2,1)S(1)} %pair.3.own_ref), channel_id=1, source_target_pairs={{0,1},{1,0},{8,9},{9,8},{2,3},{3,2},{10,11},{11,10},{4,5},{5,4},{1... | collective-permute-start | bytes 245768 | tf_op jit(solution)/shard_map/ppermute | solution.py:165
  15.3 7.1 %collective-permute-start.2 = (bf16[8,10240]{1,0:T(8,128)(2,1)S(1)}, bf16[8,10240]{1,0:T(8,128)(2,1)S(1)}, u32[]{:S(2)}, u32[]{:S(2)}) collective-permute-start(bf16[8,10240]{1,0:T(8,128)(2,1)S(1)} %pair.4.own_ref), channel_id=1, source_target_pairs={{0,9},{1,8},{8,1},{9,0},{2,11},{3,10},{10,3},{11,2},{4,13},{5,12},... | collective-permute-start | bytes 491528 | tf_op jit(solution)/shard_map/ppermute | solution.py:165
  22.5 5.4 %collective-permute-start.3 = (bf16[16,5120]{1,0:T(8,128)(2,1)S(1)}, bf16[16,5120]{1,0:T(8,128)(2,1)S(1)}, u32[]{:S(2)}, u32[]{:S(2)}) collective-permute-start(bf16[16,5120]{1,0:T(8,128)(2,1)S(1)} %get-tuple-element.50.refs_0_), channel_id=1, source_target_pairs={{0,2},{2,0},{4,6},{6,4},{1,3},{3,1},{5,7},{7,5},{8,10},{10,8},{12,... | collective-permute-start | bytes 491528 | tf_op jit(solution)/shard_map/ppermute | solution.py:165
  24.5 5.3 %collective-permute-start.4 = (bf16[16,5120]{1,0:T(8,128)(2,1)S(1)}, bf16[16,5120]{1,0:T(8,128)(2,1)S(1)}, u32[]{:S(2)}, u32[]{:S(2)}) collective-permute-start(bf16[16,5120]{1,0:T(8,128)(2,1)S(1)} %get-tuple-element.51.refs_2_), channel_id=1, source_target_pairs={{0,16},{16,0},{32,48},{48,32},{1,17},{17,1},{33,49},{49,33},{2,18}... | collective-permute-start | bytes 491528 | tf_op jit(solution)/shard_map/ppermute | solution.py:165
  31.2 8.5 %collective-permute-start.5 = (bf16[32,5120]{1,0:T(8,128)(2,1)S(1)}, bf16[32,5120]{1,0:T(8,128)(2,1)S(1)}, u32[]{:S(2)}, u32[]{:S(2)}) collective-permute-start(bf16[32,5120]{1,0:T(8,128)(2,1)S(1)} %get-tuple-element.52.refs_0_), channel_id=1, source_target_pairs={{0,6},{2,4},{4,2},{6,0},{1,7},{3,5},{5,3},{7,1},{8,14},{10,12},{12... | collective-permute-start | bytes 983048 | tf_op jit(solution)/shard_map/ppermute | solution.py:165
  33.8 8.3 %collective-permute-start.6 = (bf16[32,5120]{1,0:T(8,128)(2,1)S(1)}, bf16[32,5120]{1,0:T(8,128)(2,1)S(1)}, u32[]{:S(2)}, u32[]{:S(2)}) collective-permute-start(bf16[32,5120]{1,0:T(8,128)(2,1)S(1)} %get-tuple-element.53.refs_2_), channel_id=1, source_target_pairs={{0,48},{16,32},{32,16},{48,0},{1,49},{17,33},{33,17},{49,1},{2,50}... | collective-permute-start | bytes 983048 | tf_op jit(solution)/shard_map/ppermute | solution.py:165
  42.9 49.2 %all-to-all-start = ((bf16[64,16,512]{2,1,0:T(8,128)(2,1)}), bf16[64,16,512]{2,1,0:T(8,128)(2,1)S(1)}, u32[]{:S(2)}, u32[]{:S(2)}) async-start(bf16[64,16,512]{2,1,0:T(8,128)(2,1)} %join.3), calls=%async_computation | async-start | bytes 2097152 | tf_op jit(solution)/shard_map/all_to_all | solution.py:50
  53.0 38.3 %copy-start.13 = (bf16[64,5120]{1,0:T(8,128)(2,1)}, bf16[64,5120]{1,0:T(8,128)(2,1)S(1)}, u32[]{:S(2)}) copy-start(bf16[64,5120]{1,0:T(8,128)(2,1)S(1)} %get-tuple-element.58.refs_0_) | copy-start | bytes 1966084
  53.0 22.5 %collective-permute-start.10 = (bf16[64,5120]{1,0:T(8,128)(2,1)S(1)}, bf16[64,5120]{1,0:T(8,128)(2,1)S(1)}, u32[]{:S(2)}, u32[]{:S(2)}) collective-permute-start(bf16[64,5120]{1,0:T(8,128)(2,1)S(1)} %get-tuple-element.59.refs_0_), channel_id=1, source_target_pairs={{0,2},{2,0},{4,6},{6,4},{1,3},{3,1},{5,7},{7,5},{8,10},{10,8},{12,... | collective-permute-start | bytes 1966088 | tf_op jit(solution)/shard_map/ppermute | solution.py:165
  54.7 22.9 %collective-permute-start.11 = (bf16[64,5120]{1,0:T(8,128)(2,1)S(1)}, bf16[64,5120]{1,0:T(8,128)(2,1)S(1)}, u32[]{:S(2)}, u32[]{:S(2)}) collective-permute-start(bf16[64,5120]{1,0:T(8,128)(2,1)S(1)} %get-tuple-element.59.refs_0_), channel_id=1, source_target_pairs={{0,6},{2,4},{4,2},{6,0},{1,7},{3,5},{5,3},{7,1},{8,14},{10,12},{12... | collective-permute-start | bytes 1966088 | tf_op jit(solution)/shard_map/ppermute | solution.py:165
  57.6 19.9 %collective-permute-start.8 = (bf16[64,5120]{1,0:T(8,128)(2,1)S(1)}, bf16[64,5120]{1,0:T(8,128)(2,1)S(1)}, u32[]{:S(2)}, u32[]{:S(2)}) collective-permute-start(bf16[64,5120]{1,0:T(8,128)(2,1)S(1)} %get-tuple-element.58.refs_0_), channel_id=1, source_target_pairs={{0,16},{16,0},{32,48},{48,32},{1,17},{17,1},{33,49},{49,33},{2,18}... | collective-permute-start | bytes 1966088 | tf_op jit(solution)/shard_map/ppermute | solution.py:165
  59.0 18.5 %collective-permute-start.9 = (bf16[64,5120]{1,0:T(8,128)(2,1)S(1)}, bf16[64,5120]{1,0:T(8,128)(2,1)S(1)}, u32[]{:S(2)}, u32[]{:S(2)}) collective-permute-start(bf16[64,5120]{1,0:T(8,128)(2,1)S(1)} %get-tuple-element.58.refs_0_), channel_id=1, source_target_pairs={{0,48},{16,32},{32,16},{48,0},{1,49},{17,33},{33,17},{49,1},{2,50}... | collective-permute-start | bytes 1966088 | tf_op jit(solution)/shard_map/ppermute | solution.py:165
  78.0 9.8 %collective-permute-start.12 = (bf16[32,5120]{1,0:T(8,128)(2,1)S(1)}, bf16[32,5120]{1,0:T(8,128)(2,1)S(1)}, u32[]{:S(2)}, u32[]{:S(2)}) collective-permute-start(bf16[32,5120]{1,0:T(8,128)(2,1)S(1)} %get-tuple-element.64), channel_id=1, source_target_pairs={{0,48},{16,32},{32,16},{48,0},{1,49},{17,33},{33,17},{49,1},{2,50}... | collective-permute-start | bytes 983048 | tf_op jit(solution)/shard_map/ppermute | solution.py:165
  80.2 8.9 %collective-permute-start.13 = (bf16[32,5120]{1,0:T(8,128)(2,1)S(1)}, bf16[32,5120]{1,0:T(8,128)(2,1)S(1)}, u32[]{:S(2)}, u32[]{:S(2)}) collective-permute-start(bf16[32,5120]{1,0:T(8,128)(2,1)S(1)} %get-tuple-element.65), channel_id=1, source_target_pairs={{0,16},{16,0},{32,48},{48,32},{1,17},{17,1},{33,49},{49,33},{2,18}... | collective-permute-start | bytes 983048 | tf_op jit(solution)/shard_map/ppermute | solution.py:165
  80.5 10.0 %collective-permute-start.14 = (bf16[32,5120]{1,0:T(8,128)(2,1)S(1)}, bf16[32,5120]{1,0:T(8,128)(2,1)S(1)}, u32[]{:S(2)}, u32[]{:S(2)}) collective-permute-start(bf16[32,5120]{1,0:T(8,128)(2,1)S(1)} %get-tuple-element.66), channel_id=1, source_target_pairs={{0,6},{2,4},{4,2},{6,0},{1,7},{3,5},{5,3},{7,1},{8,14},{10,12},{12... | collective-permute-start | bytes 983048 | tf_op jit(solution)/shard_map/ppermute | solution.py:165
  81.7 9.5 %collective-permute-start.15 = (bf16[32,5120]{1,0:T(8,128)(2,1)S(1)}, bf16[32,5120]{1,0:T(8,128)(2,1)S(1)}, u32[]{:S(2)}, u32[]{:S(2)}) collective-permute-start(bf16[32,5120]{1,0:T(8,128)(2,1)S(1)} %get-tuple-element.67), channel_id=1, source_target_pairs={{0,2},{2,0},{4,6},{6,4},{1,3},{3,1},{5,7},{7,5},{8,10},{10,8},{12,... | collective-permute-start | bytes 983048 | tf_op jit(solution)/shard_map/ppermute | solution.py:165
  101.5 16.7 %collective-permute-start.16 = (bf16[256,5120]{1,0:T(8,128)(2,1)}, bf16[256,5120]{1,0:T(8,128)(2,1)}, u32[]{:S(2)}, u32[]{:S(2)}) collective-permute-start(bf16[256,5120]{1,0:T(8,128)(2,1)} %whole.2.refs_0_), channel_id=1, source_target_pairs={{0,64},{64,0},{1,65},{65,1},{2,66},{66,2},{3,67},{67,3},{4,68},{68... | collective-permute-start | bytes 7864328 | tf_op jit(solution)/shard_map/ppermute | solution.py:46
  102.5 15.7 %collective-permute-start.17 = (bf16[256,5120]{1,0:T(8,128)(2,1)S(1)}, bf16[256,5120]{1,0:T(8,128)(2,1)}, u32[]{:S(2)}, u32[]{:S(2)}) collective-permute-start(bf16[256,5120]{1,0:T(8,128)(2,1)S(1)} %whole.3.refs_1_), channel_id=1, source_target_pairs={{0,64},{64,0},{1,65},{65,1},{2,66},{66,2},{3,67},{67,3},{4,68},{68... | collective-permute-start | bytes 7864328 | tf_op jit(solution)/shard_map/ppermute | solution.py:46
  102.5 27.1 %all-to-all-start.2 = ((bf16[64,16,512]{2,1,0:T(8,128)(2,1)}), bf16[64,16,512]{2,1,0:T(8,128)(2,1)}, u32[]{:S(2)}, u32[]{:S(2)}) async-start(bf16[64,16,512]{2,1,0:T(8,128)(2,1)} %copy-done.11), calls=%async_computation.2 | async-start | bytes 2097152 | tf_op jit(solution)/shard_map/all_to_all | solution.py:50
  118.2 21.5 %copy-start.32 = (f32[256]{0:T(256)S(1)}, f32[256]{0:T(256)}, u32[]{:S(2)}) copy-start(f32[256]{0:T(256)} %param.23) | copy-start | bytes 3076
  127.6 1.2 collective-permute-start.18
  129.6 21.0 %all-to-all-start.1 = ((f32[64,8,128]{2,1,0:T(8,128)}), f32[64,8,128]{2,1,0:T(8,128)S(1)}, u32[]{:S(2)}, u32[]{:S(2)}) async-start(f32[64,8,128]{2,1,0:T(8,128)} %chip_stats.1), calls=%async_computation.1 | async-start | bytes 524288 | tf_op jit(solution)/shard_map/all_to_all | solution.py:50
  140.1 14.4 %collective-permute-start.20 = (bf16[64,16,512]{2,1,0:T(8,128)(2,1)}, bf16[64,16,512]{2,1,0:T(8,128)(2,1)S(1)}, u32[]{:S(2)}, u32[]{:S(2)}) collective-permute-start(bf16[64,16,512]{2,1,0:T(8,128)(2,1)} %all-to-all-done.2.own_ref), channel_id=1, source_target_pairs={{0,64},{64,0},{1,65},{65,1},{2,66},{66,2},{3,67},{67,3},{4,68},{68... | collective-permute-start | bytes 3145736 | tf_op jit(solution)/shard_map/ppermute | solution.py:46
  154.2 3.4 %collective-permute-start.19 = (bf16[128,4096]{1,0:T(8,128)(2,1)S(1)}, bf16[128,4096]{1,0:T(8,128)(2,1)S(1)}, u32[]{:S(2)}, u32[]{:S(2)}) collective-permute-start(bf16[128,4096]{1,0:T(8,128)(2,1)S(1)} %get-tuple-element.85), channel_id=1, source_target_pairs={{0,64},{64,0},{1,65},{65,1},{2,66},{66,2},{3,67},{67,3},{4,68},{68... | collective-permute-start | bytes 3145736 | tf_op jit(solution)/shard_map/ppermute | solution.py:46
  157.5 25.4 %copy-start.27 = (bf16[2,4096]{1,0:T(2,128)(2,1)S(1)}, bf16[2,4096]{1,0:T(2,128)(2,1)}, u32[]{:S(2)}) copy-start(bf16[2,4096]{1,0:T(2,128)(2,1)} %states_ref.1) | copy-start | bytes 49156
  157.5 25.4 %copy-start.30 = (bf16[4096]{0:T(1024)(128)(2,1)S(1)}, bf16[4096]{0:T(1024)(128)(2,1)}, u32[]{:S(2)}) copy-start(bf16[4096]{0:T(1024)(128)(2,1)} %param.16) | copy-start | bytes 24580
  158.9 49.6 %copy-start.12 = (bf16[112,4096]{1,0:T(8,128)(2,1)S(1)}, bf16[112,4096]{1,0:T(8,128)(2,1)}, u32[]{:S(2)}) copy-start(bf16[112,4096]{1,0:T(8,128)(2,1)} %down_ref.1) | copy-start | bytes 2752516
  205.8 2.7 %collective-permute-start.21 = (bf16[64,16,512]{2,1,0:T(8,128)(2,1)S(1)}, bf16[64,16,512]{2,1,0:T(8,128)(2,1)S(1)}, u32[]{:S(2)}, u32[]{:S(2)}) collective-permute-start(bf16[64,16,512]{2,1,0:T(8,128)(2,1)S(1)} %all_to_all.31.own_ref), channel_id=1, source_target_pairs={{0,64},{64,0},{1,65},{65,1},{2,66},{66,2},{3,67},{67,3},{4,68},{68... | collective-permute-start | bytes 3145736 | tf_op jit(solution)/shard_map/ppermute | solution.py:46
  211.5 2.7 %collective-permute-start.22 = (bf16[128,4096]{1,0:T(8,128)(2,1)S(1)}, bf16[128,4096]{1,0:T(8,128)(2,1)S(1)}, u32[]{:S(2)}, u32[]{:S(2)}) collective-permute-start(bf16[128,4096]{1,0:T(8,128)(2,1)S(1)} %get-tuple-element.91), channel_id=1, source_target_pairs={{0,64},{64,0},{1,65},{65,1},{2,66},{66,2},{3,67},{67,3},{4,68},{68... | collective-permute-start | bytes 3145736 | tf_op jit(solution)/shard_map/ppermute | solution.py:46
  216.6 24.0 %all-to-all-start.5 = ((bf16[64,16,512]{2,1,0:T(8,128)(2,1)}), bf16[64,16,512]{2,1,0:T(8,128)(2,1)S(1)}, u32[]{:S(2)}, u32[]{:S(2)}) async-start(bf16[64,16,512]{2,1,0:T(8,128)(2,1)} %join.5), calls=%async_computation.5 | async-start | bytes 2097152 | tf_op jit(solution)/shard_map/all_to_all | solution.py:50
  (28 other events, 74.6 us)

commit v10 on v8

--- a/solution.py
+++ b/solution.py
@@ -658,6 +658,7 @@
         in_specs=[VMEM] * 2,
         out_specs=VMEM,
     )(stats, swap_cores(stats))
+    stats, ffn_rows = lax.optimization_barrier((stats, ffn_rows))
     every = exchange(stats, CHIPS)
 
     weight = token_weight.reshape(2, 4, 2, 4, 2, 2).transpose(1, 3, 2, 4, 0, 5).reshape(1, 256)
@@ -679,6 +680,7 @@
     weights = (down_weight, gate_t, up_t)
     others = swap_cores(blocks)
     own = ffn_grad_part(blocks, jnp.float32, *weights)
+    others, own = lax.optimization_barrier((others, own))
     send = ffn_grad_part(others, jnp.bfloat16, *weights)
     ffn_grad = exchange(join_part(own, swap_cores(send)), CHIPS)
     state_grad = kernel_call(

time: 244 us -> 231 us (0.947)
  waiting for transfers between devices: 105 us -> 72.1 us
  blocking collectives: 33.6 us -> 57.4 us
  local copies, waits for them, and re-layouts: 7.47 us -> 3.29 us
    all_to_all x4 -> x3, waiting for transfers between devices: 62.1 us -> 28.9 us  [exchange(): return lax.all_to_all(blocks, axes, split_axis=0, concat_axis=0, tiled=True)]
    all_to_all x1 -> x2, blocking collectives: 33.6 us -> 57.4 us  [exchange(): return lax.all_to_all(blocks, axes, split_axis=0, concat_axis=0, tiled=True)]
    unnamed x26 -> x20, local copies, waits for them, and re-layouts: 5.68 us -> 1.49 us
    pallas_call x3, Pallas kernels: 8.06 us -> 4.86 us  [join_part(): kernel_call(join_kernel, 'join', shape_of((chips, height * len(pairs) //...]
    all_to_all x4 -> x3, starting transfers between devices: 23.5 us -> 23.4 us  [exchange(): return lax.all_to_all(blocks, axes, split_axis=0, concat_axis=0, tiled=True)]
  transfers between devices with their start and end apart: 26 -> 25, of which waited for: 17 -> 16; matrix products, arithmetic and copies ran while one was open for 1% -> 1% of each run, Pallas kernels for 10% -> 13%
where the time goes in v10:
time: 231 us; the launch traced here: 230 us
  waiting for transfers between devices  72.1 us (31%)
  blocking collectives  57.4 us (25%)
  Pallas kernels  49.9 us (22%)
  starting transfers between devices  45.6 us (20%)
  local copies, waits for them, and re-layouts  3.29 us (1%)
    all_to_all x2, blocking collectives, exchange(): return lax.all_to_all(blocks, axes, split_axis=0, concat_axis=0, tiled=True)  57.4 us
    ppermute x14, waiting for transfers between devices, along(): return lax.ppermute(block, line, [(i, i ^ mask) for i in range(4)])  36.8 us
    all_to_all x3, waiting for transfers between devices, exchange(): return lax.all_to_all(blocks, axes, split_axis=0, concat_axis=0, tiled=True)  28.9 us
    all_to_all x3, starting transfers between devices, exchange(): return lax.all_to_all(blocks, axes, split_axis=0, concat_axis=0, tiled=True)  23.4 us
    ppermute x14, starting transfers between devices, along(): return lax.ppermute(block, line, [(i, i ^ mask) for i in range(4)])  20.8 us
    pallas_call x2, Pallas kernels, logits_part(): kernel_call(functools.partial(logits_kernel, last), 'logits', out_shape,...  17.6 us
    pallas_call x2, Pallas kernels, ffn_grad_part(): kernel_call(ffn_grad_kernel, 'ffn_grad', shape_of((2 * chips, SEGMENTS *...  8.62 us
    ppermute x8, waiting for transfers between devices, swap_cores(): return lax.ppermute(values, 'core', [(0, 1), (1, 0)])  6.36 us
  transfers between devices with their start and end apart: 25, of which 16 were waited for; matrix products, arithmetic and copies ran while one was open for 1% of the time, Pallas kernels for 13%

profile of v10, /device:TPU:0, one launch (start us, length us, event | category | flops | bytes accessed | tf_op | source)
XLA Modules:
  0.0 230.1 jit_solution(7209737117399915875)
XLA Ops:
  0.6 1.9 rows.1
  4.9 1.7 collective-permute-start.1
  6.6 2.9 %collective-permute-done.1.came_ref = bf16[4,10240]{1,0:T(4,128)(2,1)S(1)} collective-permute-done((bf16[4,10240]{1,0:T(4,128)(2,1)S(1)}, bf16[4,10240]{1,0:T(4,128)(2,1)S(1)}, u32[]{:S(2)}, u32[]{:S(2)}) %collective-permute-start.1) | collective-permute-done | bytes 81952 | tf_op jit(solution)/shard_map/ppermute | solution.py:165
  9.5 3.2 %collective-permute-start.2 = (bf16[8,10240]{1,0:T(8,128)(2,1)S(1)}, bf16[8,10240]{1,0:T(8,128)(2,1)S(1)}, u32[]{:S(2)}, u32[]{:S(2)}) collective-permute-start(bf16[8,10240]{1,0:T(8,128)(2,1)S(1)} %pair.4.own_ref), channel_id=1, source_target_pairs={{0,9},{1,8},{8,1},{9,0},{2,11},{3,10},{10,3},{11,2},{4,13},{5,12},... | collective-permute-start | bytes 491528 | tf_op jit(solution)/shard_map/ppermute | solution.py:165
  12.7 3.7 %collective-permute-done.2.came_ref = bf16[8,10240]{1,0:T(8,128)(2,1)S(1)} collective-permute-done((bf16[8,10240]{1,0:T(8,128)(2,1)S(1)}, bf16[8,10240]{1,0:T(8,128)(2,1)S(1)}, u32[]{:S(2)}, u32[]{:S(2)}) %collective-permute-start.2) | collective-permute-done | bytes 163872 | tf_op jit(solution)/shard_map/ppermute | solution.py:165
  16.5 2.0 collective-permute-start.3
  20.7 3.6 %pick.1 = (bf16[128,4096]{1,0:T(8,128)(2,1)S(1)}, bf16[128,4096]{1,0:T(8,128)(2,1)S(1)}) custom-call(s32[2]{0:T(128)S(1)} %pad_add_fusion.1.place_ref, s32[1,256]{1,0:T(1,128)S(1)} %bitcast.24, bf16[501,4096]{1,0:T(8,128)(2,1)} %bitcast.27), custom_call_target="tpu_custom_call" | custom-call | flops 1 | bytes 1 | tf_op jit(solution)/shard_map/pick/pallas_call | solution.py:408
  25.9 2.6 %collective-permute-start.5 = (bf16[32,5120]{1,0:T(8,128)(2,1)S(1)}, bf16[32,5120]{1,0:T(8,128)(2,1)S(1)}, u32[]{:S(2)}, u32[]{:S(2)}) collective-permute-start(bf16[32,5120]{1,0:T(8,128)(2,1)S(1)} %get-tuple-element.49.refs_0_), channel_id=1, source_target_pairs={{0,6},{2,4},{4,2},{6,0},{1,7},{3,5},{5,3},{7,1},{8,14},{10,12},{12... | collective-permute-start | bytes 983048 | tf_op jit(solution)/shard_map/ppermute | solution.py:165
  28.5 2.1 collective-permute-start.6
  30.7 6.6 %collective-permute-done.5.refs_1_ = bf16[32,5120]{1,0:T(8,128)(2,1)S(1)} collective-permute-done((bf16[32,5120]{1,0:T(8,128)(2,1)S(1)}, bf16[32,5120]{1,0:T(8,128)(2,1)S(1)}, u32[]{:S(2)}, u32[]{:S(2)}) %collective-permute-start.5) | collective-permute-done | bytes 327712 | tf_op jit(solution)/shard_map/ppermute | solution.py:165
  37.3 2.2 collective-permute-done.6.refs_3_
  40.6 2.2 collective-permute-start.8
  45.5 12.5 %collective-permute-done.8.refs_1_.refs_2_ = bf16[64,5120]{1,0:T(8,128)(2,1)S(1)} collective-permute-done((bf16[64,5120]{1,0:T(8,128)(2,1)S(1)}, bf16[64,5120]{1,0:T(8,128)(2,1)S(1)}, u32[]{:S(2)}, u32[]{:S(2)}) %collective-permute-start.8) | collective-permute-done | bytes 655392 | tf_op jit(solution)/shard_map/ppermute | solution.py:165
  62.6 1.7 collective-permute-start.14
  64.3 5.0 %collective-permute-done.12.refs_3_ = bf16[32,5120]{1,0:T(8,128)(2,1)S(1)} collective-permute-done((bf16[32,5120]{1,0:T(8,128)(2,1)S(1)}, bf16[32,5120]{1,0:T(8,128)(2,1)S(1)}, u32[]{:S(2)}, u32[]{:S(2)}) %collective-permute-start.12) | collective-permute-done | bytes 327712 | tf_op jit(solution)/shard_map/ppermute | solution.py:165
  69.3 1.5 collective-permute-done.14.refs_3_
  72.3 2.4 %whole.3.refs_1_ = bf16[256,5120]{1,0:T(8,128)(2,1)} custom-call(s32[1]{0:T(128)} %bitcast.2.place_ref, bf16[64,5120]{1,0:T(8,128)(2,1)S(1)} %get-tuple-element.52.refs_0_, bf16[64,5120]{1,0:T(8,128)(2,1)S(1)} %collective-permute-done.9.refs_2_.refs_1_, bf16[64,5120]{1,0:T(8,128)(2,1)S(1)} %collective-permute-done.10.refs_3_.refs_2_, ...), custom_call_target="tpu_custom_call" | custom-call | flops 1 | bytes 1 | tf_op jit(solution)/shard_map/whole/pallas_call | solution.py:185
  75.3 8.5 %all-to-all-start = ((bf16[64,16,512]{2,1,0:T(8,128)(2,1)}), bf16[64,16,512]{2,1,0:T(8,128)(2,1)}, u32[]{:S(2)}, u32[]{:S(2)}) async-start(bf16[64,16,512]{2,1,0:T(8,128)(2,1)} %copy-done), calls=%async_computation | async-start | bytes 2097152 | tf_op jit(solution)/shard_map/all_to_all | solution.py:50
  83.7 8.3 %logits.2 = (f32[501,256]{1,0:T(8,128)S(1)}, f32[501,256]{1,0:T(8,128)S(1)}, f32[501,256]{1,0:T(8,128)S(1)}) custom-call(s32[1]{0:T(128)} %bitcast.core_ref.place_ref, bf16[256,5120]{1,0:T(8,128)(2,1)S(1)} %whole.2.refs_0_, bf16[256,5120]{1,0:T(8,128)(2,1)} %whole.3.refs_1_, bf16[501,4096]{1,0:T(8,128)(2,1)} %bitcast.28, bf16[501,16384]{1,0:T(8,128)(2,1)} %bitcast.25), custom_call_target="tpu_custom_call" | custom-call | flops 1 | bytes 1 | tf_op jit(solution)/shard_map/logits/pallas_call | solution.py:290
  92.1 9.3 %logits.3 = (f32[501,256]{1,0:T(8,128)S(1)}, f32[501,256]{1,0:T(8,128)S(1)}, f32[8,128]{1,0:T(8,128)S(1)}) custom-call(s32[1]{0:T(128)S(6)} %sub.3.place_ref, bf16[256,5120]{1,0:T(8,128)(2,1)} %collective-permute-done.16.refs_0_, bf16[256,5120]{1,0:T(8,128)(2,1)} %collective-permute-done.17.refs_1_, bf16[501,4096]{1,0:T(8,128)(2,1)} %bitcast.29, ...), custom_call_target="tpu_custom_call" | custom-call | flops 1 | bytes 1 | tf_op jit(solution)/shard_map/logits/pallas_call | solution.py:290
  104.8 9.2 %all-to-all-start.1 = ((f32[64,8,128]{2,1,0:T(8,128)}), f32[64,8,128]{2,1,0:T(8,128)S(1)}, u32[]{:S(2)}, u32[]{:S(2)}) async-start(f32[64,8,128]{2,1,0:T(8,128)} %chip_stats.1), calls=%async_computation.1 | async-start | bytes 524288 | tf_op jit(solution)/shard_map/all_to_all | solution.py:50
  114.3 10.8 %all-to-all-done.1.every_ref = f32[64,8,128]{2,1,0:T(8,128)S(1)} async-done(((f32[64,8,128]{2,1,0:T(8,128)}), f32[64,8,128]{2,1,0:T(8,128)S(1)}, u32[]{:S(2)}, u32[]{:S(2)}) %all-to-all-start.1) | async-done | bytes 262176 | tf_op jit(solution)/shard_map/all_to_all | solution.py:50
  125.1 3.4 %row_grad.1 = (f32[128,4096]{1,0:T(8,128)S(1)}, bf16[128,4096]{1,0:T(8,128)(2,1)S(1)}, f32[1,256]{1,0:T(1,128)S(1)}) custom-call(s32[1]{0:T(128)} %bitcast.core_ref.place_ref, f32[64,8,128]{2,1,0:T(8,128)S(1)} %all-to-all-done.1.every_ref, f32[1,256]{1,0:T(1,128)S(1)} %reshape.46.weight_ref, f32[501,256]{1,0:T(8,128)S(1)} %get-tuple-element.77.teacher_ref, ...), custom_call_target="tpu_custom_call" | custom-call | flops 1 | bytes 1 | tf_op jit(solution)/shard_map/row_grad/pallas_call | solution.py:369
  128.6 2.6 %collective-permute-done.19.refs_1_ = bf16[128,4096]{1,0:T(8,128)(2,1)S(1)} collective-permute-done((bf16[128,4096]{1,0:T(8,128)(2,1)S(1)}, bf16[128,4096]{1,0:T(8,128)(2,1)S(1)}, u32[]{:S(2)}, u32[]{:S(2)}) %collective-permute-start.19) | collective-permute-done | bytes 1048608 | tf_op jit(solution)/shard_map/ppermute | solution.py:46
  132.6 23.6 %all_to_all.25.blocks_ref = bf16[64,16,512]{2,1,0:T(8,128)(2,1)S(1)} all-to-all(bf16[64,16,512]{2,1,0:T(8,128)(2,1)S(1)} %join.4), channel_id=1, replica_groups=mesh['core'=2,'x'=4,'yh'=2,'z'=4,'yl'=2] {'x','yh','z','yl'}, dimensions={0} | all-to-all | bytes 2097152 | tf_op jit(solution)/shard_map/all_to_all | solution.py:50
  156.6 33.7 %all_to_all.26.blocks_ref = bf16[64,32,512]{2,1,0:T(8,128)(2,1)S(1)} all-to-all(bf16[64,32,512]{2,1,0:T(8,128)(2,1)S(1)} %get-tuple-element.83), channel_id=1, replica_groups=mesh['core'=2,'x'=4,'yh'=2,'z'=4,'yl'=2] {'x','yh','z','yl'}, dimensions={0} | all-to-all | bytes 4194304 | tf_op jit(solution)/shard_map/all_to_all | solution.py:50
  190.3 4.3 %ffn_grad.2.refs_0_ = f32[128,4096]{1,0:T(8,128)S(1)} custom-call(bf16[64,32,512]{2,1,0:T(8,128)(2,1)S(1)} %all_to_all.26.blocks_ref, bf16[112,4096]{1,0:T(8,128)(2,1)S(1)} %copy-done.1, bf16[112,4096]{1,0:T(8,128)(2,1)S(1)} %bitcast.16, bf16[112,4096]{1,0:T(8,128)(2,1)S(1)} %bitcast.18), custom_call_target="tpu_custom_call" | custom-call | flops 1 | bytes 1 | tf_op jit(solution)/shard_map/ffn_grad/pallas_call | solution.py:566
  194.7 4.3 %ffn_grad.3 = bf16[128,4096]{1,0:T(8,128)(2,1)S(1)} custom-call(bf16[64,32,512]{2,1,0:T(8,128)(2,1)S(1)} %collective-permute-done.20.blocks_ref, bf16[112,4096]{1,0:T(8,128)(2,1)S(1)} %copy-done.1, bf16[112,4096]{1,0:T(8,128)(2,1)S(1)} %bitcast.17, bf16[112,4096]{1,0:T(8,128)(2,1)S(1)} %bitcast.19), custom_call_target="tpu_custom_call" | custom-call | flops 1 | bytes 1 | tf_op jit(solution)/shard_map/ffn_grad/pallas_call | solution.py:566
  199.6 2.3 collective-permute-done.21.refs_1_
  201.8 2.3 %join.5 = bf16[64,16,512]{2,1,0:T(8,128)(2,1)} custom-call(f32[128,4096]{1,0:T(8,128)S(1)} %ffn_grad.2.refs_0_, bf16[128,4096]{1,0:T(8,128)(2,1)S(1)} %collective-permute-done.21.refs_1_), custom_call_target="tpu_custom_call" | custom-call | flops 1 | bytes 1 | tf_op jit(solution)/shard_map/join/pallas_call | solution.py:444
  204.1 5.7 %all-to-all-start.4 = ((bf16[64,16,512]{2,1,0:T(8,128)(2,1)}), bf16[64,16,512]{2,1,0:T(8,128)(2,1)S(1)}, u32[]{:S(2)}, u32[]{:S(2)}) async-start(bf16[64,16,512]{2,1,0:T(8,128)(2,1)} %join.5), calls=%async_computation.4 | async-start | bytes 2097152 | tf_op jit(solution)/shard_map/all_to_all | solution.py:50
  212.0 17.2 %all-to-all-done.4.blocks_ref = bf16[64,16,512]{2,1,0:T(8,128)(2,1)S(1)} async-done(((bf16[64,16,512]{2,1,0:T(8,128)(2,1)}), bf16[64,16,512]{2,1,0:T(8,128)(2,1)S(1)}, u32[]{:S(2)}, u32[]{:S(2)}) %all-to-all-start.4) | async-done | bytes 1048608 | tf_op jit(solution)/shard_map/all_to_all | solution.py:50
  (73 shorter events, 25.8 us)
Async XLA Ops:
  2.5 1.5 collective-permute-start
  4.9 4.6 %collective-permute-start.1 = (bf16[4,10240]{1,0:T(4,128)(2,1)S(1)}, bf16[4,10240]{1,0:T(4,128)(2,1)S(1)}, u32[]{:S(2)}, u32[]{:S(2)}) collective-permute-start(bf16[4,10240]{1,0:T(4,128)(2,1)S(1)} %pair.3.own_ref), channel_id=1, source_target_pairs={{0,1},{1,0},{8,9},{9,8},{2,3},{3,2},{10,11},{11,10},{4,5},{5,4},{1... | collective-permute-start | bytes 245768 | tf_op jit(solution)/shard_map/ppermute | solution.py:165
  9.5 6.9 %collective-permute-start.2 = (bf16[8,10240]{1,0:T(8,128)(2,1)S(1)}, bf16[8,10240]{1,0:T(8,128)(2,1)S(1)}, u32[]{:S(2)}, u32[]{:S(2)}) collective-permute-start(bf16[8,10240]{1,0:T(8,128)(2,1)S(1)} %pair.4.own_ref), channel_id=1, source_target_pairs={{0,9},{1,8},{8,1},{9,0},{2,11},{3,10},{10,3},{11,2},{4,13},{5,12},... | collective-permute-start | bytes 491528 | tf_op jit(solution)/shard_map/ppermute | solution.py:165
  16.5 8.0 %collective-permute-start.3 = (bf16[16,5120]{1,0:T(8,128)(2,1)S(1)}, bf16[16,5120]{1,0:T(8,128)(2,1)S(1)}, u32[]{:S(2)}, u32[]{:S(2)}) collective-permute-start(bf16[16,5120]{1,0:T(8,128)(2,1)S(1)} %get-tuple-element.47.refs_0_), channel_id=1, source_target_pairs={{0,2},{2,0},{4,6},{6,4},{1,3},{3,1},{5,7},{7,5},{8,10},{10,8},{12,... | collective-permute-start | bytes 491528 | tf_op jit(solution)/shard_map/ppermute | solution.py:165
  18.5 6.0 %collective-permute-start.4 = (bf16[16,5120]{1,0:T(8,128)(2,1)S(1)}, bf16[16,5120]{1,0:T(8,128)(2,1)S(1)}, u32[]{:S(2)}, u32[]{:S(2)}) collective-permute-start(bf16[16,5120]{1,0:T(8,128)(2,1)S(1)} %get-tuple-element.48.refs_2_), channel_id=1, source_target_pairs={{0,16},{16,0},{32,48},{48,32},{1,17},{17,1},{33,49},{49,33},{2,18}... | collective-permute-start | bytes 491528 | tf_op jit(solution)/shard_map/ppermute | solution.py:165
  24.3 19.9 %collective-permute-start.11 = (bf16[128,4096]{1,0:T(8,128)(2,1)S(1)}, bf16[128,4096]{1,0:T(8,128)(2,1)S(1)}, u32[]{:S(2)}, u32[]{:S(2)}) collective-permute-start(bf16[128,4096]{1,0:T(8,128)(2,1)S(1)} %get-tuple-element.54), channel_id=1, source_target_pairs={{0,64},{64,0},{1,65},{65,1},{2,66},{66,2},{3,67},{67,3},{4,68},{68... | collective-permute-start | bytes 3145736 | tf_op jit(solution)/shard_map/ppermute | solution.py:46
  25.9 11.4 %collective-permute-start.5 = (bf16[32,5120]{1,0:T(8,128)(2,1)S(1)}, bf16[32,5120]{1,0:T(8,128)(2,1)S(1)}, u32[]{:S(2)}, u32[]{:S(2)}) collective-permute-start(bf16[32,5120]{1,0:T(8,128)(2,1)S(1)} %get-tuple-element.49.refs_0_), channel_id=1, source_target_pairs={{0,6},{2,4},{4,2},{6,0},{1,7},{3,5},{5,3},{7,1},{8,14},{10,12},{12... | collective-permute-start | bytes 983048 | tf_op jit(solution)/shard_map/ppermute | solution.py:165
  28.5 11.0 %collective-permute-start.6 = (bf16[32,5120]{1,0:T(8,128)(2,1)S(1)}, bf16[32,5120]{1,0:T(8,128)(2,1)S(1)}, u32[]{:S(2)}, u32[]{:S(2)}) collective-permute-start(bf16[32,5120]{1,0:T(8,128)(2,1)S(1)} %get-tuple-element.50.refs_2_), channel_id=1, source_target_pairs={{0,48},{16,32},{32,16},{48,0},{1,49},{17,33},{33,17},{49,1},{2,50}... | collective-permute-start | bytes 983048 | tf_op jit(solution)/shard_map/ppermute | solution.py:165
  40.6 17.3 %collective-permute-start.8 = (bf16[64,5120]{1,0:T(8,128)(2,1)S(1)}, bf16[64,5120]{1,0:T(8,128)(2,1)S(1)}, u32[]{:S(2)}, u32[]{:S(2)}) collective-permute-start(bf16[64,5120]{1,0:T(8,128)(2,1)S(1)} %get-tuple-element.51.refs_0_), channel_id=1, source_target_pairs={{0,48},{16,32},{32,16},{48,0},{1,49},{17,33},{33,17},{49,1},{2,50}... | collective-permute-start | bytes 1966088 | tf_op jit(solution)/shard_map/ppermute | solution.py:165
  42.8 15.8 %collective-permute-start.7 = (bf16[64,5120]{1,0:T(8,128)(2,1)S(1)}, bf16[64,5120]{1,0:T(8,128)(2,1)S(1)}, u32[]{:S(2)}, u32[]{:S(2)}) collective-permute-start(bf16[64,5120]{1,0:T(8,128)(2,1)S(1)} %get-tuple-element.51.refs_0_), channel_id=1, source_target_pairs={{0,16},{16,0},{32,48},{48,32},{1,17},{17,1},{33,49},{49,33},{2,18}... | collective-permute-start | bytes 1966088 | tf_op jit(solution)/shard_map/ppermute | solution.py:165
  42.8 17.0 %collective-permute-start.10 = (bf16[64,5120]{1,0:T(8,128)(2,1)S(1)}, bf16[64,5120]{1,0:T(8,128)(2,1)S(1)}, u32[]{:S(2)}, u32[]{:S(2)}) collective-permute-start(bf16[64,5120]{1,0:T(8,128)(2,1)S(1)} %get-tuple-element.52.refs_0_), channel_id=1, source_target_pairs={{0,6},{2,4},{4,2},{6,0},{1,7},{3,5},{5,3},{7,1},{8,14},{10,12},{12... | collective-permute-start | bytes 1966088 | tf_op jit(solution)/shard_map/ppermute | solution.py:165
  43.6 16.1 %collective-permute-start.9 = (bf16[64,5120]{1,0:T(8,128)(2,1)S(1)}, bf16[64,5120]{1,0:T(8,128)(2,1)S(1)}, u32[]{:S(2)}, u32[]{:S(2)}) collective-permute-start(bf16[64,5120]{1,0:T(8,128)(2,1)S(1)} %get-tuple-element.52.refs_0_), channel_id=1, source_target_pairs={{0,2},{2,0},{4,6},{6,4},{1,3},{3,1},{5,7},{7,5},{8,10},{10,8},{12,... | collective-permute-start | bytes 1966088 | tf_op jit(solution)/shard_map/ppermute | solution.py:165
  45.5 26.8 %copy-start = (bf16[64,16,512]{2,1,0:T(8,128)(2,1)}, bf16[64,16,512]{2,1,0:T(8,128)(2,1)S(1)}, u32[]{:S(2)}) copy-start(bf16[64,16,512]{2,1,0:T(8,128)(2,1)S(1)} %join.3) | copy-start | bytes 3145732
  60.2 9.1 %collective-permute-start.12 = (bf16[32,5120]{1,0:T(8,128)(2,1)S(1)}, bf16[32,5120]{1,0:T(8,128)(2,1)S(1)}, u32[]{:S(2)}, u32[]{:S(2)}) collective-permute-start(bf16[32,5120]{1,0:T(8,128)(2,1)S(1)} %get-tuple-element.59), channel_id=1, source_target_pairs={{0,48},{16,32},{32,16},{48,0},{1,49},{17,33},{33,17},{49,1},{2,50}... | collective-permute-start | bytes 983048 | tf_op jit(solution)/shard_map/ppermute | solution.py:165
  61.4 7.9 %collective-permute-start.13 = (bf16[32,5120]{1,0:T(8,128)(2,1)S(1)}, bf16[32,5120]{1,0:T(8,128)(2,1)S(1)}, u32[]{:S(2)}, u32[]{:S(2)}) collective-permute-start(bf16[32,5120]{1,0:T(8,128)(2,1)S(1)} %get-tuple-element.60), channel_id=1, source_target_pairs={{0,16},{16,0},{32,48},{48,32},{1,17},{17,1},{33,49},{49,33},{2,18}... | collective-permute-start | bytes 983048 | tf_op jit(solution)/shard_map/ppermute | solution.py:165
  62.6 8.3 %collective-permute-start.14 = (bf16[32,5120]{1,0:T(8,128)(2,1)S(1)}, bf16[32,5120]{1,0:T(8,128)(2,1)S(1)}, u32[]{:S(2)}, u32[]{:S(2)}) collective-permute-start(bf16[32,5120]{1,0:T(8,128)(2,1)S(1)} %get-tuple-element.61), channel_id=1, source_target_pairs={{0,6},{2,4},{4,2},{6,0},{1,7},{3,5},{5,3},{7,1},{8,14},{10,12},{12... | collective-permute-start | bytes 983048 | tf_op jit(solution)/shard_map/ppermute | solution.py:165
  64.3 7.1 %collective-permute-start.15 = (bf16[32,5120]{1,0:T(8,128)(2,1)S(1)}, bf16[32,5120]{1,0:T(8,128)(2,1)S(1)}, u32[]{:S(2)}, u32[]{:S(2)}) collective-permute-start(bf16[32,5120]{1,0:T(8,128)(2,1)S(1)} %get-tuple-element.62), channel_id=1, source_target_pairs={{0,2},{2,0},{4,6},{6,4},{1,3},{3,1},{5,7},{7,5},{8,10},{10,8},{12,... | collective-permute-start | bytes 983048 | tf_op jit(solution)/shard_map/ppermute | solution.py:165
  74.7 17.4 %collective-permute-start.16 = (bf16[256,5120]{1,0:T(8,128)(2,1)S(1)}, bf16[256,5120]{1,0:T(8,128)(2,1)}, u32[]{:S(2)}, u32[]{:S(2)}) collective-permute-start(bf16[256,5120]{1,0:T(8,128)(2,1)S(1)} %whole.2.refs_0_), channel_id=1, source_target_pairs={{0,64},{64,0},{1,65},{65,1},{2,66},{66,2},{3,67},{67,3},{4,68},{68... | collective-permute-start | bytes 7864328 | tf_op jit(solution)/shard_map/ppermute | solution.py:46
  74.8 17.3 %collective-permute-start.17 = (bf16[256,5120]{1,0:T(8,128)(2,1)}, bf16[256,5120]{1,0:T(8,128)(2,1)}, u32[]{:S(2)}, u32[]{:S(2)}) collective-permute-start(bf16[256,5120]{1,0:T(8,128)(2,1)} %whole.3.refs_1_), channel_id=1, source_target_pairs={{0,64},{64,0},{1,65},{65,1},{2,66},{66,2},{3,67},{67,3},{4,68},{68... | collective-permute-start | bytes 7864328 | tf_op jit(solution)/shard_map/ppermute | solution.py:46
  75.3 27.2 %all-to-all-start = ((bf16[64,16,512]{2,1,0:T(8,128)(2,1)}), bf16[64,16,512]{2,1,0:T(8,128)(2,1)}, u32[]{:S(2)}, u32[]{:S(2)}) async-start(bf16[64,16,512]{2,1,0:T(8,128)(2,1)} %copy-done), calls=%async_computation | async-start | bytes 2097152 | tf_op jit(solution)/shard_map/all_to_all | solution.py:50
  92.1 21.9 %copy-start.9 = (f32[256]{0:T(256)S(1)}, f32[256]{0:T(256)}, u32[]{:S(2)}) copy-start(f32[256]{0:T(256)} %param.23) | copy-start | bytes 3076
  101.4 2.6 %collective-permute-start.18 = (f32[8,128]{1,0:T(8,128)S(1)}, f32[8,128]{1,0:T(8,128)S(1)}, u32[]{:S(2)}, u32[]{:S(2)}) collective-permute-start(f32[8,128]{1,0:T(8,128)S(1)} %get-tuple-element.73.own_ref), channel_id=1, source_target_pairs={{0,64},{64,0},{1,65},{65,1},{2,66},{66,2},{3,67},{67,3},{4,68},{68... | collective-permute-start | bytes 12296 | tf_op jit(solution)/shard_map/ppermute | solution.py:46
  104.8 20.4 %all-to-all-start.1 = ((f32[64,8,128]{2,1,0:T(8,128)}), f32[64,8,128]{2,1,0:T(8,128)S(1)}, u32[]{:S(2)}, u32[]{:S(2)}) async-start(f32[64,8,128]{2,1,0:T(8,128)} %chip_stats.1), calls=%async_computation.1 | async-start | bytes 524288 | tf_op jit(solution)/shard_map/all_to_all | solution.py:50
  128.5 2.7 %collective-permute-start.19 = (bf16[128,4096]{1,0:T(8,128)(2,1)S(1)}, bf16[128,4096]{1,0:T(8,128)(2,1)S(1)}, u32[]{:S(2)}, u32[]{:S(2)}) collective-permute-start(bf16[128,4096]{1,0:T(8,128)(2,1)S(1)} %get-tuple-element.81), channel_id=1, source_target_pairs={{0,64},{64,0},{1,65},{65,1},{2,66},{66,2},{3,67},{67,3},{4,68},{68... | collective-permute-start | bytes 3145736 | tf_op jit(solution)/shard_map/ppermute | solution.py:46
  131.3 24.9 %copy-start.4 = (bf16[2,4096]{1,0:T(2,128)(2,1)S(1)}, bf16[2,4096]{1,0:T(2,128)(2,1)}, u32[]{:S(2)}) copy-start(bf16[2,4096]{1,0:T(2,128)(2,1)} %states_ref.1) | copy-start | bytes 49156
  131.3 24.9 %copy-start.7 = (bf16[4096]{0:T(1024)(128)(2,1)S(1)}, bf16[4096]{0:T(1024)(128)(2,1)}, u32[]{:S(2)}) copy-start(bf16[4096]{0:T(1024)(128)(2,1)} %param.16) | copy-start | bytes 24580
  156.2 34.1 %copy-start.1 = (bf16[112,4096]{1,0:T(8,128)(2,1)S(1)}, bf16[112,4096]{1,0:T(8,128)(2,1)}, u32[]{:S(2)}) copy-start(bf16[112,4096]{1,0:T(8,128)(2,1)} %down_ref.3) | copy-start | bytes 2752516
  156.2 34.1 %copy-start.2 = (bf16[4096,112]{0,1:T(8,128)(2,1)S(1)}, bf16[4096,112]{0,1:T(8,128)(2,1)}, u32[]{:S(2)}) copy-start(bf16[4096,112]{0,1:T(8,128)(2,1)} %param.20) | copy-start | bytes 2752516
  156.2 34.1 %copy-start.3 = (bf16[4096,112]{0,1:T(8,128)(2,1)S(1)}, bf16[4096,112]{0,1:T(8,128)(2,1)}, u32[]{:S(2)}) copy-start(bf16[4096,112]{0,1:T(8,128)(2,1)} %param.21) | copy-start | bytes 2752516
  190.3 4.3 %collective-permute-start.20 = (bf16[64,32,512]{2,1,0:T(8,128)(2,1)S(1)}, bf16[64,32,512]{2,1,0:T(8,128)(2,1)S(1)}, u32[]{:S(2)}, u32[]{:S(2)}) collective-permute-start(bf16[64,32,512]{2,1,0:T(8,128)(2,1)S(1)} %all_to_all.26.blocks_ref), channel_id=1, source_target_pairs={{0,64},{64,0},{1,65},{65,1},{2,66},{66,2},{3,67},{67,3},{4,68},{68... | collective-permute-start | bytes 6291464 | tf_op jit(solution)/shard_map/ppermute | solution.py:46
  199.0 2.9 %collective-permute-start.21 = (bf16[128,4096]{1,0:T(8,128)(2,1)S(1)}, bf16[128,4096]{1,0:T(8,128)(2,1)S(1)}, u32[]{:S(2)}, u32[]{:S(2)}) collective-permute-start(bf16[128,4096]{1,0:T(8,128)(2,1)S(1)} %ffn_grad.3), channel_id=1, source_target_pairs={{0,64},{64,0},{1,65},{65,1},{2,66},{66,2},{3,67},{67,3},{4,68},{68... | collective-permute-start | bytes 3145736 | tf_op jit(solution)/shard_map/ppermute | solution.py:46
  204.1 25.0 %all-to-all-start.4 = ((bf16[64,16,512]{2,1,0:T(8,128)(2,1)}), bf16[64,16,512]{2,1,0:T(8,128)(2,1)S(1)}, u32[]{:S(2)}, u32[]{:S(2)}) async-start(bf16[64,16,512]{2,1,0:T(8,128)(2,1)} %join.5), calls=%async_computation.4 | async-start | bytes 2097152 | tf_op jit(solution)/shard_map/all_to_all | solution.py:50
  (3 other events, 11.9 us)

commit v11 on v10

--- a/solution.py
+++ b/solution.py
@@ -625,9 +625,11 @@
         came = (along(first, "z", mask), along(second, "x", mask))
         bits = (jnp.stack([z, x]) >> bit) & 1
         first, second = in_pairs(bits, (first, came[0], second, came[1]))
+    ids = token_ids.reshape(1, 256)
+    ids, first, second = lax.optimization_barrier((ids, first, second))
     came = [along(first, "x", 1), along(first, "x", 3), along(second, "z", 1), along(second, "z", 3)]
     place = jnp.stack([core, device]).astype(jnp.int32)
-    own, send = pick_part(place, token_ids.reshape(1, 256), student_head_t)
+    own, send = pick_part(place, ids, student_head_t)
     came, picked = lax.optimization_barrier((came, join_part(own, swap_cores(send))))
     halves = halves_of(came)
     far = [
@@ -640,13 +642,7 @@
         whole_rows(z.reshape(1), [second] + came[2:] + far[2:]),
     )
     rows, picked = lax.optimization_barrier((rows, picked))
-    embedded, ffn_rows = kernel_call(
-        embed_kernel,
-        "embed",
-        [shape_of(BLOCK, jnp.float32), shape_of(BLOCK)],
-        in_specs=[VMEM] * 2,
-        out_specs=[VMEM] * 2,
-    )(exchange(picked, CHIPS), ffn_gain)
+    picked = exchange(picked, CHIPS)
     others = tuple(swap_cores(part) for part in rows)
     sums = logits_part(own_core, rows, heads)
     student, teacher, stats = logits_part(1 - own_core, others, heads, sums)
@@ -658,8 +654,15 @@
         in_specs=[VMEM] * 2,
         out_specs=VMEM,
     )(stats, swap_cores(stats))
-    stats, ffn_rows = lax.optimization_barrier((stats, ffn_rows))
+    stats, picked = lax.optimization_barrier((stats, picked))
     every = exchange(stats, CHIPS)
+    embedded, ffn_rows = kernel_call(
+        embed_kernel,
+        "embed",
+        [shape_of(BLOCK, jnp.float32), shape_of(BLOCK)],
+        in_specs=[VMEM] * 2,
+        out_specs=[VMEM] * 2,
+    )(picked, ffn_gain)
 
     weight = token_weight.reshape(2, 4, 2, 4, 2, 2).transpose(1, 3, 2, 4, 0, 5).reshape(1, 256)
     own, send, divergence = row_grad_part(

time: 231 us -> 235 us (1.017)
  blocking collectives: 57.4 us -> 33.8 us
  waiting for transfers between devices: 72.1 us -> 91.5 us
  starting transfers between devices: 45.6 us -> 53 us
    all_to_all x2 -> x1, blocking collectives: 57.4 us -> 33.8 us  [exchange(): return lax.all_to_all(blocks, axes, split_axis=0, concat_axis=0, tiled=True)]
    all_to_all x3 -> x4, waiting for transfers between devices: 28.9 us -> 45.2 us  [exchange(): return lax.all_to_all(blocks, axes, split_axis=0, concat_axis=0, tiled=True)]
    all_to_all x3 -> x4, starting transfers between devices: 23.4 us -> 29.6 us  [exchange(): return lax.all_to_all(blocks, axes, split_axis=0, concat_axis=0, tiled=True)]
  transfers between devices with their start and end apart: 25 -> 26, of which waited for: 16 -> 20; matrix products, arithmetic and copies ran while one was open for 1% -> 1% of each run, Pallas kernels for 13% -> 11%
where the time goes in v11:
time: 235 us; the launch traced here: 234 us
  waiting for transfers between devices  91.5 us (39%)
  starting transfers between devices  53 us (23%)
  Pallas kernels  51.3 us (22%)
  blocking collectives  33.8 us (14%)
  local copies, waits for them, and re-layouts  2.61 us (1%)
    all_to_all x4, waiting for transfers between devices, exchange(): return lax.all_to_all(blocks, axes, split_axis=0, concat_axis=0, tiled=True)  45.2 us
    ppermute x14, waiting for transfers between devices, along(): return lax.ppermute(block, line, [(i, i ^ mask) for i in range(4)])  38.8 us
    all_to_all x1, blocking collectives, exchange(): return lax.all_to_all(blocks, axes, split_axis=0, concat_axis=0, tiled=True)  33.8 us
    all_to_all x4, starting transfers between devices, exchange(): return lax.all_to_all(blocks, axes, split_axis=0, concat_axis=0, tiled=True)  29.6 us
    ppermute x14, starting transfers between devices, along(): return lax.ppermute(block, line, [(i, i ^ mask) for i in range(4)])  21.9 us
    pallas_call x2, Pallas kernels, logits_part(): kernel_call(functools.partial(logits_kernel, last), 'logits', out_shape,...  18.1 us
    pallas_call x2, Pallas kernels, ffn_grad_part(): kernel_call(ffn_grad_kernel, 'ffn_grad', shape_of((2 * chips, SEGMENTS *...  8.62 us
    ppermute x8, waiting for transfers between devices, swap_cores(): return lax.ppermute(values, 'core', [(0, 1), (1, 0)])  7.51 us
  transfers between devices with their start and end apart: 26, of which 20 were waited for; matrix products, arithmetic and copies ran while one was open for 1% of the time, Pallas kernels for 11%

profile of v11, /device:TPU:0, one launch (start us, length us, event | category | flops | bytes accessed | tf_op | source)
XLA Modules:
  0.0 234.1 jit_solution(6475367684426689805)
XLA Ops:
  6.6 2.9 %collective-permute-done.1.came_ref = bf16[4,10240]{1,0:T(4,128)(2,1)S(1)} collective-permute-done((bf16[4,10240]{1,0:T(4,128)(2,1)S(1)}, bf16[4,10240]{1,0:T(4,128)(2,1)S(1)}, u32[]{:S(2)}, u32[]{:S(2)}) %collective-permute-start.1) | collective-permute-done | bytes 81952 | tf_op jit(solution)/shard_map/ppermute | solution.py:165
  9.5 3.2 %collective-permute-start.2 = (bf16[8,10240]{1,0:T(8,128)(2,1)S(1)}, bf16[8,10240]{1,0:T(8,128)(2,1)S(1)}, u32[]{:S(2)}, u32[]{:S(2)}) collective-permute-start(bf16[8,10240]{1,0:T(8,128)(2,1)S(1)} %pair.4.own_ref), channel_id=1, source_target_pairs={{0,9},{1,8},{8,1},{9,0},{2,11},{3,10},{10,3},{11,2},{4,13},{5,12},... | collective-permute-start | bytes 491528 | tf_op jit(solution)/shard_map/ppermute | solution.py:165
  12.7 3.7 %collective-permute-done.2.came_ref = bf16[8,10240]{1,0:T(8,128)(2,1)S(1)} collective-permute-done((bf16[8,10240]{1,0:T(8,128)(2,1)S(1)}, bf16[8,10240]{1,0:T(8,128)(2,1)S(1)}, u32[]{:S(2)}, u32[]{:S(2)}) %collective-permute-start.2) | collective-permute-done | bytes 163872 | tf_op jit(solution)/shard_map/ppermute | solution.py:165
  16.5 2.0 collective-permute-start.3
  21.9 1.9 collective-permute-done.4.refs_3_
  25.3 2.6 %collective-permute-start.5 = (bf16[32,5120]{1,0:T(8,128)(2,1)S(1)}, bf16[32,5120]{1,0:T(8,128)(2,1)S(1)}, u32[]{:S(2)}, u32[]{:S(2)}) collective-permute-start(bf16[32,5120]{1,0:T(8,128)(2,1)S(1)} %get-tuple-element.52.refs_0_), channel_id=1, source_target_pairs={{0,6},{2,4},{4,2},{6,0},{1,7},{3,5},{5,3},{7,1},{8,14},{10,12},{12... | collective-permute-start | bytes 983048 | tf_op jit(solution)/shard_map/ppermute | solution.py:165
  27.9 2.8 %collective-permute-start.6 = (bf16[32,5120]{1,0:T(8,128)(2,1)S(1)}, bf16[32,5120]{1,0:T(8,128)(2,1)S(1)}, u32[]{:S(2)}, u32[]{:S(2)}) collective-permute-start(bf16[32,5120]{1,0:T(8,128)(2,1)S(1)} %get-tuple-element.53.refs_2_), channel_id=1, source_target_pairs={{0,48},{16,32},{32,16},{48,0},{1,49},{17,33},{33,17},{49,1},{2,50}... | collective-permute-start | bytes 983048 | tf_op jit(solution)/shard_map/ppermute | solution.py:165
  30.8 2.8 %collective-permute-done.5.refs_1_ = bf16[32,5120]{1,0:T(8,128)(2,1)S(1)} collective-permute-done((bf16[32,5120]{1,0:T(8,128)(2,1)S(1)}, bf16[32,5120]{1,0:T(8,128)(2,1)S(1)}, u32[]{:S(2)}, u32[]{:S(2)}) %collective-permute-start.5) | collective-permute-done | bytes 327712 | tf_op jit(solution)/shard_map/ppermute | solution.py:165
  33.6 2.5 %collective-permute-done.6.refs_3_ = bf16[32,5120]{1,0:T(8,128)(2,1)S(1)} collective-permute-done((bf16[32,5120]{1,0:T(8,128)(2,1)S(1)}, bf16[32,5120]{1,0:T(8,128)(2,1)S(1)}, u32[]{:S(2)}, u32[]{:S(2)}) %collective-permute-start.6) | collective-permute-done | bytes 327712 | tf_op jit(solution)/shard_map/ppermute | solution.py:165
  37.2 3.6 %pick.1 = (bf16[128,4096]{1,0:T(8,128)(2,1)S(1)}, bf16[128,4096]{1,0:T(8,128)(2,1)S(1)}) custom-call(s32[2]{0:T(128)S(1)} %pad_add_fusion.1.place_ref, s32[1,256]{1,0:T(1,128)S(1)} %bitcast.24, bf16[501,4096]{1,0:T(8,128)(2,1)} %bitcast.27), custom_call_target="tpu_custom_call" | custom-call | flops 1 | bytes 1 | tf_op jit(solution)/shard_map/pick/pallas_call | solution.py:408
  42.4 2.1 collective-permute-start.8
  46.2 13.0 %collective-permute-done.10.refs_3_.refs_2_ = bf16[64,5120]{1,0:T(8,128)(2,1)S(1)} collective-permute-done((bf16[64,5120]{1,0:T(8,128)(2,1)S(1)}, bf16[64,5120]{1,0:T(8,128)(2,1)S(1)}, u32[]{:S(2)}, u32[]{:S(2)}) %collective-permute-start.10) | collective-permute-done | bytes 655392 | tf_op jit(solution)/shard_map/ppermute | solution.py:165
  62.9 2.5 %collective-permute-start.14 = (bf16[32,5120]{1,0:T(8,128)(2,1)S(1)}, bf16[32,5120]{1,0:T(8,128)(2,1)S(1)}, u32[]{:S(2)}, u32[]{:S(2)}) collective-permute-start(bf16[32,5120]{1,0:T(8,128)(2,1)S(1)} %get-tuple-element.67), channel_id=1, source_target_pairs={{0,6},{2,4},{4,2},{6,0},{1,7},{3,5},{5,3},{7,1},{8,14},{10,12},{12... | collective-permute-start | bytes 983048 | tf_op jit(solution)/shard_map/ppermute | solution.py:165
  65.5 5.7 %collective-permute-done.12.refs_3_ = bf16[32,5120]{1,0:T(8,128)(2,1)S(1)} collective-permute-done((bf16[32,5120]{1,0:T(8,128)(2,1)S(1)}, bf16[32,5120]{1,0:T(8,128)(2,1)S(1)}, u32[]{:S(2)}, u32[]{:S(2)}) %collective-permute-start.12) | collective-permute-done | bytes 327712 | tf_op jit(solution)/shard_map/ppermute | solution.py:165
  74.8 2.4 %whole.2.refs_0_ = bf16[256,5120]{1,0:T(8,128)(2,1)} custom-call(s32[1]{0:T(128)} %bitcast.1.place_ref, bf16[64,5120]{1,0:T(8,128)(2,1)S(1)} %get-tuple-element.56.refs_0_, bf16[64,5120]{1,0:T(8,128)(2,1)S(1)} %collective-permute-done.7.refs_0_.refs_1_, bf16[64,5120]{1,0:T(8,128)(2,1)S(1)} %collective-permute-done.8.refs_1_.refs_2_, ...), custom_call_target="tpu_custom_call" | custom-call | flops 1 | bytes 1 | tf_op jit(solution)/shard_map/whole/pallas_call | solution.py:185
  77.8 8.7 %all-to-all-start = ((bf16[64,16,512]{2,1,0:T(8,128)(2,1)}), bf16[64,16,512]{2,1,0:T(8,128)(2,1)}, u32[]{:S(2)}, u32[]{:S(2)}) async-start(bf16[64,16,512]{2,1,0:T(8,128)(2,1)} %copy-done.1), calls=%async_computation | async-start | bytes 2097152 | tf_op jit(solution)/shard_map/all_to_all | solution.py:50
  86.4 8.7 %logits.2 = (f32[501,256]{1,0:T(8,128)S(1)}, f32[501,256]{1,0:T(8,128)S(1)}, f32[501,256]{1,0:T(8,128)S(1)}) custom-call(s32[1]{0:T(128)} %bitcast.core_ref.place_ref, bf16[256,5120]{1,0:T(8,128)(2,1)} %whole.2.refs_0_, bf16[256,5120]{1,0:T(8,128)(2,1)} %copy-done, bf16[501,4096]{1,0:T(8,128)(2,1)} %bitcast.28, bf16[501,16384]{1,0:T(8,128)(2,1)} %bitcast.25), custom_call_target="tpu_custom_call" | custom-call | flops 1 | bytes 1 | tf_op jit(solution)/shard_map/logits/pallas_call | solution.py:290
  95.2 9.3 %logits.3 = (f32[501,256]{1,0:T(8,128)S(1)}, f32[501,256]{1,0:T(8,128)S(1)}, f32[8,128]{1,0:T(8,128)S(1)}) custom-call(s32[1]{0:T(128)S(6)} %sub.3.place_ref, bf16[256,5120]{1,0:T(8,128)(2,1)} %collective-permute-done.16.refs_0_, bf16[256,5120]{1,0:T(8,128)(2,1)} %collective-permute-done.17.refs_1_, bf16[501,4096]{1,0:T(8,128)(2,1)} %bitcast.29, ...), custom_call_target="tpu_custom_call" | custom-call | flops 1 | bytes 1 | tf_op jit(solution)/shard_map/logits/pallas_call | solution.py:290
  106.5 10.1 %all-to-all-start.1 = ((f32[64,8,128]{2,1,0:T(8,128)}), f32[64,8,128]{2,1,0:T(8,128)S(1)}, u32[]{:S(2)}, u32[]{:S(2)}) async-start(f32[64,8,128]{2,1,0:T(8,128)} %chip_stats.1), calls=%async_computation.1 | async-start | bytes 524288 | tf_op jit(solution)/shard_map/all_to_all | solution.py:50
  117.0 10.5 %all-to-all-done.1.every_ref = f32[64,8,128]{2,1,0:T(8,128)S(1)} async-done(((f32[64,8,128]{2,1,0:T(8,128)}), f32[64,8,128]{2,1,0:T(8,128)S(1)}, u32[]{:S(2)}, u32[]{:S(2)}) %all-to-all-start.1) | async-done | bytes 262176 | tf_op jit(solution)/shard_map/all_to_all | solution.py:50
  127.5 3.4 %row_grad.1 = (f32[128,4096]{1,0:T(8,128)S(1)}, bf16[128,4096]{1,0:T(8,128)(2,1)S(1)}, f32[1,256]{1,0:T(1,128)S(1)}) custom-call(s32[1]{0:T(128)} %bitcast.core_ref.place_ref, f32[64,8,128]{2,1,0:T(8,128)S(1)} %all-to-all-done.1.every_ref, f32[1,256]{1,0:T(1,128)S(1)} %reshape.45.weight_ref, f32[501,256]{1,0:T(8,128)S(1)} %get-tuple-element.82.teacher_ref, ...), custom_call_target="tpu_custom_call" | custom-call | flops 1 | bytes 1 | tf_op jit(solution)/shard_map/row_grad/pallas_call | solution.py:369
  131.0 2.6 %collective-permute-done.19.refs_1_ = bf16[128,4096]{1,0:T(8,128)(2,1)S(1)} collective-permute-done((bf16[128,4096]{1,0:T(8,128)(2,1)S(1)}, bf16[128,4096]{1,0:T(8,128)(2,1)S(1)}, u32[]{:S(2)}, u32[]{:S(2)}) %collective-permute-start.19) | collective-permute-done | bytes 1048608 | tf_op jit(solution)/shard_map/ppermute | solution.py:46
  133.6 2.3 join.4
  135.9 5.1 %all-to-all-start.2 = ((bf16[64,16,512]{2,1,0:T(8,128)(2,1)}), bf16[64,16,512]{2,1,0:T(8,128)(2,1)S(1)}, u32[]{:S(2)}, u32[]{:S(2)}) async-start(bf16[64,16,512]{2,1,0:T(8,128)(2,1)} %join.4), calls=%async_computation.2 | async-start | bytes 2097152 | tf_op jit(solution)/shard_map/all_to_all | solution.py:50
  142.6 17.6 %all-to-all-done.2.blocks_ref = bf16[64,16,512]{2,1,0:T(8,128)(2,1)S(1)} async-done(((bf16[64,16,512]{2,1,0:T(8,128)(2,1)}), bf16[64,16,512]{2,1,0:T(8,128)(2,1)S(1)}, u32[]{:S(2)}, u32[]{:S(2)}) %all-to-all-start.2) | async-done | bytes 1048608 | tf_op jit(solution)/shard_map/all_to_all | solution.py:50
  160.5 33.8 %all_to_all.25.blocks_ref = bf16[64,32,512]{2,1,0:T(8,128)(2,1)S(1)} all-to-all(bf16[64,32,512]{2,1,0:T(8,128)(2,1)S(1)} %get-tuple-element.89), channel_id=1, replica_groups=mesh['core'=2,'x'=4,'yh'=2,'z'=4,'yl'=2] {'x','yh','z','yl'}, dimensions={0} | all-to-all | bytes 4194304 | tf_op jit(solution)/shard_map/all_to_all | solution.py:50
  194.3 4.3 %ffn_grad.2.refs_0_ = f32[128,4096]{1,0:T(8,128)S(1)} custom-call(bf16[64,32,512]{2,1,0:T(8,128)(2,1)S(1)} %all_to_all.25.blocks_ref, bf16[112,4096]{1,0:T(8,128)(2,1)S(1)} %copy-done.2, bf16[112,4096]{1,0:T(8,128)(2,1)S(1)} %bitcast.16, bf16[112,4096]{1,0:T(8,128)(2,1)S(1)} %bitcast.18), custom_call_target="tpu_custom_call" | custom-call | flops 1 | bytes 1 | tf_op jit(solution)/shard_map/ffn_grad/pallas_call | solution.py:566
  198.6 4.3 %ffn_grad.3 = bf16[128,4096]{1,0:T(8,128)(2,1)S(1)} custom-call(bf16[64,32,512]{2,1,0:T(8,128)(2,1)S(1)} %collective-permute-done.20.blocks_ref, bf16[112,4096]{1,0:T(8,128)(2,1)S(1)} %copy-done.2, bf16[112,4096]{1,0:T(8,128)(2,1)S(1)} %bitcast.17, bf16[112,4096]{1,0:T(8,128)(2,1)S(1)} %bitcast.19), custom_call_target="tpu_custom_call" | custom-call | flops 1 | bytes 1 | tf_op jit(solution)/shard_map/ffn_grad/pallas_call | solution.py:566
  203.5 2.3 collective-permute-done.21.refs_1_
  205.8 2.3 join.5
  208.1 5.7 %all-to-all-start.4 = ((bf16[64,16,512]{2,1,0:T(8,128)(2,1)}), bf16[64,16,512]{2,1,0:T(8,128)(2,1)S(1)}, u32[]{:S(2)}, u32[]{:S(2)}) async-start(bf16[64,16,512]{2,1,0:T(8,128)(2,1)} %join.5), calls=%async_computation.4 | async-start | bytes 2097152 | tf_op jit(solution)/shard_map/all_to_all | solution.py:50
  215.9 17.2 %all-to-all-done.4.blocks_ref = bf16[64,16,512]{2,1,0:T(8,128)(2,1)S(1)} async-done(((bf16[64,16,512]{2,1,0:T(8,128)(2,1)}), bf16[64,16,512]{2,1,0:T(8,128)(2,1)S(1)}, u32[]{:S(2)}, u32[]{:S(2)}) %all-to-all-start.4) | async-done | bytes 1048608 | tf_op jit(solution)/shard_map/all_to_all | solution.py:50
  (76 shorter events, 31.3 us)
Async XLA Ops:
  0.6 36.5 %copy-start.9 = (s32[256]{0:T(256)S(1)}, s32[256]{0:T(256)}, u32[]{:S(2)}) copy-start(s32[256]{0:T(256)} %param.18) | copy-start | bytes 3076
  2.5 1.5 collective-permute-start
  4.9 4.6 %collective-permute-start.1 = (bf16[4,10240]{1,0:T(4,128)(2,1)S(1)}, bf16[4,10240]{1,0:T(4,128)(2,1)S(1)}, u32[]{:S(2)}, u32[]{:S(2)}) collective-permute-start(bf16[4,10240]{1,0:T(4,128)(2,1)S(1)} %pair.3.own_ref), channel_id=1, source_target_pairs={{0,1},{1,0},{8,9},{9,8},{2,3},{3,2},{10,11},{11,10},{4,5},{5,4},{1... | collective-permute-start | bytes 245768 | tf_op jit(solution)/shard_map/ppermute | solution.py:165
  9.5 6.9 %collective-permute-start.2 = (bf16[8,10240]{1,0:T(8,128)(2,1)S(1)}, bf16[8,10240]{1,0:T(8,128)(2,1)S(1)}, u32[]{:S(2)}, u32[]{:S(2)}) collective-permute-start(bf16[8,10240]{1,0:T(8,128)(2,1)S(1)} %pair.4.own_ref), channel_id=1, source_target_pairs={{0,9},{1,8},{8,1},{9,0},{2,11},{3,10},{10,3},{11,2},{4,13},{5,12},... | collective-permute-start | bytes 491528 | tf_op jit(solution)/shard_map/ppermute | solution.py:165
  16.5 5.4 %collective-permute-start.3 = (bf16[16,5120]{1,0:T(8,128)(2,1)S(1)}, bf16[16,5120]{1,0:T(8,128)(2,1)S(1)}, u32[]{:S(2)}, u32[]{:S(2)}) collective-permute-start(bf16[16,5120]{1,0:T(8,128)(2,1)S(1)} %get-tuple-element.50.refs_0_), channel_id=1, source_target_pairs={{0,2},{2,0},{4,6},{6,4},{1,3},{3,1},{5,7},{7,5},{8,10},{10,8},{12,... | collective-permute-start | bytes 491528 | tf_op jit(solution)/shard_map/ppermute | solution.py:165
  18.5 5.3 %collective-permute-start.4 = (bf16[16,5120]{1,0:T(8,128)(2,1)S(1)}, bf16[16,5120]{1,0:T(8,128)(2,1)S(1)}, u32[]{:S(2)}, u32[]{:S(2)}) collective-permute-start(bf16[16,5120]{1,0:T(8,128)(2,1)S(1)} %get-tuple-element.51.refs_2_), channel_id=1, source_target_pairs={{0,16},{16,0},{32,48},{48,32},{1,17},{17,1},{33,49},{49,33},{2,18}... | collective-permute-start | bytes 491528 | tf_op jit(solution)/shard_map/ppermute | solution.py:165
  25.3 8.4 %collective-permute-start.5 = (bf16[32,5120]{1,0:T(8,128)(2,1)S(1)}, bf16[32,5120]{1,0:T(8,128)(2,1)S(1)}, u32[]{:S(2)}, u32[]{:S(2)}) collective-permute-start(bf16[32,5120]{1,0:T(8,128)(2,1)S(1)} %get-tuple-element.52.refs_0_), channel_id=1, source_target_pairs={{0,6},{2,4},{4,2},{6,0},{1,7},{3,5},{5,3},{7,1},{8,14},{10,12},{12... | collective-permute-start | bytes 983048 | tf_op jit(solution)/shard_map/ppermute | solution.py:165
  27.9 8.3 %collective-permute-start.6 = (bf16[32,5120]{1,0:T(8,128)(2,1)S(1)}, bf16[32,5120]{1,0:T(8,128)(2,1)S(1)}, u32[]{:S(2)}, u32[]{:S(2)}) collective-permute-start(bf16[32,5120]{1,0:T(8,128)(2,1)S(1)} %get-tuple-element.53.refs_2_), channel_id=1, source_target_pairs={{0,48},{16,32},{32,16},{48,0},{1,49},{17,33},{33,17},{49,1},{2,50}... | collective-permute-start | bytes 983048 | tf_op jit(solution)/shard_map/ppermute | solution.py:165
  40.8 4.1 %collective-permute-start.11 = (bf16[128,4096]{1,0:T(8,128)(2,1)S(1)}, bf16[128,4096]{1,0:T(8,128)(2,1)S(1)}, u32[]{:S(2)}, u32[]{:S(2)}) collective-permute-start(bf16[128,4096]{1,0:T(8,128)(2,1)S(1)} %get-tuple-element.60), channel_id=1, source_target_pairs={{0,64},{64,0},{1,65},{65,1},{2,66},{66,2},{3,67},{67,3},{4,68},{68... | collective-permute-start | bytes 3145736 | tf_op jit(solution)/shard_map/ppermute | solution.py:46
  40.8 18.4 %collective-permute-start.10 = (bf16[64,5120]{1,0:T(8,128)(2,1)S(1)}, bf16[64,5120]{1,0:T(8,128)(2,1)S(1)}, u32[]{:S(2)}, u32[]{:S(2)}) collective-permute-start(bf16[64,5120]{1,0:T(8,128)(2,1)S(1)} %get-tuple-element.57.refs_0_), channel_id=1, source_target_pairs={{0,6},{2,4},{4,2},{6,0},{1,7},{3,5},{5,3},{7,1},{8,14},{10,12},{12... | collective-permute-start | bytes 1966088 | tf_op jit(solution)/shard_map/ppermute | solution.py:165
  41.6 17.6 %collective-permute-start.7 = (bf16[64,5120]{1,0:T(8,128)(2,1)S(1)}, bf16[64,5120]{1,0:T(8,128)(2,1)S(1)}, u32[]{:S(2)}, u32[]{:S(2)}) collective-permute-start(bf16[64,5120]{1,0:T(8,128)(2,1)S(1)} %get-tuple-element.56.refs_0_), channel_id=1, source_target_pairs={{0,16},{16,0},{32,48},{48,32},{1,17},{17,1},{33,49},{49,33},{2,18}... | collective-permute-start | bytes 1966088 | tf_op jit(solution)/shard_map/ppermute | solution.py:165
  42.4 17.7 %collective-permute-start.8 = (bf16[64,5120]{1,0:T(8,128)(2,1)S(1)}, bf16[64,5120]{1,0:T(8,128)(2,1)S(1)}, u32[]{:S(2)}, u32[]{:S(2)}) collective-permute-start(bf16[64,5120]{1,0:T(8,128)(2,1)S(1)} %get-tuple-element.56.refs_0_), channel_id=1, source_target_pairs={{0,48},{16,32},{32,16},{48,0},{1,49},{17,33},{33,17},{49,1},{2,50}... | collective-permute-start | bytes 1966088 | tf_op jit(solution)/shard_map/ppermute | solution.py:165
  44.5 16.4 %collective-permute-start.9 = (bf16[64,5120]{1,0:T(8,128)(2,1)S(1)}, bf16[64,5120]{1,0:T(8,128)(2,1)S(1)}, u32[]{:S(2)}, u32[]{:S(2)}) collective-permute-start(bf16[64,5120]{1,0:T(8,128)(2,1)S(1)} %get-tuple-element.57.refs_0_), channel_id=1, source_target_pairs={{0,2},{2,0},{4,6},{6,4},{1,3},{3,1},{5,7},{7,5},{8,10},{10,8},{12,... | collective-permute-start | bytes 1966088 | tf_op jit(solution)/shard_map/ppermute | solution.py:165
  46.2 28.6 %copy-start.1 = (bf16[64,16,512]{2,1,0:T(8,128)(2,1)}, bf16[64,16,512]{2,1,0:T(8,128)(2,1)S(1)}, u32[]{:S(2)}) copy-start(bf16[64,16,512]{2,1,0:T(8,128)(2,1)S(1)} %join.3) | copy-start | bytes 3145732
  61.4 9.8 %collective-permute-start.12 = (bf16[32,5120]{1,0:T(8,128)(2,1)S(1)}, bf16[32,5120]{1,0:T(8,128)(2,1)S(1)}, u32[]{:S(2)}, u32[]{:S(2)}) collective-permute-start(bf16[32,5120]{1,0:T(8,128)(2,1)S(1)} %get-tuple-element.65), channel_id=1, source_target_pairs={{0,48},{16,32},{32,16},{48,0},{1,49},{17,33},{33,17},{49,1},{2,50}... | collective-permute-start | bytes 983048 | tf_op jit(solution)/shard_map/ppermute | solution.py:165
  62.9 8.6 %collective-permute-start.13 = (bf16[32,5120]{1,0:T(8,128)(2,1)S(1)}, bf16[32,5120]{1,0:T(8,128)(2,1)S(1)}, u32[]{:S(2)}, u32[]{:S(2)}) collective-permute-start(bf16[32,5120]{1,0:T(8,128)(2,1)S(1)} %get-tuple-element.66), channel_id=1, source_target_pairs={{0,16},{16,0},{32,48},{48,32},{1,17},{17,1},{33,49},{49,33},{2,18}... | collective-permute-start | bytes 983048 | tf_op jit(solution)/shard_map/ppermute | solution.py:165
  62.9 9.8 %collective-permute-start.14 = (bf16[32,5120]{1,0:T(8,128)(2,1)S(1)}, bf16[32,5120]{1,0:T(8,128)(2,1)S(1)}, u32[]{:S(2)}, u32[]{:S(2)}) collective-permute-start(bf16[32,5120]{1,0:T(8,128)(2,1)S(1)} %get-tuple-element.67), channel_id=1, source_target_pairs={{0,6},{2,4},{4,2},{6,0},{1,7},{3,5},{5,3},{7,1},{8,14},{10,12},{12... | collective-permute-start | bytes 983048 | tf_op jit(solution)/shard_map/ppermute | solution.py:165
  65.5 8.4 %collective-permute-start.15 = (bf16[32,5120]{1,0:T(8,128)(2,1)S(1)}, bf16[32,5120]{1,0:T(8,128)(2,1)S(1)}, u32[]{:S(2)}, u32[]{:S(2)}) collective-permute-start(bf16[32,5120]{1,0:T(8,128)(2,1)S(1)} %get-tuple-element.68), channel_id=1, source_target_pairs={{0,2},{2,0},{4,6},{6,4},{1,3},{3,1},{5,7},{7,5},{8,10},{10,8},{12,... | collective-permute-start | bytes 983048 | tf_op jit(solution)/shard_map/ppermute | solution.py:165
  77.2 18.0 %collective-permute-start.16 = (bf16[256,5120]{1,0:T(8,128)(2,1)}, bf16[256,5120]{1,0:T(8,128)(2,1)}, u32[]{:S(2)}, u32[]{:S(2)}) collective-permute-start(bf16[256,5120]{1,0:T(8,128)(2,1)} %whole.2.refs_0_), channel_id=1, source_target_pairs={{0,64},{64,0},{1,65},{65,1},{2,66},{66,2},{3,67},{67,3},{4,68},{68... | collective-permute-start | bytes 7864328 | tf_op jit(solution)/shard_map/ppermute | solution.py:46
  77.3 17.9 %collective-permute-start.17 = (bf16[256,5120]{1,0:T(8,128)(2,1)S(1)}, bf16[256,5120]{1,0:T(8,128)(2,1)}, u32[]{:S(2)}, u32[]{:S(2)}) collective-permute-start(bf16[256,5120]{1,0:T(8,128)(2,1)S(1)} %whole.3.refs_1_), channel_id=1, source_target_pairs={{0,64},{64,0},{1,65},{65,1},{2,66},{66,2},{3,67},{67,3},{4,68},{68... | collective-permute-start | bytes 7864328 | tf_op jit(solution)/shard_map/ppermute | solution.py:46
  77.8 28.8 %all-to-all-start = ((bf16[64,16,512]{2,1,0:T(8,128)(2,1)}), bf16[64,16,512]{2,1,0:T(8,128)(2,1)}, u32[]{:S(2)}, u32[]{:S(2)}) async-start(bf16[64,16,512]{2,1,0:T(8,128)(2,1)} %copy-done.1), calls=%async_computation | async-start | bytes 2097152 | tf_op jit(solution)/shard_map/all_to_all | solution.py:50
  104.5 1.2 collective-permute-start.18
  106.5 21.0 %all-to-all-start.1 = ((f32[64,8,128]{2,1,0:T(8,128)}), f32[64,8,128]{2,1,0:T(8,128)S(1)}, u32[]{:S(2)}, u32[]{:S(2)}) async-start(f32[64,8,128]{2,1,0:T(8,128)} %chip_stats.1), calls=%async_computation.1 | async-start | bytes 524288 | tf_op jit(solution)/shard_map/all_to_all | solution.py:50
  130.9 2.7 %collective-permute-start.19 = (bf16[128,4096]{1,0:T(8,128)(2,1)S(1)}, bf16[128,4096]{1,0:T(8,128)(2,1)S(1)}, u32[]{:S(2)}, u32[]{:S(2)}) collective-permute-start(bf16[128,4096]{1,0:T(8,128)(2,1)S(1)} %get-tuple-element.86), channel_id=1, source_target_pairs={{0,64},{64,0},{1,65},{65,1},{2,66},{66,2},{3,67},{67,3},{4,68},{68... | collective-permute-start | bytes 3145736 | tf_op jit(solution)/shard_map/ppermute | solution.py:46
  135.9 24.2 %copy-start.8 = (bf16[4096]{0:T(1024)(128)(2,1)S(1)}, bf16[4096]{0:T(1024)(128)(2,1)}, u32[]{:S(2)}) copy-start(bf16[4096]{0:T(1024)(128)(2,1)} %param.16) | copy-start | bytes 24580
  135.9 24.2 %all-to-all-start.2 = ((bf16[64,16,512]{2,1,0:T(8,128)(2,1)}), bf16[64,16,512]{2,1,0:T(8,128)(2,1)S(1)}, u32[]{:S(2)}, u32[]{:S(2)}) async-start(bf16[64,16,512]{2,1,0:T(8,128)(2,1)} %join.4), calls=%async_computation.2 | async-start | bytes 2097152 | tf_op jit(solution)/shard_map/all_to_all | solution.py:50
  160.1 34.2 %copy-start.2 = (bf16[112,4096]{1,0:T(8,128)(2,1)S(1)}, bf16[112,4096]{1,0:T(8,128)(2,1)}, u32[]{:S(2)}) copy-start(bf16[112,4096]{1,0:T(8,128)(2,1)} %down_ref.3) | copy-start | bytes 2752516
  160.1 34.2 %copy-start.3 = (bf16[4096,112]{0,1:T(8,128)(2,1)S(1)}, bf16[4096,112]{0,1:T(8,128)(2,1)}, u32[]{:S(2)}) copy-start(bf16[4096,112]{0,1:T(8,128)(2,1)} %param.20) | copy-start | bytes 2752516
  160.1 34.2 %copy-start.4 = (bf16[4096,112]{0,1:T(8,128)(2,1)S(1)}, bf16[4096,112]{0,1:T(8,128)(2,1)}, u32[]{:S(2)}) copy-start(bf16[4096,112]{0,1:T(8,128)(2,1)} %param.21) | copy-start | bytes 2752516
  194.3 4.3 %collective-permute-start.20 = (bf16[64,32,512]{2,1,0:T(8,128)(2,1)S(1)}, bf16[64,32,512]{2,1,0:T(8,128)(2,1)S(1)}, u32[]{:S(2)}, u32[]{:S(2)}) collective-permute-start(bf16[64,32,512]{2,1,0:T(8,128)(2,1)S(1)} %all_to_all.25.blocks_ref), channel_id=1, source_target_pairs={{0,64},{64,0},{1,65},{65,1},{2,66},{66,2},{3,67},{67,3},{4,68},{68... | collective-permute-start | bytes 6291464 | tf_op jit(solution)/shard_map/ppermute | solution.py:46
  203.0 2.9 %collective-permute-start.21 = (bf16[128,4096]{1,0:T(8,128)(2,1)S(1)}, bf16[128,4096]{1,0:T(8,128)(2,1)S(1)}, u32[]{:S(2)}, u32[]{:S(2)}) collective-permute-start(bf16[128,4096]{1,0:T(8,128)(2,1)S(1)} %ffn_grad.3), channel_id=1, source_target_pairs={{0,64},{64,0},{1,65},{65,1},{2,66},{66,2},{3,67},{67,3},{4,68},{68... | collective-permute-start | bytes 3145736 | tf_op jit(solution)/shard_map/ppermute | solution.py:46
  208.1 25.1 %all-to-all-start.4 = ((bf16[64,16,512]{2,1,0:T(8,128)(2,1)}), bf16[64,16,512]{2,1,0:T(8,128)(2,1)S(1)}, u32[]{:S(2)}, u32[]{:S(2)}) async-start(bf16[64,16,512]{2,1,0:T(8,128)(2,1)} %join.5), calls=%async_computation.4 | async-start | bytes 2097152 | tf_op jit(solution)/shard_map/all_to_all | solution.py:50
  (5 other events, 56.3 us)

commit v12 on v11

--- a/solution.py
+++ b/solution.py
@@ -419,37 +419,36 @@
     )(place, ids, student_head_t)
 
 
-def join_kernel(*refs):
-    pairs, out_ref, rows = refs[:-2], refs[-2], refs[-1]
+def join_kernel(own_ref, came_ref, *refs):
+    out_ref, rows = refs[-2:]
     chips, height = out_ref.shape[0], 2 * SEGMENTS
-    for base, (own_ref, came_ref) in enumerate(zip(pairs[::2], pairs[1::2])):
-        for t in range(2):
-            for i in range(SEGMENTS):
-                for k in range(SEGMENT // 128):
-                    part = slice(t * chips, (t + 1) * chips)
-                    lanes = slice(i * SEGMENT + k * 128, i * SEGMENT + (k + 1) * 128)
-                    total = own_ref[part, lanes].astype(jnp.float32)
-                    total = total + came_ref[part, lanes].astype(jnp.float32)
-                    at = pl.ds(t * SEGMENTS + i, chips, stride=height)
-                    rows[k, at, :] = total
-        for k in range(SEGMENT // 128):
-            out_ref[:, base * height : (base + 1) * height, k * 128 : (k + 1) * 128] = (
-                rows[k].reshape(chips, height, 128).astype(jnp.bfloat16)
-            )
-
-
-def join_part(*pairs):
-    chips = pairs[0].shape[0] // 2
-    height = 2 * SEGMENTS
+    for t in range(2):
+        for i in range(SEGMENTS):
+            for k in range(SEGMENT // 128):
+                part = slice(t * chips, (t + 1) * chips)
+                lanes = slice(i * SEGMENT + k * 128, i * SEGMENT + (k + 1) * 128)
+                total = own_ref[part, lanes].astype(jnp.float32)
+                total = total + came_ref[part, lanes].astype(jnp.float32)
+                rows[k, pl.ds(t * SEGMENTS + i, chips, stride=height), :] = total
+    for k in range(SEGMENT // 128):
+        out_ref[:, :height, k * 128 : (k + 1) * 128] = (
+            rows[k].reshape(chips, height, 128).astype(jnp.bfloat16)
+        )
+    if len(refs) > 2:
+        out_ref[:, height:, :] = jnp.broadcast_to(refs[0][...][None], (chips, height, SEGMENT))
+
+
+def join_part(own, came, *every):
+    chips, height = own.shape[0] // 2, 2 * SEGMENTS
     return kernel_call(
         join_kernel,
         "join",
-        shape_of((chips, height * len(pairs) // 2, SEGMENT)),
+        shape_of((chips, height * (1 + len(every)), SEGMENT)),
         limit=14,
-        in_specs=[VMEM] * len(pairs),
+        in_specs=[VMEM] * (2 + len(every)),
         out_specs=VMEM,
         scratch_shapes=[pltpu.VMEM((SEGMENT // 128, chips * height, 128), jnp.float32)],
-    )(*pairs)
+    )(own, came, *every)
 
 
 def block_gain(gain_ref):
@@ -485,7 +484,7 @@
 
 
 def block_sum(blocks_ref):
-    return jnp.sum(blocks_ref[...].astype(jnp.float32), axis=0)
+    return jnp.sum(blocks_ref[:, : 2 * SEGMENTS, :].astype(jnp.float32), axis=0)
 
 
 def embed_kernel(blocks_ref, gain_ref, embedded_ref, rows_ref):
@@ -495,17 +494,14 @@
     rows_ref[...] = rows.astype(jnp.bfloat16)
 
 
-def final_kernel(blocks_ref, states_ref, gain_ref, rows_ref, grad_ref, out_ref, states):
+def final_kernel(blocks_ref, states_ref, gain_ref, grad_ref, out_ref, states):
     for i in range(SEGMENTS):
         part = states_ref[:, i * SEGMENT : (i + 1) * SEGMENT].astype(jnp.float32)
         for t in range(2):
             states[t * SEGMENTS + i : t * SEGMENTS + i + 1, :] = part[t : t + 1]
     grad = block_back(block_sum(blocks_ref), states[...], block_gain(gain_ref))
     grad_ref[...] = grad
-    height = 2 * SEGMENTS
-    half = (out_ref.shape[0], height, SEGMENT)
-    out_ref[:, :height, :] = jnp.broadcast_to(grad.astype(jnp.bfloat16)[None], half)
-    out_ref[:, height:, :] = jnp.broadcast_to(rows_ref[...][None], half)
+    out_ref[...] = jnp.broadcast_to(grad.astype(jnp.bfloat16)[None], out_ref.shape)
 
 
 def state_kernel(blocks_ref, grad_ref, embedded_ref, gain_ref, out_ref):
@@ -521,30 +517,44 @@
 BLOCK = (2 * SEGMENTS, SEGMENT)
 
 
-def segment_rows(rows, first):
-    height = 4 * SEGMENTS
-    parts = []
-    for t in range(2):
-        at = pl.ds(first + t * SEGMENTS, rows.shape[1] // height, stride=height)
-        parts.append(jnp.concatenate([rows[k, at, :] for k in range(SEGMENT // 128)], axis=1))
-    return jnp.concatenate(parts, axis=0).astype(jnp.bfloat16)
-
-
-def ffn_grad_kernel(blocks_ref, down_ref, gate_ref, up_ref, out_ref, rows):
-    values = blocks_ref[...].astype(jnp.float32)
+def spread_rows(values, rows):
+    values = values.astype(jnp.float32)
     values = values.reshape(values.shape[0] * values.shape[1], values.shape[2])
     for k in range(SEGMENT // 128):
         rows[k] = values[:, k * 128 : (k + 1) * 128]
+
+
+def segment_rows(rows, segment):
+    height = 2 * SEGMENTS
+    parts = []
+    for t in range(2):
+        at = pl.ds(t * SEGMENTS + segment, rows.shape[1] // height, stride=height)
+        parts.append(jnp.concatenate([rows[k, at, :] for k in range(SEGMENT // 128)], axis=1))
+    return jnp.concatenate(parts, axis=0).astype(jnp.bfloat16)
+
+
+def gate_kernel(own_ref, other_ref, gate_ref, up_ref, *refs):
+    rows = refs[-1]
+    for ref, out in zip((own_ref, other_ref), refs):
+        spread_rows(ref[:, 2 * SEGMENTS :, :], rows)
+        hidden = None
+        for i in range(SEGMENTS):
+            columns = slice(i * SEGMENT, (i + 1) * SEGMENT)
+            weight = jnp.concatenate([gate_ref[:, columns], up_ref[:, columns]], axis=0)
+            term = row_product(weight, segment_rows(rows, i))
+            hidden = term if hidden is None else hidden + term
+        out[...] = hidden
+
+
+def ffn_grad_kernel(blocks_ref, hidden_ref, down_ref, gate_ref, up_ref, out_ref, rows):
+    spread_rows(blocks_ref[...], rows)
     units = down_ref.shape[0]
-    hidden, act_grad = None, None
+    act_grad = None
     for i in range(SEGMENTS):
         columns = slice(i * SEGMENT, (i + 1) * SEGMENT)
-        weight = jnp.concatenate([gate_ref[:, columns], up_ref[:, columns]], axis=0)
-        term = row_product(weight, segment_rows(rows, 2 * SEGMENTS + i))
-        hidden = term if hidden is None else hidden + term
         term = row_product(down_ref[:, columns], segment_rows(rows, i))
         act_grad = term if act_grad is None else act_grad + term
-    gate, upper = hidden[:units, :], hidden[units:, :]
+    gate, upper = hidden_ref[:units, :], hidden_ref[units:, :]
     sigmoid_gate = jax.nn.sigmoid(gate)
     gate_grad = act_grad * upper * sigmoid_gate * (1.0 + gate * (1.0 - sigmoid_gate))
     upper_grad = act_grad * gate * sigmoid_gate
@@ -561,17 +571,16 @@
         out_ref[:, columns] = out.astype(out_ref.dtype)
 
 
-def ffn_grad_part(blocks, dtype, *weights):
-    chips, height, _ = blocks.shape
-    return kernel_call(
-        ffn_grad_kernel,
-        "ffn_grad",
-        shape_of((2 * chips, SEGMENTS * SEGMENT), dtype),
+def ffn_part(body, name, out_shape, *operands):
+    return kernel_call(
+        body,
+        name,
+        out_shape,
         limit=20,
-        in_specs=[VMEM] * (1 + len(weights)),
-        out_specs=VMEM,
-        scratch_shapes=[pltpu.VMEM((SEGMENT // 128, chips * height, 128), jnp.float32)],
-    )(blocks, *weights)
+        in_specs=[VMEM] * len(operands),
+        out_specs=[VMEM] * len(out_shape),
+        scratch_shapes=[pltpu.VMEM((SEGMENT // 128, 64 * 2 * SEGMENTS, 128), jnp.float32)],
+    )(*operands)
 
 
 def shards(
@@ -625,11 +634,9 @@
         came = (along(first, "z", mask), along(second, "x", mask))
         bits = (jnp.stack([z, x]) >> bit) & 1
         first, second = in_pairs(bits, (first, came[0], second, came[1]))
-    ids = token_ids.reshape(1, 256)
-    ids, first, second = lax.optimization_barrier((ids, first, second))
     came = [along(first, "x", 1), along(first, "x", 3), along(second, "z", 1), along(second, "z", 3)]
     place = jnp.stack([core, device]).astype(jnp.int32)
-    own, send = pick_part(place, ids, student_head_t)
+    own, send = pick_part(place, token_ids.reshape(1, 256), student_head_t)
     came, picked = lax.optimization_barrier((came, join_part(own, swap_cores(send))))
     halves = halves_of(came)
     far = [
@@ -669,22 +676,34 @@
         own_core, every, weight, teacher, student, student_head_t
     )
     divergence = divergence.reshape(4, 4, 2, 2, 2, 2).transpose(4, 0, 2, 1, 3, 5).reshape(256)
-    blocks = exchange(join_part(own, swap_cores(send)), CHIPS)
-    final_grad, blocks = kernel_call(
+    blocks = exchange(join_part(own, swap_cores(send), ffn_rows), CHIPS)
+    final_grad, halves = kernel_call(
         final_kernel,
         "final",
-        [shape_of(BLOCK, jnp.float32), shape_of((64, 2 * BLOCK[0], BLOCK[1]))],
+        [shape_of(BLOCK, jnp.float32), shape_of((64,) + BLOCK)],
         limit=12,
-        in_specs=[VMEM] * 4,
+        in_specs=[VMEM] * 3,
         out_specs=[VMEM] * 2,
         scratch_shapes=[pltpu.VMEM(BLOCK, jnp.float32)],
-    )(blocks, student_states, student_gain, ffn_rows)
-    blocks = exchange(blocks, CHIPS)
+    )(blocks, student_states, student_gain)
+    hidden = ffn_part(
+        gate_kernel,
+        "gate_upper",
+        [shape_of((2 * gate_t.shape[0], 128), jnp.float32)] * 2,
+        blocks,
+        swap_cores(blocks),
+        gate_t,
+        up_t,
+    )
+    halves = exchange(halves, CHIPS)
     weights = (down_weight, gate_t, up_t)
-    others = swap_cores(blocks)
-    own = ffn_grad_part(blocks, jnp.float32, *weights)
+    shape = (128, SEGMENTS * SEGMENT)
+    others = swap_cores(halves)
+    (own,) = ffn_part(
+        ffn_grad_kernel, "ffn_grad", [shape_of(shape, jnp.float32)], halves, hidden[0], *weights
+    )
     others, own = lax.optimization_barrier((others, own))
-    send = ffn_grad_part(others, jnp.bfloat16, *weights)
+    (send,) = ffn_part(ffn_grad_kernel, "ffn_grad", [shape_of(shape)], others, hidden[1], *weights)
     ffn_grad = exchange(join_part(own, swap_cores(send)), CHIPS)
     state_grad = kernel_call(
         state_kernel,

time: 235 us -> 230 us (0.979)
  blocking collectives: 33.8 us -> 59.7 us
  waiting for transfers between devices: 91.5 us -> 70.7 us
  starting transfers between devices: 53 us -> 45.6 us
  Pallas kernels: 51.3 us -> 48.1 us
    all_to_all x1 -> x2, blocking collectives: 33.8 us -> 59.7 us  [exchange(): return lax.all_to_all(blocks, axes, split_axis=0, concat_axis=0, tiled=True)]
    all_to_all x4 -> x3, waiting for transfers between devices: 45.2 us -> 28 us  [exchange(): return lax.all_to_all(blocks, axes, split_axis=0, concat_axis=0, tiled=True)]
    all_to_all x4 -> x3, starting transfers between devices: 29.6 us -> 23.9 us  [exchange(): return lax.all_to_all(blocks, axes, split_axis=0, concat_axis=0, tiled=True)]
    pallas_call x5 -> x6, Pallas kernels: 14.5 us -> 11.2 us  [the longest x3 6.29 us: ffn_part(): kernel_call(body, name, out_shape, limit=20, in_specs=[VMEM] * len(operan...]
    ppermute x8 -> x9, waiting for transfers between devices: 7.51 us -> 5.98 us  [swap_cores(): return lax.ppermute(values, 'core', [(0, 1), (1, 0)])]
  transfers between devices with their start and end apart: 26 -> 26, of which waited for: 20 -> 17; matrix products, arithmetic and copies ran while one was open for 1% -> 1% of each run, Pallas kernels for 11% -> 14%
where the time goes in v12:
time: 230 us; the launch traced here: 229 us
  waiting for transfers between devices  70.7 us (31%)
  blocking collectives  59.7 us (26%)
  Pallas kernels  48.1 us (21%)
  starting transfers between devices  45.6 us (20%)
  local copies, waits for them, and re-layouts  3.29 us (1%)
    all_to_all x2, blocking collectives, exchange(): return lax.all_to_all(blocks, axes, split_axis=0, concat_axis=0, tiled=True)  59.7 us
    ppermute x14, waiting for transfers between devices, along(): return lax.ppermute(block, line, [(i, i ^ mask) for i in range(4)])  36.7 us
    all_to_all x3, waiting for transfers between devices, exchange(): return lax.all_to_all(blocks, axes, split_axis=0, concat_axis=0, tiled=True)  28 us
    all_to_all x3, starting transfers between devices, exchange(): return lax.all_to_all(blocks, axes, split_axis=0, concat_axis=0, tiled=True)  23.9 us
    ppermute x14, starting transfers between devices, along(): return lax.ppermute(block, line, [(i, i ^ mask) for i in range(4)])  20.2 us
    pallas_call x2, Pallas kernels, logits_part(): kernel_call(functools.partial(logits_kernel, last), 'logits', out_shape,...  18.1 us
    pallas_call x3, Pallas kernels, ffn_part(): kernel_call(body, name, out_shape, limit=20, in_specs=[VMEM] * len(operan...  6.29 us
    ppermute x9, waiting for transfers between devices, swap_cores(): return lax.ppermute(values, 'core', [(0, 1), (1, 0)])  5.98 us
  transfers between devices with their start and end apart: 26, of which 17 were waited for; matrix products, arithmetic and copies ran while one was open for 1% of the time, Pallas kernels for 14%

profile of v12, /device:TPU:0, one launch (start us, length us, event | category | flops | bytes accessed | tf_op | source)
XLA Modules:
  0.0 229.2 jit_solution(7445369425858535716)
XLA Ops:
  0.6 1.9 rows.1
  4.9 1.7 collective-permute-start.1
  6.6 2.9 %collective-permute-done.1.came_ref = bf16[4,10240]{1,0:T(4,128)(2,1)S(1)} collective-permute-done((bf16[4,10240]{1,0:T(4,128)(2,1)S(1)}, bf16[4,10240]{1,0:T(4,128)(2,1)S(1)}, u32[]{:S(2)}, u32[]{:S(2)}) %collective-permute-start.1) | collective-permute-done | bytes 81952 | tf_op jit(solution)/shard_map/ppermute | solution.py:165
  9.5 3.2 %collective-permute-start.2 = (bf16[8,10240]{1,0:T(8,128)(2,1)S(1)}, bf16[8,10240]{1,0:T(8,128)(2,1)S(1)}, u32[]{:S(2)}, u32[]{:S(2)}) collective-permute-start(bf16[8,10240]{1,0:T(8,128)(2,1)S(1)} %pair.4.own_ref), channel_id=1, source_target_pairs={{0,9},{1,8},{8,1},{9,0},{2,11},{3,10},{10,3},{11,2},{4,13},{5,12},... | collective-permute-start | bytes 491528 | tf_op jit(solution)/shard_map/ppermute | solution.py:165
  12.7 3.7 %collective-permute-done.2.came_ref = bf16[8,10240]{1,0:T(8,128)(2,1)S(1)} collective-permute-done((bf16[8,10240]{1,0:T(8,128)(2,1)S(1)}, bf16[8,10240]{1,0:T(8,128)(2,1)S(1)}, u32[]{:S(2)}, u32[]{:S(2)}) %collective-permute-start.2) | collective-permute-done | bytes 163872 | tf_op jit(solution)/shard_map/ppermute | solution.py:165
  16.5 2.0 collective-permute-start.3
  20.7 3.6 %pick.1 = (bf16[128,4096]{1,0:T(8,128)(2,1)S(1)}, bf16[128,4096]{1,0:T(8,128)(2,1)S(1)}) custom-call(s32[2]{0:T(128)S(1)} %pad_add_fusion.1.place_ref, s32[1,256]{1,0:T(1,128)S(1)} %bitcast.26, bf16[501,4096]{1,0:T(8,128)(2,1)} %bitcast.29), custom_call_target="tpu_custom_call" | custom-call | flops 1 | bytes 1 | tf_op jit(solution)/shard_map/pick/pallas_call | solution.py:408
  25.9 2.6 %collective-permute-start.5 = (bf16[32,5120]{1,0:T(8,128)(2,1)S(1)}, bf16[32,5120]{1,0:T(8,128)(2,1)S(1)}, u32[]{:S(2)}, u32[]{:S(2)}) collective-permute-start(bf16[32,5120]{1,0:T(8,128)(2,1)S(1)} %get-tuple-element.51.refs_0_), channel_id=1, source_target_pairs={{0,6},{2,4},{4,2},{6,0},{1,7},{3,5},{5,3},{7,1},{8,14},{10,12},{12... | collective-permute-start | bytes 983048 | tf_op jit(solution)/shard_map/ppermute | solution.py:165
  28.5 2.1 collective-permute-start.6
  30.7 6.6 %collective-permute-done.5.refs_1_ = bf16[32,5120]{1,0:T(8,128)(2,1)S(1)} collective-permute-done((bf16[32,5120]{1,0:T(8,128)(2,1)S(1)}, bf16[32,5120]{1,0:T(8,128)(2,1)S(1)}, u32[]{:S(2)}, u32[]{:S(2)}) %collective-permute-start.5) | collective-permute-done | bytes 327712 | tf_op jit(solution)/shard_map/ppermute | solution.py:165
  37.3 2.2 collective-permute-done.6.refs_3_
  41.5 2.8 %collective-permute-start.8 = (bf16[64,5120]{1,0:T(8,128)(2,1)S(1)}, bf16[64,5120]{1,0:T(8,128)(2,1)S(1)}, u32[]{:S(2)}, u32[]{:S(2)}) collective-permute-start(bf16[64,5120]{1,0:T(8,128)(2,1)S(1)} %get-tuple-element.53.refs_0_), channel_id=1, source_target_pairs={{0,48},{16,32},{32,16},{48,0},{1,49},{17,33},{33,17},{49,1},{2,50}... | collective-permute-start | bytes 1966088 | tf_op jit(solution)/shard_map/ppermute | solution.py:165
  45.5 12.4 %collective-permute-done.10.refs_3_.refs_2_ = bf16[64,5120]{1,0:T(8,128)(2,1)S(1)} collective-permute-done((bf16[64,5120]{1,0:T(8,128)(2,1)S(1)}, bf16[64,5120]{1,0:T(8,128)(2,1)S(1)}, u32[]{:S(2)}, u32[]{:S(2)}) %collective-permute-start.10) | collective-permute-done | bytes 655392 | tf_op jit(solution)/shard_map/ppermute | solution.py:165
  60.2 1.6 collective-permute-start.12
  61.8 1.9 collective-permute-start.14
  63.7 5.4 %collective-permute-done.12.refs_3_ = bf16[32,5120]{1,0:T(8,128)(2,1)S(1)} collective-permute-done((bf16[32,5120]{1,0:T(8,128)(2,1)S(1)}, bf16[32,5120]{1,0:T(8,128)(2,1)S(1)}, u32[]{:S(2)}, u32[]{:S(2)}) %collective-permute-start.12) | collective-permute-done | bytes 327712 | tf_op jit(solution)/shard_map/ppermute | solution.py:165
  71.7 2.4 %whole.2.refs_0_ = bf16[256,5120]{1,0:T(8,128)(2,1)} custom-call(s32[1]{0:T(128)} %bitcast.1.place_ref, bf16[64,5120]{1,0:T(8,128)(2,1)S(1)} %get-tuple-element.53.refs_0_, bf16[64,5120]{1,0:T(8,128)(2,1)S(1)} %collective-permute-done.7.refs_0_.refs_1_, bf16[64,5120]{1,0:T(8,128)(2,1)S(1)} %collective-permute-done.8.refs_1_.refs_2_, ...), custom_call_target="tpu_custom_call" | custom-call | flops 1 | bytes 1 | tf_op jit(solution)/shard_map/whole/pallas_call | solution.py:185
  74.7 9.1 %all-to-all-start = ((bf16[64,16,512]{2,1,0:T(8,128)(2,1)}), bf16[64,16,512]{2,1,0:T(8,128)(2,1)}, u32[]{:S(2)}, u32[]{:S(2)}) async-start(bf16[64,16,512]{2,1,0:T(8,128)(2,1)} %copy-done.3), calls=%async_computation | async-start | bytes 2097152 | tf_op jit(solution)/shard_map/all_to_all | solution.py:50
  83.8 8.7 %logits.2 = (f32[501,256]{1,0:T(8,128)S(1)}, f32[501,256]{1,0:T(8,128)S(1)}, f32[501,256]{1,0:T(8,128)S(1)}) custom-call(s32[1]{0:T(128)} %bitcast.core_ref.place_ref, bf16[256,5120]{1,0:T(8,128)(2,1)} %whole.2.refs_0_, bf16[256,5120]{1,0:T(8,128)(2,1)} %copy-done, bf16[501,4096]{1,0:T(8,128)(2,1)} %bitcast.30, bf16[501,16384]{1,0:T(8,128)(2,1)} %bitcast.27), custom_call_target="tpu_custom_call" | custom-call | flops 1 | bytes 1 | tf_op jit(solution)/shard_map/logits/pallas_call | solution.py:290
  92.6 9.3 %logits.3 = (f32[501,256]{1,0:T(8,128)S(1)}, f32[501,256]{1,0:T(8,128)S(1)}, f32[8,128]{1,0:T(8,128)S(1)}) custom-call(s32[1]{0:T(128)S(6)} %sub.3.place_ref, bf16[256,5120]{1,0:T(8,128)(2,1)} %collective-permute-done.16.refs_0_, bf16[256,5120]{1,0:T(8,128)(2,1)} %collective-permute-done.17.refs_1_, bf16[501,4096]{1,0:T(8,128)(2,1)} %bitcast.31, ...), custom_call_target="tpu_custom_call" | custom-call | flops 1 | bytes 1 | tf_op jit(solution)/shard_map/logits/pallas_call | solution.py:290
  103.9 10.1 %all-to-all-start.1 = ((f32[64,8,128]{2,1,0:T(8,128)}), f32[64,8,128]{2,1,0:T(8,128)S(1)}, u32[]{:S(2)}, u32[]{:S(2)}) async-start(f32[64,8,128]{2,1,0:T(8,128)} %chip_stats.1), calls=%async_computation.1 | async-start | bytes 524288 | tf_op jit(solution)/shard_map/all_to_all | solution.py:50
  114.4 10.5 %all-to-all-done.1.every_ref = f32[64,8,128]{2,1,0:T(8,128)S(1)} async-done(((f32[64,8,128]{2,1,0:T(8,128)}), f32[64,8,128]{2,1,0:T(8,128)S(1)}, u32[]{:S(2)}, u32[]{:S(2)}) %all-to-all-start.1) | async-done | bytes 262176 | tf_op jit(solution)/shard_map/all_to_all | solution.py:50
  124.9 3.4 %row_grad.1 = (f32[128,4096]{1,0:T(8,128)S(1)}, bf16[128,4096]{1,0:T(8,128)(2,1)S(1)}, f32[1,256]{1,0:T(1,128)S(1)}) custom-call(s32[1]{0:T(128)} %bitcast.core_ref.place_ref, f32[64,8,128]{2,1,0:T(8,128)S(1)} %all-to-all-done.1.every_ref, f32[1,256]{1,0:T(1,128)S(1)} %reshape.45.weight_ref, f32[501,256]{1,0:T(8,128)S(1)} %get-tuple-element.78.teacher_ref, ...), custom_call_target="tpu_custom_call" | custom-call | flops 1 | bytes 1 | tf_op jit(solution)/shard_map/row_grad/pallas_call | solution.py:369
  132.4 34.8 %all_to_all.25.blocks_ref.own_ref = bf16[64,32,512]{2,1,0:T(8,128)(2,1)S(1)} all-to-all(bf16[64,32,512]{2,1,0:T(8,128)(2,1)S(1)} %join.4), channel_id=1, replica_groups=mesh['core'=2,'x'=4,'yh'=2,'z'=4,'yl'=2] {'x','yh','z','yl'}, dimensions={0} | all-to-all | bytes 4194304 | tf_op jit(solution)/shard_map/all_to_all | solution.py:50
  167.6 24.9 %all_to_all.26.blocks_ref = bf16[64,16,512]{2,1,0:T(8,128)(2,1)S(1)} all-to-all(bf16[64,16,512]{2,1,0:T(8,128)(2,1)S(1)} %get-tuple-element.85), channel_id=1, replica_groups=mesh['core'=2,'x'=4,'yh'=2,'z'=4,'yl'=2] {'x','yh','z','yl'}, dimensions={0} | all-to-all | bytes 2097152 | tf_op jit(solution)/shard_map/all_to_all | solution.py:50
  192.5 2.8 %gate_upper.1 = (f32[224,128]{1,0:T(8,128)S(1)}, f32[224,128]{1,0:T(8,128)S(1)}) custom-call(bf16[64,32,512]{2,1,0:T(8,128)(2,1)S(1)} %all_to_all.25.blocks_ref.own_ref, bf16[64,32,512]{2,1,0:T(8,128)(2,1)S(1)} %collective-permute-done.21.other_ref, bf16[112,4096]{1,0:T(8,128)(2,1)S(1)} %bitcast.16, bf16[112,4096]{1,0:T(8,128)(2,1)S(1)} %bitcast.19), custom_call_target="tpu_custom_call" | custom-call | flops 1 | bytes 1 | tf_op jit(solution)/shard_map/gate_upper/pallas_call | solution.py:575
  195.3 1.8 ffn_grad.2.own_ref
  197.1 1.8 ffn_grad.3
  199.4 2.3 collective-permute-done.22.came_ref
  201.7 2.3 join.5
  204.0 4.7 %all-to-all-start.4 = ((bf16[64,16,512]{2,1,0:T(8,128)(2,1)}), bf16[64,16,512]{2,1,0:T(8,128)(2,1)S(1)}, u32[]{:S(2)}, u32[]{:S(2)}) async-start(bf16[64,16,512]{2,1,0:T(8,128)(2,1)} %join.5), calls=%async_computation.4 | async-start | bytes 2097152 | tf_op jit(solution)/shard_map/all_to_all | solution.py:50
  210.8 17.5 %all-to-all-done.4.blocks_ref = bf16[64,16,512]{2,1,0:T(8,128)(2,1)S(1)} async-done(((bf16[64,16,512]{2,1,0:T(8,128)(2,1)}), bf16[64,16,512]{2,1,0:T(8,128)(2,1)S(1)}, u32[]{:S(2)}, u32[]{:S(2)}) %all-to-all-start.4) | async-done | bytes 1048608 | tf_op jit(solution)/shard_map/all_to_all | solution.py:50
  (78 shorter events, 25.5 us)
Async XLA Ops:
  2.5 1.5 collective-permute-start
  4.9 4.6 %collective-permute-start.1 = (bf16[4,10240]{1,0:T(4,128)(2,1)S(1)}, bf16[4,10240]{1,0:T(4,128)(2,1)S(1)}, u32[]{:S(2)}, u32[]{:S(2)}) collective-permute-start(bf16[4,10240]{1,0:T(4,128)(2,1)S(1)} %pair.3.own_ref), channel_id=1, source_target_pairs={{0,1},{1,0},{8,9},{9,8},{2,3},{3,2},{10,11},{11,10},{4,5},{5,4},{1... | collective-permute-start | bytes 245768 | tf_op jit(solution)/shard_map/ppermute | solution.py:165
  9.5 6.9 %collective-permute-start.2 = (bf16[8,10240]{1,0:T(8,128)(2,1)S(1)}, bf16[8,10240]{1,0:T(8,128)(2,1)S(1)}, u32[]{:S(2)}, u32[]{:S(2)}) collective-permute-start(bf16[8,10240]{1,0:T(8,128)(2,1)S(1)} %pair.4.own_ref), channel_id=1, source_target_pairs={{0,9},{1,8},{8,1},{9,0},{2,11},{3,10},{10,3},{11,2},{4,13},{5,12},... | collective-permute-start | bytes 491528 | tf_op jit(solution)/shard_map/ppermute | solution.py:165
  16.5 8.0 %collective-permute-start.3 = (bf16[16,5120]{1,0:T(8,128)(2,1)S(1)}, bf16[16,5120]{1,0:T(8,128)(2,1)S(1)}, u32[]{:S(2)}, u32[]{:S(2)}) collective-permute-start(bf16[16,5120]{1,0:T(8,128)(2,1)S(1)} %get-tuple-element.49.refs_0_), channel_id=1, source_target_pairs={{0,2},{2,0},{4,6},{6,4},{1,3},{3,1},{5,7},{7,5},{8,10},{10,8},{12,... | collective-permute-start | bytes 491528 | tf_op jit(solution)/shard_map/ppermute | solution.py:165
  18.5 6.0 %collective-permute-start.4 = (bf16[16,5120]{1,0:T(8,128)(2,1)S(1)}, bf16[16,5120]{1,0:T(8,128)(2,1)S(1)}, u32[]{:S(2)}, u32[]{:S(2)}) collective-permute-start(bf16[16,5120]{1,0:T(8,128)(2,1)S(1)} %get-tuple-element.50.refs_2_), channel_id=1, source_target_pairs={{0,16},{16,0},{32,48},{48,32},{1,17},{17,1},{33,49},{49,33},{2,18}... | collective-permute-start | bytes 491528 | tf_op jit(solution)/shard_map/ppermute | solution.py:165
  24.3 20.0 %collective-permute-start.11 = (bf16[128,4096]{1,0:T(8,128)(2,1)S(1)}, bf16[128,4096]{1,0:T(8,128)(2,1)S(1)}, u32[]{:S(2)}, u32[]{:S(2)}) collective-permute-start(bf16[128,4096]{1,0:T(8,128)(2,1)S(1)} %get-tuple-element.56), channel_id=1, source_target_pairs={{0,64},{64,0},{1,65},{65,1},{2,66},{66,2},{3,67},{67,3},{4,68},{68... | collective-permute-start | bytes 3145736 | tf_op jit(solution)/shard_map/ppermute | solution.py:46
  25.9 11.4 %collective-permute-start.5 = (bf16[32,5120]{1,0:T(8,128)(2,1)S(1)}, bf16[32,5120]{1,0:T(8,128)(2,1)S(1)}, u32[]{:S(2)}, u32[]{:S(2)}) collective-permute-start(bf16[32,5120]{1,0:T(8,128)(2,1)S(1)} %get-tuple-element.51.refs_0_), channel_id=1, source_target_pairs={{0,6},{2,4},{4,2},{6,0},{1,7},{3,5},{5,3},{7,1},{8,14},{10,12},{12... | collective-permute-start | bytes 983048 | tf_op jit(solution)/shard_map/ppermute | solution.py:165
  28.5 11.0 %collective-permute-start.6 = (bf16[32,5120]{1,0:T(8,128)(2,1)S(1)}, bf16[32,5120]{1,0:T(8,128)(2,1)S(1)}, u32[]{:S(2)}, u32[]{:S(2)}) collective-permute-start(bf16[32,5120]{1,0:T(8,128)(2,1)S(1)} %get-tuple-element.52.refs_2_), channel_id=1, source_target_pairs={{0,48},{16,32},{32,16},{48,0},{1,49},{17,33},{33,17},{49,1},{2,50}... | collective-permute-start | bytes 983048 | tf_op jit(solution)/shard_map/ppermute | solution.py:165
  40.6 17.3 %collective-permute-start.10 = (bf16[64,5120]{1,0:T(8,128)(2,1)S(1)}, bf16[64,5120]{1,0:T(8,128)(2,1)S(1)}, u32[]{:S(2)}, u32[]{:S(2)}) collective-permute-start(bf16[64,5120]{1,0:T(8,128)(2,1)S(1)} %get-tuple-element.54.refs_0_), channel_id=1, source_target_pairs={{0,6},{2,4},{4,2},{6,0},{1,7},{3,5},{5,3},{7,1},{8,14},{10,12},{12... | collective-permute-start | bytes 1966088 | tf_op jit(solution)/shard_map/ppermute | solution.py:165
  41.4 16.5 %collective-permute-start.7 = (bf16[64,5120]{1,0:T(8,128)(2,1)S(1)}, bf16[64,5120]{1,0:T(8,128)(2,1)S(1)}, u32[]{:S(2)}, u32[]{:S(2)}) collective-permute-start(bf16[64,5120]{1,0:T(8,128)(2,1)S(1)} %get-tuple-element.53.refs_0_), channel_id=1, source_target_pairs={{0,16},{16,0},{32,48},{48,32},{1,17},{17,1},{33,49},{49,33},{2,18}... | collective-permute-start | bytes 1966088 | tf_op jit(solution)/shard_map/ppermute | solution.py:165
  41.5 16.9 %collective-permute-start.8 = (bf16[64,5120]{1,0:T(8,128)(2,1)S(1)}, bf16[64,5120]{1,0:T(8,128)(2,1)S(1)}, u32[]{:S(2)}, u32[]{:S(2)}) collective-permute-start(bf16[64,5120]{1,0:T(8,128)(2,1)S(1)} %get-tuple-element.53.refs_0_), channel_id=1, source_target_pairs={{0,48},{16,32},{32,16},{48,0},{1,49},{17,33},{33,17},{49,1},{2,50}... | collective-permute-start | bytes 1966088 | tf_op jit(solution)/shard_map/ppermute | solution.py:165
  44.3 15.5 %collective-permute-start.9 = (bf16[64,5120]{1,0:T(8,128)(2,1)S(1)}, bf16[64,5120]{1,0:T(8,128)(2,1)S(1)}, u32[]{:S(2)}, u32[]{:S(2)}) collective-permute-start(bf16[64,5120]{1,0:T(8,128)(2,1)S(1)} %get-tuple-element.54.refs_0_), channel_id=1, source_target_pairs={{0,2},{2,0},{4,6},{6,4},{1,3},{3,1},{5,7},{7,5},{8,10},{10,8},{12,... | collective-permute-start | bytes 1966088 | tf_op jit(solution)/shard_map/ppermute | solution.py:165
  45.5 26.1 %copy-start.3 = (bf16[64,16,512]{2,1,0:T(8,128)(2,1)}, bf16[64,16,512]{2,1,0:T(8,128)(2,1)S(1)}, u32[]{:S(2)}) copy-start(bf16[64,16,512]{2,1,0:T(8,128)(2,1)S(1)} %join.3) | copy-start | bytes 3145732
  60.2 8.9 %collective-permute-start.12 = (bf16[32,5120]{1,0:T(8,128)(2,1)S(1)}, bf16[32,5120]{1,0:T(8,128)(2,1)S(1)}, u32[]{:S(2)}, u32[]{:S(2)}) collective-permute-start(bf16[32,5120]{1,0:T(8,128)(2,1)S(1)} %get-tuple-element.61), channel_id=1, source_target_pairs={{0,48},{16,32},{32,16},{48,0},{1,49},{17,33},{33,17},{49,1},{2,50}... | collective-permute-start | bytes 983048 | tf_op jit(solution)/shard_map/ppermute | solution.py:165
  61.8 7.6 %collective-permute-start.13 = (bf16[32,5120]{1,0:T(8,128)(2,1)S(1)}, bf16[32,5120]{1,0:T(8,128)(2,1)S(1)}, u32[]{:S(2)}, u32[]{:S(2)}) collective-permute-start(bf16[32,5120]{1,0:T(8,128)(2,1)S(1)} %get-tuple-element.62), channel_id=1, source_target_pairs={{0,16},{16,0},{32,48},{48,32},{1,17},{17,1},{33,49},{49,33},{2,18}... | collective-permute-start | bytes 983048 | tf_op jit(solution)/shard_map/ppermute | solution.py:165
  61.8 8.8 %collective-permute-start.14 = (bf16[32,5120]{1,0:T(8,128)(2,1)S(1)}, bf16[32,5120]{1,0:T(8,128)(2,1)S(1)}, u32[]{:S(2)}, u32[]{:S(2)}) collective-permute-start(bf16[32,5120]{1,0:T(8,128)(2,1)S(1)} %get-tuple-element.63), channel_id=1, source_target_pairs={{0,6},{2,4},{4,2},{6,0},{1,7},{3,5},{5,3},{7,1},{8,14},{10,12},{12... | collective-permute-start | bytes 983048 | tf_op jit(solution)/shard_map/ppermute | solution.py:165
  63.7 7.1 %collective-permute-start.15 = (bf16[32,5120]{1,0:T(8,128)(2,1)S(1)}, bf16[32,5120]{1,0:T(8,128)(2,1)S(1)}, u32[]{:S(2)}, u32[]{:S(2)}) collective-permute-start(bf16[32,5120]{1,0:T(8,128)(2,1)S(1)} %get-tuple-element.64), channel_id=1, source_target_pairs={{0,2},{2,0},{4,6},{6,4},{1,3},{3,1},{5,7},{7,5},{8,10},{10,8},{12,... | collective-permute-start | bytes 983048 | tf_op jit(solution)/shard_map/ppermute | solution.py:165
  74.1 18.4 %collective-permute-start.16 = (bf16[256,5120]{1,0:T(8,128)(2,1)}, bf16[256,5120]{1,0:T(8,128)(2,1)}, u32[]{:S(2)}, u32[]{:S(2)}) collective-permute-start(bf16[256,5120]{1,0:T(8,128)(2,1)} %whole.2.refs_0_), channel_id=1, source_target_pairs={{0,64},{64,0},{1,65},{65,1},{2,66},{66,2},{3,67},{67,3},{4,68},{68... | collective-permute-start | bytes 7864328 | tf_op jit(solution)/shard_map/ppermute | solution.py:46
  74.2 18.3 %collective-permute-start.17 = (bf16[256,5120]{1,0:T(8,128)(2,1)S(1)}, bf16[256,5120]{1,0:T(8,128)(2,1)}, u32[]{:S(2)}, u32[]{:S(2)}) collective-permute-start(bf16[256,5120]{1,0:T(8,128)(2,1)S(1)} %whole.3.refs_1_), channel_id=1, source_target_pairs={{0,64},{64,0},{1,65},{65,1},{2,66},{66,2},{3,67},{67,3},{4,68},{68... | collective-permute-start | bytes 7864328 | tf_op jit(solution)/shard_map/ppermute | solution.py:46
  74.7 29.2 %all-to-all-start = ((bf16[64,16,512]{2,1,0:T(8,128)(2,1)}), bf16[64,16,512]{2,1,0:T(8,128)(2,1)}, u32[]{:S(2)}, u32[]{:S(2)}) async-start(bf16[64,16,512]{2,1,0:T(8,128)(2,1)} %copy-done.3), calls=%async_computation | async-start | bytes 2097152 | tf_op jit(solution)/shard_map/all_to_all | solution.py:50
  92.5 21.5 %copy-start.10 = (f32[256]{0:T(256)S(1)}, f32[256]{0:T(256)}, u32[]{:S(2)}) copy-start(f32[256]{0:T(256)} %param.23) | copy-start | bytes 3076
  101.9 1.2 collective-permute-start.18
  103.9 21.0 %all-to-all-start.1 = ((f32[64,8,128]{2,1,0:T(8,128)}), f32[64,8,128]{2,1,0:T(8,128)S(1)}, u32[]{:S(2)}, u32[]{:S(2)}) async-start(f32[64,8,128]{2,1,0:T(8,128)} %chip_stats.1), calls=%async_computation.1 | async-start | bytes 524288 | tf_op jit(solution)/shard_map/all_to_all | solution.py:50
  128.3 2.7 %collective-permute-start.19 = (bf16[128,4096]{1,0:T(8,128)(2,1)S(1)}, bf16[128,4096]{1,0:T(8,128)(2,1)S(1)}, u32[]{:S(2)}, u32[]{:S(2)}) collective-permute-start(bf16[128,4096]{1,0:T(8,128)(2,1)S(1)} %get-tuple-element.82), channel_id=1, source_target_pairs={{0,64},{64,0},{1,65},{65,1},{2,66},{66,2},{3,67},{67,3},{4,68},{68... | collective-permute-start | bytes 3145736 | tf_op jit(solution)/shard_map/ppermute | solution.py:46
  132.4 34.8 %copy-start.5 = (bf16[2,4096]{1,0:T(2,128)(2,1)S(1)}, bf16[2,4096]{1,0:T(2,128)(2,1)}, u32[]{:S(2)}) copy-start(bf16[2,4096]{1,0:T(2,128)(2,1)} %states_ref.1) | copy-start | bytes 49156
  132.4 34.8 %copy-start.8 = (bf16[4096]{0:T(1024)(128)(2,1)S(1)}, bf16[4096]{0:T(1024)(128)(2,1)}, u32[]{:S(2)}) copy-start(bf16[4096]{0:T(1024)(128)(2,1)} %param.16) | copy-start | bytes 24580
  167.2 25.3 %copy-start.1 = (bf16[4096,112]{0,1:T(8,128)(2,1)S(1)}, bf16[4096,112]{0,1:T(8,128)(2,1)}, u32[]{:S(2)}) copy-start(bf16[4096,112]{0,1:T(8,128)(2,1)} %param.20) | copy-start | bytes 2752516
  167.2 25.3 %copy-start.2 = (bf16[4096,112]{0,1:T(8,128)(2,1)S(1)}, bf16[4096,112]{0,1:T(8,128)(2,1)}, u32[]{:S(2)}) copy-start(bf16[4096,112]{0,1:T(8,128)(2,1)} %param.21) | copy-start | bytes 2752516
  167.2 25.3 %collective-permute-start.21 = (bf16[64,32,512]{2,1,0:T(8,128)(2,1)S(1)}, bf16[64,32,512]{2,1,0:T(8,128)(2,1)S(1)}, u32[]{:S(2)}, u32[]{:S(2)}) collective-permute-start(bf16[64,32,512]{2,1,0:T(8,128)(2,1)S(1)} %all_to_all.25.blocks_ref.own_ref), channel_id=1, source_target_pairs={{0,64},{64,0},{1,65},{65,1},{2,66},{66,2},{3,67},{67,3},{4,68},{68... | collective-permute-start | bytes 6291464 | tf_op jit(solution)/shard_map/ppermute | solution.py:46
  192.5 4.6 %collective-permute-start.20 = (bf16[64,16,512]{2,1,0:T(8,128)(2,1)S(1)}, bf16[64,16,512]{2,1,0:T(8,128)(2,1)S(1)}, u32[]{:S(2)}, u32[]{:S(2)}) collective-permute-start(bf16[64,16,512]{2,1,0:T(8,128)(2,1)S(1)} %all_to_all.26.blocks_ref), channel_id=1, source_target_pairs={{0,64},{64,0},{1,65},{65,1},{2,66},{66,2},{3,67},{67,3},{4,68},{68... | collective-permute-start | bytes 3145736 | tf_op jit(solution)/shard_map/ppermute | solution.py:46
  198.9 2.9 %collective-permute-start.22 = (bf16[128,4096]{1,0:T(8,128)(2,1)S(1)}, bf16[128,4096]{1,0:T(8,128)(2,1)S(1)}, u32[]{:S(2)}, u32[]{:S(2)}) collective-permute-start(bf16[128,4096]{1,0:T(8,128)(2,1)S(1)} %ffn_grad.3), channel_id=1, source_target_pairs={{0,64},{64,0},{1,65},{65,1},{2,66},{66,2},{3,67},{67,3},{4,68},{68... | collective-permute-start | bytes 3145736 | tf_op jit(solution)/shard_map/ppermute | solution.py:46
  204.0 24.3 %all-to-all-start.4 = ((bf16[64,16,512]{2,1,0:T(8,128)(2,1)}), bf16[64,16,512]{2,1,0:T(8,128)(2,1)S(1)}, u32[]{:S(2)}, u32[]{:S(2)}) async-start(bf16[64,16,512]{2,1,0:T(8,128)(2,1)} %join.5), calls=%async_computation.4 | async-start | bytes 2097152 | tf_op jit(solution)/shard_map/all_to_all | solution.py:50
  (5 other events, 10.3 us)

commit v13 on v12

--- a/solution.py
+++ b/solution.py
@@ -634,9 +634,10 @@
         came = (along(first, "z", mask), along(second, "x", mask))
         bits = (jnp.stack([z, x]) >> bit) & 1
         first, second = in_pairs(bits, (first, came[0], second, came[1]))
-    came = [along(first, "x", 1), along(first, "x", 3), along(second, "z", 1), along(second, "z", 3)]
     place = jnp.stack([core, device]).astype(jnp.int32)
     own, send = pick_part(place, token_ids.reshape(1, 256), student_head_t)
+    send, first, second = lax.optimization_barrier((send, first, second))
+    came = [along(first, "x", 1), along(first, "x", 3), along(second, "z", 1), along(second, "z", 3)]
     came, picked = lax.optimization_barrier((came, join_part(own, swap_cores(send))))
     halves = halves_of(came)
     far = [

time: 230 us -> 229 us (level)
  transfers between devices with their start and end apart: 26 -> 26, of which waited for: 17 -> 18; matrix products, arithmetic and copies ran while one was open for 1% -> 1% of each run, Pallas kernels for 14% -> 13%
where the time goes in v13:
time: 229 us; the launch traced here: 228 us
  waiting for transfers between devices  68.5 us (30%)
  blocking collectives  59.7 us (26%)
  Pallas kernels  48.1 us (21%)
  starting transfers between devices  46.8 us (20%)
  local copies, waits for them, and re-layouts  3.29 us (1%)
    all_to_all x2, blocking collectives, exchange(): return lax.all_to_all(blocks, axes, split_axis=0, concat_axis=0, tiled=True)  59.7 us
    ppermute x14, waiting for transfers between devices, along(): return lax.ppermute(block, line, [(i, i ^ mask) for i in range(4)])  34.5 us
    all_to_all x3, waiting for transfers between devices, exchange(): return lax.all_to_all(blocks, axes, split_axis=0, concat_axis=0, tiled=True)  28 us
    all_to_all x3, starting transfers between devices, exchange(): return lax.all_to_all(blocks, axes, split_axis=0, concat_axis=0, tiled=True)  23.4 us
    ppermute x14, starting transfers between devices, along(): return lax.ppermute(block, line, [(i, i ^ mask) for i in range(4)])  21.9 us
    pallas_call x2, Pallas kernels, logits_part(): kernel_call(functools.partial(logits_kernel, last), 'logits', out_shape,...  18.1 us
    pallas_call x3, Pallas kernels, ffn_part(): kernel_call(body, name, out_shape, limit=20, in_specs=[VMEM] * len(operan...  6.29 us
    ppermute x9, waiting for transfers between devices, swap_cores(): return lax.ppermute(values, 'core', [(0, 1), (1, 0)])  5.98 us
  transfers between devices with their start and end apart: 26, of which 18 were waited for; matrix products, arithmetic and copies ran while one was open for 1% of the time, Pallas kernels for 13%

profile of v13, /device:TPU:0, one launch (start us, length us, event | category | flops | bytes accessed | tf_op | source)
XLA Modules:
  0.0 228.3 jit_solution(13180747708870463991)
XLA Ops:
  0.6 1.9 rows.1
  4.9 1.7 collective-permute-start.1
  6.6 2.9 %collective-permute-done.1.came_ref = bf16[4,10240]{1,0:T(4,128)(2,1)S(1)} collective-permute-done((bf16[4,10240]{1,0:T(4,128)(2,1)S(1)}, bf16[4,10240]{1,0:T(4,128)(2,1)S(1)}, u32[]{:S(2)}, u32[]{:S(2)}) %collective-permute-start.1) | collective-permute-done | bytes 81952 | tf_op jit(solution)/shard_map/ppermute | solution.py:165
  9.5 3.2 %collective-permute-start.2 = (bf16[8,10240]{1,0:T(8,128)(2,1)S(1)}, bf16[8,10240]{1,0:T(8,128)(2,1)S(1)}, u32[]{:S(2)}, u32[]{:S(2)}) collective-permute-start(bf16[8,10240]{1,0:T(8,128)(2,1)S(1)} %pair.4.own_ref), channel_id=1, source_target_pairs={{0,9},{1,8},{8,1},{9,0},{2,11},{3,10},{10,3},{11,2},{4,13},{5,12},... | collective-permute-start | bytes 491528 | tf_op jit(solution)/shard_map/ppermute | solution.py:165
  12.7 3.7 %collective-permute-done.2.came_ref = bf16[8,10240]{1,0:T(8,128)(2,1)S(1)} collective-permute-done((bf16[8,10240]{1,0:T(8,128)(2,1)S(1)}, bf16[8,10240]{1,0:T(8,128)(2,1)S(1)}, u32[]{:S(2)}, u32[]{:S(2)}) %collective-permute-start.2) | collective-permute-done | bytes 163872 | tf_op jit(solution)/shard_map/ppermute | solution.py:165
  16.5 2.0 collective-permute-start.3
  20.0 1.8 collective-permute-done.3.refs_1_
  21.9 1.9 collective-permute-done.4.refs_3_
  25.2 2.6 %collective-permute-start.5 = (bf16[32,5120]{1,0:T(8,128)(2,1)S(1)}, bf16[32,5120]{1,0:T(8,128)(2,1)S(1)}, u32[]{:S(2)}, u32[]{:S(2)}) collective-permute-start(bf16[32,5120]{1,0:T(8,128)(2,1)S(1)} %get-tuple-element.55.refs_0_), channel_id=1, source_target_pairs={{0,6},{2,4},{4,2},{6,0},{1,7},{3,5},{5,3},{7,1},{8,14},{10,12},{12... | collective-permute-start | bytes 983048 | tf_op jit(solution)/shard_map/ppermute | solution.py:165
  27.9 2.8 %collective-permute-start.6 = (bf16[32,5120]{1,0:T(8,128)(2,1)S(1)}, bf16[32,5120]{1,0:T(8,128)(2,1)S(1)}, u32[]{:S(2)}, u32[]{:S(2)}) collective-permute-start(bf16[32,5120]{1,0:T(8,128)(2,1)S(1)} %get-tuple-element.56.refs_2_), channel_id=1, source_target_pairs={{0,48},{16,32},{32,16},{48,0},{1,49},{17,33},{33,17},{49,1},{2,50}... | collective-permute-start | bytes 983048 | tf_op jit(solution)/shard_map/ppermute | solution.py:165
  31.4 3.6 %pick.1 = (bf16[128,4096]{1,0:T(8,128)(2,1)S(1)}, bf16[128,4096]{1,0:T(8,128)(2,1)S(1)}) custom-call(s32[2]{0:T(128)S(1)} %pad_add_fusion.place_ref, s32[1,256]{1,0:T(1,128)S(1)} %bitcast.26, bf16[501,4096]{1,0:T(8,128)(2,1)} %bitcast.29), custom_call_target="tpu_custom_call" | custom-call | flops 1 | bytes 1 | tf_op jit(solution)/shard_map/pick/pallas_call | solution.py:408
  38.8 2.1 collective-permute-start.8
  42.6 13.0 %collective-permute-done.10.refs_3_.refs_2_ = bf16[64,5120]{1,0:T(8,128)(2,1)S(1)} collective-permute-done((bf16[64,5120]{1,0:T(8,128)(2,1)S(1)}, bf16[64,5120]{1,0:T(8,128)(2,1)S(1)}, u32[]{:S(2)}, u32[]{:S(2)}) %collective-permute-start.10) | collective-permute-done | bytes 655392 | tf_op jit(solution)/shard_map/ppermute | solution.py:165
  57.8 1.6 collective-permute-start.12
  59.4 2.5 %collective-permute-start.14 = (bf16[32,5120]{1,0:T(8,128)(2,1)S(1)}, bf16[32,5120]{1,0:T(8,128)(2,1)S(1)}, u32[]{:S(2)}, u32[]{:S(2)}) collective-permute-start(bf16[32,5120]{1,0:T(8,128)(2,1)S(1)} %get-tuple-element.69), channel_id=1, source_target_pairs={{0,6},{2,4},{4,2},{6,0},{1,7},{3,5},{5,3},{7,1},{8,14},{10,12},{12... | collective-permute-start | bytes 983048 | tf_op jit(solution)/shard_map/ppermute | solution.py:165
  61.9 5.7 %collective-permute-done.12.refs_3_ = bf16[32,5120]{1,0:T(8,128)(2,1)S(1)} collective-permute-done((bf16[32,5120]{1,0:T(8,128)(2,1)S(1)}, bf16[32,5120]{1,0:T(8,128)(2,1)S(1)}, u32[]{:S(2)}, u32[]{:S(2)}) %collective-permute-start.12) | collective-permute-done | bytes 327712 | tf_op jit(solution)/shard_map/ppermute | solution.py:165
  71.2 2.4 %whole.2.refs_0_ = bf16[256,5120]{1,0:T(8,128)(2,1)} custom-call(s32[1]{0:T(128)} %bitcast.1.place_ref, bf16[64,5120]{1,0:T(8,128)(2,1)S(1)} %get-tuple-element.59.refs_0_, bf16[64,5120]{1,0:T(8,128)(2,1)S(1)} %collective-permute-done.7.refs_0_.refs_1_, bf16[64,5120]{1,0:T(8,128)(2,1)S(1)} %collective-permute-done.8.refs_1_.refs_2_, ...), custom_call_target="tpu_custom_call" | custom-call | flops 1 | bytes 1 | tf_op jit(solution)/shard_map/whole/pallas_call | solution.py:185
  74.2 8.7 %all-to-all-start = ((bf16[64,16,512]{2,1,0:T(8,128)(2,1)}), bf16[64,16,512]{2,1,0:T(8,128)(2,1)}, u32[]{:S(2)}, u32[]{:S(2)}) async-start(bf16[64,16,512]{2,1,0:T(8,128)(2,1)} %copy-done.3), calls=%async_computation | async-start | bytes 2097152 | tf_op jit(solution)/shard_map/all_to_all | solution.py:50
  82.8 8.7 %logits.2 = (f32[501,256]{1,0:T(8,128)S(1)}, f32[501,256]{1,0:T(8,128)S(1)}, f32[501,256]{1,0:T(8,128)S(1)}) custom-call(s32[1]{0:T(128)} %bitcast.core_ref.place_ref, bf16[256,5120]{1,0:T(8,128)(2,1)} %whole.2.refs_0_, bf16[256,5120]{1,0:T(8,128)(2,1)} %copy-done, bf16[501,4096]{1,0:T(8,128)(2,1)} %bitcast.30, bf16[501,16384]{1,0:T(8,128)(2,1)} %bitcast.27), custom_call_target="tpu_custom_call" | custom-call | flops 1 | bytes 1 | tf_op jit(solution)/shard_map/logits/pallas_call | solution.py:290
  91.6 9.3 %logits.3 = (f32[501,256]{1,0:T(8,128)S(1)}, f32[501,256]{1,0:T(8,128)S(1)}, f32[8,128]{1,0:T(8,128)S(1)}) custom-call(s32[1]{0:T(128)S(6)} %sub.3.place_ref, bf16[256,5120]{1,0:T(8,128)(2,1)} %collective-permute-done.16.refs_0_, bf16[256,5120]{1,0:T(8,128)(2,1)} %collective-permute-done.17.refs_1_, bf16[501,4096]{1,0:T(8,128)(2,1)} %bitcast.31, ...), custom_call_target="tpu_custom_call" | custom-call | flops 1 | bytes 1 | tf_op jit(solution)/shard_map/logits/pallas_call | solution.py:290
  102.9 10.1 %all-to-all-start.1 = ((f32[64,8,128]{2,1,0:T(8,128)}), f32[64,8,128]{2,1,0:T(8,128)S(1)}, u32[]{:S(2)}, u32[]{:S(2)}) async-start(f32[64,8,128]{2,1,0:T(8,128)} %chip_stats.1), calls=%async_computation.1 | async-start | bytes 524288 | tf_op jit(solution)/shard_map/all_to_all | solution.py:50
  113.4 10.5 %all-to-all-done.1.every_ref = f32[64,8,128]{2,1,0:T(8,128)S(1)} async-done(((f32[64,8,128]{2,1,0:T(8,128)}), f32[64,8,128]{2,1,0:T(8,128)S(1)}, u32[]{:S(2)}, u32[]{:S(2)}) %all-to-all-start.1) | async-done | bytes 262176 | tf_op jit(solution)/shard_map/all_to_all | solution.py:50
  123.9 3.4 %row_grad.1 = (f32[128,4096]{1,0:T(8,128)S(1)}, bf16[128,4096]{1,0:T(8,128)(2,1)S(1)}, f32[1,256]{1,0:T(1,128)S(1)}) custom-call(s32[1]{0:T(128)} %bitcast.core_ref.place_ref, f32[64,8,128]{2,1,0:T(8,128)S(1)} %all-to-all-done.1.every_ref, f32[1,256]{1,0:T(1,128)S(1)} %reshape.45.weight_ref, f32[501,256]{1,0:T(8,128)S(1)} %get-tuple-element.84.teacher_ref, ...), custom_call_target="tpu_custom_call" | custom-call | flops 1 | bytes 1 | tf_op jit(solution)/shard_map/row_grad/pallas_call | solution.py:369
  131.4 34.8 %all_to_all.25.blocks_ref.own_ref = bf16[64,32,512]{2,1,0:T(8,128)(2,1)S(1)} all-to-all(bf16[64,32,512]{2,1,0:T(8,128)(2,1)S(1)} %join.4), channel_id=1, replica_groups=mesh['core'=2,'x'=4,'yh'=2,'z'=4,'yl'=2] {'x','yh','z','yl'}, dimensions={0} | all-to-all | bytes 4194304 | tf_op jit(solution)/shard_map/all_to_all | solution.py:50
  166.6 24.9 %all_to_all.26.blocks_ref = bf16[64,16,512]{2,1,0:T(8,128)(2,1)S(1)} all-to-all(bf16[64,16,512]{2,1,0:T(8,128)(2,1)S(1)} %get-tuple-element.91), channel_id=1, replica_groups=mesh['core'=2,'x'=4,'yh'=2,'z'=4,'yl'=2] {'x','yh','z','yl'}, dimensions={0} | all-to-all | bytes 2097152 | tf_op jit(solution)/shard_map/all_to_all | solution.py:50
  191.6 2.8 %gate_upper.1 = (f32[224,128]{1,0:T(8,128)S(1)}, f32[224,128]{1,0:T(8,128)S(1)}) custom-call(bf16[64,32,512]{2,1,0:T(8,128)(2,1)S(1)} %all_to_all.25.blocks_ref.own_ref, bf16[64,32,512]{2,1,0:T(8,128)(2,1)S(1)} %collective-permute-done.21.other_ref, bf16[112,4096]{1,0:T(8,128)(2,1)S(1)} %bitcast.16, bf16[112,4096]{1,0:T(8,128)(2,1)S(1)} %bitcast.19), custom_call_target="tpu_custom_call" | custom-call | flops 1 | bytes 1 | tf_op jit(solution)/shard_map/gate_upper/pallas_call | solution.py:575
  194.4 1.8 ffn_grad.2.own_ref
  196.1 1.8 ffn_grad.3
  198.5 2.3 %collective-permute-done.22.came_ref = bf16[128,4096]{1,0:T(8,128)(2,1)S(1)} collective-permute-done((bf16[128,4096]{1,0:T(8,128)(2,1)S(1)}, bf16[128,4096]{1,0:T(8,128)(2,1)S(1)}, u32[]{:S(2)}, u32[]{:S(2)}) %collective-permute-start.22) | collective-permute-done | bytes 1048608 | tf_op jit(solution)/shard_map/ppermute | solution.py:46
  200.8 2.3 %join.5 = bf16[64,16,512]{2,1,0:T(8,128)(2,1)} custom-call(f32[128,4096]{1,0:T(8,128)S(1)} %ffn_grad.2.own_ref, bf16[128,4096]{1,0:T(8,128)(2,1)S(1)} %collective-permute-done.22.came_ref), custom_call_target="tpu_custom_call" | custom-call | flops 1 | bytes 1 | tf_op jit(solution)/shard_map/join/pallas_call | solution.py:443
  203.0 4.7 %all-to-all-start.4 = ((bf16[64,16,512]{2,1,0:T(8,128)(2,1)}), bf16[64,16,512]{2,1,0:T(8,128)(2,1)S(1)}, u32[]{:S(2)}, u32[]{:S(2)}) async-start(bf16[64,16,512]{2,1,0:T(8,128)(2,1)} %join.5), calls=%async_computation.4 | async-start | bytes 2097152 | tf_op jit(solution)/shard_map/all_to_all | solution.py:50
  209.8 17.5 %all-to-all-done.4.blocks_ref = bf16[64,16,512]{2,1,0:T(8,128)(2,1)S(1)} async-done(((bf16[64,16,512]{2,1,0:T(8,128)(2,1)}), bf16[64,16,512]{2,1,0:T(8,128)(2,1)S(1)}, u32[]{:S(2)}, u32[]{:S(2)}) %all-to-all-start.4) | async-done | bytes 1048608 | tf_op jit(solution)/shard_map/all_to_all | solution.py:50
  (78 shorter events, 28.5 us)
Async XLA Ops:
  2.5 1.5 collective-permute-start
  4.9 4.6 %collective-permute-start.1 = (bf16[4,10240]{1,0:T(4,128)(2,1)S(1)}, bf16[4,10240]{1,0:T(4,128)(2,1)S(1)}, u32[]{:S(2)}, u32[]{:S(2)}) collective-permute-start(bf16[4,10240]{1,0:T(4,128)(2,1)S(1)} %pair.3.own_ref), channel_id=1, source_target_pairs={{0,1},{1,0},{8,9},{9,8},{2,3},{3,2},{10,11},{11,10},{4,5},{5,4},{1... | collective-permute-start | bytes 245768 | tf_op jit(solution)/shard_map/ppermute | solution.py:165
  9.5 6.9 %collective-permute-start.2 = (bf16[8,10240]{1,0:T(8,128)(2,1)S(1)}, bf16[8,10240]{1,0:T(8,128)(2,1)S(1)}, u32[]{:S(2)}, u32[]{:S(2)}) collective-permute-start(bf16[8,10240]{1,0:T(8,128)(2,1)S(1)} %pair.4.own_ref), channel_id=1, source_target_pairs={{0,9},{1,8},{8,1},{9,0},{2,11},{3,10},{10,3},{11,2},{4,13},{5,12},... | collective-permute-start | bytes 491528 | tf_op jit(solution)/shard_map/ppermute | solution.py:165
  16.5 5.4 %collective-permute-start.3 = (bf16[16,5120]{1,0:T(8,128)(2,1)S(1)}, bf16[16,5120]{1,0:T(8,128)(2,1)S(1)}, u32[]{:S(2)}, u32[]{:S(2)}) collective-permute-start(bf16[16,5120]{1,0:T(8,128)(2,1)S(1)} %get-tuple-element.53.refs_0_), channel_id=1, source_target_pairs={{0,2},{2,0},{4,6},{6,4},{1,3},{3,1},{5,7},{7,5},{8,10},{10,8},{12,... | collective-permute-start | bytes 491528 | tf_op jit(solution)/shard_map/ppermute | solution.py:165
  18.5 5.3 %collective-permute-start.4 = (bf16[16,5120]{1,0:T(8,128)(2,1)S(1)}, bf16[16,5120]{1,0:T(8,128)(2,1)S(1)}, u32[]{:S(2)}, u32[]{:S(2)}) collective-permute-start(bf16[16,5120]{1,0:T(8,128)(2,1)S(1)} %get-tuple-element.54.refs_2_), channel_id=1, source_target_pairs={{0,16},{16,0},{32,48},{48,32},{1,17},{17,1},{33,49},{49,33},{2,18}... | collective-permute-start | bytes 491528 | tf_op jit(solution)/shard_map/ppermute | solution.py:165
  25.2 9.8 %collective-permute-start.5 = (bf16[32,5120]{1,0:T(8,128)(2,1)S(1)}, bf16[32,5120]{1,0:T(8,128)(2,1)S(1)}, u32[]{:S(2)}, u32[]{:S(2)}) collective-permute-start(bf16[32,5120]{1,0:T(8,128)(2,1)S(1)} %get-tuple-element.55.refs_0_), channel_id=1, source_target_pairs={{0,6},{2,4},{4,2},{6,0},{1,7},{3,5},{5,3},{7,1},{8,14},{10,12},{12... | collective-permute-start | bytes 983048 | tf_op jit(solution)/shard_map/ppermute | solution.py:165
  27.9 8.3 %collective-permute-start.6 = (bf16[32,5120]{1,0:T(8,128)(2,1)S(1)}, bf16[32,5120]{1,0:T(8,128)(2,1)S(1)}, u32[]{:S(2)}, u32[]{:S(2)}) collective-permute-start(bf16[32,5120]{1,0:T(8,128)(2,1)S(1)} %get-tuple-element.56.refs_2_), channel_id=1, source_target_pairs={{0,48},{16,32},{32,16},{48,0},{1,49},{17,33},{33,17},{49,1},{2,50}... | collective-permute-start | bytes 983048 | tf_op jit(solution)/shard_map/ppermute | solution.py:165
  37.2 4.1 %collective-permute-start.11 = (bf16[128,4096]{1,0:T(8,128)(2,1)S(1)}, bf16[128,4096]{1,0:T(8,128)(2,1)S(1)}, u32[]{:S(2)}, u32[]{:S(2)}) collective-permute-start(bf16[128,4096]{1,0:T(8,128)(2,1)S(1)} %get-tuple-element.62), channel_id=1, source_target_pairs={{0,64},{64,0},{1,65},{65,1},{2,66},{66,2},{3,67},{67,3},{4,68},{68... | collective-permute-start | bytes 3145736 | tf_op jit(solution)/shard_map/ppermute | solution.py:46
  37.3 18.4 %collective-permute-start.10 = (bf16[64,5120]{1,0:T(8,128)(2,1)S(1)}, bf16[64,5120]{1,0:T(8,128)(2,1)S(1)}, u32[]{:S(2)}, u32[]{:S(2)}) collective-permute-start(bf16[64,5120]{1,0:T(8,128)(2,1)S(1)} %get-tuple-element.60.refs_0_), channel_id=1, source_target_pairs={{0,6},{2,4},{4,2},{6,0},{1,7},{3,5},{5,3},{7,1},{8,14},{10,12},{12... | collective-permute-start | bytes 1966088 | tf_op jit(solution)/shard_map/ppermute | solution.py:165
  38.0 17.6 %collective-permute-start.7 = (bf16[64,5120]{1,0:T(8,128)(2,1)S(1)}, bf16[64,5120]{1,0:T(8,128)(2,1)S(1)}, u32[]{:S(2)}, u32[]{:S(2)}) collective-permute-start(bf16[64,5120]{1,0:T(8,128)(2,1)S(1)} %get-tuple-element.59.refs_0_), channel_id=1, source_target_pairs={{0,16},{16,0},{32,48},{48,32},{1,17},{17,1},{33,49},{49,33},{2,18}... | collective-permute-start | bytes 1966088 | tf_op jit(solution)/shard_map/ppermute | solution.py:165
  38.8 17.7 %collective-permute-start.8 = (bf16[64,5120]{1,0:T(8,128)(2,1)S(1)}, bf16[64,5120]{1,0:T(8,128)(2,1)S(1)}, u32[]{:S(2)}, u32[]{:S(2)}) collective-permute-start(bf16[64,5120]{1,0:T(8,128)(2,1)S(1)} %get-tuple-element.59.refs_0_), channel_id=1, source_target_pairs={{0,48},{16,32},{32,16},{48,0},{1,49},{17,33},{33,17},{49,1},{2,50}... | collective-permute-start | bytes 1966088 | tf_op jit(solution)/shard_map/ppermute | solution.py:165
  40.9 16.4 %collective-permute-start.9 = (bf16[64,5120]{1,0:T(8,128)(2,1)S(1)}, bf16[64,5120]{1,0:T(8,128)(2,1)S(1)}, u32[]{:S(2)}, u32[]{:S(2)}) collective-permute-start(bf16[64,5120]{1,0:T(8,128)(2,1)S(1)} %get-tuple-element.60.refs_0_), channel_id=1, source_target_pairs={{0,2},{2,0},{4,6},{6,4},{1,3},{3,1},{5,7},{7,5},{8,10},{10,8},{12,... | collective-permute-start | bytes 1966088 | tf_op jit(solution)/shard_map/ppermute | solution.py:165
  42.6 28.6 %copy-start.3 = (bf16[64,16,512]{2,1,0:T(8,128)(2,1)}, bf16[64,16,512]{2,1,0:T(8,128)(2,1)S(1)}, u32[]{:S(2)}) copy-start(bf16[64,16,512]{2,1,0:T(8,128)(2,1)S(1)} %join.3) | copy-start | bytes 3145732
  57.8 9.8 %collective-permute-start.12 = (bf16[32,5120]{1,0:T(8,128)(2,1)S(1)}, bf16[32,5120]{1,0:T(8,128)(2,1)S(1)}, u32[]{:S(2)}, u32[]{:S(2)}) collective-permute-start(bf16[32,5120]{1,0:T(8,128)(2,1)S(1)} %get-tuple-element.67), channel_id=1, source_target_pairs={{0,48},{16,32},{32,16},{48,0},{1,49},{17,33},{33,17},{49,1},{2,50}... | collective-permute-start | bytes 983048 | tf_op jit(solution)/shard_map/ppermute | solution.py:165
  59.3 8.6 %collective-permute-start.13 = (bf16[32,5120]{1,0:T(8,128)(2,1)S(1)}, bf16[32,5120]{1,0:T(8,128)(2,1)S(1)}, u32[]{:S(2)}, u32[]{:S(2)}) collective-permute-start(bf16[32,5120]{1,0:T(8,128)(2,1)S(1)} %get-tuple-element.68), channel_id=1, source_target_pairs={{0,16},{16,0},{32,48},{48,32},{1,17},{17,1},{33,49},{49,33},{2,18}... | collective-permute-start | bytes 983048 | tf_op jit(solution)/shard_map/ppermute | solution.py:165
  59.4 9.8 %collective-permute-start.14 = (bf16[32,5120]{1,0:T(8,128)(2,1)S(1)}, bf16[32,5120]{1,0:T(8,128)(2,1)S(1)}, u32[]{:S(2)}, u32[]{:S(2)}) collective-permute-start(bf16[32,5120]{1,0:T(8,128)(2,1)S(1)} %get-tuple-element.69), channel_id=1, source_target_pairs={{0,6},{2,4},{4,2},{6,0},{1,7},{3,5},{5,3},{7,1},{8,14},{10,12},{12... | collective-permute-start | bytes 983048 | tf_op jit(solution)/shard_map/ppermute | solution.py:165
  61.9 8.4 %collective-permute-start.15 = (bf16[32,5120]{1,0:T(8,128)(2,1)S(1)}, bf16[32,5120]{1,0:T(8,128)(2,1)S(1)}, u32[]{:S(2)}, u32[]{:S(2)}) collective-permute-start(bf16[32,5120]{1,0:T(8,128)(2,1)S(1)} %get-tuple-element.70), channel_id=1, source_target_pairs={{0,2},{2,0},{4,6},{6,4},{1,3},{3,1},{5,7},{7,5},{8,10},{10,8},{12,... | collective-permute-start | bytes 983048 | tf_op jit(solution)/shard_map/ppermute | solution.py:165
  73.6 18.0 %collective-permute-start.16 = (bf16[256,5120]{1,0:T(8,128)(2,1)}, bf16[256,5120]{1,0:T(8,128)(2,1)}, u32[]{:S(2)}, u32[]{:S(2)}) collective-permute-start(bf16[256,5120]{1,0:T(8,128)(2,1)} %whole.2.refs_0_), channel_id=1, source_target_pairs={{0,64},{64,0},{1,65},{65,1},{2,66},{66,2},{3,67},{67,3},{4,68},{68... | collective-permute-start | bytes 7864328 | tf_op jit(solution)/shard_map/ppermute | solution.py:46
  73.7 17.9 %collective-permute-start.17 = (bf16[256,5120]{1,0:T(8,128)(2,1)S(1)}, bf16[256,5120]{1,0:T(8,128)(2,1)}, u32[]{:S(2)}, u32[]{:S(2)}) collective-permute-start(bf16[256,5120]{1,0:T(8,128)(2,1)S(1)} %whole.3.refs_1_), channel_id=1, source_target_pairs={{0,64},{64,0},{1,65},{65,1},{2,66},{66,2},{3,67},{67,3},{4,68},{68... | collective-permute-start | bytes 7864328 | tf_op jit(solution)/shard_map/ppermute | solution.py:46
  74.2 28.8 %all-to-all-start = ((bf16[64,16,512]{2,1,0:T(8,128)(2,1)}), bf16[64,16,512]{2,1,0:T(8,128)(2,1)}, u32[]{:S(2)}, u32[]{:S(2)}) async-start(bf16[64,16,512]{2,1,0:T(8,128)(2,1)} %copy-done.3), calls=%async_computation | async-start | bytes 2097152 | tf_op jit(solution)/shard_map/all_to_all | solution.py:50
  91.6 21.5 %copy-start.10 = (f32[256]{0:T(256)S(1)}, f32[256]{0:T(256)}, u32[]{:S(2)}) copy-start(f32[256]{0:T(256)} %param.23) | copy-start | bytes 3076
  101.0 1.2 collective-permute-start.18
  102.9 21.0 %all-to-all-start.1 = ((f32[64,8,128]{2,1,0:T(8,128)}), f32[64,8,128]{2,1,0:T(8,128)S(1)}, u32[]{:S(2)}, u32[]{:S(2)}) async-start(f32[64,8,128]{2,1,0:T(8,128)} %chip_stats.1), calls=%async_computation.1 | async-start | bytes 524288 | tf_op jit(solution)/shard_map/all_to_all | solution.py:50
  127.3 2.7 %collective-permute-start.19 = (bf16[128,4096]{1,0:T(8,128)(2,1)S(1)}, bf16[128,4096]{1,0:T(8,128)(2,1)S(1)}, u32[]{:S(2)}, u32[]{:S(2)}) collective-permute-start(bf16[128,4096]{1,0:T(8,128)(2,1)S(1)} %get-tuple-element.88), channel_id=1, source_target_pairs={{0,64},{64,0},{1,65},{65,1},{2,66},{66,2},{3,67},{67,3},{4,68},{68... | collective-permute-start | bytes 3145736 | tf_op jit(solution)/shard_map/ppermute | solution.py:46
  131.4 34.8 %copy-start.5 = (bf16[2,4096]{1,0:T(2,128)(2,1)S(1)}, bf16[2,4096]{1,0:T(2,128)(2,1)}, u32[]{:S(2)}) copy-start(bf16[2,4096]{1,0:T(2,128)(2,1)} %states_ref.1) | copy-start | bytes 49156
  131.4 34.8 %copy-start.8 = (bf16[4096]{0:T(1024)(128)(2,1)S(1)}, bf16[4096]{0:T(1024)(128)(2,1)}, u32[]{:S(2)}) copy-start(bf16[4096]{0:T(1024)(128)(2,1)} %param.16) | copy-start | bytes 24580
  166.2 25.3 %copy-start.1 = (bf16[4096,112]{0,1:T(8,128)(2,1)S(1)}, bf16[4096,112]{0,1:T(8,128)(2,1)}, u32[]{:S(2)}) copy-start(bf16[4096,112]{0,1:T(8,128)(2,1)} %param.20) | copy-start | bytes 2752516
  166.2 25.3 %copy-start.2 = (bf16[4096,112]{0,1:T(8,128)(2,1)S(1)}, bf16[4096,112]{0,1:T(8,128)(2,1)}, u32[]{:S(2)}) copy-start(bf16[4096,112]{0,1:T(8,128)(2,1)} %param.21) | copy-start | bytes 2752516
  166.2 25.3 %collective-permute-start.21 = (bf16[64,32,512]{2,1,0:T(8,128)(2,1)S(1)}, bf16[64,32,512]{2,1,0:T(8,128)(2,1)S(1)}, u32[]{:S(2)}, u32[]{:S(2)}) collective-permute-start(bf16[64,32,512]{2,1,0:T(8,128)(2,1)S(1)} %all_to_all.25.blocks_ref.own_ref), channel_id=1, source_target_pairs={{0,64},{64,0},{1,65},{65,1},{2,66},{66,2},{3,67},{67,3},{4,68},{68... | collective-permute-start | bytes 6291464 | tf_op jit(solution)/shard_map/ppermute | solution.py:46
  191.5 4.6 %collective-permute-start.20 = (bf16[64,16,512]{2,1,0:T(8,128)(2,1)S(1)}, bf16[64,16,512]{2,1,0:T(8,128)(2,1)S(1)}, u32[]{:S(2)}, u32[]{:S(2)}) collective-permute-start(bf16[64,16,512]{2,1,0:T(8,128)(2,1)S(1)} %all_to_all.26.blocks_ref), channel_id=1, source_target_pairs={{0,64},{64,0},{1,65},{65,1},{2,66},{66,2},{3,67},{67,3},{4,68},{68... | collective-permute-start | bytes 3145736 | tf_op jit(solution)/shard_map/ppermute | solution.py:46
  197.9 2.9 %collective-permute-start.22 = (bf16[128,4096]{1,0:T(8,128)(2,1)S(1)}, bf16[128,4096]{1,0:T(8,128)(2,1)S(1)}, u32[]{:S(2)}, u32[]{:S(2)}) collective-permute-start(bf16[128,4096]{1,0:T(8,128)(2,1)S(1)} %ffn_grad.3), channel_id=1, source_target_pairs={{0,64},{64,0},{1,65},{65,1},{2,66},{66,2},{3,67},{67,3},{4,68},{68... | collective-permute-start | bytes 3145736 | tf_op jit(solution)/shard_map/ppermute | solution.py:46
  203.0 24.3 %all-to-all-start.4 = ((bf16[64,16,512]{2,1,0:T(8,128)(2,1)}), bf16[64,16,512]{2,1,0:T(8,128)(2,1)S(1)}, u32[]{:S(2)}, u32[]{:S(2)}) async-start(bf16[64,16,512]{2,1,0:T(8,128)(2,1)} %join.5), calls=%async_computation.4 | async-start | bytes 2097152 | tf_op jit(solution)/shard_map/all_to_all | solution.py:50
  (5 other events, 10.3 us)
